TPU v7x, 32 devices: a whole 2x2x4 slice. The times are simulated.
32 devices in a mesh: sub: 8 (over z, x), col: 4 (over y, core).
Axes of the slice: x: 2, y: 2, z: 4, core: 2. Of those that a mesh axis runs over, the one named last changes fastest.
Arguments:
- trace_start: bfloat16 [8, 4, 1536, 128], P('sub', 'col'), may hold values from -6 to 6
- neumann_load: bfloat16 [8, 4, 1536, 128], P('sub', 'col'), may hold values from -6 to 6
- double_layer: bfloat16 [8, 4, 1536, 1536], P('sub', 'col'), may hold values from -0.15625 to 0.15625
- single_inverse: bfloat16 [8, 4, 1536, 1536], P('sub', 'col'), may hold values from -0.15625 to 0.15625
- interface_nodes: int32 [8, 4, 8, 128], P('sub', 'col'), may hold values from -1 to 1023, as said below
- node_mode: int32 [8, 4, 1536], P('sub', 'col'), may hold values from 0 to 63
- mode_weight: bfloat16 [8, 4, 1536], P('sub', 'col'), may hold values from 0.5 to 1.5
- coarse_inverse: bfloat16 [2048, 2048], P('sub', 'col'), may hold values from -0.015625 to 0.015625
Outputs:
- final_trace: bfloat16 [8, 4, 1536, 128], P('sub', 'col')
- final_residual: bfloat16 [8, 4, 1536, 128], P('sub', 'col')
Inputs may be any that keep to these rules, and one draw needn't show every extreme that they name: `interface_nodes`: entry k of block (s, d) is a boundary node of s, within nodes d * 128 to (d + 1) * 128 - 1, distinct within the block, and matches entry k of the neighbour's block for direction 7 - d; valid entries come first and the rest are -1; blocks toward outside the grid are all -1; blocks of directions 1, 3, 4, 6 have 128 / 2 to 128 valid entries, the others 1 to 16, and some block has 128.
All inputs are finite; a program needn't handle non-finite values.
Results may differ from a plain program's by a relative error of at most 0.019.
Values may be sent and summed in bfloat16 or wider, within the bound.
No kernel may reach another device: no remote copies, remote signals or barrier semaphores. Data moves between devices by JAX's collectives and lax.ppermute only.
A program may use at most 64 MiB of HBM per device.

v0:
```python
import jax
import jax.numpy as jnp
from jax import lax
from jax.sharding import PartitionSpec as P

MODES = 64
ITERS = 3


DIRECTIONS = ((-1, -1), (-1, 0), (-1, 1), (0, -1), (0, 1), (1, -1), (1, 0), (1, 1))


def from_behind(value, axis, by):
    devices = lax.axis_size(axis)
    pairs = [(i, i + by) for i in range(devices) if 0 <= i + by < devices]
    return lax.ppermute(value, axis, pairs)


def deliver_bundled(outgoing):
    after_col = {}
    for col_step in (-1, 1):
        members = [toward for toward in range(8) if DIRECTIONS[toward][1] == col_step]
        stacked = jnp.stack([outgoing[7 - toward] for toward in members])
        shifted = from_behind(stacked, "col", -col_step)
        for position, toward in enumerate(members):
            after_col[toward] = shifted[position]
    arrived = {3: after_col[3], 4: after_col[4]}
    for row_step in (-1, 1):
        members = [toward for toward in range(8) if DIRECTIONS[toward][0] == row_step]
        stacked = jnp.stack(
            [
                after_col[toward] if toward in after_col else outgoing[7 - toward]
                for toward in members
            ]
        )
        shifted = from_behind(stacked, "sub", -row_step)
        for position, toward in enumerate(members):
            arrived[toward] = shifted[position]
    return jnp.stack([arrived[toward] for toward in range(8)])


def local(
    trace_start,
    neumann_load,
    double_layer,
    single_inverse,
    interface_nodes,
    node_mode,
    mode_weight,
    coarse_inverse,
):
    trace_now = trace_start[0, 0]
    load_block = neumann_load[0, 0].astype(jnp.float32)
    kernel = double_layer[0, 0]
    inverse = single_inverse[0, 0]
    node_count = kernel.shape[0]
    interface = interface_nodes[0, 0]
    slot_count = interface.shape[1]
    band_rows = 8 * slot_count
    local_index = interface - (jnp.arange(8, dtype=jnp.int32) * slot_count)[:, None]
    selector = (
        local_index[:, :, None] == jnp.arange(slot_count, dtype=jnp.int32)[None, None, :]
    ).astype(jnp.bfloat16)
    mode_basis = jnp.where(
        node_mode[0, 0][None, :] == jnp.arange(MODES, dtype=jnp.int32)[:, None],
        mode_weight[0, 0][None, :],
        jnp.zeros((), jnp.bfloat16),
    )
    rhs_count = trace_now.shape[1]
    residual = trace_now
    rest_zeros = jnp.zeros((node_count - band_rows, rhs_count), jnp.float32)
    for iteration in range(ITERS):
        mixed_trace = (
            0.5 * trace_now.astype(jnp.float32)
            + jnp.dot(kernel, trace_now, preferred_element_type=jnp.float32)
        ).astype(jnp.bfloat16)
        flux_now = jnp.dot(inverse, mixed_trace, preferred_element_type=jnp.float32).astype(
            jnp.bfloat16
        )
        banded = flux_now[:band_rows].reshape(8, slot_count, rhs_count)
        outgoing = jnp.einsum(
            "dpq,dqr->dpr", selector, banded, preferred_element_type=jnp.float32
        ).astype(jnp.bfloat16)
        received = deliver_bundled(outgoing)
        placed = jnp.einsum(
            "dpq,dpr->dqr", selector, received, preferred_element_type=jnp.float32
        ).reshape(band_rows, rhs_count)
        assembled = flux_now.astype(jnp.float32) + jnp.concatenate([placed, rest_zeros], axis=0)
        residual = (load_block - assembled).astype(jnp.bfloat16)
        residual = lax.optimization_barrier(residual)
        coarse_rhs = jnp.dot(mode_basis, residual, preferred_element_type=jnp.float32).astype(
            jnp.bfloat16
        )
        partial_value = jnp.dot(
            coarse_inverse,
            lax.all_gather(coarse_rhs, "sub", axis=0, tiled=True),
            preferred_element_type=jnp.float32,
        )
        coarse_out = lax.psum_scatter(
            partial_value.astype(jnp.bfloat16), "col", scatter_dimension=0, tiled=True
        )
        correction = lax.dot_general(
            mode_basis, coarse_out, (((0,), (0,)), ((), ())), preferred_element_type=jnp.float32
        )
        trace_now = (
            trace_now.astype(jnp.float32) + 0.25 * residual.astype(jnp.float32) + correction
        ).astype(jnp.bfloat16)
    return (trace_now[None, None], residual[None, None])


def solution(mesh):
    placed = (
        P("sub", "col", None, None),
        P("sub", "col", None, None),
        P("sub", "col", None, None),
        P("sub", "col", None, None),
        P("sub", "col", None, None),
        P("sub", "col", None),
        P("sub", "col", None),
        P("sub", "col"),
    )
    return jax.shard_map(
        local,
        mesh=mesh,
        in_specs=placed,
        out_specs=(P("sub", "col", None, None), P("sub", "col", None, None)),
        check_vma=False,
    )
```

profile of v0, /device:TPU:0, one launch (start us, length us, event | category | flops | bytes accessed | tf_op | source)
XLA Modules:
  0.0 250.7 jit_solution(11415998356432885254)
XLA Ops:
  7.2 1.2 copy.26
  8.5 7.1 %fusion.54 = bf16[1536,128]{0,1:T(8,128)(2,1)S(1)} fusion(bf16[1,1,1536,1536]{3,2,1,0:T(8,128)(2,1)} %param.11, bf16[1,1,1536,1536]{3,2,1,0:T(8,128)(2,1)} %param.10, bf16[1,1,1536,128]{3,2,1,0:T(8,128)(2,1)} %param.8, bf16[1,1,1536,128]{2,3,1,0:T(8,128)(2,1)S(1)} %copy.26), kind=kOutput, calls=%fused_computation.31 | convolution fusion | flops 1208942592 | bytes 10616832 | tf_op jit(solution)/shard_map/dot_general | solution.py:77
  15.9 0.3 convolution_convert_fusion.2
  16.3 2.4 collective-permute-start
  18.7 1.3 collective-permute-start.1
  20.0 4.0 %collective-permute-done.1 = bf16[3,128,128]{2,1,0:T(8,128)(2,1)S(1)} collective-permute-done((bf16[3,128,128]{2,1,0:T(8,128)(2,1)S(1)}, bf16[3,128,128]{2,1,0:T(8,128)(2,1)S(1)}, u32[]{:S(2)}, u32[]{:S(2)}) %collective-permute-start.1) | collective-permute-done | bytes 98336 | tf_op jit(solution)/shard_map/ppermute | solution.py:16
  24.0 1.3 collective-permute-start.3
  25.4 4.6 %collective-permute-start.2 = (bf16[3,128,128]{2,1,0:T(8,128)(2,1)S(1)}, bf16[3,128,128]{2,1,0:T(8,128)(2,1)S(1)}, u32[]{:S(2)}, u32[]{:S(2)}) collective-permute-start(bf16[3,128,128]{2,1,0:T(8,128)(2,1)S(1)} %pad_maximum_fusion.2), channel_id=1, source_target_pairs={{0,4},{4,8},{8,12},{12,16},{16,20},{20,24},{24,28},{1,5},{5,9},{9,... | collective-permute-start | bytes 294920 | tf_op jit(solution)/shard_map/ppermute | solution.py:16
  30.2 0.4 collective-permute-done.3
  30.5 2.6 %collective-permute-done.2 = bf16[3,128,128]{2,1,0:T(8,128)(2,1)S(1)} collective-permute-done((bf16[3,128,128]{2,1,0:T(8,128)(2,1)S(1)}, bf16[3,128,128]{2,1,0:T(8,128)(2,1)S(1)}, u32[]{:S(2)}, u32[]{:S(2)}) %collective-permute-start.2) | collective-permute-done | bytes 98336 | tf_op jit(solution)/shard_map/ppermute | solution.py:16
  33.7 0.2 convolution_convert_fusion.8
  33.9 32.6 %all_gather.9 = bf16[512,128]{1,0:T(8,128)(2,1)S(1)} all-gather(bf16[64,128]{1,0:T(8,128)(2,1)S(1)} %convolution_convert_fusion.8), channel_id=1, replica_groups=mesh['sub'=8,'col'=4] {'sub'}, dimensions={0}, use_global_device_ids=true | all-gather | bytes 147456 | tf_op jit(solution)/shard_map/all_gather | solution.py:96
  66.5 0.2 fusion.58
  66.7 0.7 copy.54
  67.5 20.2 %reduce-scatter.10.cloned.1.call-done = bf16[64,128]{1,0:T(8,128)(2,1)} async-done(((bf16[256,128]{1,0:T(8,128)(2,1)}), bf16[64,128]{1,0:T(8,128)(2,1)}) %reduce-scatter.10.cloned.1.call-update) | async-done | bytes 16400
  87.7 1.0 fusion.27
  88.7 6.9 %fusion.51 = bf16[1536,128]{0,1:T(8,128)(2,1)S(1)} fusion(bf16[1,1,1536,1536]{3,2,1,0:T(8,128)(2,1)} %param.11, bf16[1536,128]{0,1:T(8,128)(2,1)S(1)} %fusion.27, bf16[1,1,1536,1536]{3,2,1,0:T(8,128)(2,1)} %param.10), kind=kOutput, calls=%fused_computation.30 | convolution fusion | flops 1208942592 | bytes 10223616 | tf_op jit(solution)/shard_map/dot_general | solution.py:77
  95.8 0.3 convolution_convert_fusion.1
  96.2 1.3 collective-permute-start.4
  97.6 1.3 collective-permute-start.5
  98.9 2.3 collective-permute-done.5
  101.2 1.3 collective-permute-start.7
  102.5 4.6 %collective-permute-start.6 = (bf16[3,128,128]{2,1,0:T(8,128)(2,1)S(1)}, bf16[3,128,128]{2,1,0:T(8,128)(2,1)S(1)}, u32[]{:S(2)}, u32[]{:S(2)}) collective-permute-start(bf16[3,128,128]{2,1,0:T(8,128)(2,1)S(1)} %pad_maximum_fusion.6), channel_id=1, source_target_pairs={{0,4},{4,8},{8,12},{12,16},{16,20},{20,24},{24,28},{1,5},{5,9},{9,... | collective-permute-start | bytes 294920 | tf_op jit(solution)/shard_map/ppermute | solution.py:16
  107.1 0.6 collective-permute-done.7
  107.7 1.6 collective-permute-done.6
  109.8 0.2 convolution_convert_fusion.7
  110.1 33.7 %all_gather.10 = bf16[512,128]{1,0:T(8,128)(2,1)S(1)} all-gather(bf16[64,128]{1,0:T(8,128)(2,1)S(1)} %convolution_convert_fusion.7), channel_id=1, replica_groups=mesh['sub'=8,'col'=4] {'sub'}, dimensions={0}, use_global_device_ids=true | all-gather | bytes 147456 | tf_op jit(solution)/shard_map/all_gather | solution.py:96
  143.8 0.2 fusion.59
  144.1 0.7 copy.56
  144.9 20.1 %reduce-scatter.12.cloned.1.call-done = bf16[64,128]{1,0:T(8,128)(2,1)} async-done(((bf16[256,128]{1,0:T(8,128)(2,1)}), bf16[64,128]{1,0:T(8,128)(2,1)}) %reduce-scatter.12.cloned.1.call-update) | async-done | bytes 16400
  165.0 1.0 fusion.28
  166.0 6.9 %fusion.48 = bf16[1536,128]{0,1:T(8,128)(2,1)S(1)} fusion(bf16[1,1,1536,1536]{3,2,1,0:T(8,128)(2,1)} %param.11, bf16[1536,128]{0,1:T(8,128)(2,1)S(1)} %fusion.28, bf16[1,1,1536,1536]{3,2,1,0:T(8,128)(2,1)} %param.10), kind=kOutput, calls=%fused_computation.29 | convolution fusion | flops 1208942592 | bytes 10223616 | tf_op jit(solution)/shard_map/dot_general | solution.py:77
  173.1 0.3 convolution_convert_fusion
  173.5 1.3 collective-permute-start.8
  174.8 1.3 collective-permute-start.9
  176.2 2.3 collective-permute-done.9
  178.5 1.3 collective-permute-start.11
  179.8 4.6 %collective-permute-start.10 = (bf16[3,128,128]{2,1,0:T(8,128)(2,1)S(1)}, bf16[3,128,128]{2,1,0:T(8,128)(2,1)S(1)}, u32[]{:S(2)}, u32[]{:S(2)}) collective-permute-start(bf16[3,128,128]{2,1,0:T(8,128)(2,1)S(1)} %pad_maximum_fusion.10), channel_id=1, source_target_pairs={{0,4},{4,8},{8,12},{12,16},{16,20},{20,24},{24,28},{1,5},{5,9},{9,... | collective-permute-start | bytes 294920 | tf_op jit(solution)/shard_map/ppermute | solution.py:16
  184.3 0.6 collective-permute-done.11
  185.0 1.6 collective-permute-done.10
  187.1 0.2 convolution_convert_fusion.6
  187.3 33.8 %all_gather.11 = bf16[512,128]{1,0:T(8,128)(2,1)S(1)} all-gather(bf16[64,128]{1,0:T(8,128)(2,1)S(1)} %convolution_convert_fusion.6), channel_id=1, replica_groups=mesh['sub'=8,'col'=4] {'sub'}, dimensions={0}, use_global_device_ids=true | all-gather | bytes 147456 | tf_op jit(solution)/shard_map/all_gather | solution.py:96
  221.1 0.2 fusion.60
  221.4 0.7 copy.58
  222.1 0.9 copy.41
  223.0 19.2 %reduce-scatter.14.cloned.1.call-done = bf16[64,128]{1,0:T(8,128)(2,1)} async-done(((bf16[256,128]{1,0:T(8,128)(2,1)}), bf16[64,128]{1,0:T(8,128)(2,1)}) %reduce-scatter.14.cloned.1.call-update) | async-done | bytes 16400
  242.3 1.0 fusion.57
  243.3 0.9 copy.40
  (60 shorter events, 3.0 us)
Async XLA Ops:
  7.2 59.3 %copy-start = (bf16[256,512]{1,0:T(8,128)(2,1)S(1)}, bf16[256,512]{1,0:T(8,128)(2,1)}, u32[]{:S(2)}) copy-start(bf16[256,512]{1,0:T(8,128)(2,1)} %param.15) | copy-start | bytes 786436
  7.2 80.5 %reduce-scatter.10.cloned.1.call-start = ((), (), s32[]{:S(2)}) async-start(), calls=%async_computation.3 | async-start | bytes 81920
  8.4 7.4 %copy-start.4 = (s32[1,1,8,128]{3,2,1,0:T(8,128)S(1)}, s32[1,1,8,128]{3,2,1,0:T(8,128)}, u32[]{:S(2)}) copy-start(s32[1,1,8,128]{3,2,1,0:T(8,128)} %param.12) | copy-start | bytes 12292
  8.5 21.5 %copy-start.1 = (bf16[1,1,1536,128]{3,2,1,0:T(8,128)(2,1)S(1)}, bf16[1,1,1536,128]{3,2,1,0:T(8,128)(2,1)}, u32[]{:S(2)}) copy-start(bf16[1,1,1536,128]{3,2,1,0:T(8,128)(2,1)} %param.9) | copy-start | bytes 1179652
  8.5 21.6 %copy-start.2 = (bf16[1,1,1536]{2,1,0:T(2,128)(2,1)S(1)}, bf16[1,1,1536]{2,1,0:T(2,128)(2,1)}, u32[]{:S(2)}) copy-start(bf16[1,1,1536]{2,1,0:T(2,128)(2,1)} %param.14) | copy-start | bytes 9220
  8.5 21.7 %copy-start.3 = (s32[1,1,1536]{2,1,0:T(1,128)S(1)}, s32[1,1,1536]{2,1,0:T(1,128)}, u32[]{:S(2)}) copy-start(s32[1,1,1536]{2,1,0:T(1,128)} %param.13) | copy-start | bytes 18436
  16.3 3.7 %collective-permute-start = (bf16[3,128,128]{2,1,0:T(8,128)(2,1)S(1)}, bf16[3,128,128]{2,1,0:T(8,128)(2,1)S(1)}, u32[]{:S(2)}, u32[]{:S(2)}) collective-permute-start(bf16[3,128,128]{2,1,0:T(8,128)(2,1)S(1)} %pad_maximum_fusion), channel_id=1, source_target_pairs={{0,1},{1,2},{2,3},{4,5},{5,6},{6,7},{8,9},{9,10},{10,11},{12,13},{... | collective-permute-start | bytes 294920 | tf_op jit(solution)/shard_map/ppermute | solution.py:16
  18.7 5.3 %collective-permute-start.1 = (bf16[3,128,128]{2,1,0:T(8,128)(2,1)S(1)}, bf16[3,128,128]{2,1,0:T(8,128)(2,1)S(1)}, u32[]{:S(2)}, u32[]{:S(2)}) collective-permute-start(bf16[3,128,128]{2,1,0:T(8,128)(2,1)S(1)} %pad_maximum_fusion.1), channel_id=1, source_target_pairs={{1,0},{2,1},{3,2},{5,4},{6,5},{7,6},{9,8},{10,9},{11,10},{13,12},{... | collective-permute-start | bytes 294920 | tf_op jit(solution)/shard_map/ppermute | solution.py:16
  24.0 6.5 %collective-permute-start.3 = (bf16[3,128,128]{2,1,0:T(8,128)(2,1)S(1)}, bf16[3,128,128]{2,1,0:T(8,128)(2,1)S(1)}, u32[]{:S(2)}, u32[]{:S(2)}) collective-permute-start(bf16[3,128,128]{2,1,0:T(8,128)(2,1)S(1)} %pad_maximum_fusion.3), channel_id=1, source_target_pairs={{4,0},{8,4},{12,8},{16,12},{20,16},{24,20},{28,24},{5,1},{9,5},{13... | collective-permute-start | bytes 294920 | tf_op jit(solution)/shard_map/ppermute | solution.py:16
  25.4 7.8 %collective-permute-start.2 = (bf16[3,128,128]{2,1,0:T(8,128)(2,1)S(1)}, bf16[3,128,128]{2,1,0:T(8,128)(2,1)S(1)}, u32[]{:S(2)}, u32[]{:S(2)}) collective-permute-start(bf16[3,128,128]{2,1,0:T(8,128)(2,1)S(1)} %pad_maximum_fusion.2), channel_id=1, source_target_pairs={{0,4},{4,8},{8,12},{12,16},{16,20},{20,24},{24,28},{1,5},{5,9},{9,... | collective-permute-start | bytes 294920 | tf_op jit(solution)/shard_map/ppermute | solution.py:16
  67.5 97.5 %reduce-scatter.12.cloned.1.call-start = ((), (), s32[]{:S(2)}) async-start(), calls=%async_computation.4 | async-start | bytes 81920
  96.2 2.6 %collective-permute-start.4 = (bf16[3,128,128]{2,1,0:T(8,128)(2,1)S(1)}, bf16[3,128,128]{2,1,0:T(8,128)(2,1)S(1)}, u32[]{:S(2)}, u32[]{:S(2)}) collective-permute-start(bf16[3,128,128]{2,1,0:T(8,128)(2,1)S(1)} %pad_maximum_fusion.4), channel_id=1, source_target_pairs={{0,1},{1,2},{2,3},{4,5},{5,6},{6,7},{8,9},{9,10},{10,11},{12,13},{... | collective-permute-start | bytes 294920 | tf_op jit(solution)/shard_map/ppermute | solution.py:16
  97.6 3.6 %collective-permute-start.5 = (bf16[3,128,128]{2,1,0:T(8,128)(2,1)S(1)}, bf16[3,128,128]{2,1,0:T(8,128)(2,1)S(1)}, u32[]{:S(2)}, u32[]{:S(2)}) collective-permute-start(bf16[3,128,128]{2,1,0:T(8,128)(2,1)S(1)} %pad_maximum_fusion.5), channel_id=1, source_target_pairs={{1,0},{2,1},{3,2},{5,4},{6,5},{7,6},{9,8},{10,9},{11,10},{13,12},{... | collective-permute-start | bytes 294920 | tf_op jit(solution)/shard_map/ppermute | solution.py:16
  101.2 6.5 %collective-permute-start.7 = (bf16[3,128,128]{2,1,0:T(8,128)(2,1)S(1)}, bf16[3,128,128]{2,1,0:T(8,128)(2,1)S(1)}, u32[]{:S(2)}, u32[]{:S(2)}) collective-permute-start(bf16[3,128,128]{2,1,0:T(8,128)(2,1)S(1)} %pad_maximum_fusion.7), channel_id=1, source_target_pairs={{4,0},{8,4},{12,8},{16,12},{20,16},{24,20},{28,24},{5,1},{9,5},{13... | collective-permute-start | bytes 294920 | tf_op jit(solution)/shard_map/ppermute | solution.py:16
  102.5 6.8 %collective-permute-start.6 = (bf16[3,128,128]{2,1,0:T(8,128)(2,1)S(1)}, bf16[3,128,128]{2,1,0:T(8,128)(2,1)S(1)}, u32[]{:S(2)}, u32[]{:S(2)}) collective-permute-start(bf16[3,128,128]{2,1,0:T(8,128)(2,1)S(1)} %pad_maximum_fusion.6), channel_id=1, source_target_pairs={{0,4},{4,8},{8,12},{12,16},{16,20},{20,24},{24,28},{1,5},{5,9},{9,... | collective-permute-start | bytes 294920 | tf_op jit(solution)/shard_map/ppermute | solution.py:16
  144.8 97.4 %reduce-scatter.14.cloned.1.call-start = ((), (), s32[]{:S(2)}) async-start(), calls=%async_computation.5 | async-start | bytes 81920
  173.5 2.6 %collective-permute-start.8 = (bf16[3,128,128]{2,1,0:T(8,128)(2,1)S(1)}, bf16[3,128,128]{2,1,0:T(8,128)(2,1)S(1)}, u32[]{:S(2)}, u32[]{:S(2)}) collective-permute-start(bf16[3,128,128]{2,1,0:T(8,128)(2,1)S(1)} %pad_maximum_fusion.8), channel_id=1, source_target_pairs={{0,1},{1,2},{2,3},{4,5},{5,6},{6,7},{8,9},{9,10},{10,11},{12,13},{... | collective-permute-start | bytes 294920 | tf_op jit(solution)/shard_map/ppermute | solution.py:16
  174.8 3.6 %collective-permute-start.9 = (bf16[3,128,128]{2,1,0:T(8,128)(2,1)S(1)}, bf16[3,128,128]{2,1,0:T(8,128)(2,1)S(1)}, u32[]{:S(2)}, u32[]{:S(2)}) collective-permute-start(bf16[3,128,128]{2,1,0:T(8,128)(2,1)S(1)} %pad_maximum_fusion.9), channel_id=1, source_target_pairs={{1,0},{2,1},{3,2},{5,4},{6,5},{7,6},{9,8},{10,9},{11,10},{13,12},{... | collective-permute-start | bytes 294920 | tf_op jit(solution)/shard_map/ppermute | solution.py:16
  178.5 6.5 %collective-permute-start.11 = (bf16[3,128,128]{2,1,0:T(8,128)(2,1)S(1)}, bf16[3,128,128]{2,1,0:T(8,128)(2,1)S(1)}, u32[]{:S(2)}, u32[]{:S(2)}) collective-permute-start(bf16[3,128,128]{2,1,0:T(8,128)(2,1)S(1)} %pad_maximum_fusion.11), channel_id=1, source_target_pairs={{4,0},{8,4},{12,8},{16,12},{20,16},{24,20},{28,24},{5,1},{9,5},{13... | collective-permute-start | bytes 294920 | tf_op jit(solution)/shard_map/ppermute | solution.py:16
  179.8 6.8 %collective-permute-start.10 = (bf16[3,128,128]{2,1,0:T(8,128)(2,1)S(1)}, bf16[3,128,128]{2,1,0:T(8,128)(2,1)S(1)}, u32[]{:S(2)}, u32[]{:S(2)}) collective-permute-start(bf16[3,128,128]{2,1,0:T(8,128)(2,1)S(1)} %pad_maximum_fusion.10), channel_id=1, source_target_pairs={{0,4},{4,8},{8,12},{12,16},{16,20},{20,24},{24,28},{1,5},{5,9},{9,... | collective-permute-start | bytes 294920 | tf_op jit(solution)/shard_map/ppermute | solution.py:16
Sparse Core Ops, SparseCore 0:
  67.6 20.0 reduce-scatter.9
  145.0 19.9 reduce-scatter.11
  222.2 19.9 reduce-scatter.13
where the time goes:
time: 251 us
  blocking collectives  100 us (40%)
  waiting for transfers between devices  75.4 us (30%)
  matrix products  27.1 us (11%)
  starting transfers between devices  26.5 us (11%)
  between operations  14.3 us (6%)
  local copies, waits for them, and re-layouts  6.72 us (3%)
    all_gather x3, blocking collectives, local(): lax.all_gather(coarse_rhs, 'sub', axis=0, tiled=True)  100 us
    unnamed x6, waiting for transfers between devices  59.5 us
    ppermute x12, starting transfers between devices, from_behind(): return lax.ppermute(value, axis, pairs)  26.4 us
    dot_general x3, matrix products, local(): jnp.dot(inverse, mixed_trace, preferred_element_type=jnp.float32)  21 us
    ppermute x12, waiting for transfers between devices, from_behind(): return lax.ppermute(value, axis, pairs)  15.9 us
    unnamed x17, local copies, waits for them, and re-layouts  5.45 us
  transfers between devices with their start and end apart: 15, of which 12 were waited for; matrix products, arithmetic and copies ran while one was open for 1% of the time, Pallas kernels for 0%

commit v1 on v0

v1 whole, which is shorter than its diff:
```python
import jax
import jax.numpy as jnp
from jax import lax
from jax.sharding import PartitionSpec as P

MODES = 64
ITERS = 3

bf16 = jnp.bfloat16
f32 = jnp.float32


def dot(a, b, dims=(((1,), (0,)), ((), ()))):
    return lax.dot_general(a, b, dims, preferred_element_type=f32)


def pair_relay(axis, forward, backward):
    devices = lax.axis_size(axis)
    even = lax.axis_index(axis) % 2 == 0
    sent = jnp.stack([jnp.where(even, forward, backward), jnp.where(even, backward, forward)])
    got = lax.ppermute(sent, axis, [(i, i ^ 1) for i in range(devices)])
    onward = [(i, i + 2) for i in range(0, devices - 2, 2)]
    back = [(i + 2, i) for i in range(1, devices - 2, 2)]
    relayed = lax.ppermute(got[1], axis, onward + back)
    from_next = jnp.where(even, got[0], relayed)
    from_previous = jnp.where(even, relayed, got[0])
    return from_next, from_previous


def exchange(outgoing, corner):
    face = outgoing.shape[1]
    right = jnp.concatenate([outgoing[4], outgoing[2, :corner], outgoing[7, :corner]])
    left = jnp.concatenate([outgoing[3], outgoing[0, :corner], outgoing[5, :corner]])
    from_right, from_left = pair_relay("col", right, left)
    up = jnp.concatenate([outgoing[6], from_right[face + corner :], from_left[face + corner :]])
    down = jnp.concatenate(
        [outgoing[1], from_right[face : face + corner], from_left[face : face + corner]]
    )
    from_up, from_down = pair_relay("sub", up, down)
    wide = lambda rows: jnp.pad(rows, ((0, face - corner), (0, 0)))
    return jnp.stack(
        [
            wide(from_down[face + corner :]),
            from_down[:face],
            wide(from_down[face : face + corner]),
            from_left[:face],
            from_right[:face],
            wide(from_up[face + corner :]),
            from_up[:face],
            wide(from_up[face : face + corner]),
        ]
    )


def sum_over_columns(partial, axis):
    devices = lax.axis_size(axis)
    index = lax.axis_index(axis)
    step = devices // 2
    while step:
        half = partial.shape[0] // 2
        upper = (index // step) % 2 == 1
        low, high = partial[:half], partial[half:]
        sent = jnp.where(upper, low, high).astype(bf16)
        got = lax.ppermute(sent, axis, [(i, i ^ step) for i in range(devices)])
        partial = jnp.where(upper, high, low) + got.astype(f32)
        step //= 2
    return partial.astype(bf16)


def local(
    trace_start,
    neumann_load,
    double_layer,
    single_inverse,
    interface_nodes,
    node_mode,
    mode_weight,
    coarse_inverse,
):
    trace_now = trace_start[0, 0]
    load_block = neumann_load[0, 0].astype(f32)
    kernel = double_layer[0, 0]
    inverse = single_inverse[0, 0]
    node_count, rhs_count = trace_now.shape
    interface = interface_nodes[0, 0]
    slot_count = interface.shape[1]
    corner = slot_count // 8
    band_rows = 8 * slot_count
    local_index = interface - (jnp.arange(8, dtype=jnp.int32) * slot_count)[:, None]
    selector = (
        local_index[:, :, None] == jnp.arange(slot_count, dtype=jnp.int32)[None, None, :]
    ).astype(bf16)
    mode_basis = jnp.where(
        node_mode[0, 0][None, :] == jnp.arange(MODES, dtype=jnp.int32)[:, None],
        mode_weight[0, 0][None, :],
        jnp.zeros((), bf16),
    )
    residual = trace_now
    rest_zeros = jnp.zeros((node_count - band_rows, rhs_count), f32)
    subs = lax.axis_size("sub")
    for iteration in range(ITERS):
        mixed = (0.5 * trace_now.astype(f32) + dot(kernel, trace_now)).astype(bf16)
        flux_now = dot(inverse, mixed).astype(bf16)
        banded = flux_now[:band_rows].reshape(8, slot_count, rhs_count)
        outgoing = jnp.einsum(
            "dpq,dqr->dpr", selector, banded, preferred_element_type=f32
        ).astype(bf16)
        received = exchange(outgoing, corner)
        placed = jnp.einsum("dpq,dpr->dqr", selector, received, preferred_element_type=f32)
        placed = placed.reshape(band_rows, rhs_count)
        assembled = flux_now.astype(f32) + jnp.concatenate([placed, rest_zeros], axis=0)
        residual = (load_block - assembled).astype(bf16)
        coarse_rhs = dot(mode_basis, residual).astype(bf16)
        copies = jnp.broadcast_to(coarse_rhs[None], (subs, MODES, rhs_count))
        gathered = lax.all_to_all(copies.reshape(subs * MODES, rhs_count), "sub", 0, 0, tiled=True)
        coarse_out = sum_over_columns(dot(coarse_inverse, gathered), "col")
        correction = dot(mode_basis, coarse_out, (((0,), (0,)), ((), ())))
        trace_now = (
            trace_now.astype(f32) + 0.25 * residual.astype(f32) + correction
        ).astype(bf16)
    return (trace_now[None, None], residual[None, None])


def solution(mesh):
    placed = (
        P("sub", "col", None, None),
        P("sub", "col", None, None),
        P("sub", "col", None, None),
        P("sub", "col", None, None),
        P("sub", "col", None, None),
        P("sub", "col", None),
        P("sub", "col", None),
        P("sub", "col"),
    )
    return jax.shard_map(
        local,
        mesh=mesh,
        in_specs=placed,
        out_specs=(P("sub", "col", None, None), P("sub", "col", None, None)),
        check_vma=False,
    )
```

time: 251 us -> 132 us (0.53)
  blocking collectives: 100 us -> 23.2 us
  waiting for transfers between devices: 75.4 us -> 39.9 us
  between operations: 14.3 us -> 1.49 us
  starting transfers between devices: 26.5 us -> 35.7 us
    all_gather x3 -> x0, blocking collectives: 100 us -> none  [local(): lax.all_gather(coarse_rhs, 'sub', axis=0, tiled=True)]
    unnamed x6 -> x0, waiting for transfers between devices: 59.5 us -> none
    all_to_all x0 -> x2, blocking collectives: none -> 23.2 us  [local(): lax.all_to_all(copies.reshape(subs * MODES, rhs_count), 'sub', 0, 0, tile...]
    ppermute x12 -> x18, waiting for transfers between devices: 15.9 us -> 32.6 us  [the longest x6 14.6 us: pair_relay(): got = lax.ppermute(sent, axis, [(i, i ^ 1) for i in range(devices)])]
    all_to_all x0 -> x1, waiting for transfers between devices: none -> 7.34 us  [local(): lax.all_to_all(copies.reshape(subs * MODES, rhs_count), 'sub', 0, 0, tile...]
    all_to_all x0 -> x1, starting transfers between devices: none -> 5.62 us  [local(): lax.all_to_all(copies.reshape(subs * MODES, rhs_count), 'sub', 0, 0, tile...]
    ppermute x12 -> x18, starting transfers between devices: 26.4 us -> 30 us  [the longest x6 19.6 us: pair_relay(): relayed = lax.ppermute(got[1], axis, onward + back)]
    unnamed x17 -> x35, local copies, waits for them, and re-layouts: 5.45 us -> 3.46 us
  transfers between devices with their start and end apart: 15 -> 19, of which waited for: 12 -> 19; matrix products, arithmetic and copies ran while one was open for 1% -> 1% of each run, Pallas kernels for 0% -> 0%
where the time goes in v1:
time: 132 us
  waiting for transfers between devices  39.9 us (30%)
  starting transfers between devices  35.7 us (27%)
  matrix products  25 us (19%)
  blocking collectives  23.2 us (18%)
  local copies, waits for them, and re-layouts  5.48 us (4%)
  between operations  1.49 us (1%)
    dot_general x12, matrix products, dot(): return lax.dot_general(a, b, dims, preferred_element_type=f32)  23.4 us
    all_to_all x2, blocking collectives, local(): lax.all_to_all(copies.reshape(subs * MODES, rhs_count), 'sub', 0, 0, tile...  23.2 us
    ppermute x6, starting transfers between devices, pair_relay(): relayed = lax.ppermute(got[1], axis, onward + back)  19.6 us
    ppermute x6, waiting for transfers between devices, pair_relay(): got = lax.ppermute(sent, axis, [(i, i ^ 1) for i in range(devices)])  14.6 us
    ppermute x6, waiting for transfers between devices, pair_relay(): relayed = lax.ppermute(got[1], axis, onward + back)  9.64 us
    ppermute x6, waiting for transfers between devices, sum_over_columns(): got = lax.ppermute(sent, axis, [(i, i ^ step) for i in range(devices)])  8.35 us
    ppermute x6, starting transfers between devices, sum_over_columns(): got = lax.ppermute(sent, axis, [(i, i ^ step) for i in range(devices)])  7.39 us
    all_to_all x1, waiting for transfers between devices, local(): lax.all_to_all(copies.reshape(subs * MODES, rhs_count), 'sub', 0, 0, tile...  7.34 us
  transfers between devices with their start and end apart: 19, of which 19 were waited for; matrix products, arithmetic and copies ran while one was open for 1% of the time, Pallas kernels for 0%

profile of v1, /device:TPU:0, one launch (start us, length us, event | category | flops | bytes accessed | tf_op | source)
XLA Modules:
  0.0 131.8 jit_solution(14867044423469698358)
XLA Ops:
  0.7 1.2 copy.10
  1.9 7.1 %fusion.54 = bf16[1536,128]{0,1:T(8,128)(2,1)S(1)} fusion(bf16[1,1,1536,1536]{3,2,1,0:T(8,128)(2,1)} %param.11, bf16[1,1,1536,1536]{3,2,1,0:T(8,128)(2,1)} %param.10, bf16[1,1,1536,128]{3,2,1,0:T(8,128)(2,1)} %param.8, bf16[1,1,1536,128]{2,3,1,0:T(8,128)(2,1)S(1)} %copy.10), kind=kOutput, calls=%fused_computation.31 | convolution fusion | flops 1208942592 | bytes 10616832 | tf_op jit(solution)/shard_map/dot_general | solution.py:14
  9.3 0.3 convolution_convert_fusion.2
  9.8 0.5 collective-permute-start
  10.3 0.9 collective-permute-done
  11.2 4.8 %collective-permute-start.1 = (bf16[160,128]{1,0:T(8,128)(2,1)S(1)}, bf16[160,128]{1,0:T(8,128)(2,1)S(1)}, u32[]{:S(2)}, u32[]{:S(2)}) collective-permute-start(bf16[160,128]{1,0:T(8,128)(2,1)S(1)} %slice_bitcast_fusion.10), channel_id=1, source_target_pairs={{0,2},{3,1},{4,6},{7,5},{8,10},{11,9},{12,14},{15,13},{16,18},{19,... | collective-permute-start | bytes 122888 | tf_op jit(solution)/shard_map/ppermute | solution.py:24
  16.0 1.6 %collective-permute-done.1 = bf16[160,128]{1,0:T(8,128)(2,1)S(1)} collective-permute-done((bf16[160,128]{1,0:T(8,128)(2,1)S(1)}, bf16[160,128]{1,0:T(8,128)(2,1)S(1)}, u32[]{:S(2)}, u32[]{:S(2)}) %collective-permute-start.1) | collective-permute-done | bytes 40992 | tf_op jit(solution)/shard_map/ppermute | solution.py:24
  17.7 1.6 %collective-permute-start.2 = (bf16[2,160,128]{2,1,0:T(8,128)(2,1)S(1)}, bf16[2,160,128]{2,1,0:T(8,128)(2,1)S(1)}, u32[]{:S(2)}, u32[]{:S(2)}) collective-permute-start(bf16[2,160,128]{2,1,0:T(8,128)(2,1)S(1)} %pad_maximum_fusion.1), channel_id=1, source_target_pairs={{0,4},{4,0},{8,12},{12,8},{16,20},{20,16},{24,28},{28,24},{1,5},{5... | collective-permute-start | bytes 245768 | tf_op jit(solution)/shard_map/ppermute | solution.py:21
  19.3 3.0 %collective-permute-done.2 = bf16[2,160,128]{2,1,0:T(8,128)(2,1)S(1)} collective-permute-done((bf16[2,160,128]{2,1,0:T(8,128)(2,1)S(1)}, bf16[2,160,128]{2,1,0:T(8,128)(2,1)S(1)}, u32[]{:S(2)}, u32[]{:S(2)}) %collective-permute-start.2) | collective-permute-done | bytes 81952 | tf_op jit(solution)/shard_map/ppermute | solution.py:21
  22.2 3.5 %collective-permute-start.3 = (bf16[160,128]{1,0:T(8,128)(2,1)S(1)}, bf16[160,128]{1,0:T(8,128)(2,1)S(1)}, u32[]{:S(2)}, u32[]{:S(2)}) collective-permute-start(bf16[160,128]{1,0:T(8,128)(2,1)S(1)} %slice_bitcast_fusion.9), channel_id=1, source_target_pairs={{0,8},{8,16},{16,24},{12,4},{20,12},{28,20},{1,9},{9,17},{17,25},{... | collective-permute-start | bytes 122888 | tf_op jit(solution)/shard_map/ppermute | solution.py:24
  26.0 1.4 %collective-permute-done.3 = bf16[160,128]{1,0:T(8,128)(2,1)S(1)} collective-permute-done((bf16[160,128]{1,0:T(8,128)(2,1)S(1)}, bf16[160,128]{1,0:T(8,128)(2,1)S(1)}, u32[]{:S(2)}, u32[]{:S(2)}) %collective-permute-start.3) | collective-permute-done | bytes 40992 | tf_op jit(solution)/shard_map/ppermute | solution.py:24
  28.3 0.7 broadcast_in_dim.46
  29.0 5.6 %all-to-all-start = ((bf16[8,64,128]{2,1,0:T(8,128)(2,1)}), bf16[8,64,128]{2,1,0:T(8,128)(2,1)S(1)}, u32[]{:S(2)}, u32[]{:S(2)}) async-start(bf16[8,64,128]{2,1,0:T(8,128)(2,1)} %broadcast_in_dim.46), calls=%async_computation | async-start | bytes 262144 | tf_op jit(solution)/shard_map/all_to_all | solution.py:115
  34.6 7.3 %all-to-all-done = bf16[8,64,128]{2,1,0:T(8,128)(2,1)S(1)} async-done(((bf16[8,64,128]{2,1,0:T(8,128)(2,1)}), bf16[8,64,128]{2,1,0:T(8,128)(2,1)S(1)}, u32[]{:S(2)}, u32[]{:S(2)}) %all-to-all-start) | async-done | bytes 131104 | tf_op jit(solution)/shard_map/all_to_all | solution.py:115
  42.2 2.4 %collective-permute-start.4 = (bf16[128,128]{0,1:T(8,128)(2,1)S(1)}, bf16[128,128]{0,1:T(8,128)(2,1)S(1)}, u32[]{:S(2)}, u32[]{:S(2)}) collective-permute-start(bf16[128,128]{0,1:T(8,128)(2,1)S(1)} %select_convert_fusion.5), channel_id=1, source_target_pairs={{0,2},{1,3},{2,0},{3,1},{4,6},{5,7},{6,4},{7,5},{8,10},{9,11},{10,... | collective-permute-start | bytes 98312 | tf_op jit(solution)/shard_map/ppermute | solution.py:64
  44.6 1.9 %collective-permute-done.4 = bf16[128,128]{0,1:T(8,128)(2,1)S(1)} collective-permute-done((bf16[128,128]{0,1:T(8,128)(2,1)S(1)}, bf16[128,128]{0,1:T(8,128)(2,1)S(1)}, u32[]{:S(2)}, u32[]{:S(2)}) %collective-permute-start.4) | collective-permute-done | bytes 32800 | tf_op jit(solution)/shard_map/ppermute | solution.py:64
  46.7 1.2 collective-permute-done.5
  47.9 0.3 fusion.27
  48.2 6.9 %fusion.51 = bf16[1536,128]{0,1:T(8,128)(2,1)S(1)} fusion(bf16[1,1,1536,1536]{3,2,1,0:T(8,128)(2,1)} %param.11, bf16[1536,128]{0,1:T(8,128)(2,1)S(1)} %fusion.27, bf16[1,1,1536,1536]{3,2,1,0:T(8,128)(2,1)} %param.10), kind=kOutput, calls=%fused_computation.30 | convolution fusion | flops 1208942592 | bytes 10223616 | tf_op jit(solution)/shard_map/dot_general | solution.py:14
  55.3 0.3 convolution_convert_fusion.1
  56.0 1.1 collective-permute-done.6
  57.1 3.9 %collective-permute-start.7 = (bf16[160,128]{1,0:T(8,128)(2,1)S(1)}, bf16[160,128]{1,0:T(8,128)(2,1)S(1)}, u32[]{:S(2)}, u32[]{:S(2)}) collective-permute-start(bf16[160,128]{1,0:T(8,128)(2,1)S(1)} %slice_bitcast_fusion.6), channel_id=1, source_target_pairs={{0,2},{3,1},{4,6},{7,5},{8,10},{11,9},{12,14},{15,13},{16,18},{19,... | collective-permute-start | bytes 122888 | tf_op jit(solution)/shard_map/ppermute | solution.py:24
  61.0 1.7 %collective-permute-done.7 = bf16[160,128]{1,0:T(8,128)(2,1)S(1)} collective-permute-done((bf16[160,128]{1,0:T(8,128)(2,1)S(1)}, bf16[160,128]{1,0:T(8,128)(2,1)S(1)}, u32[]{:S(2)}, u32[]{:S(2)}) %collective-permute-start.7) | collective-permute-done | bytes 40992 | tf_op jit(solution)/shard_map/ppermute | solution.py:24
  62.8 0.3 collective-permute-start.8
  63.0 4.2 %collective-permute-done.8 = bf16[2,160,128]{2,1,0:T(8,128)(2,1)S(1)} collective-permute-done((bf16[2,160,128]{2,1,0:T(8,128)(2,1)S(1)}, bf16[2,160,128]{2,1,0:T(8,128)(2,1)S(1)}, u32[]{:S(2)}, u32[]{:S(2)}) %collective-permute-start.8) | collective-permute-done | bytes 81952 | tf_op jit(solution)/shard_map/ppermute | solution.py:21
  67.3 1.8 %collective-permute-start.9 = (bf16[160,128]{1,0:T(8,128)(2,1)S(1)}, bf16[160,128]{1,0:T(8,128)(2,1)S(1)}, u32[]{:S(2)}, u32[]{:S(2)}) collective-permute-start(bf16[160,128]{1,0:T(8,128)(2,1)S(1)} %slice_bitcast_fusion.5), channel_id=1, source_target_pairs={{0,8},{8,16},{16,24},{12,4},{20,12},{28,20},{1,9},{9,17},{17,25},{... | collective-permute-start | bytes 122888 | tf_op jit(solution)/shard_map/ppermute | solution.py:24
  69.0 1.7 %collective-permute-done.9 = bf16[160,128]{1,0:T(8,128)(2,1)S(1)} collective-permute-done((bf16[160,128]{1,0:T(8,128)(2,1)S(1)}, bf16[160,128]{1,0:T(8,128)(2,1)S(1)}, u32[]{:S(2)}, u32[]{:S(2)}) %collective-permute-start.9) | collective-permute-done | bytes 40992 | tf_op jit(solution)/shard_map/ppermute | solution.py:24
  71.7 11.6 %all_to_all.27 = bf16[8,64,128]{2,1,0:T(8,128)(2,1)S(1)} all-to-all(bf16[8,64,128]{2,1,0:T(8,128)(2,1)S(1)} %broadcast_in_dim.47), channel_id=1, replica_groups=mesh['sub'=8,'col'=4] {'sub'}, dimensions={0} | all-to-all | bytes 262144 | tf_op jit(solution)/shard_map/all_to_all | solution.py:115
  83.6 2.4 %collective-permute-start.10 = (bf16[128,128]{0,1:T(8,128)(2,1)S(1)}, bf16[128,128]{0,1:T(8,128)(2,1)S(1)}, u32[]{:S(2)}, u32[]{:S(2)}) collective-permute-start(bf16[128,128]{0,1:T(8,128)(2,1)S(1)} %select_convert_fusion.3), channel_id=1, source_target_pairs={{0,2},{1,3},{2,0},{3,1},{4,6},{5,7},{6,4},{7,5},{8,10},{9,11},{10,... | collective-permute-start | bytes 98312 | tf_op jit(solution)/shard_map/ppermute | solution.py:64
  86.0 1.9 %collective-permute-done.10 = bf16[128,128]{0,1:T(8,128)(2,1)S(1)} collective-permute-done((bf16[128,128]{0,1:T(8,128)(2,1)S(1)}, bf16[128,128]{0,1:T(8,128)(2,1)S(1)}, u32[]{:S(2)}, u32[]{:S(2)}) %collective-permute-start.10) | collective-permute-done | bytes 32800 | tf_op jit(solution)/shard_map/ppermute | solution.py:64
  88.0 1.2 collective-permute-done.11
  89.2 0.3 fusion.28
  89.5 6.9 %fusion.48 = bf16[1536,128]{0,1:T(8,128)(2,1)S(1)} fusion(bf16[1,1,1536,1536]{3,2,1,0:T(8,128)(2,1)} %param.11, bf16[1536,128]{0,1:T(8,128)(2,1)S(1)} %fusion.28, bf16[1,1,1536,1536]{3,2,1,0:T(8,128)(2,1)} %param.10), kind=kOutput, calls=%fused_computation.29 | convolution fusion | flops 1208942592 | bytes 10223616 | tf_op jit(solution)/shard_map/dot_general | solution.py:14
  96.7 0.3 convolution_convert_fusion
  97.3 1.1 collective-permute-done.12
  98.5 3.9 %collective-permute-start.13 = (bf16[160,128]{1,0:T(8,128)(2,1)S(1)}, bf16[160,128]{1,0:T(8,128)(2,1)S(1)}, u32[]{:S(2)}, u32[]{:S(2)}) collective-permute-start(bf16[160,128]{1,0:T(8,128)(2,1)S(1)} %slice_bitcast_fusion.2), channel_id=1, source_target_pairs={{0,2},{3,1},{4,6},{7,5},{8,10},{11,9},{12,14},{15,13},{16,18},{19,... | collective-permute-start | bytes 122888 | tf_op jit(solution)/shard_map/ppermute | solution.py:24
  102.4 1.7 %collective-permute-done.13 = bf16[160,128]{1,0:T(8,128)(2,1)S(1)} collective-permute-done((bf16[160,128]{1,0:T(8,128)(2,1)S(1)}, bf16[160,128]{1,0:T(8,128)(2,1)S(1)}, u32[]{:S(2)}, u32[]{:S(2)}) %collective-permute-start.13) | collective-permute-done | bytes 40992 | tf_op jit(solution)/shard_map/ppermute | solution.py:24
  104.1 0.3 collective-permute-start.14
  104.4 4.2 %collective-permute-done.14 = bf16[2,160,128]{2,1,0:T(8,128)(2,1)S(1)} collective-permute-done((bf16[2,160,128]{2,1,0:T(8,128)(2,1)S(1)}, bf16[2,160,128]{2,1,0:T(8,128)(2,1)S(1)}, u32[]{:S(2)}, u32[]{:S(2)}) %collective-permute-start.14) | collective-permute-done | bytes 81952 | tf_op jit(solution)/shard_map/ppermute | solution.py:21
  108.6 1.8 %collective-permute-start.15 = (bf16[160,128]{1,0:T(8,128)(2,1)S(1)}, bf16[160,128]{1,0:T(8,128)(2,1)S(1)}, u32[]{:S(2)}, u32[]{:S(2)}) collective-permute-start(bf16[160,128]{1,0:T(8,128)(2,1)S(1)} %slice_bitcast_fusion.1), channel_id=1, source_target_pairs={{0,8},{8,16},{16,24},{12,4},{20,12},{28,20},{1,9},{9,17},{17,25},{... | collective-permute-start | bytes 122888 | tf_op jit(solution)/shard_map/ppermute | solution.py:24
  110.4 1.7 %collective-permute-done.15 = bf16[160,128]{1,0:T(8,128)(2,1)S(1)} collective-permute-done((bf16[160,128]{1,0:T(8,128)(2,1)S(1)}, bf16[160,128]{1,0:T(8,128)(2,1)S(1)}, u32[]{:S(2)}, u32[]{:S(2)}) %collective-permute-start.15) | collective-permute-done | bytes 40992 | tf_op jit(solution)/shard_map/ppermute | solution.py:24
  113.0 11.6 %all_to_all.28 = bf16[8,64,128]{2,1,0:T(8,128)(2,1)S(1)} all-to-all(bf16[8,64,128]{2,1,0:T(8,128)(2,1)S(1)} %broadcast_in_dim.48), channel_id=1, replica_groups=mesh['sub'=8,'col'=4] {'sub'}, dimensions={0} | all-to-all | bytes 262144 | tf_op jit(solution)/shard_map/all_to_all | solution.py:115
  124.9 2.4 %collective-permute-start.16 = (bf16[128,128]{0,1:T(8,128)(2,1)S(1)}, bf16[128,128]{0,1:T(8,128)(2,1)S(1)}, u32[]{:S(2)}, u32[]{:S(2)}) collective-permute-start(bf16[128,128]{0,1:T(8,128)(2,1)S(1)} %select_convert_fusion.1), channel_id=1, source_target_pairs={{0,2},{1,3},{2,0},{3,1},{4,6},{5,7},{6,4},{7,5},{8,10},{9,11},{10,... | collective-permute-start | bytes 98312 | tf_op jit(solution)/shard_map/ppermute | solution.py:64
  127.3 1.9 %collective-permute-done.16 = bf16[128,128]{0,1:T(8,128)(2,1)S(1)} collective-permute-done((bf16[128,128]{0,1:T(8,128)(2,1)S(1)}, bf16[128,128]{0,1:T(8,128)(2,1)S(1)}, u32[]{:S(2)}, u32[]{:S(2)}) %collective-permute-start.16) | collective-permute-done | bytes 32800 | tf_op jit(solution)/shard_map/ppermute | solution.py:64
  129.4 0.9 copy.25
  130.3 0.3 collective-permute-done.17
  130.6 0.3 fusion.57
  130.9 0.9 copy.24
  (117 shorter events, 5.6 us)
Async XLA Ops:
  0.6 41.3 %copy-start = (bf16[256,512]{1,0:T(8,128)(2,1)S(1)}, bf16[256,512]{1,0:T(8,128)(2,1)}, u32[]{:S(2)}) copy-start(bf16[256,512]{1,0:T(8,128)(2,1)} %param.15) | copy-start | bytes 786436
  1.9 7.4 %copy-start.4 = (s32[1,1,8,128]{3,2,1,0:T(8,128)S(1)}, s32[1,1,8,128]{3,2,1,0:T(8,128)}, u32[]{:S(2)}) copy-start(s32[1,1,8,128]{3,2,1,0:T(8,128)} %param.12) | copy-start | bytes 12292
  1.9 23.8 %copy-start.2 = (s32[1,1,1536]{2,1,0:T(1,128)S(1)}, s32[1,1,1536]{2,1,0:T(1,128)}, u32[]{:S(2)}) copy-start(s32[1,1,1536]{2,1,0:T(1,128)} %param.13) | copy-start | bytes 18436
  1.9 23.8 %copy-start.1 = (bf16[1,1,1536,128]{3,2,1,0:T(8,128)(2,1)S(1)}, bf16[1,1,1536,128]{3,2,1,0:T(8,128)(2,1)}, u32[]{:S(2)}) copy-start(bf16[1,1,1536,128]{3,2,1,0:T(8,128)(2,1)} %param.9) | copy-start | bytes 1179652
  1.9 24.0 %copy-start.3 = (bf16[1,1,1536]{2,1,0:T(2,128)(2,1)S(1)}, bf16[1,1,1536]{2,1,0:T(2,128)(2,1)}, u32[]{:S(2)}) copy-start(bf16[1,1,1536]{2,1,0:T(2,128)(2,1)} %param.14) | copy-start | bytes 9220
  9.8 1.4 %collective-permute-start = (bf16[2,160,128]{2,1,0:T(8,128)(2,1)S(1)}, bf16[2,160,128]{2,1,0:T(8,128)(2,1)S(1)}, u32[]{:S(2)}, u32[]{:S(2)}) collective-permute-start(bf16[2,160,128]{2,1,0:T(8,128)(2,1)S(1)} %pad_maximum_fusion), channel_id=1, source_target_pairs={{0,1},{1,0},{2,3},{3,2},{4,5},{5,4},{6,7},{7,6},{8,9},{9,8},{10,11... | collective-permute-start | bytes 245768 | tf_op jit(solution)/shard_map/ppermute | solution.py:21
  11.2 6.4 %collective-permute-start.1 = (bf16[160,128]{1,0:T(8,128)(2,1)S(1)}, bf16[160,128]{1,0:T(8,128)(2,1)S(1)}, u32[]{:S(2)}, u32[]{:S(2)}) collective-permute-start(bf16[160,128]{1,0:T(8,128)(2,1)S(1)} %slice_bitcast_fusion.10), channel_id=1, source_target_pairs={{0,2},{3,1},{4,6},{7,5},{8,10},{11,9},{12,14},{15,13},{16,18},{19,... | collective-permute-start | bytes 122888 | tf_op jit(solution)/shard_map/ppermute | solution.py:24
  17.7 4.5 %collective-permute-start.2 = (bf16[2,160,128]{2,1,0:T(8,128)(2,1)S(1)}, bf16[2,160,128]{2,1,0:T(8,128)(2,1)S(1)}, u32[]{:S(2)}, u32[]{:S(2)}) collective-permute-start(bf16[2,160,128]{2,1,0:T(8,128)(2,1)S(1)} %pad_maximum_fusion.1), channel_id=1, source_target_pairs={{0,4},{4,0},{8,12},{12,8},{16,20},{20,16},{24,28},{28,24},{1,5},{5... | collective-permute-start | bytes 245768 | tf_op jit(solution)/shard_map/ppermute | solution.py:21
  22.2 5.1 %collective-permute-start.3 = (bf16[160,128]{1,0:T(8,128)(2,1)S(1)}, bf16[160,128]{1,0:T(8,128)(2,1)S(1)}, u32[]{:S(2)}, u32[]{:S(2)}) collective-permute-start(bf16[160,128]{1,0:T(8,128)(2,1)S(1)} %slice_bitcast_fusion.9), channel_id=1, source_target_pairs={{0,8},{8,16},{16,24},{12,4},{20,12},{28,20},{1,9},{9,17},{17,25},{... | collective-permute-start | bytes 122888 | tf_op jit(solution)/shard_map/ppermute | solution.py:24
  29.0 13.0 %all-to-all-start = ((bf16[8,64,128]{2,1,0:T(8,128)(2,1)}), bf16[8,64,128]{2,1,0:T(8,128)(2,1)S(1)}, u32[]{:S(2)}, u32[]{:S(2)}) async-start(bf16[8,64,128]{2,1,0:T(8,128)(2,1)} %broadcast_in_dim.46), calls=%async_computation | async-start | bytes 262144 | tf_op jit(solution)/shard_map/all_to_all | solution.py:115
  42.2 4.3 %collective-permute-start.4 = (bf16[128,128]{0,1:T(8,128)(2,1)S(1)}, bf16[128,128]{0,1:T(8,128)(2,1)S(1)}, u32[]{:S(2)}, u32[]{:S(2)}) collective-permute-start(bf16[128,128]{0,1:T(8,128)(2,1)S(1)} %select_convert_fusion.5), channel_id=1, source_target_pairs={{0,2},{1,3},{2,0},{3,1},{4,6},{5,7},{6,4},{7,5},{8,10},{9,11},{10,... | collective-permute-start | bytes 98312 | tf_op jit(solution)/shard_map/ppermute | solution.py:64
  46.6 1.3 collective-permute-start.5
  55.7 1.3 %collective-permute-start.6 = (bf16[2,160,128]{2,1,0:T(8,128)(2,1)S(1)}, bf16[2,160,128]{2,1,0:T(8,128)(2,1)S(1)}, u32[]{:S(2)}, u32[]{:S(2)}) collective-permute-start(bf16[2,160,128]{2,1,0:T(8,128)(2,1)S(1)} %pad_maximum_fusion.2), channel_id=1, source_target_pairs={{0,1},{1,0},{2,3},{3,2},{4,5},{5,4},{6,7},{7,6},{8,9},{9,8},{10,11... | collective-permute-start | bytes 245768 | tf_op jit(solution)/shard_map/ppermute | solution.py:21
  57.1 5.6 %collective-permute-start.7 = (bf16[160,128]{1,0:T(8,128)(2,1)S(1)}, bf16[160,128]{1,0:T(8,128)(2,1)S(1)}, u32[]{:S(2)}, u32[]{:S(2)}) collective-permute-start(bf16[160,128]{1,0:T(8,128)(2,1)S(1)} %slice_bitcast_fusion.6), channel_id=1, source_target_pairs={{0,2},{3,1},{4,6},{7,5},{8,10},{11,9},{12,14},{15,13},{16,18},{19,... | collective-permute-start | bytes 122888 | tf_op jit(solution)/shard_map/ppermute | solution.py:24
  62.8 4.5 %collective-permute-start.8 = (bf16[2,160,128]{2,1,0:T(8,128)(2,1)S(1)}, bf16[2,160,128]{2,1,0:T(8,128)(2,1)S(1)}, u32[]{:S(2)}, u32[]{:S(2)}) collective-permute-start(bf16[2,160,128]{2,1,0:T(8,128)(2,1)S(1)} %pad_maximum_fusion.3), channel_id=1, source_target_pairs={{0,4},{4,0},{8,12},{12,8},{16,20},{20,16},{24,28},{28,24},{1,5},{5... | collective-permute-start | bytes 245768 | tf_op jit(solution)/shard_map/ppermute | solution.py:21
  67.3 3.4 %collective-permute-start.9 = (bf16[160,128]{1,0:T(8,128)(2,1)S(1)}, bf16[160,128]{1,0:T(8,128)(2,1)S(1)}, u32[]{:S(2)}, u32[]{:S(2)}) collective-permute-start(bf16[160,128]{1,0:T(8,128)(2,1)S(1)} %slice_bitcast_fusion.5), channel_id=1, source_target_pairs={{0,8},{8,16},{16,24},{12,4},{20,12},{28,20},{1,9},{9,17},{17,25},{... | collective-permute-start | bytes 122888 | tf_op jit(solution)/shard_map/ppermute | solution.py:24
  83.6 4.3 %collective-permute-start.10 = (bf16[128,128]{0,1:T(8,128)(2,1)S(1)}, bf16[128,128]{0,1:T(8,128)(2,1)S(1)}, u32[]{:S(2)}, u32[]{:S(2)}) collective-permute-start(bf16[128,128]{0,1:T(8,128)(2,1)S(1)} %select_convert_fusion.3), channel_id=1, source_target_pairs={{0,2},{1,3},{2,0},{3,1},{4,6},{5,7},{6,4},{7,5},{8,10},{9,11},{10,... | collective-permute-start | bytes 98312 | tf_op jit(solution)/shard_map/ppermute | solution.py:64
  88.0 1.3 collective-permute-start.11
  97.1 1.3 %collective-permute-start.12 = (bf16[2,160,128]{2,1,0:T(8,128)(2,1)S(1)}, bf16[2,160,128]{2,1,0:T(8,128)(2,1)S(1)}, u32[]{:S(2)}, u32[]{:S(2)}) collective-permute-start(bf16[2,160,128]{2,1,0:T(8,128)(2,1)S(1)} %pad_maximum_fusion.4), channel_id=1, source_target_pairs={{0,1},{1,0},{2,3},{3,2},{4,5},{5,4},{6,7},{7,6},{8,9},{9,8},{10,11... | collective-permute-start | bytes 245768 | tf_op jit(solution)/shard_map/ppermute | solution.py:21
  98.5 5.6 %collective-permute-start.13 = (bf16[160,128]{1,0:T(8,128)(2,1)S(1)}, bf16[160,128]{1,0:T(8,128)(2,1)S(1)}, u32[]{:S(2)}, u32[]{:S(2)}) collective-permute-start(bf16[160,128]{1,0:T(8,128)(2,1)S(1)} %slice_bitcast_fusion.2), channel_id=1, source_target_pairs={{0,2},{3,1},{4,6},{7,5},{8,10},{11,9},{12,14},{15,13},{16,18},{19,... | collective-permute-start | bytes 122888 | tf_op jit(solution)/shard_map/ppermute | solution.py:24
  104.1 4.5 %collective-permute-start.14 = (bf16[2,160,128]{2,1,0:T(8,128)(2,1)S(1)}, bf16[2,160,128]{2,1,0:T(8,128)(2,1)S(1)}, u32[]{:S(2)}, u32[]{:S(2)}) collective-permute-start(bf16[2,160,128]{2,1,0:T(8,128)(2,1)S(1)} %pad_maximum_fusion.5), channel_id=1, source_target_pairs={{0,4},{4,0},{8,12},{12,8},{16,20},{20,16},{24,28},{28,24},{1,5},{5... | collective-permute-start | bytes 245768 | tf_op jit(solution)/shard_map/ppermute | solution.py:21
  108.6 3.4 %collective-permute-start.15 = (bf16[160,128]{1,0:T(8,128)(2,1)S(1)}, bf16[160,128]{1,0:T(8,128)(2,1)S(1)}, u32[]{:S(2)}, u32[]{:S(2)}) collective-permute-start(bf16[160,128]{1,0:T(8,128)(2,1)S(1)} %slice_bitcast_fusion.1), channel_id=1, source_target_pairs={{0,8},{8,16},{16,24},{12,4},{20,12},{28,20},{1,9},{9,17},{17,25},{... | collective-permute-start | bytes 122888 | tf_op jit(solution)/shard_map/ppermute | solution.py:24
  124.9 4.3 %collective-permute-start.16 = (bf16[128,128]{0,1:T(8,128)(2,1)S(1)}, bf16[128,128]{0,1:T(8,128)(2,1)S(1)}, u32[]{:S(2)}, u32[]{:S(2)}) collective-permute-start(bf16[128,128]{0,1:T(8,128)(2,1)S(1)} %select_convert_fusion.1), channel_id=1, source_target_pairs={{0,2},{1,3},{2,0},{3,1},{4,6},{5,7},{6,4},{7,5},{8,10},{9,11},{10,... | collective-permute-start | bytes 98312 | tf_op jit(solution)/shard_map/ppermute | solution.py:64
  129.3 1.3 collective-permute-start.17

commit v2 on v1

--- a/solution.py
+++ b/solution.py
@@ -1,6 +1,10 @@
+import functools
+
 import jax
 import jax.numpy as jnp
 from jax import lax
+from jax.experimental import pallas as pl
+from jax.experimental.pallas import tpu as pltpu
 from jax.sharding import PartitionSpec as P
 
 MODES = 64
@@ -12,6 +16,63 @@
 
 def dot(a, b, dims=(((1,), (0,)), ((), ()))):
     return lax.dot_general(a, b, dims, preferred_element_type=f32)
+
+
+def products_kernel(face, corner, chunk, u_ref, k_hbm, s_hbm, sel_ref, flux_ref, packed_ref, kbuf, sbuf, mixed, sems):
+    nodes = u_ref.shape[0]
+    count = nodes // chunk
+    copies = []
+    for which, (source, target) in enumerate(((k_hbm, kbuf), (s_hbm, sbuf))):
+        for i in range(count):
+            rows = pl.ds(i * chunk, chunk)
+            copy = pltpu.make_async_copy(source.at[rows], target.at[rows], sems.at[which, i])
+            copy.start()
+            copies.append(copy)
+    u = u_ref[...]
+    for i in range(count):
+        rows = pl.ds(i * chunk, chunk)
+        copies[i].wait()
+        product = dot(kbuf[rows, :], u)
+        mixed[rows, :] = (0.5 * u_ref[rows, :].astype(f32) + product).astype(bf16)
+    m = mixed[...]
+    for i in range(count):
+        rows = pl.ds(i * chunk, chunk)
+        copies[count + i].wait()
+        flux_ref[rows, :] = dot(sbuf[rows, :], m).astype(bf16)
+    at = 0
+    for d, size in ((4, face), (2, corner), (7, corner), (3, face), (0, corner), (5, corner), (6, face), (1, face)):
+        picked = dot(sel_ref[d, :size, :], flux_ref[d * face : (d + 1) * face, :])
+        packed_ref[at : at + size, :] = picked.astype(bf16)
+        at += size
+
+
+def products(u, kernel, inverse, selector):
+    nodes, width = u.shape
+    face = selector.shape[1]
+    corner = face // 8
+    chunk = 256 if nodes % 256 == 0 else nodes
+    vmem = pl.BlockSpec(memory_space=pltpu.VMEM)
+    hbm = pl.BlockSpec(memory_space=pl.ANY)
+    return pl.pallas_call(
+        functools.partial(products_kernel, face, corner, chunk),
+        out_shape=(
+            jax.ShapeDtypeStruct((nodes, width), bf16),
+            jax.ShapeDtypeStruct((4 * (face + corner), width), bf16),
+        ),
+        in_specs=[vmem, hbm, hbm, vmem],
+        out_specs=(vmem, vmem),
+        scratch_shapes=[
+            pltpu.VMEM((nodes, nodes), bf16),
+            pltpu.VMEM((nodes, nodes), bf16),
+            pltpu.VMEM((nodes, width), bf16),
+            pltpu.SemaphoreType.DMA((2, nodes // chunk)),
+        ],
+        compiler_params=pltpu.CompilerParams(vmem_limit_bytes=32 * 1024 * 1024),
+        cost_estimate=pl.CostEstimate(
+            flops=4 * nodes * nodes * width, bytes_accessed=4 * nodes * nodes, transcendentals=0
+        ),
+        name="products",
+    )(u, kernel, inverse, selector)
 
 
 def pair_relay(axis, forward, backward):
@@ -27,14 +88,14 @@
     return from_next, from_previous
 
 
-def exchange(outgoing, corner):
-    face = outgoing.shape[1]
-    right = jnp.concatenate([outgoing[4], outgoing[2, :corner], outgoing[7, :corner]])
-    left = jnp.concatenate([outgoing[3], outgoing[0, :corner], outgoing[5, :corner]])
+def exchange(packed, face, corner):
+    group = face + 2 * corner
+    right, left = packed[:group], packed[group : 2 * group]
+    six, one = packed[2 * group : 2 * group + face], packed[2 * group + face :]
     from_right, from_left = pair_relay("col", right, left)
-    up = jnp.concatenate([outgoing[6], from_right[face + corner :], from_left[face + corner :]])
+    up = jnp.concatenate([six, from_right[face + corner :], from_left[face + corner :]])
     down = jnp.concatenate(
-        [outgoing[1], from_right[face : face + corner], from_left[face : face + corner]]
+        [one, from_right[face : face + corner], from_left[face : face + corner]]
     )
     from_up, from_down = pair_relay("sub", up, down)
     wide = lambda rows: jnp.pad(rows, ((0, face - corner), (0, 0)))
@@ -99,13 +160,8 @@
     rest_zeros = jnp.zeros((node_count - band_rows, rhs_count), f32)
     subs = lax.axis_size("sub")
     for iteration in range(ITERS):
-        mixed = (0.5 * trace_now.astype(f32) + dot(kernel, trace_now)).astype(bf16)
-        flux_now = dot(inverse, mixed).astype(bf16)
-        banded = flux_now[:band_rows].reshape(8, slot_count, rhs_count)
-        outgoing = jnp.einsum(
-            "dpq,dqr->dpr", selector, banded, preferred_element_type=f32
-        ).astype(bf16)
-        received = exchange(outgoing, corner)
+        flux_now, packed = products(trace_now, kernel, inverse, selector)
+        received = exchange(packed, slot_count, corner)
         placed = jnp.einsum("dpq,dpr->dqr", selector, received, preferred_element_type=f32)
         placed = placed.reshape(band_rows, rhs_count)
         assembled = flux_now.astype(f32) + jnp.concatenate([placed, rest_zeros], axis=0)

time: 132 us -> 135 us (1.023)
  matrix products: 25 us -> 4.51 us
  Pallas kernels: 0 us -> 15.5 us
  local copies, waits for them, and re-layouts: 5.48 us -> 11.4 us
    dot_general x12 -> x9, matrix products: 23.4 us -> 3.1 us  [dot(): return lax.dot_general(a, b, dims, preferred_element_type=f32)]
    pallas_call x0 -> x3, Pallas kernels: none -> 15.5 us  [products(): pl.pallas_call(functools.partial(products_kernel, face, corner, chunk), o...]
    unnamed x35 -> x43, local copies, waits for them, and re-layouts: 3.46 us -> 10.6 us
  transfers between devices with their start and end apart: 19 -> 19, of which waited for: 19 -> 19; matrix products, arithmetic and copies ran while one was open for 1% -> 0% of each run, Pallas kernels for 0% -> 0%
where the time goes in v2:
time: 135 us
  waiting for transfers between devices  41 us (30%)
  starting transfers between devices  35.7 us (26%)
  blocking collectives  23.2 us (17%)
  Pallas kernels  15.5 us (11%)
  local copies, waits for them, and re-layouts  11.4 us (8%)
  matrix products  4.51 us (3%)
  other arithmetic  1.96 us (1%)
  between operations  1.38 us (1%)
    all_to_all x2, blocking collectives, local(): lax.all_to_all(copies.reshape(subs * MODES, rhs_count), 'sub', 0, 0, tile...  23.2 us
    ppermute x6, starting transfers between devices, pair_relay(): relayed = lax.ppermute(got[1], axis, onward + back)  19.6 us
    pallas_call x3, Pallas kernels, products(): pl.pallas_call(functools.partial(products_kernel, face, corner, chunk), o...  15.5 us
    ppermute x6, waiting for transfers between devices, pair_relay(): got = lax.ppermute(sent, axis, [(i, i ^ 1) for i in range(devices)])  14.6 us
    unnamed x43, local copies, waits for them, and re-layouts  10.6 us
    ppermute x6, waiting for transfers between devices, pair_relay(): relayed = lax.ppermute(got[1], axis, onward + back)  9.79 us
    ppermute x6, waiting for transfers between devices, sum_over_columns(): got = lax.ppermute(sent, axis, [(i, i ^ step) for i in range(devices)])  9.27 us
    ppermute x6, starting transfers between devices, sum_over_columns(): got = lax.ppermute(sent, axis, [(i, i ^ step) for i in range(devices)])  7.39 us
  transfers between devices with their start and end apart: 19, of which 19 were waited for; matrix products, arithmetic and copies ran while one was open for 0% of the time, Pallas kernels for 0%

profile of v2, /device:TPU:0, one launch (start us, length us, event | category | flops | bytes accessed | tf_op | source)
XLA Modules:
  0.0 134.6 jit_solution(13712580228063846512)
XLA Ops:
  0.7 0.8 bitcast_subtract_fusion
  1.7 2.3 %copy-done.1 = bf16[1,1,1536,1536]{3,2,1,0:T(8,128)(2,1)S(1)} copy-done((bf16[1,1,1536,1536]{3,2,1,0:T(8,128)(2,1)S(1)}, bf16[1,1,1536,1536]{3,2,1,0:T(8,128)(2,1)}, u32[]{:S(2)}) %copy-start.1) | copy-done | bytes 4718616
  4.0 2.3 %copy-done.3 = bf16[1,1,1536,1536]{3,2,1,0:T(8,128)(2,1)S(1)} copy-done((bf16[1,1,1536,1536]{3,2,1,0:T(8,128)(2,1)S(1)}, bf16[1,1,1536,1536]{3,2,1,0:T(8,128)(2,1)}, u32[]{:S(2)}) %copy-start.3) | copy-done | bytes 4718616
  6.4 1.0 copy-done.5
  7.4 5.2 %products.3 = (bf16[1536,128]{1,0:T(8,128)(2,1)S(1)}, bf16[576,128]{1,0:T(8,128)(2,1)S(1)}) custom-call(bf16[1536,128]{1,0:T(8,128)(2,1)S(1)} %bitcast.212, bf16[1536,1536]{1,0:T(8,128)(2,1)S(1)} %bitcast.206, bf16[1536,1536]{1,0:T(8,128)(2,1)S(1)} %bitcast.209, bf16[8,128,128]{2,1,0:T(8,128)(2,1)S(1)} %fusion.10.sel_ref), custom_call_target="tpu_custom_call" | custom-call | flops 1207959552 | bytes 9437184 | tf_op jit(solution)/shard_map/products/pallas_call | solution.py:56
  12.6 0.5 collective-permute-start
  13.1 0.9 collective-permute-done
  14.0 4.8 %collective-permute-start.1 = (bf16[160,128]{1,0:T(8,128)(2,1)S(1)}, bf16[160,128]{1,0:T(8,128)(2,1)S(1)}, u32[]{:S(2)}, u32[]{:S(2)}) collective-permute-start(bf16[160,128]{1,0:T(8,128)(2,1)S(1)} %slice_bitcast_fusion.10), channel_id=1, source_target_pairs={{0,2},{3,1},{4,6},{7,5},{8,10},{11,9},{12,14},{15,13},{16,18},{19,... | collective-permute-start | bytes 122888 | tf_op jit(solution)/shard_map/ppermute | solution.py:85
  18.8 1.6 %collective-permute-done.1 = bf16[160,128]{1,0:T(8,128)(2,1)S(1)} collective-permute-done((bf16[160,128]{1,0:T(8,128)(2,1)S(1)}, bf16[160,128]{1,0:T(8,128)(2,1)S(1)}, u32[]{:S(2)}, u32[]{:S(2)}) %collective-permute-start.1) | collective-permute-done | bytes 40992 | tf_op jit(solution)/shard_map/ppermute | solution.py:85
  20.5 1.6 %collective-permute-start.2 = (bf16[2,160,128]{2,1,0:T(8,128)(2,1)S(1)}, bf16[2,160,128]{2,1,0:T(8,128)(2,1)S(1)}, u32[]{:S(2)}, u32[]{:S(2)}) collective-permute-start(bf16[2,160,128]{2,1,0:T(8,128)(2,1)S(1)} %pad_maximum_fusion.1), channel_id=1, source_target_pairs={{0,4},{4,0},{8,12},{12,8},{16,20},{20,16},{24,28},{28,24},{1,5},{5... | collective-permute-start | bytes 245768 | tf_op jit(solution)/shard_map/ppermute | solution.py:82
  22.1 3.0 %collective-permute-done.2 = bf16[2,160,128]{2,1,0:T(8,128)(2,1)S(1)} collective-permute-done((bf16[2,160,128]{2,1,0:T(8,128)(2,1)S(1)}, bf16[2,160,128]{2,1,0:T(8,128)(2,1)S(1)}, u32[]{:S(2)}, u32[]{:S(2)}) %collective-permute-start.2) | collective-permute-done | bytes 81952 | tf_op jit(solution)/shard_map/ppermute | solution.py:82
  25.0 3.5 %collective-permute-start.3 = (bf16[160,128]{1,0:T(8,128)(2,1)S(1)}, bf16[160,128]{1,0:T(8,128)(2,1)S(1)}, u32[]{:S(2)}, u32[]{:S(2)}) collective-permute-start(bf16[160,128]{1,0:T(8,128)(2,1)S(1)} %slice_bitcast_fusion.9), channel_id=1, source_target_pairs={{0,8},{8,16},{16,24},{12,4},{20,12},{28,20},{1,9},{9,17},{17,25},{... | collective-permute-start | bytes 122888 | tf_op jit(solution)/shard_map/ppermute | solution.py:85
  28.6 1.6 %collective-permute-done.3 = bf16[160,128]{1,0:T(8,128)(2,1)S(1)} collective-permute-done((bf16[160,128]{1,0:T(8,128)(2,1)S(1)}, bf16[160,128]{1,0:T(8,128)(2,1)S(1)}, u32[]{:S(2)}, u32[]{:S(2)}) %collective-permute-start.3) | collective-permute-done | bytes 40992 | tf_op jit(solution)/shard_map/ppermute | solution.py:85
  30.3 0.5 fusion.9
  31.1 0.7 broadcast_in_dim.46
  31.8 5.6 %all-to-all-start = ((bf16[8,64,128]{2,1,0:T(8,128)(2,1)}), bf16[8,64,128]{2,1,0:T(8,128)(2,1)S(1)}, u32[]{:S(2)}, u32[]{:S(2)}) async-start(bf16[8,64,128]{2,1,0:T(8,128)(2,1)} %broadcast_in_dim.46), calls=%async_computation | async-start | bytes 262144 | tf_op jit(solution)/shard_map/all_to_all | solution.py:171
  37.5 7.3 %all-to-all-done = bf16[8,64,128]{2,1,0:T(8,128)(2,1)S(1)} async-done(((bf16[8,64,128]{2,1,0:T(8,128)(2,1)}), bf16[8,64,128]{2,1,0:T(8,128)(2,1)S(1)}, u32[]{:S(2)}, u32[]{:S(2)}) %all-to-all-start) | async-done | bytes 131104 | tf_op jit(solution)/shard_map/all_to_all | solution.py:171
  45.1 2.4 %collective-permute-start.4 = (bf16[128,128]{0,1:T(8,128)(2,1)S(1)}, bf16[128,128]{0,1:T(8,128)(2,1)S(1)}, u32[]{:S(2)}, u32[]{:S(2)}) collective-permute-start(bf16[128,128]{0,1:T(8,128)(2,1)S(1)} %select_convert_fusion.5), channel_id=1, source_target_pairs={{0,2},{1,3},{2,0},{3,1},{4,6},{5,7},{6,4},{7,5},{8,10},{9,11},{10,... | collective-permute-start | bytes 98312 | tf_op jit(solution)/shard_map/ppermute | solution.py:125
  47.4 1.9 %collective-permute-done.4 = bf16[128,128]{0,1:T(8,128)(2,1)S(1)} collective-permute-done((bf16[128,128]{0,1:T(8,128)(2,1)S(1)}, bf16[128,128]{0,1:T(8,128)(2,1)S(1)}, u32[]{:S(2)}, u32[]{:S(2)}) %collective-permute-start.4) | collective-permute-done | bytes 32800 | tf_op jit(solution)/shard_map/ppermute | solution.py:125
  49.5 1.2 collective-permute-done.5
  51.1 2.3 %copy-done.2 = bf16[1,1,1536,1536]{3,2,1,0:T(8,128)(2,1)S(1)} copy-done((bf16[1,1,1536,1536]{3,2,1,0:T(8,128)(2,1)S(1)}, bf16[1,1,1536,1536]{3,2,1,0:T(8,128)(2,1)}, u32[]{:S(2)}) %copy-start.2) | copy-done | bytes 4718616
  53.4 2.3 %copy-done.4 = bf16[1,1,1536,1536]{3,2,1,0:T(8,128)(2,1)S(1)} copy-done((bf16[1,1,1536,1536]{3,2,1,0:T(8,128)(2,1)S(1)}, bf16[1,1,1536,1536]{3,2,1,0:T(8,128)(2,1)}, u32[]{:S(2)}) %copy-start.4) | copy-done | bytes 4718616
  55.8 5.2 %products.4 = (bf16[1536,128]{1,0:T(8,128)(2,1)S(1)}, bf16[576,128]{1,0:T(8,128)(2,1)S(1)}) custom-call(bf16[1536,128]{1,0:T(8,128)(2,1)S(1)} %fusion.u_ref, bf16[1536,1536]{1,0:T(8,128)(2,1)S(1)} %bitcast.207, bf16[1536,1536]{1,0:T(8,128)(2,1)S(1)} %bitcast.210, bf16[8,128,128]{2,1,0:T(8,128)(2,1)S(1)} %fusion.10.sel_ref), custom_call_target="tpu_custom_call" | custom-call | flops 1207959552 | bytes 9437184 | tf_op jit(solution)/shard_map/products/pallas_call | solution.py:56
  61.2 1.1 collective-permute-done.6
  62.3 3.9 %collective-permute-start.7 = (bf16[160,128]{1,0:T(8,128)(2,1)S(1)}, bf16[160,128]{1,0:T(8,128)(2,1)S(1)}, u32[]{:S(2)}, u32[]{:S(2)}) collective-permute-start(bf16[160,128]{1,0:T(8,128)(2,1)S(1)} %slice_bitcast_fusion.6), channel_id=1, source_target_pairs={{0,2},{3,1},{4,6},{7,5},{8,10},{11,9},{12,14},{15,13},{16,18},{19,... | collective-permute-start | bytes 122888 | tf_op jit(solution)/shard_map/ppermute | solution.py:85
  66.2 1.6 %collective-permute-done.7 = bf16[160,128]{1,0:T(8,128)(2,1)S(1)} collective-permute-done((bf16[160,128]{1,0:T(8,128)(2,1)S(1)}, bf16[160,128]{1,0:T(8,128)(2,1)S(1)}, u32[]{:S(2)}, u32[]{:S(2)}) %collective-permute-start.7) | collective-permute-done | bytes 40992 | tf_op jit(solution)/shard_map/ppermute | solution.py:85
  68.2 4.2 %collective-permute-done.8 = bf16[2,160,128]{2,1,0:T(8,128)(2,1)S(1)} collective-permute-done((bf16[2,160,128]{2,1,0:T(8,128)(2,1)S(1)}, bf16[2,160,128]{2,1,0:T(8,128)(2,1)S(1)}, u32[]{:S(2)}, u32[]{:S(2)}) %collective-permute-start.8) | collective-permute-done | bytes 81952 | tf_op jit(solution)/shard_map/ppermute | solution.py:82
  72.5 1.8 %collective-permute-start.9 = (bf16[160,128]{1,0:T(8,128)(2,1)S(1)}, bf16[160,128]{1,0:T(8,128)(2,1)S(1)}, u32[]{:S(2)}, u32[]{:S(2)}) collective-permute-start(bf16[160,128]{1,0:T(8,128)(2,1)S(1)} %slice_bitcast_fusion.5), channel_id=1, source_target_pairs={{0,8},{8,16},{16,24},{12,4},{20,12},{28,20},{1,9},{9,17},{17,25},{... | collective-permute-start | bytes 122888 | tf_op jit(solution)/shard_map/ppermute | solution.py:85
  74.2 1.7 %collective-permute-done.9 = bf16[160,128]{1,0:T(8,128)(2,1)S(1)} collective-permute-done((bf16[160,128]{1,0:T(8,128)(2,1)S(1)}, bf16[160,128]{1,0:T(8,128)(2,1)S(1)}, u32[]{:S(2)}, u32[]{:S(2)}) %collective-permute-start.9) | collective-permute-done | bytes 40992 | tf_op jit(solution)/shard_map/ppermute | solution.py:85
  76.1 0.5 fusion.8
  76.9 11.6 %all_to_all.27 = bf16[8,64,128]{2,1,0:T(8,128)(2,1)S(1)} all-to-all(bf16[8,64,128]{2,1,0:T(8,128)(2,1)S(1)} %broadcast_in_dim.47), channel_id=1, replica_groups=mesh['sub'=8,'col'=4] {'sub'}, dimensions={0} | all-to-all | bytes 262144 | tf_op jit(solution)/shard_map/all_to_all | solution.py:171
  88.8 2.4 %collective-permute-start.10 = (bf16[128,128]{0,1:T(8,128)(2,1)S(1)}, bf16[128,128]{0,1:T(8,128)(2,1)S(1)}, u32[]{:S(2)}, u32[]{:S(2)}) collective-permute-start(bf16[128,128]{0,1:T(8,128)(2,1)S(1)} %select_convert_fusion.3), channel_id=1, source_target_pairs={{0,2},{1,3},{2,0},{3,1},{4,6},{5,7},{6,4},{7,5},{8,10},{9,11},{10,... | collective-permute-start | bytes 98312 | tf_op jit(solution)/shard_map/ppermute | solution.py:125
  91.2 1.9 %collective-permute-done.10 = bf16[128,128]{0,1:T(8,128)(2,1)S(1)} collective-permute-done((bf16[128,128]{0,1:T(8,128)(2,1)S(1)}, bf16[128,128]{0,1:T(8,128)(2,1)S(1)}, u32[]{:S(2)}, u32[]{:S(2)}) %collective-permute-start.10) | collective-permute-done | bytes 32800 | tf_op jit(solution)/shard_map/ppermute | solution.py:125
  93.2 1.2 collective-permute-done.11
  94.4 0.4 fusion.1.u_ref
  94.8 5.2 %products.5 = (bf16[1536,128]{1,0:T(8,128)(2,1)S(1)}, bf16[576,128]{1,0:T(8,128)(2,1)S(1)}) custom-call(bf16[1536,128]{1,0:T(8,128)(2,1)S(1)} %fusion.1.u_ref, bf16[1536,1536]{1,0:T(8,128)(2,1)S(1)} %bitcast.208, bf16[1536,1536]{1,0:T(8,128)(2,1)S(1)} %bitcast.211, bf16[8,128,128]{2,1,0:T(8,128)(2,1)S(1)} %fusion.10.sel_ref), custom_call_target="tpu_custom_call" | custom-call | flops 1207959552 | bytes 9437184 | tf_op jit(solution)/shard_map/products/pallas_call | solution.py:56
  100.2 1.1 collective-permute-done.12
  101.4 3.9 %collective-permute-start.13 = (bf16[160,128]{1,0:T(8,128)(2,1)S(1)}, bf16[160,128]{1,0:T(8,128)(2,1)S(1)}, u32[]{:S(2)}, u32[]{:S(2)}) collective-permute-start(bf16[160,128]{1,0:T(8,128)(2,1)S(1)} %slice_bitcast_fusion.2), channel_id=1, source_target_pairs={{0,2},{3,1},{4,6},{7,5},{8,10},{11,9},{12,14},{15,13},{16,18},{19,... | collective-permute-start | bytes 122888 | tf_op jit(solution)/shard_map/ppermute | solution.py:85
  105.3 1.6 %collective-permute-done.13 = bf16[160,128]{1,0:T(8,128)(2,1)S(1)} collective-permute-done((bf16[160,128]{1,0:T(8,128)(2,1)S(1)}, bf16[160,128]{1,0:T(8,128)(2,1)S(1)}, u32[]{:S(2)}, u32[]{:S(2)}) %collective-permute-start.13) | collective-permute-done | bytes 40992 | tf_op jit(solution)/shard_map/ppermute | solution.py:85
  107.3 4.2 %collective-permute-done.14 = bf16[2,160,128]{2,1,0:T(8,128)(2,1)S(1)} collective-permute-done((bf16[2,160,128]{2,1,0:T(8,128)(2,1)S(1)}, bf16[2,160,128]{2,1,0:T(8,128)(2,1)S(1)}, u32[]{:S(2)}, u32[]{:S(2)}) %collective-permute-start.14) | collective-permute-done | bytes 81952 | tf_op jit(solution)/shard_map/ppermute | solution.py:82
  111.5 1.8 %collective-permute-start.15 = (bf16[160,128]{1,0:T(8,128)(2,1)S(1)}, bf16[160,128]{1,0:T(8,128)(2,1)S(1)}, u32[]{:S(2)}, u32[]{:S(2)}) collective-permute-start(bf16[160,128]{1,0:T(8,128)(2,1)S(1)} %slice_bitcast_fusion.1), channel_id=1, source_target_pairs={{0,8},{8,16},{16,24},{12,4},{20,12},{28,20},{1,9},{9,17},{17,25},{... | collective-permute-start | bytes 122888 | tf_op jit(solution)/shard_map/ppermute | solution.py:85
  113.3 1.7 %collective-permute-done.15 = bf16[160,128]{1,0:T(8,128)(2,1)S(1)} collective-permute-done((bf16[160,128]{1,0:T(8,128)(2,1)S(1)}, bf16[160,128]{1,0:T(8,128)(2,1)S(1)}, u32[]{:S(2)}, u32[]{:S(2)}) %collective-permute-start.15) | collective-permute-done | bytes 40992 | tf_op jit(solution)/shard_map/ppermute | solution.py:85
  115.1 0.5 fusion.7
  116.0 11.6 %all_to_all.28 = bf16[8,64,128]{2,1,0:T(8,128)(2,1)S(1)} all-to-all(bf16[8,64,128]{2,1,0:T(8,128)(2,1)S(1)} %broadcast_in_dim.48), channel_id=1, replica_groups=mesh['sub'=8,'col'=4] {'sub'}, dimensions={0} | all-to-all | bytes 262144 | tf_op jit(solution)/shard_map/all_to_all | solution.py:171
  127.8 2.4 %collective-permute-start.16 = (bf16[128,128]{0,1:T(8,128)(2,1)S(1)}, bf16[128,128]{0,1:T(8,128)(2,1)S(1)}, u32[]{:S(2)}, u32[]{:S(2)}) collective-permute-start(bf16[128,128]{0,1:T(8,128)(2,1)S(1)} %select_convert_fusion.1), channel_id=1, source_target_pairs={{0,2},{1,3},{2,0},{3,1},{4,6},{5,7},{6,4},{7,5},{8,10},{9,11},{10,... | collective-permute-start | bytes 98312 | tf_op jit(solution)/shard_map/ppermute | solution.py:125
  130.2 1.9 %collective-permute-done.16 = bf16[128,128]{0,1:T(8,128)(2,1)S(1)} collective-permute-done((bf16[128,128]{0,1:T(8,128)(2,1)S(1)}, bf16[128,128]{0,1:T(8,128)(2,1)S(1)}, u32[]{:S(2)}, u32[]{:S(2)}) %collective-permute-start.16) | collective-permute-done | bytes 32800 | tf_op jit(solution)/shard_map/ppermute | solution.py:125
  132.3 1.2 collective-permute-done.17
  133.5 1.1 fusion.3
  (111 shorter events, 4.4 us)
Async XLA Ops:
  0.6 44.2 %copy-start = (bf16[256,512]{1,0:T(8,128)(2,1)S(1)}, bf16[256,512]{1,0:T(8,128)(2,1)}, u32[]{:S(2)}) copy-start(bf16[256,512]{1,0:T(8,128)(2,1)} %param.15) | copy-start | bytes 786436
  1.7 2.3 %copy-start.1 = (bf16[1,1,1536,1536]{3,2,1,0:T(8,128)(2,1)S(1)}, bf16[1,1,1536,1536]{3,2,1,0:T(8,128)(2,1)}, u32[]{:S(2)}) copy-start(bf16[1,1,1536,1536]{3,2,1,0:T(8,128)(2,1)} %param.10) | copy-start | bytes 14155780
  4.0 2.3 %copy-start.3 = (bf16[1,1,1536,1536]{3,2,1,0:T(8,128)(2,1)S(1)}, bf16[1,1,1536,1536]{3,2,1,0:T(8,128)(2,1)}, u32[]{:S(2)}) copy-start(bf16[1,1,1536,1536]{3,2,1,0:T(8,128)(2,1)} %param.11) | copy-start | bytes 14155780
  6.4 1.0 copy-start.5
  7.4 21.2 %copy-start.9 = (s32[1,1,1536]{2,1,0:T(1,128)S(1)}, s32[1,1,1536]{2,1,0:T(1,128)}, u32[]{:S(2)}) copy-start(s32[1,1,1536]{2,1,0:T(1,128)} %param.13) | copy-start | bytes 18436
  7.4 21.2 %copy-start.10 = (bf16[1,1,1536]{2,1,0:T(2,128)(2,1)S(1)}, bf16[1,1,1536]{2,1,0:T(2,128)(2,1)}, u32[]{:S(2)}) copy-start(bf16[1,1,1536]{2,1,0:T(2,128)(2,1)} %param.14) | copy-start | bytes 9220
  7.4 23.4 %copy-start.7 = (bf16[1,1,1536,128]{3,2,1,0:T(8,128)(2,1)S(1)}, bf16[1,1,1536,128]{3,2,1,0:T(8,128)(2,1)}, u32[]{:S(2)}) copy-start(bf16[1,1,1536,128]{3,2,1,0:T(8,128)(2,1)} %param.9) | copy-start | bytes 1179652
  12.5 38.2 %copy-start.6 = (bf16[1,1,1536,128]{3,2,1,0:T(8,128)(2,1)S(1)}, bf16[1,1,1536,128]{3,2,1,0:T(8,128)(2,1)}, u32[]{:S(2)}) copy-start(bf16[1,1,1536,128]{3,2,1,0:T(8,128)(2,1)} %param.8) | copy-start | bytes 1179652
  12.6 1.4 %collective-permute-start = (bf16[2,160,128]{2,1,0:T(8,128)(2,1)S(1)}, bf16[2,160,128]{2,1,0:T(8,128)(2,1)S(1)}, u32[]{:S(2)}, u32[]{:S(2)}) collective-permute-start(bf16[2,160,128]{2,1,0:T(8,128)(2,1)S(1)} %pad_maximum_fusion), channel_id=1, source_target_pairs={{0,1},{1,0},{2,3},{3,2},{4,5},{5,4},{6,7},{7,6},{8,9},{9,8},{10,11... | collective-permute-start | bytes 245768 | tf_op jit(solution)/shard_map/ppermute | solution.py:82
  14.0 6.4 %collective-permute-start.1 = (bf16[160,128]{1,0:T(8,128)(2,1)S(1)}, bf16[160,128]{1,0:T(8,128)(2,1)S(1)}, u32[]{:S(2)}, u32[]{:S(2)}) collective-permute-start(bf16[160,128]{1,0:T(8,128)(2,1)S(1)} %slice_bitcast_fusion.10), channel_id=1, source_target_pairs={{0,2},{3,1},{4,6},{7,5},{8,10},{11,9},{12,14},{15,13},{16,18},{19,... | collective-permute-start | bytes 122888 | tf_op jit(solution)/shard_map/ppermute | solution.py:85
  20.5 4.5 %collective-permute-start.2 = (bf16[2,160,128]{2,1,0:T(8,128)(2,1)S(1)}, bf16[2,160,128]{2,1,0:T(8,128)(2,1)S(1)}, u32[]{:S(2)}, u32[]{:S(2)}) collective-permute-start(bf16[2,160,128]{2,1,0:T(8,128)(2,1)S(1)} %pad_maximum_fusion.1), channel_id=1, source_target_pairs={{0,4},{4,0},{8,12},{12,8},{16,20},{20,16},{24,28},{28,24},{1,5},{5... | collective-permute-start | bytes 245768 | tf_op jit(solution)/shard_map/ppermute | solution.py:82
  25.0 5.1 %collective-permute-start.3 = (bf16[160,128]{1,0:T(8,128)(2,1)S(1)}, bf16[160,128]{1,0:T(8,128)(2,1)S(1)}, u32[]{:S(2)}, u32[]{:S(2)}) collective-permute-start(bf16[160,128]{1,0:T(8,128)(2,1)S(1)} %slice_bitcast_fusion.9), channel_id=1, source_target_pairs={{0,8},{8,16},{16,24},{12,4},{20,12},{28,20},{1,9},{9,17},{17,25},{... | collective-permute-start | bytes 122888 | tf_op jit(solution)/shard_map/ppermute | solution.py:85
  31.8 13.0 %all-to-all-start = ((bf16[8,64,128]{2,1,0:T(8,128)(2,1)}), bf16[8,64,128]{2,1,0:T(8,128)(2,1)S(1)}, u32[]{:S(2)}, u32[]{:S(2)}) async-start(bf16[8,64,128]{2,1,0:T(8,128)(2,1)} %broadcast_in_dim.46), calls=%async_computation | async-start | bytes 262144 | tf_op jit(solution)/shard_map/all_to_all | solution.py:171
  45.1 4.3 %collective-permute-start.4 = (bf16[128,128]{0,1:T(8,128)(2,1)S(1)}, bf16[128,128]{0,1:T(8,128)(2,1)S(1)}, u32[]{:S(2)}, u32[]{:S(2)}) collective-permute-start(bf16[128,128]{0,1:T(8,128)(2,1)S(1)} %select_convert_fusion.5), channel_id=1, source_target_pairs={{0,2},{1,3},{2,0},{3,1},{4,6},{5,7},{6,4},{7,5},{8,10},{9,11},{10,... | collective-permute-start | bytes 98312 | tf_op jit(solution)/shard_map/ppermute | solution.py:125
  49.4 1.3 collective-permute-start.5
  51.1 2.3 %copy-start.2 = (bf16[1,1,1536,1536]{3,2,1,0:T(8,128)(2,1)S(1)}, bf16[1,1,1536,1536]{3,2,1,0:T(8,128)(2,1)}, u32[]{:S(2)}) copy-start(bf16[1,1,1536,1536]{3,2,1,0:T(8,128)(2,1)} %param.10) | copy-start | bytes 14155780
  53.4 2.3 %copy-start.4 = (bf16[1,1,1536,1536]{3,2,1,0:T(8,128)(2,1)S(1)}, bf16[1,1,1536,1536]{3,2,1,0:T(8,128)(2,1)}, u32[]{:S(2)}) copy-start(bf16[1,1,1536,1536]{3,2,1,0:T(8,128)(2,1)} %param.11) | copy-start | bytes 14155780
  61.0 1.3 collective-permute-start.6
  62.3 5.6 %collective-permute-start.7 = (bf16[160,128]{1,0:T(8,128)(2,1)S(1)}, bf16[160,128]{1,0:T(8,128)(2,1)S(1)}, u32[]{:S(2)}, u32[]{:S(2)}) collective-permute-start(bf16[160,128]{1,0:T(8,128)(2,1)S(1)} %slice_bitcast_fusion.6), channel_id=1, source_target_pairs={{0,2},{3,1},{4,6},{7,5},{8,10},{11,9},{12,14},{15,13},{16,18},{19,... | collective-permute-start | bytes 122888 | tf_op jit(solution)/shard_map/ppermute | solution.py:85
  68.0 4.5 %collective-permute-start.8 = (bf16[2,160,128]{2,1,0:T(8,128)(2,1)S(1)}, bf16[2,160,128]{2,1,0:T(8,128)(2,1)S(1)}, u32[]{:S(2)}, u32[]{:S(2)}) collective-permute-start(bf16[2,160,128]{2,1,0:T(8,128)(2,1)S(1)} %pad_maximum_fusion.3), channel_id=1, source_target_pairs={{0,4},{4,0},{8,12},{12,8},{16,20},{20,16},{24,28},{28,24},{1,5},{5... | collective-permute-start | bytes 245768 | tf_op jit(solution)/shard_map/ppermute | solution.py:82
  72.5 3.4 %collective-permute-start.9 = (bf16[160,128]{1,0:T(8,128)(2,1)S(1)}, bf16[160,128]{1,0:T(8,128)(2,1)S(1)}, u32[]{:S(2)}, u32[]{:S(2)}) collective-permute-start(bf16[160,128]{1,0:T(8,128)(2,1)S(1)} %slice_bitcast_fusion.5), channel_id=1, source_target_pairs={{0,8},{8,16},{16,24},{12,4},{20,12},{28,20},{1,9},{9,17},{17,25},{... | collective-permute-start | bytes 122888 | tf_op jit(solution)/shard_map/ppermute | solution.py:85
  88.8 4.3 %collective-permute-start.10 = (bf16[128,128]{0,1:T(8,128)(2,1)S(1)}, bf16[128,128]{0,1:T(8,128)(2,1)S(1)}, u32[]{:S(2)}, u32[]{:S(2)}) collective-permute-start(bf16[128,128]{0,1:T(8,128)(2,1)S(1)} %select_convert_fusion.3), channel_id=1, source_target_pairs={{0,2},{1,3},{2,0},{3,1},{4,6},{5,7},{6,4},{7,5},{8,10},{9,11},{10,... | collective-permute-start | bytes 98312 | tf_op jit(solution)/shard_map/ppermute | solution.py:125
  93.2 1.3 collective-permute-start.11
  100.0 1.3 collective-permute-start.12
  101.4 5.6 %collective-permute-start.13 = (bf16[160,128]{1,0:T(8,128)(2,1)S(1)}, bf16[160,128]{1,0:T(8,128)(2,1)S(1)}, u32[]{:S(2)}, u32[]{:S(2)}) collective-permute-start(bf16[160,128]{1,0:T(8,128)(2,1)S(1)} %slice_bitcast_fusion.2), channel_id=1, source_target_pairs={{0,2},{3,1},{4,6},{7,5},{8,10},{11,9},{12,14},{15,13},{16,18},{19,... | collective-permute-start | bytes 122888 | tf_op jit(solution)/shard_map/ppermute | solution.py:85
  107.0 4.5 %collective-permute-start.14 = (bf16[2,160,128]{2,1,0:T(8,128)(2,1)S(1)}, bf16[2,160,128]{2,1,0:T(8,128)(2,1)S(1)}, u32[]{:S(2)}, u32[]{:S(2)}) collective-permute-start(bf16[2,160,128]{2,1,0:T(8,128)(2,1)S(1)} %pad_maximum_fusion.5), channel_id=1, source_target_pairs={{0,4},{4,0},{8,12},{12,8},{16,20},{20,16},{24,28},{28,24},{1,5},{5... | collective-permute-start | bytes 245768 | tf_op jit(solution)/shard_map/ppermute | solution.py:82
  111.5 3.4 %collective-permute-start.15 = (bf16[160,128]{1,0:T(8,128)(2,1)S(1)}, bf16[160,128]{1,0:T(8,128)(2,1)S(1)}, u32[]{:S(2)}, u32[]{:S(2)}) collective-permute-start(bf16[160,128]{1,0:T(8,128)(2,1)S(1)} %slice_bitcast_fusion.1), channel_id=1, source_target_pairs={{0,8},{8,16},{16,24},{12,4},{20,12},{28,20},{1,9},{9,17},{17,25},{... | collective-permute-start | bytes 122888 | tf_op jit(solution)/shard_map/ppermute | solution.py:85
  115.7 18.9 %copy-start.8 = (bf16[1536,128]{1,0:T(8,128)(2,1)}, bf16[1536,128]{1,0:T(8,128)(2,1)S(1)}, u32[]{:S(2)}) copy-start(bf16[1536,128]{1,0:T(8,128)(2,1)S(1)} %fusion.6) | copy-start | bytes 1179652
  127.8 4.3 %collective-permute-start.16 = (bf16[128,128]{0,1:T(8,128)(2,1)S(1)}, bf16[128,128]{0,1:T(8,128)(2,1)S(1)}, u32[]{:S(2)}, u32[]{:S(2)}) collective-permute-start(bf16[128,128]{0,1:T(8,128)(2,1)S(1)} %select_convert_fusion.1), channel_id=1, source_target_pairs={{0,2},{1,3},{2,0},{3,1},{4,6},{5,7},{6,4},{7,5},{8,10},{9,11},{10,... | collective-permute-start | bytes 98312 | tf_op jit(solution)/shard_map/ppermute | solution.py:125
  132.2 1.3 collective-permute-start.17

commit v3 on v0

v3 whole, which is shorter than its diff:
```python
import functools

import jax
import jax.numpy as jnp
from jax import lax
from jax.experimental import pallas as pl
from jax.experimental.pallas import tpu as pltpu
from jax.sharding import PartitionSpec as P

MODES = 64
ITERS = 3
LANES = 128

bf16 = jnp.bfloat16
f32 = jnp.float32
BOTH = ("sub", "col")
DIRECTIONS = ((-1, -1), (-1, 0), (-1, 1), (0, -1), (0, 1), (1, -1), (1, 0), (1, 1))
PACKED = ((4, 1), (2, 0), (7, 0), (3, 1), (0, 0), (5, 0), (6, 1), (1, 1))

vmem = pl.BlockSpec(memory_space=pltpu.VMEM)
smem = pl.BlockSpec(memory_space=pltpu.SMEM)
hbm = pl.BlockSpec(memory_space=pl.ANY)
shape_of = jax.ShapeDtypeStruct
params = pltpu.CompilerParams(vmem_limit_bytes=24 * 1024 * 1024)
large = pltpu.CompilerParams(vmem_limit_bytes=50 * 1024 * 1024)


def dot(a, b):
    return jnp.dot(a, b, preferred_element_type=f32)


def pick(face, sel_ref, flux_ref, packed_ref):
    at = 0
    for d, whole in PACKED:
        size = face if whole else face // 8
        rows = dot(sel_ref[d, :size, :], flux_ref[d * face : (d + 1) * face, :])
        packed_ref[at : at + size, :] = rows.astype(bf16)
        at += size


def load_kernel(face, chunk, ahead, u_ref, k_hbm, s_hbm, sel_ref, flux_ref, packed_ref, k_ref, s_ref, mixed, sems):
    count = u_ref.shape[0] // chunk
    copies = []
    for which, (source, target) in enumerate(((k_hbm, k_ref), (s_hbm, s_ref))):
        for i in range(count):
            rows = pl.ds(i * chunk, chunk)
            copies.append(pltpu.make_async_copy(source.at[rows], target.at[rows], sems.at[which, i]))
    for copy in copies[:ahead]:
        copy.start()
    u = u_ref[...]
    for i in range(2 * count):
        copies[i].wait()
        if i + ahead < 2 * count:
            copies[i + ahead].start()
        rows = pl.ds(i % count * chunk, chunk)
        if i < count:
            mixed[rows, :] = (0.5 * u_ref[rows, :].astype(f32) + dot(k_ref[rows, :], u)).astype(bf16)
        else:
            flux_ref[rows, :] = dot(s_ref[rows, :], mixed[...]).astype(bf16)
    pick(face, sel_ref, flux_ref, packed_ref)


def products_kernel(face, chunk, u_ref, k_ref, s_ref, sel_ref, flux_ref, packed_ref, mixed):
    u = u_ref[...]
    for i in range(u_ref.shape[0] // chunk):
        rows = pl.ds(i * chunk, chunk)
        mixed[rows, :] = (0.5 * u_ref[rows, :].astype(f32) + dot(k_ref[rows, :], u)).astype(bf16)
    m = mixed[...]
    for i in range(u_ref.shape[0] // chunk):
        rows = pl.ds(i * chunk, chunk)
        flux_ref[rows, :] = dot(s_ref[rows, :], m).astype(bf16)
    pick(face, sel_ref, flux_ref, packed_ref)


def products(u, kernel, inverse, selector, load=False):
    nodes, width = u.shape
    face = selector.shape[1]
    chunk = 256 if nodes % 256 == 0 else nodes
    outs = [shape_of((nodes, width), bf16), shape_of((4 * (face + face // 8), width), bf16)]
    scratch = [pltpu.VMEM((nodes, width), bf16)]
    body = functools.partial(products_kernel, face, chunk)
    if load:
        outs += [pltpu.VMEM((nodes, nodes), bf16)] * 2
        scratch += [pltpu.SemaphoreType.DMA((2, nodes // chunk))]
        body = functools.partial(load_kernel, face, chunk, 3)
    return pl.pallas_call(
        body,
        out_shape=outs,
        in_specs=[vmem] + [hbm if load else vmem] * 2 + [vmem],
        out_specs=[vmem] * len(outs),
        scratch_shapes=scratch,
        compiler_params=large if load else params,
        cost_estimate=pl.CostEstimate(
            flops=4 * nodes * nodes * 2 * LANES, bytes_accessed=4 * nodes * nodes, transcendentals=0
        ),
        name="load_products" if load else "products",
    )(u, kernel, inverse, selector)


def update_kernel(face, first, place, rows_ref, flux_ref, load_ref, state_ref, selt_ref, basis_ref, tall_ref, c_ref, w_ref, wrows_ref, res_ref, next_ref, u_ref, rhs_ref):
    corner = face // 8
    modes = basis_ref.shape[0]
    found = {4: (0, 0), 3: (1, 0), 6: (2, 0), 1: (3, 0)}
    found |= {7: (2, face), 5: (2, face + corner), 2: (3, face), 0: (3, face + corner)}
    flux = flux_ref[...].astype(f32)
    state = state_ref[...].astype(f32)
    if not first:
        start = pl.multiple_of(place[1], modes)
        own = c_ref[place[0], pl.ds(start, modes), :]
        flux = (flux + dot(w_ref[:, :modes], own)).astype(bf16).astype(f32)
        state = state + dot(tall_ref[:, :modes], own)
    assembled = []
    for d in range(8):
        group, at = found[d]
        size = face if DIRECTIONS[d][0] * DIRECTIONS[d][1] == 0 else corner
        arrived = rows_ref[group, at : at + size, :]
        if not first:
            start = pl.multiple_of(place[2 * d + 3], modes)
            theirs = c_ref[place[2 * d + 2], pl.ds(start, modes), :]
            wide = wrows_ref[group, at : at + size, :modes]
            arrived = (arrived.astype(f32) + dot(wide, theirs)).astype(bf16)
        assembled.append(flux[d * face : (d + 1) * face] + dot(selt_ref[d, :, :size], arrived))
    assembled.append(flux[8 * face :])
    residual = (load_ref[...].astype(f32) - jnp.concatenate(assembled)).astype(bf16)
    res_ref[...] = residual
    following = state + 0.25 * residual.astype(f32)
    next_ref[...] = following
    u_ref[...] = following.astype(bf16)
    rhs_ref[...] = dot(basis_ref[...], residual).astype(bf16)


def update(place, rows, flux, load, state, selector_t, basis, tall, coarse, wide, wide_rows):
    first = coarse is None
    nodes, width = load.shape
    modes = basis.shape[0]
    operands = [place, rows, flux, load, state, selector_t, basis, tall]
    body = functools.partial(update_kernel, selector_t.shape[1], first)
    if first:
        inner = body
        body = lambda *refs: inner(*refs[:8], None, None, None, *refs[8:])
    else:
        operands += [coarse, wide, wide_rows]
    return pl.pallas_call(
        body,
        out_shape=[
            shape_of((nodes, width), bf16),
            shape_of((nodes, width), f32),
            shape_of((nodes, width), bf16),
            shape_of((modes, width), bf16),
        ],
        in_specs=[smem] + [vmem] * (len(operands) - 1),
        out_specs=[vmem] * 4,
        compiler_params=params,
        cost_estimate=pl.CostEstimate(
            flops=8 * nodes * LANES * width, bytes_accessed=12 * nodes * width, transcendentals=0
        ),
        name="update",
    )(*operands)


def coarse_kernel(modes, place, pieces_ref, *refs):
    matrices, out_ref, full = refs[:-2], refs[-2], refs[-1]
    count = pieces_ref.shape[0]
    for m in range(count):
        start = pl.multiple_of((place[0] ^ m) * modes, modes)
        for j in range(2):
            full[j, pl.ds(start, modes), :] = pieces_ref[m, j * modes : (j + 1) * modes, :]
    for i, matrix in enumerate(matrices):
        out_ref[i] = dot(matrix[0], full[0]) + dot(matrix[1], full[1])


def coarse_product(place, pieces, matrices):
    count, twice, width = pieces.shape
    rows = matrices[0].shape[1]
    return pl.pallas_call(
        functools.partial(coarse_kernel, twice // 2),
        out_shape=shape_of((len(matrices), rows, width), f32),
        in_specs=[smem] + [vmem] * (1 + len(matrices)),
        out_specs=vmem,
        scratch_shapes=[pltpu.VMEM((2, count * twice // 2, width), bf16)],
        compiler_params=params,
        cost_estimate=pl.CostEstimate(
            flops=2 * len(matrices) * rows * count * twice * width,
            bytes_accessed=2 * len(matrices) * rows * count * twice,
            transcendentals=0,
        ),
        name="coarse_product",
    )(place, pieces, *matrices)


def chip_pairs(subs, cols, step):
    pairs = []
    for sub in range(subs):
        for chip in range(cols // 2):
            to = step(sub, chip)
            if 0 <= to[0] < subs and 0 <= to[1] < cols // 2:
                pairs.append((sub * cols + 2 * chip + 1, to[0] * cols + 2 * to[1] + 1))
    return pairs


class Moves:
    def __init__(self):
        self.subs, self.cols = lax.axis_size("sub"), lax.axis_size("col")
        self.even_sub = lax.axis_index("sub") % 2 == 0
        self.odd_core = lax.axis_index("col") % 2 == 1
        self.chip = lax.axis_index("col") // 2

    def between(self, value, step):
        return lax.ppermute(value, BOTH, chip_pairs(self.subs, self.cols, step))

    def to_odd(self, value):
        return lax.ppermute(value, "col", [(i, i + 1) for i in range(0, self.cols, 2)])

    def to_even(self, value):
        return lax.ppermute(value, "col", [(i + 1, i) for i in range(0, self.cols, 2)])

    def pair(self, value):
        return self.between(value, lambda sub, chip: (sub ^ 1, chip))

    def relay(self, value):
        return self.between(value, lambda sub, chip: (sub + 2 if sub % 2 == 0 else sub - 2, chip))

    def sum_chips(self, value):
        bit = 1
        while bit < self.cols // 2:
            got = self.between(value.astype(bf16), lambda sub, chip: (sub, chip ^ bit))
            value = value + got.astype(f32)
            bit *= 2
        value = value.astype(bf16)
        return jnp.where(self.odd_core, value, self.to_even(value))

    def gather_rows(self, value):
        pieces = value[None]
        while pieces.shape[0] < self.subs:
            bit = pieces.shape[0]
            got = self.between(pieces, lambda sub, chip: (sub ^ bit, chip))
            pieces = jnp.concatenate([pieces, got])
        return pieces

    def exchange(self, packed, face):
        corner = face // 8
        group = face + 2 * corner
        right_way, left_way = slice(0, group), slice(group, 2 * group)
        even = self.to_odd(packed)
        if self.cols == 4:
            sent = jnp.where(self.chip == 0, packed[right_way], even[left_way])
            from_right = from_left = self.between(sent, lambda sub, chip: (sub, 1 - chip))
        else:
            from_left = self.between(packed[right_way], lambda sub, chip: (sub, chip + 1))
            from_right = self.between(even[left_way], lambda sub, chip: (sub, chip - 1))
        right = (packed[left_way], from_right)
        left = (from_left, even[right_way])
        up, down = [], []
        for j, mine in enumerate((even, packed)):
            six, one = mine[2 * group : 2 * group + face], mine[2 * group + face :]
            up.append(jnp.concatenate([six, right[j][face + corner :], left[j][face + corner :]]))
            down.append(
                jnp.concatenate([one, right[j][face : face + corner], left[j][face : face + corner]])
            )
        up, down = jnp.stack(up), jnp.stack(down)
        got = self.pair(
            jnp.stack([jnp.where(self.even_sub, up, down), jnp.where(self.even_sub, down, up)])
        )
        relayed = self.relay(got[1])
        above = jnp.where(self.even_sub, got[0], relayed)
        below = jnp.where(self.even_sub, relayed, got[0])
        theirs, own = (jnp.stack([right[j], left[j], above[j], below[j]]) for j in range(2))
        return jnp.where(self.odd_core, own, self.to_even(theirs))


def local(
    trace_start,
    neumann_load,
    double_layer,
    single_inverse,
    interface_nodes,
    node_mode,
    mode_weight,
    coarse_inverse,
):
    moves = Moves()
    subs, cols = moves.subs, moves.cols
    row, col = lax.axis_index("sub"), lax.axis_index("col")
    trace = trace_start[0, 0]
    load = neumann_load[0, 0]
    width = trace.shape[1]
    interface = interface_nodes[0, 0]
    face = interface.shape[1]
    position = interface - (jnp.arange(8, dtype=jnp.int32) * face)[:, None]
    slots = jnp.arange(face, dtype=jnp.int32)
    selector = (position[:, :, None] == slots[None, None, :]).astype(bf16)
    selector_t = (position[:, None, :] == slots[None, :, None]).astype(bf16)
    nothing = jnp.zeros((), bf16)
    mode, weight = node_mode[0, 0], mode_weight[0, 0]
    modes = jnp.arange(MODES, dtype=jnp.int32)
    lanes = jnp.arange(LANES, dtype=jnp.int32)
    basis = jnp.where(mode[None, :] == modes[:, None], weight[None, :], nothing)
    tall = jnp.where(mode[:, None] == lanes[None, :], weight[:, None], nothing)

    place = [jnp.zeros((), jnp.int32), col * MODES]
    for row_step, col_step in DIRECTIONS:
        source = {0: 0, 1: jnp.where(moves.even_sub, 1, 2), -1: jnp.where(moves.even_sub, 2, 1)}
        place += [source[row_step], jnp.clip(col + col_step, 0, cols - 1) * MODES]
    place = jnp.stack([jnp.asarray(p, jnp.int32) for p in place])
    row_place = jnp.reshape(row, (1,)).astype(jnp.int32)

    matrices = [jnp.stack([moves.to_odd(coarse_inverse), coarse_inverse])]
    matrices.append(moves.pair(matrices[0]))
    matrices.append(moves.relay(matrices[1]))

    flux, packed, kernel, inverse = products(
        trace, double_layer[0, 0], single_inverse[0, 0], selector, load=True
    )
    rows = moves.exchange(packed, face)
    state, coarse, wide, wide_rows = trace, None, None, None
    for iteration in range(ITERS):
        last = iteration == ITERS - 1
        residual, state, u, rhs = update(
            place, rows, flux, load, state, selector_t, basis, tall, coarse, wide, wide_rows
        )
        pieces = moves.gather_rows(jnp.concatenate([moves.to_odd(rhs), rhs]))
        if not last:
            entering = jnp.concatenate([u, tall], axis=1) if iteration == 0 else u
            flux, packed = products(entering, kernel, inverse, selector)
            rows = moves.exchange(packed, face)
            if iteration == 0:
                wide, wide_rows = flux[:, width:], rows[:, :, width:]
                flux, rows = flux[:, :width], rows[:, :, :width]
        partial = coarse_product(row_place, pieces, matrices[:1] if last else matrices)
        coarse = moves.sum_chips(partial)
    own = lax.dynamic_slice_in_dim(coarse[0], col * MODES, MODES)
    trace = (state + dot(tall[:, :MODES], own)).astype(bf16)
    return trace[None, None], residual[None, None]


def solution(mesh):
    placed = (
        P("sub", "col", None, None),
        P("sub", "col", None, None),
        P("sub", "col", None, None),
        P("sub", "col", None, None),
        P("sub", "col", None, None),
        P("sub", "col", None),
        P("sub", "col", None),
        P("sub", "col"),
    )
    return jax.shard_map(
        local,
        mesh=mesh,
        in_specs=placed,
        out_specs=(P("sub", "col", None, None), P("sub", "col", None, None)),
        check_vma=False,
    )
```

time: 251 us -> 164 us (0.65)
  blocking collectives: 100 us -> 0 us
  matrix products: 27.1 us -> 0.25 us
  Pallas kernels: 0 us -> 21.2 us
  starting transfers between devices: 26.5 us -> 47.6 us
  between operations: 14.3 us -> 1.86 us
  other arithmetic: 0.65 us -> 5.6 us
  waiting for transfers between devices: 75.4 us -> 78 us
    all_gather x3 -> x0, blocking collectives: 100 us -> none  [local(): lax.all_gather(coarse_rhs, 'sub', axis=0, tiled=True)]
    ppermute x12 -> x36, waiting for transfers between devices: 15.9 us -> 78 us  [the longest x6 77.1 us: to_even(): lax.ppermute(value, 'col', [(i + 1, i) for i in range(0, self.cols, 2)])]
    unnamed x6 -> x0, waiting for transfers between devices: 59.5 us -> none
    dot_general x18 -> x1, matrix products: 27.1 us -> 0.25 us  [dot(): return jnp.dot(a, b, preferred_element_type=f32)]
    ppermute x12 -> x36, starting transfers between devices: 26.4 us -> 47.6 us  [the longest x7 23.7 us: to_odd(): lax.ppermute(value, 'col', [(i, i + 1) for i in range(0, self.cols, 2)])]
    pallas_call x0 -> x9, Pallas kernels: none -> 21.2 us  [the longest x3 13.5 us: products(): pl.pallas_call(body, out_shape=outs, in_specs=[vmem] + [hbm if load else...]
    unnamed x17 -> x26, local copies, waits for them, and re-layouts: 5.45 us -> 6.76 us
  transfers between devices with their start and end apart: 15 -> 36, of which waited for: 12 -> 6; matrix products, arithmetic and copies ran while one was open for 1% -> 2% of each run, Pallas kernels for 0% -> 3%
where the time goes in v3:
time: 164 us; the launch traced here: 163 us
  waiting for transfers between devices  78 us (48%)
  starting transfers between devices  47.6 us (29%)
  Pallas kernels  21.2 us (13%)
  local copies, waits for them, and re-layouts  8.58 us (5%)
  other arithmetic  5.6 us (3%)
  between operations  1.86 us (1%)
    ppermute x6, waiting for transfers between devices, to_even(): lax.ppermute(value, 'col', [(i + 1, i) for i in range(0, self.cols, 2)])  77.1 us
    ppermute x7, starting transfers between devices, to_odd(): lax.ppermute(value, 'col', [(i, i + 1) for i in range(0, self.cols, 2)])  23.7 us
    ppermute x23, starting transfers between devices, between(): return lax.ppermute(value, BOTH, chip_pairs(self.subs, self.cols, step))  15.8 us
    pallas_call x3, Pallas kernels, products(): pl.pallas_call(body, out_shape=outs, in_specs=[vmem] + [hbm if load else...  13.5 us
    ppermute x6, starting transfers between devices, to_even(): lax.ppermute(value, 'col', [(i + 1, i) for i in range(0, self.cols, 2)])  8.06 us
    unnamed x26, local copies, waits for them, and re-layouts  6.76 us
    pallas_call x3, Pallas kernels, update(): pl.pallas_call(body, out_shape=[shape_of((nodes, width), bf16), shape_of(...  6.24 us
  transfers between devices with their start and end apart: 36, of which 6 were waited for; matrix products, arithmetic and copies ran while one was open for 2% of the time, Pallas kernels for 3%

profile of v3, /device:TPU:0, one launch (start us, length us, event | category | flops | bytes accessed | tf_op | source)
XLA Modules:
  0.0 163.0 jit_solution(6566026415151097446)
XLA Ops:
  0.6 0.8 bitcast_subtract_fusion
  1.4 0.9 fusion.2
  2.3 8.0 %load_products.1 = (bf16[1536,128]{1,0:T(8,128)(2,1)}, bf16[576,128]{1,0:T(8,128)(2,1)}, bf16[1536,1536]{1,0:T(8,128)(2,1)S(1)}, bf16[1536,1536]{1,0:T(8,128)(2,1)S(1)}) custom-call(bf16[1536,128]{1,0:T(8,128)(2,1)} %bitcast.95, bf16[1536,1536]{1,0:T(8,128)(2,1)} %bitcast.97, bf16[1536,1536]{1,0:T(8,128)(2,1)} %bitcast.98, ...), custom_call_target="tpu_custom_call" | custom-call | flops 2415919104 | bytes 9437184 | tf_op jit(solution)/shard_map/load_products/pallas_call | solution.py:86
  10.3 2.2 %copy-done = bf16[1536,1536]{1,0:T(8,128)(2,1)} copy-done((bf16[1536,1536]{1,0:T(8,128)(2,1)}, bf16[1536,1536]{1,0:T(8,128)(2,1)S(1)}, u32[]{:S(2)}) %copy-start) | copy-done | bytes 4718616
  12.5 2.2 %copy-done.2 = bf16[1536,1536]{1,0:T(8,128)(2,1)} copy-done((bf16[1536,1536]{1,0:T(8,128)(2,1)}, bf16[1536,1536]{1,0:T(8,128)(2,1)S(1)}, u32[]{:S(2)}) %copy-start.2) | copy-done | bytes 4718616
  14.7 2.5 %collective-permute-start = (bf16[576,128]{1,0:T(8,128)(2,1)}, bf16[576,128]{1,0:T(8,128)(2,1)S(1)}, u32[]{:S(2)}, u32[]{:S(2)}) collective-permute-start(bf16[576,128]{1,0:T(8,128)(2,1)} %get-tuple-element.19), channel_id=1, source_target_pairs={{0,1},{2,3},{4,5},{6,7},{8,9},{10,11},{12,13},{14,15},{16,17},{18,... | collective-permute-start | bytes 442376 | tf_op jit(solution)/shard_map/ppermute | solution.py:212
  17.2 0.8 fusion.26
  18.0 0.7 fusion.25
  18.7 0.8 slice_bitcast_fusion.9
  20.3 0.7 collective-permute-start.2
  21.0 9.3 %collective-permute-start.14 = (bf16[256,512]{1,0:T(8,128)(2,1)S(1)}, bf16[256,512]{1,0:T(8,128)(2,1)S(1)}, u32[]{:S(2)}, u32[]{:S(2)}) collective-permute-start(bf16[256,512]{1,0:T(8,128)(2,1)S(1)} %copy-done.8), channel_id=1, source_target_pairs={{0,1},{2,3},{4,5},{6,7},{8,9},{10,11},{12,13},{14,15},{16,17},{18,... | collective-permute-start | bytes 786440 | tf_op jit(solution)/shard_map/ppermute | solution.py:212
  30.4 0.7 collective-permute-start.3
  31.1 1.1 fusion.refs_7_.tall_ref
  32.3 1.3 collective-permute-start.4
  33.8 0.8 collective-permute-start.15
  34.7 3.5 %collective-permute-done.4 = bf16[4,160,128]{2,1,0:T(8,128)(2,1)S(1)} collective-permute-done((bf16[4,160,128]{2,1,0:T(8,128)(2,1)S(1)}, bf16[4,160,128]{2,1,0:T(8,128)(2,1)S(1)}, u32[]{:S(2)}, u32[]{:S(2)}) %collective-permute-start.4) | collective-permute-done | bytes 163872 | tf_op jit(solution)/shard_map/ppermute | solution.py:215
  38.3 1.6 %update.3 = (bf16[1536,128]{1,0:T(8,128)(2,1)}, f32[1536,128]{1,0:T(8,128)S(1)}, bf16[1536,128]{1,0:T(8,128)(2,1)S(1)}, bf16[64,128]{1,0:T(8,128)(2,1)S(1)}) custom-call(s32[18]{0:T(128)S(1)} %stack.162.refs_0_.place, bf16[4,160,128]{2,1,0:T(8,128)(2,1)S(1)} %maximum_select_fusion.1.refs_1_, bf16[1536,128]{1,0:T(8,128)(2,1)S(1)} %copy-done.7, ...), custom_call_target="tpu_custom_call" | custom-call | flops 201326592 | bytes 2359296 | tf_op jit(solution)/shard_map/update/pallas_call | solution.py:143
  40.0 2.3 %copy-done.3 = bf16[1536,1536]{1,0:T(8,128)(2,1)S(1)} copy-done((bf16[1536,1536]{1,0:T(8,128)(2,1)S(1)}, bf16[1536,1536]{1,0:T(8,128)(2,1)}, u32[]{:S(2)}) %copy-start.3) | copy-done | bytes 4718616
  42.4 2.7 %products.2 = (bf16[1536,256]{1,0:T(8,128)(2,1)S(1)}, bf16[576,256]{1,0:T(8,128)(2,1)S(1)}) custom-call(bf16[1536,256]{1,0:T(8,128)(2,1)S(1)} %pad_maximum_fusion.u_ref, bf16[1536,1536]{1,0:T(8,128)(2,1)S(1)} %copy-done.1, bf16[1536,1536]{1,0:T(8,128)(2,1)S(1)} %copy-done.3, bf16[8,128,128]{2,1,0:T(8,128)(2,1)S(1)} %copy-done.4), custom_call_target="tpu_custom_call" | custom-call | flops 2415919104 | bytes 9437184 | tf_op jit(solution)/shard_map/products/pallas_call | solution.py:86
  45.1 5.2 %collective-permute-start.5 = (bf16[576,256]{1,0:T(8,128)(2,1)S(1)}, bf16[576,256]{1,0:T(8,128)(2,1)S(1)}, u32[]{:S(2)}, u32[]{:S(2)}) collective-permute-start(bf16[576,256]{1,0:T(8,128)(2,1)S(1)} %get-tuple-element.24), channel_id=1, source_target_pairs={{0,1},{2,3},{4,5},{6,7},{8,9},{10,11},{12,13},{14,15},{16,17},{18,... | collective-permute-start | bytes 884744 | tf_op jit(solution)/shard_map/ppermute | solution.py:212
  50.3 1.3 collective-permute-start.10
  52.5 0.8 collective-permute-start.7
  53.4 0.8 collective-permute-start.11
  54.9 0.7 collective-permute-start.16
  55.6 0.7 collective-permute-start.13
  56.3 0.7 collective-permute-start.8
  57.7 0.7 collective-permute-start.17
  58.5 1.4 collective-permute-start.9
  60.0 1.5 collective-permute-start.18
  61.6 26.8 %collective-permute-done.18 = bf16[3,256,128]{2,1,0:T(8,128)(2,1)S(1)} collective-permute-done((bf16[3,256,128]{2,1,0:T(8,128)(2,1)S(1)}, bf16[3,256,128]{2,1,0:T(8,128)(2,1)S(1)}, u32[]{:S(2)}, u32[]{:S(2)}) %collective-permute-start.18) | collective-permute-done | bytes 196640 | tf_op jit(solution)/shard_map/ppermute | solution.py:215
  88.5 2.2 %update.4 = (bf16[1536,128]{1,0:T(8,128)(2,1)}, f32[1536,128]{1,0:T(8,128)S(1)}, bf16[1536,128]{1,0:T(8,128)(2,1)S(1)}, bf16[64,128]{1,0:T(8,128)(2,1)S(1)}) custom-call(s32[18]{0:T(128)S(1)} %stack.162.refs_0_.place, bf16[4,160,128]{2,1,0:T(8,128)(2,1)S(1)} %get-tuple-element.41.rows_ref, bf16[1536,128]{1,0:T(8,128)(2,1)S(1)} %get-tuple-element.37.flux_ref, ...), custom_call_target="tpu_custom_call" | custom-call | flops 201326592 | bytes 2359296 | tf_op jit(solution)/shard_map/update/pallas_call | solution.py:143
  90.8 2.8 %products.3 = (bf16[1536,128]{1,0:T(8,128)(2,1)S(1)}, bf16[576,128]{1,0:T(8,128)(2,1)S(1)}) custom-call(bf16[1536,128]{1,0:T(8,128)(2,1)S(1)} %get-tuple-element.28.u_ref, bf16[1536,1536]{1,0:T(8,128)(2,1)S(1)} %copy-done.1, bf16[1536,1536]{1,0:T(8,128)(2,1)S(1)} %bitcast.91, bf16[8,128,128]{2,1,0:T(8,128)(2,1)S(1)} %copy-done.4), custom_call_target="tpu_custom_call" | custom-call | flops 2415919104 | bytes 9437184 | tf_op jit(solution)/shard_map/products/pallas_call | solution.py:86
  93.6 2.0 %collective-permute-start.24 = (bf16[64,128]{1,0:T(8,128)(2,1)S(1)}, bf16[64,128]{1,0:T(8,128)(2,1)S(1)}, u32[]{:S(2)}, u32[]{:S(2)}) collective-permute-start(bf16[64,128]{1,0:T(8,128)(2,1)S(1)} %get-tuple-element.32), channel_id=1, source_target_pairs={{0,1},{2,3},{4,5},{6,7},{8,9},{10,11},{12,13},{14,15},{16,17},{18,... | collective-permute-start | bytes 49160 | tf_op jit(solution)/shard_map/ppermute | solution.py:212
  95.6 1.3 collective-permute-start.19
  99.2 0.7 collective-permute-start.21
  99.9 0.7 collective-permute-start.27
  102.0 0.7 collective-permute-start.28
  102.7 1.3 collective-permute-start.23
  104.1 1.3 collective-permute-start.29
  105.4 22.7 %collective-permute-done.23 = bf16[4,160,128]{2,1,0:T(8,128)(2,1)S(1)} collective-permute-done((bf16[4,160,128]{2,1,0:T(8,128)(2,1)S(1)}, bf16[4,160,128]{2,1,0:T(8,128)(2,1)S(1)}, u32[]{:S(2)}, u32[]{:S(2)}) %collective-permute-start.23) | collective-permute-done | bytes 163872 | tf_op jit(solution)/shard_map/ppermute | solution.py:215
  128.1 3.2 %collective-permute-done.29 = bf16[3,256,128]{2,1,0:T(8,128)(2,1)S(1)} collective-permute-done((bf16[3,256,128]{2,1,0:T(8,128)(2,1)S(1)}, bf16[3,256,128]{2,1,0:T(8,128)(2,1)S(1)}, u32[]{:S(2)}, u32[]{:S(2)}) %collective-permute-start.29) | collective-permute-done | bytes 196640 | tf_op jit(solution)/shard_map/ppermute | solution.py:215
  131.4 2.4 %update.5 = (bf16[1536,128]{1,0:T(8,128)(2,1)}, f32[1536,128]{1,0:T(8,128)S(1)}, bf16[1536,128]{1,0:T(8,128)(2,1)}, bf16[64,128]{1,0:T(8,128)(2,1)S(1)}) custom-call(s32[18]{0:T(128)S(1)} %stack.162.refs_0_.place, bf16[4,160,128]{2,1,0:T(8,128)(2,1)S(1)} %maximum_select_fusion.2.rows_ref, bf16[1536,128]{1,0:T(8,128)(2,1)S(1)} %get-tuple-element.30.flux_ref, ...), custom_call_target="tpu_custom_call" | custom-call | flops 201326592 | bytes 2359296 | tf_op jit(solution)/shard_map/update/pallas_call | solution.py:143
  133.8 2.0 %collective-permute-start.30 = (bf16[64,128]{1,0:T(8,128)(2,1)S(1)}, bf16[64,128]{1,0:T(8,128)(2,1)S(1)}, u32[]{:S(2)}, u32[]{:S(2)}) collective-permute-start(bf16[64,128]{1,0:T(8,128)(2,1)S(1)} %get-tuple-element.34), channel_id=1, source_target_pairs={{0,1},{2,3},{4,5},{6,7},{8,9},{10,11},{12,13},{14,15},{16,17},{18,... | collective-permute-start | bytes 49160 | tf_op jit(solution)/shard_map/ppermute | solution.py:212
  135.8 0.8 collective-permute-done.30
  138.0 0.7 collective-permute-start.33
  139.8 1.3 collective-permute-start.35
  141.1 20.9 %collective-permute-done.35 = bf16[1,256,128]{2,1,0:T(8,128)(2,1)S(1)} collective-permute-done((bf16[1,256,128]{2,1,0:T(8,128)(2,1)S(1)}, bf16[1,256,128]{2,1,0:T(8,128)(2,1)S(1)}, u32[]{:S(2)}, u32[]{:S(2)}) %collective-permute-start.35) | collective-permute-done | bytes 65568 | tf_op jit(solution)/shard_map/ppermute | solution.py:215
  162.2 0.8 fusion.3
  (141 shorter events, 10.0 us)
Async XLA Ops:
  2.3 18.7 %copy-start.8 = (bf16[256,512]{1,0:T(8,128)(2,1)S(1)}, bf16[256,512]{1,0:T(8,128)(2,1)}, u32[]{:S(2)}) copy-start(bf16[256,512]{1,0:T(8,128)(2,1)} %param.15) | copy-start | bytes 786436
  2.3 28.0 %copy-start.9 = (s32[1,1,1536]{2,1,0:T(1,128)S(1)}, s32[1,1,1536]{2,1,0:T(1,128)}, u32[]{:S(2)}) copy-start(s32[1,1,1536]{2,1,0:T(1,128)} %param.13) | copy-start | bytes 18436
  2.3 28.0 %copy-start.10 = (bf16[1,1,1536]{2,1,0:T(2,128)(2,1)S(1)}, bf16[1,1,1536]{2,1,0:T(2,128)(2,1)}, u32[]{:S(2)}) copy-start(bf16[1,1,1536]{2,1,0:T(2,128)(2,1)} %param.14) | copy-start | bytes 9220
  12.5 2.2 %copy-start.2 = (bf16[1536,1536]{1,0:T(8,128)(2,1)}, bf16[1536,1536]{1,0:T(8,128)(2,1)S(1)}, u32[]{:S(2)}) copy-start(bf16[1536,1536]{1,0:T(8,128)(2,1)S(1)} %get-tuple-element.23.s_ref) | copy-start | bytes 14155780
  14.7 23.6 %copy-start.5 = (bf16[1,1,1536,128]{3,2,1,0:T(8,128)(2,1)S(1)}, bf16[1,1,1536,128]{3,2,1,0:T(8,128)(2,1)}, u32[]{:S(2)}) copy-start(bf16[1,1,1536,128]{3,2,1,0:T(8,128)(2,1)} %param.9) | copy-start | bytes 1179652
  14.7 23.6 %copy-start.6 = (bf16[1,1,1536,128]{3,2,1,0:T(8,128)(2,1)S(1)}, bf16[1,1,1536,128]{3,2,1,0:T(8,128)(2,1)}, u32[]{:S(2)}) copy-start(bf16[1,1,1536,128]{3,2,1,0:T(8,128)(2,1)} %param.8) | copy-start | bytes 1179652
  14.7 23.6 %copy-start.7 = (bf16[1536,128]{1,0:T(8,128)(2,1)S(1)}, bf16[1536,128]{1,0:T(8,128)(2,1)}, u32[]{:S(2)}) copy-start(bf16[1536,128]{1,0:T(8,128)(2,1)} %get-tuple-element.20.refs_2_) | copy-start | bytes 1179652
  14.7 25.3 %copy-start.4 = (bf16[8,128,128]{2,1,0:T(8,128)(2,1)S(1)}, bf16[8,128,128]{2,1,0:T(8,128)(2,1)}, u32[]{:S(2)}) copy-start(bf16[8,128,128]{2,1,0:T(8,128)(2,1)} %get-tuple-element.112.sel_ref) | copy-start | bytes 786436
  14.7 4.0 %collective-permute-start = (bf16[576,128]{1,0:T(8,128)(2,1)}, bf16[576,128]{1,0:T(8,128)(2,1)S(1)}, u32[]{:S(2)}, u32[]{:S(2)}) collective-permute-start(bf16[576,128]{1,0:T(8,128)(2,1)} %get-tuple-element.19), channel_id=1, source_target_pairs={{0,1},{2,3},{4,5},{6,7},{8,9},{10,11},{12,13},{14,15},{16,17},{18,... | collective-permute-start | bytes 442376 | tf_op jit(solution)/shard_map/ppermute | solution.py:212
  19.5 0.7 collective-permute-start.1
  20.3 10.1 %collective-permute-start.2 = (bf16[2,2,160,128]{3,2,1,0:T(8,128)(2,1)S(1)}, bf16[2,2,160,128]{3,2,1,0:T(8,128)(2,1)S(1)}, u32[]{:S(2)}, u32[]{:S(2)}) collective-permute-start(bf16[2,2,160,128]{3,2,1,0:T(8,128)(2,1)S(1)} %pad_maximum_fusion.7), channel_id=1, source_target_pairs={{1,5},{3,7},{5,1},{7,3},{9,13},{11,15},{13,9},{15,11},{17,21},{19,... | collective-permute-start | bytes 491528 | tf_op jit(solution)/shard_map/ppermute | solution.py:209
  21.0 12.8 %collective-permute-start.14 = (bf16[256,512]{1,0:T(8,128)(2,1)S(1)}, bf16[256,512]{1,0:T(8,128)(2,1)S(1)}, u32[]{:S(2)}, u32[]{:S(2)}) collective-permute-start(bf16[256,512]{1,0:T(8,128)(2,1)S(1)} %copy-done.8), channel_id=1, source_target_pairs={{0,1},{2,3},{4,5},{6,7},{8,9},{10,11},{12,13},{14,15},{16,17},{18,... | collective-permute-start | bytes 786440 | tf_op jit(solution)/shard_map/ppermute | solution.py:212
  30.4 1.8 %collective-permute-start.3 = (bf16[2,160,128]{2,1,0:T(8,128)(2,1)S(1)}, bf16[2,160,128]{2,1,0:T(8,128)(2,1)S(1)}, u32[]{:S(2)}, u32[]{:S(2)}) collective-permute-start(bf16[2,160,128]{2,1,0:T(8,128)(2,1)S(1)} %slice_bitcast_fusion.5), channel_id=1, source_target_pairs={{1,9},{3,11},{9,17},{11,19},{13,5},{15,7},{17,25},{19,27},{21,13},... | collective-permute-start | bytes 245768 | tf_op jit(solution)/shard_map/ppermute | solution.py:209
  32.3 5.9 %collective-permute-start.4 = (bf16[4,160,128]{2,1,0:T(8,128)(2,1)S(1)}, bf16[4,160,128]{2,1,0:T(8,128)(2,1)S(1)}, u32[]{:S(2)}, u32[]{:S(2)}) collective-permute-start(bf16[4,160,128]{2,1,0:T(8,128)(2,1)S(1)} %pad_maximum_fusion.8), channel_id=1, source_target_pairs={{1,0},{3,2},{5,4},{7,6},{9,8},{11,10},{13,12},{15,14},{17,16},{19,... | collective-permute-start | bytes 491528 | tf_op jit(solution)/shard_map/ppermute | solution.py:215
  33.7 6.3 %copy-start.1 = (bf16[1536,1536]{1,0:T(8,128)(2,1)S(1)}, bf16[1536,1536]{1,0:T(8,128)(2,1)}, u32[]{:S(2)}) copy-start(bf16[1536,1536]{1,0:T(8,128)(2,1)} %copy-done) | copy-start | bytes 14155780
  33.8 21.1 %collective-permute-start.15 = (bf16[2,256,512]{2,1,0:T(8,128)(2,1)S(1)}, bf16[2,256,512]{2,1,0:T(8,128)(2,1)S(1)}, u32[]{:S(2)}, u32[]{:S(2)}) collective-permute-start(bf16[2,256,512]{2,1,0:T(8,128)(2,1)S(1)} %pad_maximum_fusion.1.refs_0_), channel_id=1, source_target_pairs={{1,5},{3,7},{5,1},{7,3},{9,13},{11,15},{13,9},{15,11},{17,21},{19,... | collective-permute-start | bytes 1572872 | tf_op jit(solution)/shard_map/ppermute | solution.py:209
  40.0 2.3 %copy-start.3 = (bf16[1536,1536]{1,0:T(8,128)(2,1)S(1)}, bf16[1536,1536]{1,0:T(8,128)(2,1)}, u32[]{:S(2)}) copy-start(bf16[1536,1536]{1,0:T(8,128)(2,1)} %copy-done.2) | copy-start | bytes 14155780
  45.1 6.6 %collective-permute-start.5 = (bf16[576,256]{1,0:T(8,128)(2,1)S(1)}, bf16[576,256]{1,0:T(8,128)(2,1)S(1)}, u32[]{:S(2)}, u32[]{:S(2)}) collective-permute-start(bf16[576,256]{1,0:T(8,128)(2,1)S(1)} %get-tuple-element.24), channel_id=1, source_target_pairs={{0,1},{2,3},{4,5},{6,7},{8,9},{10,11},{12,13},{14,15},{16,17},{18,... | collective-permute-start | bytes 884744 | tf_op jit(solution)/shard_map/ppermute | solution.py:212
  50.3 3.0 %collective-permute-start.10 = (bf16[64,128]{1,0:T(8,128)(2,1)S(1)}, bf16[64,128]{1,0:T(8,128)(2,1)S(1)}, u32[]{:S(2)}, u32[]{:S(2)}) collective-permute-start(bf16[64,128]{1,0:T(8,128)(2,1)S(1)} %get-tuple-element.27), channel_id=1, source_target_pairs={{0,1},{2,3},{4,5},{6,7},{8,9},{10,11},{12,13},{14,15},{16,17},{18,... | collective-permute-start | bytes 49160 | tf_op jit(solution)/shard_map/ppermute | solution.py:212
  51.7 0.7 collective-permute-start.6
  52.5 38.3 %slice-start = ((s8[4718592]{0:T(1024)(128)(4,1)}), s8[4194304]{0:T(1024)(128)(4,1)S(1)}, s32[]{:S(2)}) async-start(s8[4718592]{0:T(1024)(128)(4,1)} %bitcast.90), calls=%async_computation | async-start | bytes 8388608
  52.5 3.8 %collective-permute-start.7 = (bf16[2,2,160,256]{3,2,1,0:T(8,128)(2,1)S(1)}, bf16[2,2,160,256]{3,2,1,0:T(8,128)(2,1)S(1)}, u32[]{:S(2)}, u32[]{:S(2)}) collective-permute-start(bf16[2,2,160,256]{3,2,1,0:T(8,128)(2,1)S(1)} %pad_maximum_fusion.2), channel_id=1, source_target_pairs={{1,5},{3,7},{5,1},{7,3},{9,13},{11,15},{13,9},{15,11},{17,21},{19,... | collective-permute-start | bytes 983048 | tf_op jit(solution)/shard_map/ppermute | solution.py:209
  53.4 0.8 collective-permute-start.11
  54.2 1.4 collective-permute-start.12
  54.9 2.2 %collective-permute-start.16 = (bf16[2,256,512]{2,1,0:T(8,128)(2,1)S(1)}, bf16[2,256,512]{2,1,0:T(8,128)(2,1)S(1)}, u32[]{:S(2)}, u32[]{:S(2)}) collective-permute-start(bf16[2,256,512]{2,1,0:T(8,128)(2,1)S(1)} %collective-permute-done.15.refs_1_), channel_id=1, source_target_pairs={{1,9},{3,11},{9,17},{11,19},{13,5},{15,7},{17,25},{19,27},{21,13},... | collective-permute-start | bytes 1572872 | tf_op jit(solution)/shard_map/ppermute | solution.py:209
  55.6 1.4 collective-permute-start.13
  56.3 2.0 %collective-permute-start.8 = (bf16[2,160,256]{2,1,0:T(8,128)(2,1)S(1)}, bf16[2,160,256]{2,1,0:T(8,128)(2,1)S(1)}, u32[]{:S(2)}, u32[]{:S(2)}) collective-permute-start(bf16[2,160,256]{2,1,0:T(8,128)(2,1)S(1)} %slice_bitcast_fusion), channel_id=1, source_target_pairs={{1,9},{3,11},{9,17},{11,19},{13,5},{15,7},{17,25},{19,27},{21,13},... | collective-permute-start | bytes 491528 | tf_op jit(solution)/shard_map/ppermute | solution.py:209
  57.7 2.3 %collective-permute-start.17 = (bf16[3,256,128]{2,1,0:T(8,128)(2,1)S(1)}, bf16[3,256,128]{2,1,0:T(8,128)(2,1)S(1)}, u32[]{:S(2)}, u32[]{:S(2)}) collective-permute-start(bf16[3,256,128]{2,1,0:T(8,128)(2,1)S(1)} %convert_element_type.38), channel_id=1, source_target_pairs={{1,3},{3,1},{5,7},{7,5},{9,11},{11,9},{13,15},{15,13},{17,19},{19,... | collective-permute-start | bytes 589832 | tf_op jit(solution)/shard_map/ppermute | solution.py:209
  58.5 32.2 %slice-start.1 = ((s8[4718592]{0:T(1024)(128)(4,1)}), s8[524288]{0:T(1024)(128)(4,1)S(1)}, s32[]{:S(2)}) async-start(s8[4718592]{0:T(1024)(128)(4,1)} %bitcast.90), calls=%async_computation.1 | async-start | bytes 1048576
  58.5 29.9 %collective-permute-start.9 = (bf16[4,160,256]{2,1,0:T(8,128)(2,1)S(1)}, bf16[4,160,256]{2,1,0:T(8,128)(2,1)S(1)}, u32[]{:S(2)}, u32[]{:S(2)}) collective-permute-start(bf16[4,160,256]{2,1,0:T(8,128)(2,1)S(1)} %pad_maximum_fusion.3), channel_id=1, source_target_pairs={{1,0},{3,2},{5,4},{7,6},{9,8},{11,10},{13,12},{15,14},{17,16},{19,... | collective-permute-start | bytes 983048 | tf_op jit(solution)/shard_map/ppermute | solution.py:215
  60.0 28.3 %collective-permute-start.18 = (bf16[3,256,128]{2,1,0:T(8,128)(2,1)S(1)}, bf16[3,256,128]{2,1,0:T(8,128)(2,1)S(1)}, u32[]{:S(2)}, u32[]{:S(2)}) collective-permute-start(bf16[3,256,128]{2,1,0:T(8,128)(2,1)S(1)} %add_convert_fusion.2), channel_id=1, source_target_pairs={{1,0},{3,2},{5,4},{7,6},{9,8},{11,10},{13,12},{15,14},{17,16},{19,... | collective-permute-start | bytes 589832 | tf_op jit(solution)/shard_map/ppermute | solution.py:215
  93.6 3.4 %collective-permute-start.24 = (bf16[64,128]{1,0:T(8,128)(2,1)S(1)}, bf16[64,128]{1,0:T(8,128)(2,1)S(1)}, u32[]{:S(2)}, u32[]{:S(2)}) collective-permute-start(bf16[64,128]{1,0:T(8,128)(2,1)S(1)} %get-tuple-element.32), channel_id=1, source_target_pairs={{0,1},{2,3},{4,5},{6,7},{8,9},{10,11},{12,13},{14,15},{16,17},{18,... | collective-permute-start | bytes 49160 | tf_op jit(solution)/shard_map/ppermute | solution.py:212
  95.6 2.7 %collective-permute-start.19 = (bf16[576,128]{1,0:T(8,128)(2,1)S(1)}, bf16[576,128]{1,0:T(8,128)(2,1)S(1)}, u32[]{:S(2)}, u32[]{:S(2)}) collective-permute-start(bf16[576,128]{1,0:T(8,128)(2,1)S(1)} %get-tuple-element.29), channel_id=1, source_target_pairs={{0,1},{2,3},{4,5},{6,7},{8,9},{10,11},{12,13},{14,15},{16,17},{18,... | collective-permute-start | bytes 442376 | tf_op jit(solution)/shard_map/ppermute | solution.py:212
  97.0 0.7 collective-permute-start.25
  97.7 2.2 %collective-permute-start.26 = (bf16[2,128,128]{2,1,0:T(8,128)(2,1)S(1)}, bf16[2,128,128]{2,1,0:T(8,128)(2,1)S(1)}, u32[]{:S(2)}, u32[]{:S(2)}) collective-permute-start(bf16[2,128,128]{2,1,0:T(8,128)(2,1)S(1)} %pad_maximum_fusion.21), channel_id=1, source_target_pairs={{1,9},{3,11},{5,13},{7,15},{9,1},{11,3},{13,5},{15,7},{17,25},{19,... | collective-permute-start | bytes 196616 | tf_op jit(solution)/shard_map/ppermute | solution.py:209
  98.4 0.7 collective-permute-start.20
  99.2 1.4 collective-permute-start.21
  99.9 1.4 collective-permute-start.27
  100.6 2.0 %collective-permute-start.22 = (bf16[2,160,128]{2,1,0:T(8,128)(2,1)S(1)}, bf16[2,160,128]{2,1,0:T(8,128)(2,1)S(1)}, u32[]{:S(2)}, u32[]{:S(2)}) collective-permute-start(bf16[2,160,128]{2,1,0:T(8,128)(2,1)S(1)} %slice_bitcast_fusion.2), channel_id=1, source_target_pairs={{1,9},{3,11},{9,17},{11,19},{13,5},{15,7},{17,25},{19,27},{21,13},... | collective-permute-start | bytes 245768 | tf_op jit(solution)/shard_map/ppermute | solution.py:209
  102.0 2.1 %collective-permute-start.28 = (bf16[3,256,128]{2,1,0:T(8,128)(2,1)S(1)}, bf16[3,256,128]{2,1,0:T(8,128)(2,1)S(1)}, u32[]{:S(2)}, u32[]{:S(2)}) collective-permute-start(bf16[3,256,128]{2,1,0:T(8,128)(2,1)S(1)} %convert_element_type.41), channel_id=1, source_target_pairs={{1,3},{3,1},{5,7},{7,5},{9,11},{11,9},{13,15},{15,13},{17,19},{19,... | collective-permute-start | bytes 589832 | tf_op jit(solution)/shard_map/ppermute | solution.py:209
  102.7 25.4 %collective-permute-start.23 = (bf16[4,160,128]{2,1,0:T(8,128)(2,1)S(1)}, bf16[4,160,128]{2,1,0:T(8,128)(2,1)S(1)}, u32[]{:S(2)}, u32[]{:S(2)}) collective-permute-start(bf16[4,160,128]{2,1,0:T(8,128)(2,1)S(1)} %pad_maximum_fusion.12), channel_id=1, source_target_pairs={{1,0},{3,2},{5,4},{7,6},{9,8},{11,10},{13,12},{15,14},{17,16},{19,... | collective-permute-start | bytes 491528 | tf_op jit(solution)/shard_map/ppermute | solution.py:215
  104.1 27.3 %collective-permute-start.29 = (bf16[3,256,128]{2,1,0:T(8,128)(2,1)S(1)}, bf16[3,256,128]{2,1,0:T(8,128)(2,1)S(1)}, u32[]{:S(2)}, u32[]{:S(2)}) collective-permute-start(bf16[3,256,128]{2,1,0:T(8,128)(2,1)S(1)} %add_convert_fusion.1), channel_id=1, source_target_pairs={{1,0},{3,2},{5,4},{7,6},{9,8},{11,10},{13,12},{15,14},{17,16},{19,... | collective-permute-start | bytes 589832 | tf_op jit(solution)/shard_map/ppermute | solution.py:215
  133.8 2.9 %collective-permute-start.30 = (bf16[64,128]{1,0:T(8,128)(2,1)S(1)}, bf16[64,128]{1,0:T(8,128)(2,1)S(1)}, u32[]{:S(2)}, u32[]{:S(2)}) collective-permute-start(bf16[64,128]{1,0:T(8,128)(2,1)S(1)} %get-tuple-element.34), channel_id=1, source_target_pairs={{0,1},{2,3},{4,5},{6,7},{8,9},{10,11},{12,13},{14,15},{16,17},{18,... | collective-permute-start | bytes 49160 | tf_op jit(solution)/shard_map/ppermute | solution.py:212
  136.6 0.7 collective-permute-start.31
  137.3 0.7 collective-permute-start.32
  138.0 0.7 collective-permute-start.33
  139.1 0.7 collective-permute-start.34
  139.8 22.2 %collective-permute-start.35 = (bf16[1,256,128]{2,1,0:T(8,128)(2,1)S(1)}, bf16[1,256,128]{2,1,0:T(8,128)(2,1)S(1)}, u32[]{:S(2)}, u32[]{:S(2)}) collective-permute-start(bf16[1,256,128]{2,1,0:T(8,128)(2,1)S(1)} %add_convert_fusion.3), channel_id=1, source_target_pairs={{1,0},{3,2},{5,4},{7,6},{9,8},{11,10},{13,12},{15,14},{17,16},{19,... | collective-permute-start | bytes 196616 | tf_op jit(solution)/shard_map/ppermute | solution.py:215
  (1 other events, 2.2 us)

commit v4 on v3

v4 whole, which is shorter than its diff:
```python
import functools

import jax
import jax.numpy as jnp
from jax import lax
from jax.experimental import pallas as pl
from jax.experimental.pallas import tpu as pltpu
from jax.sharding import PartitionSpec as P

MODES = 64
ITERS = 3
LANES = 128

bf16 = jnp.bfloat16
f32 = jnp.float32
DIRECTIONS = ((-1, -1), (-1, 0), (-1, 1), (0, -1), (0, 1), (1, -1), (1, 0), (1, 1))
PACKED = ((4, 1), (2, 0), (7, 0), (3, 1), (0, 0), (5, 0), (6, 1), (1, 1))

vmem = pl.BlockSpec(memory_space=pltpu.VMEM)
smem = pl.BlockSpec(memory_space=pltpu.SMEM)
hbm = pl.BlockSpec(memory_space=pl.ANY)
shape_of = jax.ShapeDtypeStruct
params = pltpu.CompilerParams(vmem_limit_bytes=24 * 1024 * 1024)
large = pltpu.CompilerParams(vmem_limit_bytes=50 * 1024 * 1024)


def dot(a, b):
    return jnp.dot(a, b, preferred_element_type=f32)


def pick(face, sel_ref, flux_ref, packed_ref):
    at = 0
    for d, whole in PACKED:
        size = face if whole else face // 8
        rows = dot(sel_ref[d, :size, :], flux_ref[d * face : (d + 1) * face, :])
        packed_ref[at : at + size, :] = rows.astype(bf16)
        at += size


def load_kernel(face, chunk, ahead, u_ref, k_hbm, s_hbm, sel_ref, flux_ref, packed_ref, k_ref, s_ref, mixed, sems):
    count = u_ref.shape[0] // chunk
    copies = []
    for which, (source, target) in enumerate(((k_hbm, k_ref), (s_hbm, s_ref))):
        for i in range(count):
            rows = pl.ds(i * chunk, chunk)
            copies.append(pltpu.make_async_copy(source.at[rows], target.at[rows], sems.at[which, i]))
    for copy in copies[:ahead]:
        copy.start()
    u = u_ref[...]
    for i in range(2 * count):
        copies[i].wait()
        if i + ahead < 2 * count:
            copies[i + ahead].start()
        rows = pl.ds(i % count * chunk, chunk)
        if i < count:
            mixed[rows, :] = (0.5 * u_ref[rows, :].astype(f32) + dot(k_ref[rows, :], u)).astype(bf16)
        else:
            flux_ref[rows, :] = dot(s_ref[rows, :], mixed[...]).astype(bf16)
    pick(face, sel_ref, flux_ref, packed_ref)


def products_kernel(face, chunk, u_ref, k_ref, s_ref, sel_ref, flux_ref, packed_ref, k_out, s_out, mixed):
    u = u_ref[...]
    for i in range(u_ref.shape[0] // chunk):
        rows = pl.ds(i * chunk, chunk)
        mixed[rows, :] = (0.5 * u_ref[rows, :].astype(f32) + dot(k_ref[rows, :], u)).astype(bf16)
    m = mixed[...]
    for i in range(u_ref.shape[0] // chunk):
        rows = pl.ds(i * chunk, chunk)
        flux_ref[rows, :] = dot(s_ref[rows, :], m).astype(bf16)
    pick(face, sel_ref, flux_ref, packed_ref)


def products(u, kernel, inverse, selector, load=False):
    nodes, width = u.shape
    face = selector.shape[1]
    chunk = 256 if nodes % 256 == 0 else nodes
    scratch = [pltpu.VMEM((nodes, width), bf16)]
    body = functools.partial(products_kernel, face, chunk)
    if load:
        scratch += [pltpu.SemaphoreType.DMA((2, nodes // chunk))]
        body = functools.partial(load_kernel, face, chunk, 3)
    return pl.pallas_call(
        body,
        out_shape=[
            shape_of((nodes, width), bf16),
            shape_of((4 * (face + face // 8), width), bf16),
            pltpu.VMEM((nodes, nodes), bf16),
            pltpu.VMEM((nodes, nodes), bf16),
        ],
        in_specs=[vmem] + [hbm if load else vmem] * 2 + [vmem],
        out_specs=[vmem] * 4,
        scratch_shapes=scratch,
        input_output_aliases={} if load else {1: 2, 2: 3},
        compiler_params=large if load else params,
        cost_estimate=pl.CostEstimate(
            flops=4 * nodes * nodes * 2 * LANES, bytes_accessed=4 * nodes * nodes, transcendentals=0
        ),
        name="load_products" if load else "products",
    )(u, kernel, inverse, selector)


def update_kernel(face, first, place, rows_ref, flux_ref, load_ref, state_ref, selt_ref, basis_ref, tall_ref, c_ref, w_ref, wrows_ref, res_ref, u_ref, rhs_ref):
    corner = face // 8
    modes = basis_ref.shape[0]
    found = {4: (0, 0), 3: (1, 0), 6: (2, 0), 1: (3, 0)}
    found |= {7: (2, face), 5: (2, face + corner), 2: (3, face), 0: (3, face + corner)}
    flux = flux_ref[...].astype(f32)
    state = state_ref[...].astype(f32)
    if not first:
        start = pl.multiple_of(place[1], modes)
        own = c_ref[place[0], pl.ds(start, modes), :]
        flux = (flux + dot(w_ref[:, :modes], own)).astype(bf16).astype(f32)
        state = state + dot(tall_ref[:, :modes], own)
    assembled = []
    for d in range(8):
        group, at = found[d]
        size = face if DIRECTIONS[d][0] * DIRECTIONS[d][1] == 0 else corner
        arrived = rows_ref[group, at : at + size, :]
        if not first:
            start = pl.multiple_of(place[2 * d + 3], modes)
            theirs = c_ref[place[2 * d + 2], pl.ds(start, modes), :]
            wide = wrows_ref[group, at : at + size, :modes]
            arrived = (arrived.astype(f32) + dot(wide, theirs)).astype(bf16)
        assembled.append(flux[d * face : (d + 1) * face] + dot(selt_ref[d, :, :size], arrived))
    assembled.append(flux[8 * face :])
    residual = (load_ref[...].astype(f32) - jnp.concatenate(assembled)).astype(bf16)
    res_ref[...] = residual
    following = state + 0.25 * residual.astype(f32)
    u_ref[...] = following.astype(bf16)
    rhs_ref[...] = dot(basis_ref[...], residual).astype(bf16)


def update(place, rows, flux, load, state, selector_t, basis, tall, coarse, wide, wide_rows):
    first = coarse is None
    nodes, width = load.shape
    modes = basis.shape[0]
    operands = [place, rows, flux, load, state, selector_t, basis, tall]
    body = functools.partial(update_kernel, selector_t.shape[1], first)
    if first:
        inner = body
        body = lambda *refs: inner(*refs[:8], None, None, None, *refs[8:])
    else:
        operands += [coarse, wide, wide_rows]
    return pl.pallas_call(
        body,
        out_shape=[
            shape_of((nodes, width), bf16),
            shape_of((nodes, width), bf16),
            shape_of((modes, width), bf16),
        ],
        in_specs=[smem] + [vmem] * (len(operands) - 1),
        out_specs=[vmem] * 3,
        compiler_params=params,
        cost_estimate=pl.CostEstimate(
            flops=8 * nodes * LANES * width, bytes_accessed=12 * nodes * width, transcendentals=0
        ),
        name="update",
    )(*operands)


def coarse_kernel(modes, place, pieces_ref, *refs):
    matrices, out_ref, full = refs[:-2], refs[-2], refs[-1]
    for m in range(pieces_ref.shape[0]):
        start = pl.multiple_of((place[0] ^ m) * modes, modes)
        full[pl.ds(start, modes), :] = pieces_ref[m]
    for i, matrix in enumerate(matrices):
        out_ref[i] = dot(matrix[...], full[...])


def coarse_product(place, pieces, matrices):
    count, modes, width = pieces.shape
    rows, depth = matrices[0].shape
    return pl.pallas_call(
        functools.partial(coarse_kernel, modes),
        out_shape=shape_of((len(matrices), rows, width), f32),
        in_specs=[smem] + [vmem] * (1 + len(matrices)),
        out_specs=vmem,
        scratch_shapes=[pltpu.VMEM((depth, width), bf16)],
        compiler_params=params,
        cost_estimate=pl.CostEstimate(
            flops=2 * len(matrices) * rows * depth * width,
            bytes_accessed=2 * len(matrices) * rows * depth,
            transcendentals=0,
        ),
        name="coarse_product",
    )(place, pieces, *matrices)


def swap(value, axis, bit):
    return lax.ppermute(value, axis, [(i, i ^ bit) for i in range(lax.axis_size(axis))])


def cross(value, axis):
    n = lax.axis_size(axis)
    return lax.ppermute(value, axis, [(i, (i + 1 if i % 2 else i - 1) % n) for i in range(n)])


def trade(forward, backward, axis):
    even = lax.axis_index(axis) % 2 == 0
    near = swap(jnp.where(even, forward, backward), axis, 1)
    far = cross(jnp.where(even, backward, forward), axis)
    return jnp.where(even, near, far), jnp.where(even, far, near)


def exchange(packed, face):
    corner = face // 8
    group = face + 2 * corner
    right, left = trade(packed[:group], packed[group : 2 * group], "col")
    six, one = packed[2 * group : 2 * group + face], packed[2 * group + face :]
    up = jnp.concatenate([six, right[face + corner :], left[face + corner :]])
    down = jnp.concatenate([one, right[face : face + corner], left[face : face + corner]])
    above, below = trade(up, down, "sub")
    return jnp.stack([right, left, above, below])


def sum_over_columns(value):
    bit = lax.axis_size("col") // 2
    while bit:
        value = value + swap(value.astype(bf16), "col", bit).astype(f32)
        bit //= 2
    return value.astype(bf16)


def share_of_sum(value):
    bit = lax.axis_size("col") // 2
    while bit:
        half = value.shape[0] // 2
        upper = (lax.axis_index("col") // bit) % 2 == 1
        low, high = value[:half], value[half:]
        got = swap(jnp.where(upper, low, high).astype(bf16), "col", bit)
        value = jnp.where(upper, high, low) + got.astype(f32)
        bit //= 2
    return value.astype(bf16)


def local(
    trace_start,
    neumann_load,
    double_layer,
    single_inverse,
    interface_nodes,
    node_mode,
    mode_weight,
    coarse_inverse,
):
    subs, cols = lax.axis_size("sub"), lax.axis_size("col")
    row, col = lax.axis_index("sub"), lax.axis_index("col")
    even_sub = row % 2 == 0
    trace = trace_start[0, 0]
    load = neumann_load[0, 0]
    width = trace.shape[1]
    interface = interface_nodes[0, 0]
    face = interface.shape[1]
    position = interface - (jnp.arange(8, dtype=jnp.int32) * face)[:, None]
    slots = jnp.arange(face, dtype=jnp.int32)
    selector = (position[:, :, None] == slots[None, None, :]).astype(bf16)
    selector_t = (position[:, None, :] == slots[None, :, None]).astype(bf16)
    nothing = jnp.zeros((), bf16)
    mode, weight = node_mode[0, 0], mode_weight[0, 0]
    modes = jnp.arange(MODES, dtype=jnp.int32)
    lanes = jnp.arange(LANES, dtype=jnp.int32)
    basis = jnp.where(mode[None, :] == modes[:, None], weight[None, :], nothing)
    tall = jnp.where(mode[:, None] == lanes[None, :], weight[:, None], nothing)

    place = [jnp.zeros((), jnp.int32), col * MODES]
    for row_step, col_step in DIRECTIONS:
        source = {0: 0, 1: jnp.where(even_sub, 1, 2), -1: jnp.where(even_sub, 2, 1)}
        place += [source[row_step], jnp.clip(col + col_step, 0, cols - 1) * MODES]
    place = jnp.stack([jnp.asarray(p, jnp.int32) for p in place])
    row_place = jnp.reshape(row, (1,)).astype(jnp.int32)

    matrices = [coarse_inverse, swap(coarse_inverse, "sub", 1), cross(coarse_inverse, "sub")]

    flux, packed, kernel, inverse = products(
        trace, double_layer[0, 0], single_inverse[0, 0], selector, load=True
    )
    rows = exchange(packed, face)
    u, coarse, wide, wide_rows = trace, None, None, None
    for iteration in range(ITERS):
        last = iteration == ITERS - 1
        residual, u, rhs = update(
            place, rows, flux, load, u, selector_t, basis, tall, coarse, wide, wide_rows
        )
        got = swap(rhs, "sub", 1)
        pieces = jnp.stack([rhs, got])
        if not last:
            entering, pieces = lax.optimization_barrier((u, pieces))
            if iteration == 0:
                entering = jnp.concatenate([entering, tall], axis=1)
            flux, packed, kernel, inverse = products(entering, kernel, inverse, selector)
            rows = exchange(packed, face)
            if iteration == 0:
                wide, wide_rows = flux[:, width:], rows[:, :, width:]
                flux, rows = flux[:, :width], rows[:, :, :width]
        while pieces.shape[0] < subs:
            got = swap(pieces, "sub", pieces.shape[0])
            pieces = jnp.concatenate([pieces, got])
        if last:
            own = share_of_sum(coarse_product(row_place, pieces, matrices[:1])[0])
        else:
            coarse = sum_over_columns(coarse_product(row_place, pieces, matrices))
    trace = (u.astype(f32) + dot(tall[:, :MODES], own)).astype(bf16)
    return trace[None, None], residual[None, None]


def solution(mesh):
    placed = (
        P("sub", "col", None, None),
        P("sub", "col", None, None),
        P("sub", "col", None, None),
        P("sub", "col", None, None),
        P("sub", "col", None, None),
        P("sub", "col", None),
        P("sub", "col", None),
        P("sub", "col"),
    )
    return jax.shard_map(
        local,
        mesh=mesh,
        in_specs=placed,
        out_specs=(P("sub", "col", None, None), P("sub", "col", None, None)),
        check_vma=False,
    )
```

time: 164 us -> 117 us (0.71)
  waiting for transfers between devices: 78 us -> 42.1 us
  starting transfers between devices: 47.6 us -> 33.6 us
  local copies, waits for them, and re-layouts: 8.58 us -> 13.2 us
    ppermute x36 -> x29, waiting for transfers between devices: 78 us -> 42.1 us  [the longest x22 35 us: swap(): lax.ppermute(value, axis, [(i, i ^ bit) for i in range(lax.axis_size(axis...]
    ppermute x36 -> x29, starting transfers between devices: 47.6 us -> 33.6 us  [the longest x7 17.2 us: cross(): lax.ppermute(value, axis, [(i, (i + 1 if i % 2 else i - 1) % n) for i in...]
    unnamed x26, local copies, waits for them, and re-layouts: 6.76 us -> 12.2 us
  transfers between devices with their start and end apart: 36 -> 29, of which waited for: 6 -> 16; matrix products, arithmetic and copies ran while one was open for 2% -> 2% of each run, Pallas kernels for 3% -> 3%
where the time goes in v4:
time: 117 us; the launch traced here: 116 us
  waiting for transfers between devices  42.1 us (36%)
  starting transfers between devices  33.6 us (29%)
  Pallas kernels  20.5 us (18%)
  local copies, waits for them, and re-layouts  13.2 us (11%)
  other arithmetic  4.68 us (4%)
  between operations  1.2 us (1%)
    ppermute x22, waiting for transfers between devices, swap(): lax.ppermute(value, axis, [(i, i ^ bit) for i in range(lax.axis_size(axis...  35 us
    ppermute x7, starting transfers between devices, cross(): lax.ppermute(value, axis, [(i, (i + 1 if i % 2 else i - 1) % n) for i in...  17.2 us
    ppermute x22, starting transfers between devices, swap(): lax.ppermute(value, axis, [(i, i ^ bit) for i in range(lax.axis_size(axis...  16.5 us
    pallas_call x3, Pallas kernels, products(): pl.pallas_call(body, out_shape=[shape_of((nodes, width), bf16), shape_of(...  13.4 us
    unnamed x26, local copies, waits for them, and re-layouts  12.2 us
    ppermute x7, waiting for transfers between devices, cross(): lax.ppermute(value, axis, [(i, (i + 1 if i % 2 else i - 1) % n) for i in...  7.11 us
    pallas_call x3, Pallas kernels, update(): pl.pallas_call(body, out_shape=[shape_of((nodes, width), bf16), shape_of(...  6.12 us
  transfers between devices with their start and end apart: 29, of which 16 were waited for; matrix products, arithmetic and copies ran while one was open for 2% of the time, Pallas kernels for 3%

profile of v4, /device:TPU:0, one launch (start us, length us, event | category | flops | bytes accessed | tf_op | source)
XLA Modules:
  0.0 116.3 jit_solution(1937385196036896904)
XLA Ops:
  0.7 0.8 bitcast_subtract_fusion
  1.4 0.9 fusion.4
  2.4 8.0 %load_products.1 = (bf16[1536,128]{1,0:T(8,128)(2,1)}, bf16[576,128]{1,0:T(8,128)(2,1)}, bf16[1536,1536]{1,0:T(8,128)(2,1)S(1)}, bf16[1536,1536]{1,0:T(8,128)(2,1)S(1)}) custom-call(bf16[1536,128]{1,0:T(8,128)(2,1)} %bitcast.47, bf16[1536,1536]{1,0:T(8,128)(2,1)} %bitcast.54, bf16[1536,1536]{1,0:T(8,128)(2,1)} %bitcast.55, ...), custom_call_target="tpu_custom_call" | custom-call | flops 2415919104 | bytes 9437184 | tf_op jit(solution)/shard_map/load_products/pallas_call | solution.py:83
  10.4 2.2 %copy-done = bf16[1536,1536]{1,0:T(8,128)(2,1)} copy-done((bf16[1536,1536]{1,0:T(8,128)(2,1)}, bf16[1536,1536]{1,0:T(8,128)(2,1)S(1)}, u32[]{:S(2)}) %copy-start) | copy-done | bytes 4718616
  12.6 2.2 %copy-done.4 = bf16[1536,1536]{1,0:T(8,128)(2,1)} copy-done((bf16[1536,1536]{1,0:T(8,128)(2,1)}, bf16[1536,1536]{1,0:T(8,128)(2,1)S(1)}, u32[]{:S(2)}) %copy-start.4) | copy-done | bytes 4718616
  14.8 0.9 broadcast_select_fusion.17
  15.6 0.5 collective-permute-start
  16.1 2.6 %collective-permute-start.1 = (bf16[160,128]{1,0:T(8,128)(2,1)S(1)}, bf16[160,128]{1,0:T(8,128)(2,1)S(1)}, u32[]{:S(2)}, u32[]{:S(2)}) collective-permute-start(bf16[160,128]{1,0:T(8,128)(2,1)S(1)} %get-tuple-element.65), channel_id=1, source_target_pairs={{0,3},{1,2},{2,1},{3,0},{4,7},{5,6},{6,5},{7,4},{8,11},{9,10},{10,... | collective-permute-start | bytes 122888 | tf_op jit(solution)/shard_map/ppermute | solution.py:196
  18.8 1.3 %fusion.2.refs_7_.tall_ref = bf16[1536,128]{1,0:T(8,128)(2,1)S(1)} fusion(s32[1536]{0:T(1024)S(1)} %reduce, bf16[1536]{0:T(1024)(128)(2,1)S(1)} %reduce.1), kind=kLoop, calls=%fused_computation.5 | loop fusion | flops 393216 | bytes 402432 | tf_op jit(solution)/shard_map/jit(_where)/select_n | solution.py:264
  20.1 0.8 fusion.15
  21.0 1.6 %collective-permute-start.2 = (bf16[160,128]{1,0:T(8,128)(2,1)S(1)}, bf16[160,128]{1,0:T(8,128)(2,1)S(1)}, u32[]{:S(2)}, u32[]{:S(2)}) collective-permute-start(bf16[160,128]{1,0:T(8,128)(2,1)S(1)} %get-tuple-element.78), channel_id=1, source_target_pairs={{0,4},{4,0},{8,12},{12,8},{16,20},{20,16},{24,28},{28,24},{1,5},{5... | collective-permute-start | bytes 122888 | tf_op jit(solution)/shard_map/ppermute | solution.py:191
  22.5 3.6 %collective-permute-start.3 = (bf16[160,128]{1,0:T(8,128)(2,1)S(1)}, bf16[160,128]{1,0:T(8,128)(2,1)S(1)}, u32[]{:S(2)}, u32[]{:S(2)}) collective-permute-start(bf16[160,128]{1,0:T(8,128)(2,1)S(1)} %get-tuple-element.79), channel_id=1, source_target_pairs={{0,28},{4,8},{8,4},{12,16},{16,12},{20,24},{24,20},{28,0},{1,29},{... | collective-permute-start | bytes 122888 | tf_op jit(solution)/shard_map/ppermute | solution.py:196
  26.3 3.0 %collective-permute-done.3 = bf16[160,128]{1,0:T(8,128)(2,1)S(1)} collective-permute-done((bf16[160,128]{1,0:T(8,128)(2,1)S(1)}, bf16[160,128]{1,0:T(8,128)(2,1)S(1)}, u32[]{:S(2)}, u32[]{:S(2)}) %collective-permute-start.3) | collective-permute-done | bytes 40992 | tf_op jit(solution)/shard_map/ppermute | solution.py:196
  29.3 1.0 copy-done.10
  30.3 1.6 %update.3 = (bf16[1536,128]{1,0:T(8,128)(2,1)}, bf16[1536,128]{1,0:T(8,128)(2,1)S(1)}, bf16[64,128]{1,0:T(8,128)(2,1)S(1)}) custom-call(s32[18]{0:T(128)S(1)} %stack.108.refs_0_.place, bf16[4,160,128]{2,1,0:T(8,128)(2,1)S(1)} %pad_maximum_fusion.2.refs_1_, bf16[1536,128]{1,0:T(8,128)(2,1)S(1)} %copy-done.10, bf16[1536,128]{1,0:T(8,128)(2,1)S(1)} %bitcast.44, ...), custom_call_target="tpu_custom_call" | custom-call | flops 201326592 | bytes 2359296 | tf_op jit(solution)/shard_map/update/pallas_call | solution.py:145
  32.0 2.0 %collective-permute-start.11 = (bf16[256,512]{1,0:T(8,128)(2,1)S(1)}, bf16[256,512]{1,0:T(8,128)(2,1)S(1)}, u32[]{:S(2)}, u32[]{:S(2)}) collective-permute-start(bf16[256,512]{1,0:T(8,128)(2,1)S(1)} %copy-done.8), channel_id=1, source_target_pairs={{0,4},{4,0},{8,12},{12,8},{16,20},{20,16},{24,28},{28,24},{1,5},{5... | collective-permute-start | bytes 786440 | tf_op jit(solution)/shard_map/ppermute | solution.py:191
  34.0 3.6 %collective-permute-start.12 = (bf16[256,512]{1,0:T(8,128)(2,1)S(1)}, bf16[256,512]{1,0:T(8,128)(2,1)S(1)}, u32[]{:S(2)}, u32[]{:S(2)}) collective-permute-start(bf16[256,512]{1,0:T(8,128)(2,1)S(1)} %copy-done.8), channel_id=1, source_target_pairs={{0,28},{4,8},{8,4},{12,16},{16,12},{20,24},{24,20},{28,0},{1,29},{... | collective-permute-start | bytes 786440 | tf_op jit(solution)/shard_map/ppermute | solution.py:196
  37.7 2.3 %copy-done.1 = bf16[1536,1536]{1,0:T(8,128)(2,1)S(1)} copy-done((bf16[1536,1536]{1,0:T(8,128)(2,1)S(1)}, bf16[1536,1536]{1,0:T(8,128)(2,1)}, u32[]{:S(2)}) %copy-start.1) | copy-done | bytes 4718616
  40.0 2.3 %copy-done.5 = bf16[1536,1536]{1,0:T(8,128)(2,1)S(1)} copy-done((bf16[1536,1536]{1,0:T(8,128)(2,1)S(1)}, bf16[1536,1536]{1,0:T(8,128)(2,1)}, u32[]{:S(2)}) %copy-start.5) | copy-done | bytes 4718616
  42.4 2.7 %products.2 = (bf16[1536,256]{1,0:T(8,128)(2,1)S(1)}, bf16[576,256]{1,0:T(8,128)(2,1)S(1)}, bf16[1536,1536]{1,0:T(8,128)(2,1)S(1)}, bf16[1536,1536]{1,0:T(8,128)(2,1)S(1)}) custom-call(bf16[1536,256]{1,0:T(8,128)(2,1)S(1)} %pad_maximum_fusion.u_ref, bf16[1536,1536]{1,0:T(8,128)(2,1)S(1)} %copy-done.1, ...), custom_call_target="tpu_custom_call", output_to_operand_aliasing={{2}: (1, {}), {3}: (2, {})} | custom-call | flops 2415919104 | bytes 9437184 | tf_op jit(solution)/shard_map/products/pallas_call | solution.py:83
  45.1 2.2 %copy-done.2 = bf16[1536,1536]{1,0:T(8,128)(2,1)} copy-done((bf16[1536,1536]{1,0:T(8,128)(2,1)}, bf16[1536,1536]{1,0:T(8,128)(2,1)S(1)}, u32[]{:S(2)}) %copy-start.2) | copy-done | bytes 4718616
  47.4 3.8 %collective-permute-start.9 = (bf16[2,64,128]{2,1,0:T(8,128)(2,1)S(1)}, bf16[2,64,128]{2,1,0:T(8,128)(2,1)S(1)}, u32[]{:S(2)}, u32[]{:S(2)}) collective-permute-start(bf16[2,64,128]{2,1,0:T(8,128)(2,1)S(1)} %pad_maximum_fusion.16), channel_id=1, source_target_pairs={{0,8},{4,12},{8,0},{12,4},{16,24},{20,28},{24,16},{28,20},{1,9},{5... | collective-permute-start | bytes 98312 | tf_op jit(solution)/shard_map/ppermute | solution.py:191
  51.3 1.9 %collective-permute-done.9 = bf16[2,64,128]{2,1,0:T(8,128)(2,1)S(1)} collective-permute-done((bf16[2,64,128]{2,1,0:T(8,128)(2,1)S(1)}, bf16[2,64,128]{2,1,0:T(8,128)(2,1)S(1)}, u32[]{:S(2)}, u32[]{:S(2)}) %collective-permute-start.9) | collective-permute-done | bytes 32800 | tf_op jit(solution)/shard_map/ppermute | solution.py:191
  53.3 2.9 %collective-permute-start.10 = (bf16[4,64,128]{2,1,0:T(8,128)(2,1)S(1)}, bf16[4,64,128]{2,1,0:T(8,128)(2,1)S(1)}, u32[]{:S(2)}, u32[]{:S(2)}) collective-permute-start(bf16[4,64,128]{2,1,0:T(8,128)(2,1)S(1)} %pad_maximum_fusion.9), channel_id=1, source_target_pairs={{0,16},{4,20},{8,24},{12,28},{16,0},{20,4},{24,8},{28,12},{1,17},{... | collective-permute-start | bytes 196616 | tf_op jit(solution)/shard_map/ppermute | solution.py:191
  56.4 3.4 %collective-permute-start.8 = (bf16[160,256]{1,0:T(8,128)(2,1)S(1)}, bf16[160,256]{1,0:T(8,128)(2,1)S(1)}, u32[]{:S(2)}, u32[]{:S(2)}) collective-permute-start(bf16[160,256]{1,0:T(8,128)(2,1)S(1)} %get-tuple-element.55), channel_id=1, source_target_pairs={{0,28},{4,8},{8,4},{12,16},{16,12},{20,24},{24,20},{28,0},{1,29},{... | collective-permute-start | bytes 245768 | tf_op jit(solution)/shard_map/ppermute | solution.py:196
  60.4 0.5 collective-permute-done.7
  60.8 2.8 %collective-permute-done.8 = bf16[160,256]{1,0:T(8,128)(2,1)S(1)} collective-permute-done((bf16[160,256]{1,0:T(8,128)(2,1)S(1)}, bf16[160,256]{1,0:T(8,128)(2,1)S(1)}, u32[]{:S(2)}, u32[]{:S(2)}) %collective-permute-start.8) | collective-permute-done | bytes 81952 | tf_op jit(solution)/shard_map/ppermute | solution.py:196
  63.7 3.1 %collective-permute-done.13 = bf16[3,256,128]{2,1,0:T(8,128)(2,1)S(1)} collective-permute-done((bf16[3,256,128]{2,1,0:T(8,128)(2,1)S(1)}, bf16[3,256,128]{2,1,0:T(8,128)(2,1)S(1)}, u32[]{:S(2)}, u32[]{:S(2)}) %collective-permute-start.13) | collective-permute-done | bytes 196640 | tf_op jit(solution)/shard_map/ppermute | solution.py:191
  66.9 1.4 %collective-permute-done.14 = bf16[3,256,128]{2,1,0:T(8,128)(2,1)S(1)} collective-permute-done((bf16[3,256,128]{2,1,0:T(8,128)(2,1)S(1)}, bf16[3,256,128]{2,1,0:T(8,128)(2,1)S(1)}, u32[]{:S(2)}, u32[]{:S(2)}) %collective-permute-start.14) | collective-permute-done | bytes 196640 | tf_op jit(solution)/shard_map/ppermute | solution.py:191
  68.4 2.2 %update.4 = (bf16[1536,128]{1,0:T(8,128)(2,1)}, bf16[1536,128]{1,0:T(8,128)(2,1)S(1)}, bf16[64,128]{1,0:T(8,128)(2,1)S(1)}) custom-call(s32[18]{0:T(128)S(1)} %stack.108.refs_0_.place, bf16[4,160,128]{2,1,0:T(8,128)(2,1)S(1)} %get-tuple-element.47.rows_ref, bf16[1536,128]{1,0:T(8,128)(2,1)S(1)} %get-tuple-element.45.flux_ref, ...), custom_call_target="tpu_custom_call" | custom-call | flops 201326592 | bytes 2359296 | tf_op jit(solution)/shard_map/update/pallas_call | solution.py:145
  70.6 3.7 %collective-permute-done.15 = bf16[64,128]{1,0:T(8,128)(2,1)S(1)} collective-permute-done((bf16[64,128]{1,0:T(8,128)(2,1)S(1)}, bf16[64,128]{1,0:T(8,128)(2,1)S(1)}, u32[]{:S(2)}, u32[]{:S(2)}) %collective-permute-start.15) | collective-permute-done | bytes 16416 | tf_op jit(solution)/shard_map/ppermute | solution.py:191
  74.3 2.7 %products.3 = (bf16[1536,128]{1,0:T(8,128)(2,1)S(1)}, bf16[576,128]{1,0:T(8,128)(2,1)S(1)}, bf16[1536,1536]{1,0:T(8,128)(2,1)S(1)}, bf16[1536,1536]{1,0:T(8,128)(2,1)S(1)}) custom-call(bf16[1536,128]{1,0:T(8,128)(2,1)S(1)} %get-tuple-element.35.u_ref.state_ref, bf16[1536,1536]{1,0:T(8,128)(2,1)S(1)} %copy-done.3, ...), custom_call_target="tpu_custom_call", output_to_operand_aliasing={{2}: (1, {}), {3}: (2, {})} | custom-call | flops 2415919104 | bytes 9437184 | tf_op jit(solution)/shard_map/products/pallas_call | solution.py:83
  77.2 0.4 collective-permute-start.17
  77.7 3.4 %collective-permute-done.20 = bf16[2,64,128]{2,1,0:T(8,128)(2,1)S(1)} collective-permute-done((bf16[2,64,128]{2,1,0:T(8,128)(2,1)S(1)}, bf16[2,64,128]{2,1,0:T(8,128)(2,1)S(1)}, u32[]{:S(2)}, u32[]{:S(2)}) %collective-permute-start.20) | collective-permute-done | bytes 32800 | tf_op jit(solution)/shard_map/ppermute | solution.py:191
  81.1 1.0 collective-permute-start.21
  82.1 4.4 %collective-permute-done.21 = bf16[4,64,128]{2,1,0:T(8,128)(2,1)S(1)} collective-permute-done((bf16[4,64,128]{2,1,0:T(8,128)(2,1)S(1)}, bf16[4,64,128]{2,1,0:T(8,128)(2,1)S(1)}, u32[]{:S(2)}, u32[]{:S(2)}) %collective-permute-start.21) | collective-permute-done | bytes 65568 | tf_op jit(solution)/shard_map/ppermute | solution.py:191
  87.4 3.5 %collective-permute-start.19 = (bf16[160,128]{1,0:T(8,128)(2,1)S(1)}, bf16[160,128]{1,0:T(8,128)(2,1)S(1)}, u32[]{:S(2)}, u32[]{:S(2)}) collective-permute-start(bf16[160,128]{1,0:T(8,128)(2,1)S(1)} %get-tuple-element.69), channel_id=1, source_target_pairs={{0,28},{4,8},{8,4},{12,16},{16,12},{20,24},{24,20},{28,0},{1,29},{... | collective-permute-start | bytes 122888 | tf_op jit(solution)/shard_map/ppermute | solution.py:196
  90.9 1.7 %collective-permute-done.22 = bf16[3,256,128]{2,1,0:T(8,128)(2,1)S(1)} collective-permute-done((bf16[3,256,128]{2,1,0:T(8,128)(2,1)S(1)}, bf16[3,256,128]{2,1,0:T(8,128)(2,1)S(1)}, u32[]{:S(2)}, u32[]{:S(2)}) %collective-permute-start.22) | collective-permute-done | bytes 196640 | tf_op jit(solution)/shard_map/ppermute | solution.py:191
  92.7 1.4 %collective-permute-done.19 = bf16[160,128]{1,0:T(8,128)(2,1)S(1)} collective-permute-done((bf16[160,128]{1,0:T(8,128)(2,1)S(1)}, bf16[160,128]{1,0:T(8,128)(2,1)S(1)}, u32[]{:S(2)}, u32[]{:S(2)}) %collective-permute-start.19) | collective-permute-done | bytes 40992 | tf_op jit(solution)/shard_map/ppermute | solution.py:196
  94.3 2.2 %update.5 = (bf16[1536,128]{1,0:T(8,128)(2,1)}, bf16[1536,128]{1,0:T(8,128)(2,1)S(1)}, bf16[64,128]{1,0:T(8,128)(2,1)S(1)}) custom-call(s32[18]{0:T(128)S(1)} %stack.108.refs_0_.place, bf16[4,160,128]{2,1,0:T(8,128)(2,1)S(1)} %pad_maximum_fusion.3.rows_ref, bf16[1536,128]{1,0:T(8,128)(2,1)S(1)} %get-tuple-element.39.flux_ref, ...), custom_call_target="tpu_custom_call" | custom-call | flops 201326592 | bytes 2359296 | tf_op jit(solution)/shard_map/update/pallas_call | solution.py:145
  96.8 3.4 %collective-permute-done.24 = bf16[64,128]{1,0:T(8,128)(2,1)S(1)} collective-permute-done((bf16[64,128]{1,0:T(8,128)(2,1)S(1)}, bf16[64,128]{1,0:T(8,128)(2,1)S(1)}, u32[]{:S(2)}, u32[]{:S(2)}) %collective-permute-start.24) | collective-permute-done | bytes 16416 | tf_op jit(solution)/shard_map/ppermute | solution.py:191
  100.2 3.9 %collective-permute-done.25 = bf16[2,64,128]{2,1,0:T(8,128)(2,1)S(1)} collective-permute-done((bf16[2,64,128]{2,1,0:T(8,128)(2,1)S(1)}, bf16[2,64,128]{2,1,0:T(8,128)(2,1)S(1)}, u32[]{:S(2)}, u32[]{:S(2)}) %collective-permute-start.25) | collective-permute-done | bytes 32800 | tf_op jit(solution)/shard_map/ppermute | solution.py:191
  104.2 0.8 collective-permute-start.26
  105.0 4.5 %collective-permute-done.26 = bf16[4,64,128]{2,1,0:T(8,128)(2,1)S(1)} collective-permute-done((bf16[4,64,128]{2,1,0:T(8,128)(2,1)S(1)}, bf16[4,64,128]{2,1,0:T(8,128)(2,1)S(1)}, u32[]{:S(2)}, u32[]{:S(2)}) %collective-permute-start.26) | collective-permute-done | bytes 65568 | tf_op jit(solution)/shard_map/ppermute | solution.py:191
  109.8 2.3 %collective-permute-start.27 = (bf16[128,128]{1,0:T(8,128)(2,1)S(1)}, bf16[128,128]{1,0:T(8,128)(2,1)S(1)}, u32[]{:S(2)}, u32[]{:S(2)}) collective-permute-start(bf16[128,128]{1,0:T(8,128)(2,1)S(1)} %fusion.9), channel_id=1, source_target_pairs={{0,2},{1,3},{2,0},{3,1},{4,6},{5,7},{6,4},{7,5},{8,10},{9,11},{10,... | collective-permute-start | bytes 98312 | tf_op jit(solution)/shard_map/ppermute | solution.py:191
  112.1 1.9 %collective-permute-done.27 = bf16[128,128]{1,0:T(8,128)(2,1)S(1)} collective-permute-done((bf16[128,128]{1,0:T(8,128)(2,1)S(1)}, bf16[128,128]{1,0:T(8,128)(2,1)S(1)}, u32[]{:S(2)}, u32[]{:S(2)}) %collective-permute-start.27) | collective-permute-done | bytes 32800 | tf_op jit(solution)/shard_map/ppermute | solution.py:191
  114.2 1.2 %collective-permute-done.28 = bf16[64,128]{1,0:T(8,128)(2,1)S(1)} collective-permute-done((bf16[64,128]{1,0:T(8,128)(2,1)S(1)}, bf16[64,128]{1,0:T(8,128)(2,1)S(1)}, u32[]{:S(2)}, u32[]{:S(2)}) %collective-permute-start.28) | collective-permute-done | bytes 16416 | tf_op jit(solution)/shard_map/ppermute | solution.py:191
  115.3 1.0 fusion.1
  (98 shorter events, 3.7 us)
Async XLA Ops:
  2.3 16.4 %copy-start.11 = (s32[1,1,1536]{2,1,0:T(1,128)S(1)}, s32[1,1,1536]{2,1,0:T(1,128)}, u32[]{:S(2)}) copy-start(s32[1,1,1536]{2,1,0:T(1,128)} %param.13) | copy-start | bytes 18436
  2.3 16.5 %copy-start.12 = (bf16[1,1,1536]{2,1,0:T(2,128)(2,1)S(1)}, bf16[1,1,1536]{2,1,0:T(2,128)(2,1)}, u32[]{:S(2)}) copy-start(bf16[1,1,1536]{2,1,0:T(2,128)(2,1)} %param.14) | copy-start | bytes 9220
  2.3 27.0 %copy-start.7 = (bf16[1,1,1536,128]{3,2,1,0:T(8,128)(2,1)S(1)}, bf16[1,1,1536,128]{3,2,1,0:T(8,128)(2,1)}, u32[]{:S(2)}) copy-start(bf16[1,1,1536,128]{3,2,1,0:T(8,128)(2,1)} %param.9) | copy-start | bytes 1179652
  2.3 27.0 %copy-start.9 = (bf16[1,1,1536,128]{3,2,1,0:T(8,128)(2,1)S(1)}, bf16[1,1,1536,128]{3,2,1,0:T(8,128)(2,1)}, u32[]{:S(2)}) copy-start(bf16[1,1,1536,128]{3,2,1,0:T(8,128)(2,1)} %param.8) | copy-start | bytes 1179652
  2.3 29.6 %copy-start.8 = (bf16[256,512]{1,0:T(8,128)(2,1)S(1)}, bf16[256,512]{1,0:T(8,128)(2,1)}, u32[]{:S(2)}) copy-start(bf16[256,512]{1,0:T(8,128)(2,1)} %refs_0_.5) | copy-start | bytes 786436
  10.4 2.2 %copy-start = (bf16[1536,1536]{1,0:T(8,128)(2,1)}, bf16[1536,1536]{1,0:T(8,128)(2,1)S(1)}, u32[]{:S(2)}) copy-start(bf16[1536,1536]{1,0:T(8,128)(2,1)S(1)} %get-tuple-element.28.k_ref) | copy-start | bytes 14155780
  12.6 2.2 %copy-start.4 = (bf16[1536,1536]{1,0:T(8,128)(2,1)}, bf16[1536,1536]{1,0:T(8,128)(2,1)S(1)}, u32[]{:S(2)}) copy-start(bf16[1536,1536]{1,0:T(8,128)(2,1)S(1)} %get-tuple-element.29.s_ref) | copy-start | bytes 14155780
  14.7 22.9 %copy-start.6 = (bf16[8,128,128]{2,1,0:T(8,128)(2,1)S(1)}, bf16[8,128,128]{2,1,0:T(8,128)(2,1)}, u32[]{:S(2)}) copy-start(bf16[8,128,128]{2,1,0:T(8,128)(2,1)} %get-tuple-element.91.sel_ref) | copy-start | bytes 786436
  15.6 5.3 %collective-permute-start = (bf16[160,128]{1,0:T(8,128)(2,1)S(1)}, bf16[160,128]{1,0:T(8,128)(2,1)S(1)}, u32[]{:S(2)}, u32[]{:S(2)}) collective-permute-start(bf16[160,128]{1,0:T(8,128)(2,1)S(1)} %get-tuple-element.64), channel_id=1, source_target_pairs={{0,1},{1,0},{2,3},{3,2},{4,5},{5,4},{6,7},{7,6},{8,9},{9,8},{10,11... | collective-permute-start | bytes 122888 | tf_op jit(solution)/shard_map/ppermute | solution.py:191
  16.1 4.8 %collective-permute-start.1 = (bf16[160,128]{1,0:T(8,128)(2,1)S(1)}, bf16[160,128]{1,0:T(8,128)(2,1)S(1)}, u32[]{:S(2)}, u32[]{:S(2)}) collective-permute-start(bf16[160,128]{1,0:T(8,128)(2,1)S(1)} %get-tuple-element.65), channel_id=1, source_target_pairs={{0,3},{1,2},{2,1},{3,0},{4,7},{5,6},{6,5},{7,4},{8,11},{9,10},{10,... | collective-permute-start | bytes 122888 | tf_op jit(solution)/shard_map/ppermute | solution.py:196
  21.0 5.3 %collective-permute-start.2 = (bf16[160,128]{1,0:T(8,128)(2,1)S(1)}, bf16[160,128]{1,0:T(8,128)(2,1)S(1)}, u32[]{:S(2)}, u32[]{:S(2)}) collective-permute-start(bf16[160,128]{1,0:T(8,128)(2,1)S(1)} %get-tuple-element.78), channel_id=1, source_target_pairs={{0,4},{4,0},{8,12},{12,8},{16,20},{20,16},{24,28},{28,24},{1,5},{5... | collective-permute-start | bytes 122888 | tf_op jit(solution)/shard_map/ppermute | solution.py:191
  22.5 6.7 %collective-permute-start.3 = (bf16[160,128]{1,0:T(8,128)(2,1)S(1)}, bf16[160,128]{1,0:T(8,128)(2,1)S(1)}, u32[]{:S(2)}, u32[]{:S(2)}) collective-permute-start(bf16[160,128]{1,0:T(8,128)(2,1)S(1)} %get-tuple-element.79), channel_id=1, source_target_pairs={{0,28},{4,8},{8,4},{12,16},{16,12},{20,24},{24,20},{28,0},{1,29},{... | collective-permute-start | bytes 122888 | tf_op jit(solution)/shard_map/ppermute | solution.py:196
  29.3 1.0 copy-start.10
  32.0 5.6 %collective-permute-start.4 = (bf16[64,128]{1,0:T(8,128)(2,1)S(1)}, bf16[64,128]{1,0:T(8,128)(2,1)S(1)}, u32[]{:S(2)}, u32[]{:S(2)}) collective-permute-start(bf16[64,128]{1,0:T(8,128)(2,1)S(1)} %get-tuple-element.26), channel_id=1, source_target_pairs={{0,4},{4,0},{8,12},{12,8},{16,20},{20,16},{24,28},{28,24},{1,5},{5... | collective-permute-start | bytes 49160 | tf_op jit(solution)/shard_map/ppermute | solution.py:191
  32.0 27.9 %collective-permute-start.11 = (bf16[256,512]{1,0:T(8,128)(2,1)S(1)}, bf16[256,512]{1,0:T(8,128)(2,1)S(1)}, u32[]{:S(2)}, u32[]{:S(2)}) collective-permute-start(bf16[256,512]{1,0:T(8,128)(2,1)S(1)} %copy-done.8), channel_id=1, source_target_pairs={{0,4},{4,0},{8,12},{12,8},{16,20},{20,16},{24,28},{28,24},{1,5},{5... | collective-permute-start | bytes 786440 | tf_op jit(solution)/shard_map/ppermute | solution.py:191
  34.0 25.9 %collective-permute-start.12 = (bf16[256,512]{1,0:T(8,128)(2,1)S(1)}, bf16[256,512]{1,0:T(8,128)(2,1)S(1)}, u32[]{:S(2)}, u32[]{:S(2)}) collective-permute-start(bf16[256,512]{1,0:T(8,128)(2,1)S(1)} %copy-done.8), channel_id=1, source_target_pairs={{0,28},{4,8},{8,4},{12,16},{16,12},{20,24},{24,20},{28,0},{1,29},{... | collective-permute-start | bytes 786440 | tf_op jit(solution)/shard_map/ppermute | solution.py:196
  37.7 2.3 %copy-start.1 = (bf16[1536,1536]{1,0:T(8,128)(2,1)S(1)}, bf16[1536,1536]{1,0:T(8,128)(2,1)}, u32[]{:S(2)}) copy-start(bf16[1536,1536]{1,0:T(8,128)(2,1)} %copy-done) | copy-start | bytes 14155780
  40.0 2.3 %copy-start.5 = (bf16[1536,1536]{1,0:T(8,128)(2,1)S(1)}, bf16[1536,1536]{1,0:T(8,128)(2,1)}, u32[]{:S(2)}) copy-start(bf16[1536,1536]{1,0:T(8,128)(2,1)} %copy-done.4) | copy-start | bytes 14155780
  45.1 2.2 %copy-start.2 = (bf16[1536,1536]{1,0:T(8,128)(2,1)}, bf16[1536,1536]{1,0:T(8,128)(2,1)S(1)}, u32[]{:S(2)}) copy-start(bf16[1536,1536]{1,0:T(8,128)(2,1)S(1)} %get-tuple-element.36.k_ref) | copy-start | bytes 14155780
  47.3 9.0 %collective-permute-start.5 = (bf16[160,256]{1,0:T(8,128)(2,1)S(1)}, bf16[160,256]{1,0:T(8,128)(2,1)S(1)}, u32[]{:S(2)}, u32[]{:S(2)}) collective-permute-start(bf16[160,256]{1,0:T(8,128)(2,1)S(1)} %get-tuple-element.50), channel_id=1, source_target_pairs={{0,1},{1,0},{2,3},{3,2},{4,5},{5,4},{6,7},{7,6},{8,9},{9,8},{10,11... | collective-permute-start | bytes 245768 | tf_op jit(solution)/shard_map/ppermute | solution.py:191
  47.4 5.9 %collective-permute-start.9 = (bf16[2,64,128]{2,1,0:T(8,128)(2,1)S(1)}, bf16[2,64,128]{2,1,0:T(8,128)(2,1)S(1)}, u32[]{:S(2)}, u32[]{:S(2)}) collective-permute-start(bf16[2,64,128]{2,1,0:T(8,128)(2,1)S(1)} %pad_maximum_fusion.16), channel_id=1, source_target_pairs={{0,8},{4,12},{8,0},{12,4},{16,24},{20,28},{24,16},{28,20},{1,9},{5... | collective-permute-start | bytes 98312 | tf_op jit(solution)/shard_map/ppermute | solution.py:191
  51.2 23.1 %copy-start.3 = (bf16[1536,1536]{1,0:T(8,128)(2,1)S(1)}, bf16[1536,1536]{1,0:T(8,128)(2,1)}, u32[]{:S(2)}) copy-start(bf16[1536,1536]{1,0:T(8,128)(2,1)} %copy-done.2) | copy-start | bytes 14155780
  51.2 5.0 %collective-permute-start.6 = (bf16[160,256]{1,0:T(8,128)(2,1)S(1)}, bf16[160,256]{1,0:T(8,128)(2,1)S(1)}, u32[]{:S(2)}, u32[]{:S(2)}) collective-permute-start(bf16[160,256]{1,0:T(8,128)(2,1)S(1)} %get-tuple-element.51), channel_id=1, source_target_pairs={{0,3},{1,2},{2,1},{3,0},{4,7},{5,6},{6,5},{7,4},{8,11},{9,10},{10,... | collective-permute-start | bytes 245768 | tf_op jit(solution)/shard_map/ppermute | solution.py:196
  53.3 6.6 %collective-permute-start.10 = (bf16[4,64,128]{2,1,0:T(8,128)(2,1)S(1)}, bf16[4,64,128]{2,1,0:T(8,128)(2,1)S(1)}, u32[]{:S(2)}, u32[]{:S(2)}) collective-permute-start(bf16[4,64,128]{2,1,0:T(8,128)(2,1)S(1)} %pad_maximum_fusion.9), channel_id=1, source_target_pairs={{0,16},{4,20},{8,24},{12,28},{16,0},{20,4},{24,8},{28,12},{1,17},{... | collective-permute-start | bytes 196616 | tf_op jit(solution)/shard_map/ppermute | solution.py:191
  56.3 4.5 %collective-permute-start.7 = (bf16[160,256]{1,0:T(8,128)(2,1)S(1)}, bf16[160,256]{1,0:T(8,128)(2,1)S(1)}, u32[]{:S(2)}, u32[]{:S(2)}) collective-permute-start(bf16[160,256]{1,0:T(8,128)(2,1)S(1)} %get-tuple-element.54), channel_id=1, source_target_pairs={{0,4},{4,0},{8,12},{12,8},{16,20},{20,16},{24,28},{28,24},{1,5},{5... | collective-permute-start | bytes 245768 | tf_op jit(solution)/shard_map/ppermute | solution.py:191
  56.4 7.2 %collective-permute-start.8 = (bf16[160,256]{1,0:T(8,128)(2,1)S(1)}, bf16[160,256]{1,0:T(8,128)(2,1)S(1)}, u32[]{:S(2)}, u32[]{:S(2)}) collective-permute-start(bf16[160,256]{1,0:T(8,128)(2,1)S(1)} %get-tuple-element.55), channel_id=1, source_target_pairs={{0,28},{4,8},{8,4},{12,16},{16,12},{20,24},{24,20},{28,0},{1,29},{... | collective-permute-start | bytes 245768 | tf_op jit(solution)/shard_map/ppermute | solution.py:196
  60.3 6.4 %collective-permute-start.13 = (bf16[3,256,128]{2,1,0:T(8,128)(2,1)S(1)}, bf16[3,256,128]{2,1,0:T(8,128)(2,1)S(1)}, u32[]{:S(2)}, u32[]{:S(2)}) collective-permute-start(bf16[3,256,128]{2,1,0:T(8,128)(2,1)S(1)} %convert_element_type.62), channel_id=1, source_target_pairs={{0,2},{1,3},{2,0},{3,1},{4,6},{5,7},{6,4},{7,5},{8,10},{9,11},{10,... | collective-permute-start | bytes 589832 | tf_op jit(solution)/shard_map/ppermute | solution.py:191
  66.8 1.5 %collective-permute-start.14 = (bf16[3,256,128]{2,1,0:T(8,128)(2,1)S(1)}, bf16[3,256,128]{2,1,0:T(8,128)(2,1)S(1)}, u32[]{:S(2)}, u32[]{:S(2)}) collective-permute-start(bf16[3,256,128]{2,1,0:T(8,128)(2,1)S(1)} %fusion.7), channel_id=1, source_target_pairs={{0,1},{1,0},{2,3},{3,2},{4,5},{5,4},{6,7},{7,6},{8,9},{9,8},{10,11... | collective-permute-start | bytes 589832 | tf_op jit(solution)/shard_map/ppermute | solution.py:191
  70.6 3.7 %collective-permute-start.15 = (bf16[64,128]{1,0:T(8,128)(2,1)S(1)}, bf16[64,128]{1,0:T(8,128)(2,1)S(1)}, u32[]{:S(2)}, u32[]{:S(2)}) collective-permute-start(bf16[64,128]{1,0:T(8,128)(2,1)S(1)} %get-tuple-element.34), channel_id=1, source_target_pairs={{0,4},{4,0},{8,12},{12,8},{16,20},{20,16},{24,28},{28,24},{1,5},{5... | collective-permute-start | bytes 49160 | tf_op jit(solution)/shard_map/ppermute | solution.py:191
  77.1 4.0 %collective-permute-start.20 = (bf16[2,64,128]{2,1,0:T(8,128)(2,1)S(1)}, bf16[2,64,128]{2,1,0:T(8,128)(2,1)S(1)}, u32[]{:S(2)}, u32[]{:S(2)}) collective-permute-start(bf16[2,64,128]{2,1,0:T(8,128)(2,1)S(1)} %pad_maximum_fusion.17), channel_id=1, source_target_pairs={{0,8},{4,12},{8,0},{12,4},{16,24},{20,28},{24,16},{28,20},{1,9},{5... | collective-permute-start | bytes 98312 | tf_op jit(solution)/shard_map/ppermute | solution.py:191
  77.2 4.9 %collective-permute-start.16 = (bf16[160,128]{1,0:T(8,128)(2,1)S(1)}, bf16[160,128]{1,0:T(8,128)(2,1)S(1)}, u32[]{:S(2)}, u32[]{:S(2)}) collective-permute-start(bf16[160,128]{1,0:T(8,128)(2,1)S(1)} %get-tuple-element.60), channel_id=1, source_target_pairs={{0,1},{1,0},{2,3},{3,2},{4,5},{5,4},{6,7},{7,6},{8,9},{9,8},{10,11... | collective-permute-start | bytes 122888 | tf_op jit(solution)/shard_map/ppermute | solution.py:191
  77.2 4.8 %collective-permute-start.17 = (bf16[160,128]{1,0:T(8,128)(2,1)S(1)}, bf16[160,128]{1,0:T(8,128)(2,1)S(1)}, u32[]{:S(2)}, u32[]{:S(2)}) collective-permute-start(bf16[160,128]{1,0:T(8,128)(2,1)S(1)} %get-tuple-element.61), channel_id=1, source_target_pairs={{0,3},{1,2},{2,1},{3,0},{4,7},{5,6},{6,5},{7,4},{8,11},{9,10},{10,... | collective-permute-start | bytes 122888 | tf_op jit(solution)/shard_map/ppermute | solution.py:196
  81.1 5.4 %collective-permute-start.21 = (bf16[4,64,128]{2,1,0:T(8,128)(2,1)S(1)}, bf16[4,64,128]{2,1,0:T(8,128)(2,1)S(1)}, u32[]{:S(2)}, u32[]{:S(2)}) collective-permute-start(bf16[4,64,128]{2,1,0:T(8,128)(2,1)S(1)} %pad_maximum_fusion.10), channel_id=1, source_target_pairs={{0,16},{4,20},{8,24},{12,28},{16,0},{20,4},{24,8},{28,12},{1,17},{... | collective-permute-start | bytes 196616 | tf_op jit(solution)/shard_map/ppermute | solution.py:191
  86.9 5.7 %collective-permute-start.22 = (bf16[3,256,128]{2,1,0:T(8,128)(2,1)S(1)}, bf16[3,256,128]{2,1,0:T(8,128)(2,1)S(1)}, u32[]{:S(2)}, u32[]{:S(2)}) collective-permute-start(bf16[3,256,128]{2,1,0:T(8,128)(2,1)S(1)} %convert_element_type.67), channel_id=1, source_target_pairs={{0,2},{1,3},{2,0},{3,1},{4,6},{5,7},{6,4},{7,5},{8,10},{9,11},{10,... | collective-permute-start | bytes 589832 | tf_op jit(solution)/shard_map/ppermute | solution.py:191
  87.3 5.5 %collective-permute-start.18 = (bf16[160,128]{1,0:T(8,128)(2,1)S(1)}, bf16[160,128]{1,0:T(8,128)(2,1)S(1)}, u32[]{:S(2)}, u32[]{:S(2)}) collective-permute-start(bf16[160,128]{1,0:T(8,128)(2,1)S(1)} %get-tuple-element.68), channel_id=1, source_target_pairs={{0,4},{4,0},{8,12},{12,8},{16,20},{20,16},{24,28},{28,24},{1,5},{5... | collective-permute-start | bytes 122888 | tf_op jit(solution)/shard_map/ppermute | solution.py:191
  87.4 6.7 %collective-permute-start.19 = (bf16[160,128]{1,0:T(8,128)(2,1)S(1)}, bf16[160,128]{1,0:T(8,128)(2,1)S(1)}, u32[]{:S(2)}, u32[]{:S(2)}) collective-permute-start(bf16[160,128]{1,0:T(8,128)(2,1)S(1)} %get-tuple-element.69), channel_id=1, source_target_pairs={{0,28},{4,8},{8,4},{12,16},{16,12},{20,24},{24,20},{28,0},{1,29},{... | collective-permute-start | bytes 122888 | tf_op jit(solution)/shard_map/ppermute | solution.py:196
  92.7 1.5 %collective-permute-start.23 = (bf16[3,256,128]{2,1,0:T(8,128)(2,1)S(1)}, bf16[3,256,128]{2,1,0:T(8,128)(2,1)S(1)}, u32[]{:S(2)}, u32[]{:S(2)}) collective-permute-start(bf16[3,256,128]{2,1,0:T(8,128)(2,1)S(1)} %fusion.8), channel_id=1, source_target_pairs={{0,1},{1,0},{2,3},{3,2},{4,5},{5,4},{6,7},{7,6},{8,9},{9,8},{10,11... | collective-permute-start | bytes 589832 | tf_op jit(solution)/shard_map/ppermute | solution.py:191
  96.5 3.7 %collective-permute-start.24 = (bf16[64,128]{1,0:T(8,128)(2,1)S(1)}, bf16[64,128]{1,0:T(8,128)(2,1)S(1)}, u32[]{:S(2)}, u32[]{:S(2)}) collective-permute-start(bf16[64,128]{1,0:T(8,128)(2,1)S(1)} %get-tuple-element.42), channel_id=1, source_target_pairs={{0,4},{4,0},{8,12},{12,8},{16,20},{20,16},{24,28},{28,24},{1,5},{5... | collective-permute-start | bytes 49160 | tf_op jit(solution)/shard_map/ppermute | solution.py:191
  100.2 3.9 %collective-permute-start.25 = (bf16[2,64,128]{2,1,0:T(8,128)(2,1)S(1)}, bf16[2,64,128]{2,1,0:T(8,128)(2,1)S(1)}, u32[]{:S(2)}, u32[]{:S(2)}) collective-permute-start(bf16[2,64,128]{2,1,0:T(8,128)(2,1)S(1)} %pad_maximum_fusion.18), channel_id=1, source_target_pairs={{0,8},{4,12},{8,0},{12,4},{16,24},{20,28},{24,16},{28,20},{1,9},{5... | collective-permute-start | bytes 98312 | tf_op jit(solution)/shard_map/ppermute | solution.py:191
  104.2 5.4 %collective-permute-start.26 = (bf16[4,64,128]{2,1,0:T(8,128)(2,1)S(1)}, bf16[4,64,128]{2,1,0:T(8,128)(2,1)S(1)}, u32[]{:S(2)}, u32[]{:S(2)}) collective-permute-start(bf16[4,64,128]{2,1,0:T(8,128)(2,1)S(1)} %pad_maximum_fusion.11), channel_id=1, source_target_pairs={{0,16},{4,20},{8,24},{12,28},{16,0},{20,4},{24,8},{28,12},{1,17},{... | collective-permute-start | bytes 196616 | tf_op jit(solution)/shard_map/ppermute | solution.py:191
  109.8 4.2 %collective-permute-start.27 = (bf16[128,128]{1,0:T(8,128)(2,1)S(1)}, bf16[128,128]{1,0:T(8,128)(2,1)S(1)}, u32[]{:S(2)}, u32[]{:S(2)}) collective-permute-start(bf16[128,128]{1,0:T(8,128)(2,1)S(1)} %fusion.9), channel_id=1, source_target_pairs={{0,2},{1,3},{2,0},{3,1},{4,6},{5,7},{6,4},{7,5},{8,10},{9,11},{10,... | collective-permute-start | bytes 98312 | tf_op jit(solution)/shard_map/ppermute | solution.py:191
  114.1 1.2 %collective-permute-start.28 = (bf16[64,128]{1,0:T(8,128)(2,1)S(1)}, bf16[64,128]{1,0:T(8,128)(2,1)S(1)}, u32[]{:S(2)}, u32[]{:S(2)}) collective-permute-start(bf16[64,128]{1,0:T(8,128)(2,1)S(1)} %select_convert_fusion.1), channel_id=1, source_target_pairs={{0,1},{1,0},{2,3},{3,2},{4,5},{5,4},{6,7},{7,6},{8,9},{9,8},{10,11... | collective-permute-start | bytes 49160 | tf_op jit(solution)/shard_map/ppermute | solution.py:191

commit v5 on v4

--- a/solution.py
+++ b/solution.py
@@ -20,7 +20,7 @@
 smem = pl.BlockSpec(memory_space=pltpu.SMEM)
 hbm = pl.BlockSpec(memory_space=pl.ANY)
 shape_of = jax.ShapeDtypeStruct
-params = pltpu.CompilerParams(vmem_limit_bytes=24 * 1024 * 1024)
+params = pltpu.CompilerParams(vmem_limit_bytes=16 * 1024 * 1024)
 large = pltpu.CompilerParams(vmem_limit_bytes=50 * 1024 * 1024)
 
 
@@ -37,7 +37,7 @@
         at += size
 
 
-def load_kernel(face, chunk, ahead, u_ref, k_hbm, s_hbm, sel_ref, flux_ref, packed_ref, k_ref, s_ref, mixed, sems):
+def load_kernel(face, chunk, ahead, u_ref, k_hbm, s_hbm, sel_ref, flux_ref, packed_ref, mixed, k_ref, s_ref, sems):
     count = u_ref.shape[0] // chunk
     copies = []
     for which, (source, target) in enumerate(((k_hbm, k_ref), (s_hbm, s_ref))):
@@ -59,7 +59,7 @@
     pick(face, sel_ref, flux_ref, packed_ref)
 
 
-def products_kernel(face, chunk, u_ref, k_ref, s_ref, sel_ref, flux_ref, packed_ref, k_out, s_out, mixed):
+def products_kernel(face, chunk, u_ref, k_ref, s_ref, sel_ref, flux_ref, packed_ref, mixed):
     u = u_ref[...]
     for i in range(u_ref.shape[0] // chunk):
         rows = pl.ds(i * chunk, chunk)
@@ -78,6 +78,7 @@
     scratch = [pltpu.VMEM((nodes, width), bf16)]
     body = functools.partial(products_kernel, face, chunk)
     if load:
+        scratch += [pltpu.VMEM((nodes, nodes), bf16)] * 2
         scratch += [pltpu.SemaphoreType.DMA((2, nodes // chunk))]
         body = functools.partial(load_kernel, face, chunk, 3)
     return pl.pallas_call(
@@ -85,13 +86,10 @@
         out_shape=[
             shape_of((nodes, width), bf16),
             shape_of((4 * (face + face // 8), width), bf16),
-            pltpu.VMEM((nodes, nodes), bf16),
-            pltpu.VMEM((nodes, nodes), bf16),
         ],
         in_specs=[vmem] + [hbm if load else vmem] * 2 + [vmem],
-        out_specs=[vmem] * 4,
+        out_specs=[vmem] * 2,
         scratch_shapes=scratch,
-        input_output_aliases={} if load else {1: 2, 2: 3},
         compiler_params=large if load else params,
         cost_estimate=pl.CostEstimate(
             flops=4 * nodes * nodes * 2 * LANES, bytes_accessed=4 * nodes * nodes, transcendentals=0
@@ -272,9 +270,8 @@
 
     matrices = [coarse_inverse, swap(coarse_inverse, "sub", 1), cross(coarse_inverse, "sub")]
 
-    flux, packed, kernel, inverse = products(
-        trace, double_layer[0, 0], single_inverse[0, 0], selector, load=True
-    )
+    kernel, inverse = double_layer[0, 0], single_inverse[0, 0]
+    flux, packed = products(trace, kernel, inverse, selector, load=True)
     rows = exchange(packed, face)
     u, coarse, wide, wide_rows = trace, None, None, None
     for iteration in range(ITERS):
@@ -288,7 +285,7 @@
             entering, pieces = lax.optimization_barrier((u, pieces))
             if iteration == 0:
                 entering = jnp.concatenate([entering, tall], axis=1)
-            flux, packed, kernel, inverse = products(entering, kernel, inverse, selector)
+            flux, packed = products(entering, kernel, inverse, selector)
             rows = exchange(packed, face)
             if iteration == 0:
                 wide, wide_rows = flux[:, width:], rows[:, :, width:]

time: 117 us -> 105 us (0.90)
  local copies, waits for them, and re-layouts: 13.2 us -> 5.95 us
  waiting for transfers between devices: 42.1 us -> 40.2 us
  Pallas kernels: 20.5 us -> 18.7 us
  other arithmetic: 4.68 us -> 3.13 us
    unnamed x26 -> x20, local copies, waits for them, and re-layouts: 12.2 us -> 5.7 us
    ppermute x7, starting transfers between devices: 17.2 us -> 20.4 us  [cross(): lax.ppermute(value, axis, [(i, (i + 1 if i % 2 else i - 1) % n) for i in...]
    ppermute x22, starting transfers between devices: 16.5 us -> 14.1 us  [swap(): lax.ppermute(value, axis, [(i, i ^ bit) for i in range(lax.axis_size(axis...]
    ppermute x22, waiting for transfers between devices: 35 us -> 32.7 us  [swap(): lax.ppermute(value, axis, [(i, i ^ bit) for i in range(lax.axis_size(axis...]
    pallas_call x3, Pallas kernels: 13.4 us -> 11.6 us  [products(): pl.pallas_call(body, out_shape=[shape_of((nodes, width), bf16), shape_of(...]
  transfers between devices with their start and end apart: 29 -> 29, of which waited for: 16 -> 17; matrix products, arithmetic and copies ran while one was open for 2% -> 2% of each run, Pallas kernels for 3% -> 6%
where the time goes in v5:
time: 105 us
  waiting for transfers between devices  40.2 us (38%)
  starting transfers between devices  34.5 us (33%)
  Pallas kernels  18.7 us (18%)
  local copies, waits for them, and re-layouts  5.95 us (6%)
  other arithmetic  3.13 us (3%)
  between operations  1.22 us (1%)
    ppermute x22, waiting for transfers between devices, swap(): lax.ppermute(value, axis, [(i, i ^ bit) for i in range(lax.axis_size(axis...  32.7 us
    ppermute x7, starting transfers between devices, cross(): lax.ppermute(value, axis, [(i, (i + 1 if i % 2 else i - 1) % n) for i in...  20.4 us
    ppermute x22, starting transfers between devices, swap(): lax.ppermute(value, axis, [(i, i ^ bit) for i in range(lax.axis_size(axis...  14.1 us
    pallas_call x3, Pallas kernels, products(): pl.pallas_call(body, out_shape=[shape_of((nodes, width), bf16), shape_of(...  11.6 us
    ppermute x7, waiting for transfers between devices, cross(): lax.ppermute(value, axis, [(i, (i + 1 if i % 2 else i - 1) % n) for i in...  7.43 us
    pallas_call x3, Pallas kernels, update(): pl.pallas_call(body, out_shape=[shape_of((nodes, width), bf16), shape_of(...  6.12 us
    unnamed x20, local copies, waits for them, and re-layouts  5.7 us
  transfers between devices with their start and end apart: 29, of which 17 were waited for; matrix products, arithmetic and copies ran while one was open for 2% of the time, Pallas kernels for 6%

profile of v5, /device:TPU:0, one launch (start us, length us, event | category | flops | bytes accessed | tf_op | source)
XLA Modules:
  0.0 104.6 jit_solution(17004379196369492754)
XLA Ops:
  0.7 0.8 bitcast_subtract_fusion
  1.4 0.2 fusion.4
  1.6 1.0 copy-done.4
  2.6 6.2 %load_products.1 = (bf16[1536,128]{1,0:T(8,128)(2,1)S(1)}, bf16[576,128]{1,0:T(8,128)(2,1)S(1)}) custom-call(bf16[1536,128]{1,0:T(8,128)(2,1)S(1)} %bitcast.55, bf16[1536,1536]{1,0:T(8,128)(2,1)} %bitcast.44, bf16[1536,1536]{1,0:T(8,128)(2,1)} %bitcast.49, bf16[8,128,128]{2,1,0:T(8,128)(2,1)S(1)} %get-tuple-element.83.sel_ref), custom_call_target="tpu_custom_call" | custom-call | flops 2415919104 | bytes 9437184 | tf_op jit(solution)/shard_map/load_products/pallas_call | solution.py:84
  8.8 0.5 collective-permute-start
  9.4 2.6 %collective-permute-start.1 = (bf16[160,128]{1,0:T(8,128)(2,1)S(1)}, bf16[160,128]{1,0:T(8,128)(2,1)S(1)}, u32[]{:S(2)}, u32[]{:S(2)}) collective-permute-start(bf16[160,128]{1,0:T(8,128)(2,1)S(1)} %get-tuple-element.57), channel_id=1, source_target_pairs={{0,3},{1,2},{2,1},{3,0},{4,7},{5,6},{6,5},{7,4},{8,11},{9,10},{10,... | collective-permute-start | bytes 122888 | tf_op jit(solution)/shard_map/ppermute | solution.py:194
  12.1 1.3 %fusion.2.refs_7_.tall_ref = bf16[1536,128]{1,0:T(8,128)(2,1)S(1)} fusion(s32[1536]{0:T(1024)S(1)} %reduce, bf16[1536]{0:T(1024)(128)(2,1)S(1)} %reduce.1), kind=kLoop, calls=%fused_computation.5 | loop fusion | flops 393216 | bytes 402432 | tf_op jit(solution)/shard_map/jit(_where)/select_n | solution.py:262
  13.4 0.4 collective-permute-done.1
  13.9 1.6 %collective-permute-start.2 = (bf16[160,128]{1,0:T(8,128)(2,1)S(1)}, bf16[160,128]{1,0:T(8,128)(2,1)S(1)}, u32[]{:S(2)}, u32[]{:S(2)}) collective-permute-start(bf16[160,128]{1,0:T(8,128)(2,1)S(1)} %get-tuple-element.70), channel_id=1, source_target_pairs={{0,4},{4,0},{8,12},{12,8},{16,20},{20,16},{24,28},{28,24},{1,5},{5... | collective-permute-start | bytes 122888 | tf_op jit(solution)/shard_map/ppermute | solution.py:189
  15.5 3.6 %collective-permute-start.3 = (bf16[160,128]{1,0:T(8,128)(2,1)S(1)}, bf16[160,128]{1,0:T(8,128)(2,1)S(1)}, u32[]{:S(2)}, u32[]{:S(2)}) collective-permute-start(bf16[160,128]{1,0:T(8,128)(2,1)S(1)} %get-tuple-element.71), channel_id=1, source_target_pairs={{0,28},{4,8},{8,4},{12,16},{16,12},{20,24},{24,20},{28,0},{1,29},{... | collective-permute-start | bytes 122888 | tf_op jit(solution)/shard_map/ppermute | solution.py:194
  19.2 3.0 %collective-permute-done.3 = bf16[160,128]{1,0:T(8,128)(2,1)S(1)} collective-permute-done((bf16[160,128]{1,0:T(8,128)(2,1)S(1)}, bf16[160,128]{1,0:T(8,128)(2,1)S(1)}, u32[]{:S(2)}, u32[]{:S(2)}) %collective-permute-start.3) | collective-permute-done | bytes 40992 | tf_op jit(solution)/shard_map/ppermute | solution.py:194
  22.3 1.6 %update.3 = (bf16[1536,128]{1,0:T(8,128)(2,1)}, bf16[1536,128]{1,0:T(8,128)(2,1)S(1)}, bf16[64,128]{1,0:T(8,128)(2,1)S(1)}) custom-call(s32[18]{0:T(128)S(1)} %stack.108.refs_0_.place, bf16[4,160,128]{2,1,0:T(8,128)(2,1)S(1)} %pad_maximum_fusion.2.refs_1_, bf16[1536,128]{1,0:T(8,128)(2,1)S(1)} %get-tuple-element.20.refs_2_, bf16[1536,128]{1,0:T(8,128)(2,1)S(1)} %bitcast.52, ...), custom_call_target="tpu_custom_call" | custom-call | flops 201326592 | bytes 2359296 | tf_op jit(solution)/shard_map/update/pallas_call | solution.py:143
  23.9 3.6 %collective-permute-start.12 = (bf16[256,512]{1,0:T(8,128)(2,1)S(1)}, bf16[256,512]{1,0:T(8,128)(2,1)S(1)}, u32[]{:S(2)}, u32[]{:S(2)}) collective-permute-start(bf16[256,512]{1,0:T(8,128)(2,1)S(1)} %copy-done.3), channel_id=1, source_target_pairs={{0,28},{4,8},{8,4},{12,16},{16,12},{20,24},{24,20},{28,0},{1,29},{... | collective-permute-start | bytes 786440 | tf_op jit(solution)/shard_map/ppermute | solution.py:194
  27.7 3.4 %collective-permute-start.9 = (bf16[2,64,128]{2,1,0:T(8,128)(2,1)S(1)}, bf16[2,64,128]{2,1,0:T(8,128)(2,1)S(1)}, u32[]{:S(2)}, u32[]{:S(2)}) collective-permute-start(bf16[2,64,128]{2,1,0:T(8,128)(2,1)S(1)} %pad_maximum_fusion.16), channel_id=1, source_target_pairs={{0,8},{4,12},{8,0},{12,4},{16,24},{20,28},{24,16},{28,20},{1,9},{5... | collective-permute-start | bytes 98312 | tf_op jit(solution)/shard_map/ppermute | solution.py:189
  31.2 2.3 %copy-done = bf16[1,1,1536,1536]{3,2,1,0:T(8,128)(2,1)S(1)} copy-done((bf16[1,1,1536,1536]{3,2,1,0:T(8,128)(2,1)S(1)}, bf16[1,1,1536,1536]{3,2,1,0:T(8,128)(2,1)}, u32[]{:S(2)}) %copy-start) | copy-done | bytes 4718616
  33.5 2.3 %copy-done.1 = bf16[1,1,1536,1536]{3,2,1,0:T(8,128)(2,1)S(1)} copy-done((bf16[1,1,1536,1536]{3,2,1,0:T(8,128)(2,1)S(1)}, bf16[1,1,1536,1536]{3,2,1,0:T(8,128)(2,1)}, u32[]{:S(2)}) %copy-start.1) | copy-done | bytes 4718616
  35.8 2.7 %products.2 = (bf16[1536,256]{1,0:T(8,128)(2,1)S(1)}, bf16[576,256]{1,0:T(8,128)(2,1)S(1)}) custom-call(bf16[1536,256]{1,0:T(8,128)(2,1)S(1)} %pad_maximum_fusion.u_ref, bf16[1536,1536]{1,0:T(8,128)(2,1)S(1)} %bitcast.45, bf16[1536,1536]{1,0:T(8,128)(2,1)S(1)} %bitcast.50, bf16[8,128,128]{2,1,0:T(8,128)(2,1)S(1)} %get-tuple-element.83.sel_ref), custom_call_target="tpu_custom_call" | custom-call | flops 2415919104 | bytes 9437184 | tf_op jit(solution)/shard_map/products/pallas_call | solution.py:84
  38.7 1.6 %collective-permute-start.6 = (bf16[160,256]{1,0:T(8,128)(2,1)S(1)}, bf16[160,256]{1,0:T(8,128)(2,1)S(1)}, u32[]{:S(2)}, u32[]{:S(2)}) collective-permute-start(bf16[160,256]{1,0:T(8,128)(2,1)S(1)} %get-tuple-element.43), channel_id=1, source_target_pairs={{0,3},{1,2},{2,1},{3,0},{4,7},{5,6},{6,5},{7,4},{8,11},{9,10},{10,... | collective-permute-start | bytes 245768 | tf_op jit(solution)/shard_map/ppermute | solution.py:194
  40.4 2.4 %collective-permute-start.10 = (bf16[4,64,128]{2,1,0:T(8,128)(2,1)S(1)}, bf16[4,64,128]{2,1,0:T(8,128)(2,1)S(1)}, u32[]{:S(2)}, u32[]{:S(2)}) collective-permute-start(bf16[4,64,128]{2,1,0:T(8,128)(2,1)S(1)} %pad_maximum_fusion.9), channel_id=1, source_target_pairs={{0,16},{4,20},{8,24},{12,28},{16,0},{20,4},{24,8},{28,12},{1,17},{... | collective-permute-start | bytes 196616 | tf_op jit(solution)/shard_map/ppermute | solution.py:189
  42.7 0.2 collective-permute-done.6
  43.1 5.2 %collective-permute-start.8 = (bf16[160,256]{1,0:T(8,128)(2,1)S(1)}, bf16[160,256]{1,0:T(8,128)(2,1)S(1)}, u32[]{:S(2)}, u32[]{:S(2)}) collective-permute-start(bf16[160,256]{1,0:T(8,128)(2,1)S(1)} %get-tuple-element.47), channel_id=1, source_target_pairs={{0,28},{4,8},{8,4},{12,16},{16,12},{20,24},{24,20},{28,0},{1,29},{... | collective-permute-start | bytes 245768 | tf_op jit(solution)/shard_map/ppermute | solution.py:194
  48.4 0.4 coarse_product.3
  48.8 1.6 %collective-permute-start.13 = (bf16[3,256,128]{2,1,0:T(8,128)(2,1)S(1)}, bf16[3,256,128]{2,1,0:T(8,128)(2,1)S(1)}, u32[]{:S(2)}, u32[]{:S(2)}) collective-permute-start(bf16[3,256,128]{2,1,0:T(8,128)(2,1)S(1)} %convert_element_type.62), channel_id=1, source_target_pairs={{0,2},{1,3},{2,0},{3,1},{4,6},{5,7},{6,4},{7,5},{8,10},{9,11},{10,... | collective-permute-start | bytes 589832 | tf_op jit(solution)/shard_map/ppermute | solution.py:189
  50.4 0.6 collective-permute-done.8
  51.1 4.4 %collective-permute-done.13 = bf16[3,256,128]{2,1,0:T(8,128)(2,1)S(1)} collective-permute-done((bf16[3,256,128]{2,1,0:T(8,128)(2,1)S(1)}, bf16[3,256,128]{2,1,0:T(8,128)(2,1)S(1)}, u32[]{:S(2)}, u32[]{:S(2)}) %collective-permute-start.13) | collective-permute-done | bytes 196640 | tf_op jit(solution)/shard_map/ppermute | solution.py:189
  55.7 1.4 %collective-permute-done.14 = bf16[3,256,128]{2,1,0:T(8,128)(2,1)S(1)} collective-permute-done((bf16[3,256,128]{2,1,0:T(8,128)(2,1)S(1)}, bf16[3,256,128]{2,1,0:T(8,128)(2,1)S(1)}, u32[]{:S(2)}, u32[]{:S(2)}) %collective-permute-start.14) | collective-permute-done | bytes 196640 | tf_op jit(solution)/shard_map/ppermute | solution.py:189
  57.1 2.2 %update.4 = (bf16[1536,128]{1,0:T(8,128)(2,1)}, bf16[1536,128]{1,0:T(8,128)(2,1)S(1)}, bf16[64,128]{1,0:T(8,128)(2,1)S(1)}) custom-call(s32[18]{0:T(128)S(1)} %stack.108.refs_0_.place, bf16[4,160,128]{2,1,0:T(8,128)(2,1)S(1)} %get-tuple-element.39.rows_ref, bf16[1536,128]{1,0:T(8,128)(2,1)S(1)} %get-tuple-element.37.flux_ref, ...), custom_call_target="tpu_custom_call" | custom-call | flops 201326592 | bytes 2359296 | tf_op jit(solution)/shard_map/update/pallas_call | solution.py:143
  59.4 3.7 %collective-permute-done.15 = bf16[64,128]{1,0:T(8,128)(2,1)S(1)} collective-permute-done((bf16[64,128]{1,0:T(8,128)(2,1)S(1)}, bf16[64,128]{1,0:T(8,128)(2,1)S(1)}, u32[]{:S(2)}, u32[]{:S(2)}) %collective-permute-start.15) | collective-permute-done | bytes 16416 | tf_op jit(solution)/shard_map/ppermute | solution.py:189
  63.1 2.7 %products.3 = (bf16[1536,128]{1,0:T(8,128)(2,1)S(1)}, bf16[576,128]{1,0:T(8,128)(2,1)S(1)}) custom-call(bf16[1536,128]{1,0:T(8,128)(2,1)S(1)} %get-tuple-element.29.u_ref.state_ref, bf16[1536,1536]{1,0:T(8,128)(2,1)S(1)} %bitcast.48, bf16[1536,1536]{1,0:T(8,128)(2,1)S(1)} %bitcast.51, bf16[8,128,128]{2,1,0:T(8,128)(2,1)S(1)} %get-tuple-element.83.sel_ref), custom_call_target="tpu_custom_call" | custom-call | flops 2415919104 | bytes 9437184 | tf_op jit(solution)/shard_map/products/pallas_call | solution.py:84
  66.0 1.6 %collective-permute-start.17 = (bf16[160,128]{1,0:T(8,128)(2,1)S(1)}, bf16[160,128]{1,0:T(8,128)(2,1)S(1)}, u32[]{:S(2)}, u32[]{:S(2)}) collective-permute-start(bf16[160,128]{1,0:T(8,128)(2,1)S(1)} %get-tuple-element.53), channel_id=1, source_target_pairs={{0,3},{1,2},{2,1},{3,0},{4,7},{5,6},{6,5},{7,4},{8,11},{9,10},{10,... | collective-permute-start | bytes 122888 | tf_op jit(solution)/shard_map/ppermute | solution.py:194
  67.6 1.3 %collective-permute-start.21 = (bf16[4,64,128]{2,1,0:T(8,128)(2,1)S(1)}, bf16[4,64,128]{2,1,0:T(8,128)(2,1)S(1)}, u32[]{:S(2)}, u32[]{:S(2)}) collective-permute-start(bf16[4,64,128]{2,1,0:T(8,128)(2,1)S(1)} %pad_maximum_fusion.10), channel_id=1, source_target_pairs={{0,16},{4,20},{8,24},{12,28},{16,0},{20,4},{24,8},{28,12},{1,17},{... | collective-permute-start | bytes 196616 | tf_op jit(solution)/shard_map/ppermute | solution.py:189
  69.0 0.5 collective-permute-done.17
  69.5 4.1 %collective-permute-done.21 = bf16[4,64,128]{2,1,0:T(8,128)(2,1)S(1)} collective-permute-done((bf16[4,64,128]{2,1,0:T(8,128)(2,1)S(1)}, bf16[4,64,128]{2,1,0:T(8,128)(2,1)S(1)}, u32[]{:S(2)}, u32[]{:S(2)}) %collective-permute-start.21) | collective-permute-done | bytes 65568 | tf_op jit(solution)/shard_map/ppermute | solution.py:189
  73.6 0.4 coarse_product.4
  74.0 1.7 %collective-permute-start.22 = (bf16[3,256,128]{2,1,0:T(8,128)(2,1)S(1)}, bf16[3,256,128]{2,1,0:T(8,128)(2,1)S(1)}, u32[]{:S(2)}, u32[]{:S(2)}) collective-permute-start(bf16[3,256,128]{2,1,0:T(8,128)(2,1)S(1)} %convert_element_type.67), channel_id=1, source_target_pairs={{0,2},{1,3},{2,0},{3,1},{4,6},{5,7},{6,4},{7,5},{8,10},{9,11},{10,... | collective-permute-start | bytes 589832 | tf_op jit(solution)/shard_map/ppermute | solution.py:189
  75.8 2.1 %collective-permute-start.19 = (bf16[160,128]{1,0:T(8,128)(2,1)S(1)}, bf16[160,128]{1,0:T(8,128)(2,1)S(1)}, u32[]{:S(2)}, u32[]{:S(2)}) collective-permute-start(bf16[160,128]{1,0:T(8,128)(2,1)S(1)} %get-tuple-element.61), channel_id=1, source_target_pairs={{0,28},{4,8},{8,4},{12,16},{16,12},{20,24},{24,20},{28,0},{1,29},{... | collective-permute-start | bytes 122888 | tf_op jit(solution)/shard_map/ppermute | solution.py:194
  77.9 1.9 %collective-permute-done.22 = bf16[3,256,128]{2,1,0:T(8,128)(2,1)S(1)} collective-permute-done((bf16[3,256,128]{2,1,0:T(8,128)(2,1)S(1)}, bf16[3,256,128]{2,1,0:T(8,128)(2,1)S(1)}, u32[]{:S(2)}, u32[]{:S(2)}) %collective-permute-start.22) | collective-permute-done | bytes 196640 | tf_op jit(solution)/shard_map/ppermute | solution.py:189
  79.9 2.7 %collective-permute-done.19 = bf16[160,128]{1,0:T(8,128)(2,1)S(1)} collective-permute-done((bf16[160,128]{1,0:T(8,128)(2,1)S(1)}, bf16[160,128]{1,0:T(8,128)(2,1)S(1)}, u32[]{:S(2)}, u32[]{:S(2)}) %collective-permute-start.19) | collective-permute-done | bytes 40992 | tf_op jit(solution)/shard_map/ppermute | solution.py:194
  82.7 2.2 %update.5 = (bf16[1536,128]{1,0:T(8,128)(2,1)}, bf16[1536,128]{1,0:T(8,128)(2,1)S(1)}, bf16[64,128]{1,0:T(8,128)(2,1)S(1)}) custom-call(s32[18]{0:T(128)S(1)} %stack.108.refs_0_.place, bf16[4,160,128]{2,1,0:T(8,128)(2,1)S(1)} %pad_maximum_fusion.3.rows_ref, bf16[1536,128]{1,0:T(8,128)(2,1)S(1)} %get-tuple-element.31.flux_ref, ...), custom_call_target="tpu_custom_call" | custom-call | flops 201326592 | bytes 2359296 | tf_op jit(solution)/shard_map/update/pallas_call | solution.py:143
  85.1 3.6 %collective-permute-done.24 = bf16[64,128]{1,0:T(8,128)(2,1)S(1)} collective-permute-done((bf16[64,128]{1,0:T(8,128)(2,1)S(1)}, bf16[64,128]{1,0:T(8,128)(2,1)S(1)}, u32[]{:S(2)}, u32[]{:S(2)}) %collective-permute-start.24) | collective-permute-done | bytes 16416 | tf_op jit(solution)/shard_map/ppermute | solution.py:189
  88.8 3.8 %collective-permute-done.25 = bf16[2,64,128]{2,1,0:T(8,128)(2,1)S(1)} collective-permute-done((bf16[2,64,128]{2,1,0:T(8,128)(2,1)S(1)}, bf16[2,64,128]{2,1,0:T(8,128)(2,1)S(1)}, u32[]{:S(2)}, u32[]{:S(2)}) %collective-permute-start.25) | collective-permute-done | bytes 32800 | tf_op jit(solution)/shard_map/ppermute | solution.py:189
  92.6 0.3 collective-permute-start.26
  92.9 5.2 %collective-permute-done.26 = bf16[4,64,128]{2,1,0:T(8,128)(2,1)S(1)} collective-permute-done((bf16[4,64,128]{2,1,0:T(8,128)(2,1)S(1)}, bf16[4,64,128]{2,1,0:T(8,128)(2,1)S(1)}, u32[]{:S(2)}, u32[]{:S(2)}) %collective-permute-start.26) | collective-permute-done | bytes 65568 | tf_op jit(solution)/shard_map/ppermute | solution.py:189
  98.1 0.2 coarse_product.5
  98.4 0.6 collective-permute-start.27
  99.0 3.4 %collective-permute-done.27 = bf16[128,128]{1,0:T(8,128)(2,1)S(1)} collective-permute-done((bf16[128,128]{1,0:T(8,128)(2,1)S(1)}, bf16[128,128]{1,0:T(8,128)(2,1)S(1)}, u32[]{:S(2)}, u32[]{:S(2)}) %collective-permute-start.27) | collective-permute-done | bytes 32800 | tf_op jit(solution)/shard_map/ppermute | solution.py:189
  102.5 1.2 %collective-permute-done.28 = bf16[64,128]{1,0:T(8,128)(2,1)S(1)} collective-permute-done((bf16[64,128]{1,0:T(8,128)(2,1)S(1)}, bf16[64,128]{1,0:T(8,128)(2,1)S(1)}, u32[]{:S(2)}, u32[]{:S(2)}) %collective-permute-start.28) | collective-permute-done | bytes 16416 | tf_op jit(solution)/shard_map/ppermute | solution.py:189
  103.6 1.0 fusion.1
  (93 shorter events, 2.2 us)
Async XLA Ops:
  1.6 1.0 copy-start.4
  2.6 9.4 %copy-start.6 = (s32[1,1,1536]{2,1,0:T(1,128)S(1)}, s32[1,1,1536]{2,1,0:T(1,128)}, u32[]{:S(2)}) copy-start(s32[1,1,1536]{2,1,0:T(1,128)} %param.13) | copy-start | bytes 18436
  2.6 9.4 %copy-start.7 = (bf16[1,1,1536]{2,1,0:T(2,128)(2,1)S(1)}, bf16[1,1,1536]{2,1,0:T(2,128)(2,1)}, u32[]{:S(2)}) copy-start(bf16[1,1,1536]{2,1,0:T(2,128)(2,1)} %param.14) | copy-start | bytes 9220
  8.8 13.4 %copy-start.2 = (bf16[1,1,1536,128]{3,2,1,0:T(8,128)(2,1)S(1)}, bf16[1,1,1536,128]{3,2,1,0:T(8,128)(2,1)}, u32[]{:S(2)}) copy-start(bf16[1,1,1536,128]{3,2,1,0:T(8,128)(2,1)} %param.9) | copy-start | bytes 1179652
  8.8 13.4 %copy-start.5 = (bf16[1,1,1536,128]{3,2,1,0:T(8,128)(2,1)S(1)}, bf16[1,1,1536,128]{3,2,1,0:T(8,128)(2,1)}, u32[]{:S(2)}) copy-start(bf16[1,1,1536,128]{3,2,1,0:T(8,128)(2,1)} %param.8) | copy-start | bytes 1179652
  8.8 4.6 %collective-permute-start = (bf16[160,128]{1,0:T(8,128)(2,1)S(1)}, bf16[160,128]{1,0:T(8,128)(2,1)S(1)}, u32[]{:S(2)}, u32[]{:S(2)}) collective-permute-start(bf16[160,128]{1,0:T(8,128)(2,1)S(1)} %get-tuple-element.56), channel_id=1, source_target_pairs={{0,1},{1,0},{2,3},{3,2},{4,5},{5,4},{6,7},{7,6},{8,9},{9,8},{10,11... | collective-permute-start | bytes 122888 | tf_op jit(solution)/shard_map/ppermute | solution.py:189
  9.4 4.5 %collective-permute-start.1 = (bf16[160,128]{1,0:T(8,128)(2,1)S(1)}, bf16[160,128]{1,0:T(8,128)(2,1)S(1)}, u32[]{:S(2)}, u32[]{:S(2)}) collective-permute-start(bf16[160,128]{1,0:T(8,128)(2,1)S(1)} %get-tuple-element.57), channel_id=1, source_target_pairs={{0,3},{1,2},{2,1},{3,0},{4,7},{5,6},{6,5},{7,4},{8,11},{9,10},{10,... | collective-permute-start | bytes 122888 | tf_op jit(solution)/shard_map/ppermute | solution.py:194
  13.9 10.0 %copy-start.3 = (bf16[256,512]{1,0:T(8,128)(2,1)S(1)}, bf16[256,512]{1,0:T(8,128)(2,1)}, u32[]{:S(2)}) copy-start(bf16[256,512]{1,0:T(8,128)(2,1)} %refs_0_.5) | copy-start | bytes 786436
  13.9 5.3 %collective-permute-start.2 = (bf16[160,128]{1,0:T(8,128)(2,1)S(1)}, bf16[160,128]{1,0:T(8,128)(2,1)S(1)}, u32[]{:S(2)}, u32[]{:S(2)}) collective-permute-start(bf16[160,128]{1,0:T(8,128)(2,1)S(1)} %get-tuple-element.70), channel_id=1, source_target_pairs={{0,4},{4,0},{8,12},{12,8},{16,20},{20,16},{24,28},{28,24},{1,5},{5... | collective-permute-start | bytes 122888 | tf_op jit(solution)/shard_map/ppermute | solution.py:189
  15.5 6.7 %collective-permute-start.3 = (bf16[160,128]{1,0:T(8,128)(2,1)S(1)}, bf16[160,128]{1,0:T(8,128)(2,1)S(1)}, u32[]{:S(2)}, u32[]{:S(2)}) collective-permute-start(bf16[160,128]{1,0:T(8,128)(2,1)S(1)} %get-tuple-element.71), channel_id=1, source_target_pairs={{0,28},{4,8},{8,4},{12,16},{16,12},{20,24},{24,20},{28,0},{1,29},{... | collective-permute-start | bytes 122888 | tf_op jit(solution)/shard_map/ppermute | solution.py:194
  23.9 3.7 %collective-permute-start.4 = (bf16[64,128]{1,0:T(8,128)(2,1)S(1)}, bf16[64,128]{1,0:T(8,128)(2,1)S(1)}, u32[]{:S(2)}, u32[]{:S(2)}) collective-permute-start(bf16[64,128]{1,0:T(8,128)(2,1)S(1)} %get-tuple-element.22), channel_id=1, source_target_pairs={{0,4},{4,0},{8,12},{12,8},{16,20},{20,16},{24,28},{28,24},{1,5},{5... | collective-permute-start | bytes 49160 | tf_op jit(solution)/shard_map/ppermute | solution.py:189
  23.9 24.5 %collective-permute-start.12 = (bf16[256,512]{1,0:T(8,128)(2,1)S(1)}, bf16[256,512]{1,0:T(8,128)(2,1)S(1)}, u32[]{:S(2)}, u32[]{:S(2)}) collective-permute-start(bf16[256,512]{1,0:T(8,128)(2,1)S(1)} %copy-done.3), channel_id=1, source_target_pairs={{0,28},{4,8},{8,4},{12,16},{16,12},{20,24},{24,20},{28,0},{1,29},{... | collective-permute-start | bytes 786440 | tf_op jit(solution)/shard_map/ppermute | solution.py:194
  27.5 20.9 %collective-permute-start.11 = (bf16[256,512]{1,0:T(8,128)(2,1)S(1)}, bf16[256,512]{1,0:T(8,128)(2,1)S(1)}, u32[]{:S(2)}, u32[]{:S(2)}) collective-permute-start(bf16[256,512]{1,0:T(8,128)(2,1)S(1)} %copy-done.3), channel_id=1, source_target_pairs={{0,4},{4,0},{8,12},{12,8},{16,20},{20,16},{24,28},{28,24},{1,5},{5... | collective-permute-start | bytes 786440 | tf_op jit(solution)/shard_map/ppermute | solution.py:189
  27.7 12.7 %collective-permute-start.9 = (bf16[2,64,128]{2,1,0:T(8,128)(2,1)S(1)}, bf16[2,64,128]{2,1,0:T(8,128)(2,1)S(1)}, u32[]{:S(2)}, u32[]{:S(2)}) collective-permute-start(bf16[2,64,128]{2,1,0:T(8,128)(2,1)S(1)} %pad_maximum_fusion.16), channel_id=1, source_target_pairs={{0,8},{4,12},{8,0},{12,4},{16,24},{20,28},{24,16},{28,20},{1,9},{5... | collective-permute-start | bytes 98312 | tf_op jit(solution)/shard_map/ppermute | solution.py:189
  31.2 2.3 %copy-start = (bf16[1,1,1536,1536]{3,2,1,0:T(8,128)(2,1)S(1)}, bf16[1,1,1536,1536]{3,2,1,0:T(8,128)(2,1)}, u32[]{:S(2)}) copy-start(bf16[1,1,1536,1536]{3,2,1,0:T(8,128)(2,1)} %param.10) | copy-start | bytes 14155780
  33.5 2.3 %copy-start.1 = (bf16[1,1,1536,1536]{3,2,1,0:T(8,128)(2,1)S(1)}, bf16[1,1,1536,1536]{3,2,1,0:T(8,128)(2,1)}, u32[]{:S(2)}) copy-start(bf16[1,1,1536,1536]{3,2,1,0:T(8,128)(2,1)} %param.11) | copy-start | bytes 14155780
  35.8 27.3 %slice-start = ((s8[4718592]{0:T(1024)(128)(4,1)}), s8[524288]{0:T(1024)(128)(4,1)S(1)}, s32[]{:S(2)}) async-start(s8[4718592]{0:T(1024)(128)(4,1)} %bitcast.46), calls=%async_computation | async-start | bytes 1048576
  38.5 24.6 %slice-start.1 = ((s8[4718592]{0:T(1024)(128)(4,1)}), s8[4194304]{0:T(1024)(128)(4,1)S(1)}, s32[]{:S(2)}) async-start(s8[4718592]{0:T(1024)(128)(4,1)} %bitcast.46), calls=%async_computation.1 | async-start | bytes 8388608
  38.7 4.1 %collective-permute-start.5 = (bf16[160,256]{1,0:T(8,128)(2,1)S(1)}, bf16[160,256]{1,0:T(8,128)(2,1)S(1)}, u32[]{:S(2)}, u32[]{:S(2)}) collective-permute-start(bf16[160,256]{1,0:T(8,128)(2,1)S(1)} %get-tuple-element.42), channel_id=1, source_target_pairs={{0,1},{1,0},{2,3},{3,2},{4,5},{5,4},{6,7},{7,6},{8,9},{9,8},{10,11... | collective-permute-start | bytes 245768 | tf_op jit(solution)/shard_map/ppermute | solution.py:189
  38.7 4.2 %collective-permute-start.6 = (bf16[160,256]{1,0:T(8,128)(2,1)S(1)}, bf16[160,256]{1,0:T(8,128)(2,1)S(1)}, u32[]{:S(2)}, u32[]{:S(2)}) collective-permute-start(bf16[160,256]{1,0:T(8,128)(2,1)S(1)} %get-tuple-element.43), channel_id=1, source_target_pairs={{0,3},{1,2},{2,1},{3,0},{4,7},{5,6},{6,5},{7,4},{8,11},{9,10},{10,... | collective-permute-start | bytes 245768 | tf_op jit(solution)/shard_map/ppermute | solution.py:194
  40.4 8.0 %collective-permute-start.10 = (bf16[4,64,128]{2,1,0:T(8,128)(2,1)S(1)}, bf16[4,64,128]{2,1,0:T(8,128)(2,1)S(1)}, u32[]{:S(2)}, u32[]{:S(2)}) collective-permute-start(bf16[4,64,128]{2,1,0:T(8,128)(2,1)S(1)} %pad_maximum_fusion.9), channel_id=1, source_target_pairs={{0,16},{4,20},{8,24},{12,28},{16,0},{20,4},{24,8},{28,12},{1,17},{... | collective-permute-start | bytes 196616 | tf_op jit(solution)/shard_map/ppermute | solution.py:189
  43.1 7.3 %collective-permute-start.7 = (bf16[160,256]{1,0:T(8,128)(2,1)S(1)}, bf16[160,256]{1,0:T(8,128)(2,1)S(1)}, u32[]{:S(2)}, u32[]{:S(2)}) collective-permute-start(bf16[160,256]{1,0:T(8,128)(2,1)S(1)} %get-tuple-element.46), channel_id=1, source_target_pairs={{0,4},{4,0},{8,12},{12,8},{16,20},{20,16},{24,28},{28,24},{1,5},{5... | collective-permute-start | bytes 245768 | tf_op jit(solution)/shard_map/ppermute | solution.py:189
  43.1 7.9 %collective-permute-start.8 = (bf16[160,256]{1,0:T(8,128)(2,1)S(1)}, bf16[160,256]{1,0:T(8,128)(2,1)S(1)}, u32[]{:S(2)}, u32[]{:S(2)}) collective-permute-start(bf16[160,256]{1,0:T(8,128)(2,1)S(1)} %get-tuple-element.47), channel_id=1, source_target_pairs={{0,28},{4,8},{8,4},{12,16},{16,12},{20,24},{24,20},{28,0},{1,29},{... | collective-permute-start | bytes 245768 | tf_op jit(solution)/shard_map/ppermute | solution.py:194
  48.8 6.7 %collective-permute-start.13 = (bf16[3,256,128]{2,1,0:T(8,128)(2,1)S(1)}, bf16[3,256,128]{2,1,0:T(8,128)(2,1)S(1)}, u32[]{:S(2)}, u32[]{:S(2)}) collective-permute-start(bf16[3,256,128]{2,1,0:T(8,128)(2,1)S(1)} %convert_element_type.62), channel_id=1, source_target_pairs={{0,2},{1,3},{2,0},{3,1},{4,6},{5,7},{6,4},{7,5},{8,10},{9,11},{10,... | collective-permute-start | bytes 589832 | tf_op jit(solution)/shard_map/ppermute | solution.py:189
  55.5 1.5 %collective-permute-start.14 = (bf16[3,256,128]{2,1,0:T(8,128)(2,1)S(1)}, bf16[3,256,128]{2,1,0:T(8,128)(2,1)S(1)}, u32[]{:S(2)}, u32[]{:S(2)}) collective-permute-start(bf16[3,256,128]{2,1,0:T(8,128)(2,1)S(1)} %fusion.7), channel_id=1, source_target_pairs={{0,1},{1,0},{2,3},{3,2},{4,5},{5,4},{6,7},{7,6},{8,9},{9,8},{10,11... | collective-permute-start | bytes 589832 | tf_op jit(solution)/shard_map/ppermute | solution.py:189
  59.3 3.7 %collective-permute-start.15 = (bf16[64,128]{1,0:T(8,128)(2,1)S(1)}, bf16[64,128]{1,0:T(8,128)(2,1)S(1)}, u32[]{:S(2)}, u32[]{:S(2)}) collective-permute-start(bf16[64,128]{1,0:T(8,128)(2,1)S(1)} %get-tuple-element.28), channel_id=1, source_target_pairs={{0,4},{4,0},{8,12},{12,8},{16,20},{20,16},{24,28},{28,24},{1,5},{5... | collective-permute-start | bytes 49160 | tf_op jit(solution)/shard_map/ppermute | solution.py:189
  63.1 4.5 %collective-permute-start.20 = (bf16[2,64,128]{2,1,0:T(8,128)(2,1)S(1)}, bf16[2,64,128]{2,1,0:T(8,128)(2,1)S(1)}, u32[]{:S(2)}, u32[]{:S(2)}) collective-permute-start(bf16[2,64,128]{2,1,0:T(8,128)(2,1)S(1)} %pad_maximum_fusion.17), channel_id=1, source_target_pairs={{0,8},{4,12},{8,0},{12,4},{16,24},{20,28},{24,16},{28,20},{1,9},{5... | collective-permute-start | bytes 98312 | tf_op jit(solution)/shard_map/ppermute | solution.py:189
  65.9 3.1 %collective-permute-start.16 = (bf16[160,128]{1,0:T(8,128)(2,1)S(1)}, bf16[160,128]{1,0:T(8,128)(2,1)S(1)}, u32[]{:S(2)}, u32[]{:S(2)}) collective-permute-start(bf16[160,128]{1,0:T(8,128)(2,1)S(1)} %get-tuple-element.52), channel_id=1, source_target_pairs={{0,1},{1,0},{2,3},{3,2},{4,5},{5,4},{6,7},{7,6},{8,9},{9,8},{10,11... | collective-permute-start | bytes 122888 | tf_op jit(solution)/shard_map/ppermute | solution.py:189
  66.0 3.5 %collective-permute-start.17 = (bf16[160,128]{1,0:T(8,128)(2,1)S(1)}, bf16[160,128]{1,0:T(8,128)(2,1)S(1)}, u32[]{:S(2)}, u32[]{:S(2)}) collective-permute-start(bf16[160,128]{1,0:T(8,128)(2,1)S(1)} %get-tuple-element.53), channel_id=1, source_target_pairs={{0,3},{1,2},{2,1},{3,0},{4,7},{5,6},{6,5},{7,4},{8,11},{9,10},{10,... | collective-permute-start | bytes 122888 | tf_op jit(solution)/shard_map/ppermute | solution.py:194
  67.6 5.9 %collective-permute-start.21 = (bf16[4,64,128]{2,1,0:T(8,128)(2,1)S(1)}, bf16[4,64,128]{2,1,0:T(8,128)(2,1)S(1)}, u32[]{:S(2)}, u32[]{:S(2)}) collective-permute-start(bf16[4,64,128]{2,1,0:T(8,128)(2,1)S(1)} %pad_maximum_fusion.10), channel_id=1, source_target_pairs={{0,16},{4,20},{8,24},{12,28},{16,0},{20,4},{24,8},{28,12},{1,17},{... | collective-permute-start | bytes 196616 | tf_op jit(solution)/shard_map/ppermute | solution.py:189
  74.0 5.7 %collective-permute-start.22 = (bf16[3,256,128]{2,1,0:T(8,128)(2,1)S(1)}, bf16[3,256,128]{2,1,0:T(8,128)(2,1)S(1)}, u32[]{:S(2)}, u32[]{:S(2)}) collective-permute-start(bf16[3,256,128]{2,1,0:T(8,128)(2,1)S(1)} %convert_element_type.67), channel_id=1, source_target_pairs={{0,2},{1,3},{2,0},{3,1},{4,6},{5,7},{6,4},{7,5},{8,10},{9,11},{10,... | collective-permute-start | bytes 589832 | tf_op jit(solution)/shard_map/ppermute | solution.py:189
  75.7 4.2 %collective-permute-start.18 = (bf16[160,128]{1,0:T(8,128)(2,1)S(1)}, bf16[160,128]{1,0:T(8,128)(2,1)S(1)}, u32[]{:S(2)}, u32[]{:S(2)}) collective-permute-start(bf16[160,128]{1,0:T(8,128)(2,1)S(1)} %get-tuple-element.60), channel_id=1, source_target_pairs={{0,4},{4,0},{8,12},{12,8},{16,20},{20,16},{24,28},{28,24},{1,5},{5... | collective-permute-start | bytes 122888 | tf_op jit(solution)/shard_map/ppermute | solution.py:189
  75.8 6.8 %collective-permute-start.19 = (bf16[160,128]{1,0:T(8,128)(2,1)S(1)}, bf16[160,128]{1,0:T(8,128)(2,1)S(1)}, u32[]{:S(2)}, u32[]{:S(2)}) collective-permute-start(bf16[160,128]{1,0:T(8,128)(2,1)S(1)} %get-tuple-element.61), channel_id=1, source_target_pairs={{0,28},{4,8},{8,4},{12,16},{16,12},{20,24},{24,20},{28,0},{1,29},{... | collective-permute-start | bytes 122888 | tf_op jit(solution)/shard_map/ppermute | solution.py:194
  79.8 2.8 %collective-permute-start.23 = (bf16[3,256,128]{2,1,0:T(8,128)(2,1)S(1)}, bf16[3,256,128]{2,1,0:T(8,128)(2,1)S(1)}, u32[]{:S(2)}, u32[]{:S(2)}) collective-permute-start(bf16[3,256,128]{2,1,0:T(8,128)(2,1)S(1)} %fusion.8), channel_id=1, source_target_pairs={{0,1},{1,0},{2,3},{3,2},{4,5},{5,4},{6,7},{7,6},{8,9},{9,8},{10,11... | collective-permute-start | bytes 589832 | tf_op jit(solution)/shard_map/ppermute | solution.py:189
  84.9 3.7 %collective-permute-start.24 = (bf16[64,128]{1,0:T(8,128)(2,1)S(1)}, bf16[64,128]{1,0:T(8,128)(2,1)S(1)}, u32[]{:S(2)}, u32[]{:S(2)}) collective-permute-start(bf16[64,128]{1,0:T(8,128)(2,1)S(1)} %get-tuple-element.34), channel_id=1, source_target_pairs={{0,4},{4,0},{8,12},{12,8},{16,20},{20,16},{24,28},{28,24},{1,5},{5... | collective-permute-start | bytes 49160 | tf_op jit(solution)/shard_map/ppermute | solution.py:189
  88.7 3.9 %collective-permute-start.25 = (bf16[2,64,128]{2,1,0:T(8,128)(2,1)S(1)}, bf16[2,64,128]{2,1,0:T(8,128)(2,1)S(1)}, u32[]{:S(2)}, u32[]{:S(2)}) collective-permute-start(bf16[2,64,128]{2,1,0:T(8,128)(2,1)S(1)} %pad_maximum_fusion.18), channel_id=1, source_target_pairs={{0,8},{4,12},{8,0},{12,4},{16,24},{20,28},{24,16},{28,20},{1,9},{5... | collective-permute-start | bytes 98312 | tf_op jit(solution)/shard_map/ppermute | solution.py:189
  92.6 5.5 %collective-permute-start.26 = (bf16[4,64,128]{2,1,0:T(8,128)(2,1)S(1)}, bf16[4,64,128]{2,1,0:T(8,128)(2,1)S(1)}, u32[]{:S(2)}, u32[]{:S(2)}) collective-permute-start(bf16[4,64,128]{2,1,0:T(8,128)(2,1)S(1)} %pad_maximum_fusion.11), channel_id=1, source_target_pairs={{0,16},{4,20},{8,24},{12,28},{16,0},{20,4},{24,8},{28,12},{1,17},{... | collective-permute-start | bytes 196616 | tf_op jit(solution)/shard_map/ppermute | solution.py:189
  98.4 4.0 %collective-permute-start.27 = (bf16[128,128]{1,0:T(8,128)(2,1)S(1)}, bf16[128,128]{1,0:T(8,128)(2,1)S(1)}, u32[]{:S(2)}, u32[]{:S(2)}) collective-permute-start(bf16[128,128]{1,0:T(8,128)(2,1)S(1)} %fusion.9), channel_id=1, source_target_pairs={{0,2},{1,3},{2,0},{3,1},{4,6},{5,7},{6,4},{7,5},{8,10},{9,11},{10,... | collective-permute-start | bytes 98312 | tf_op jit(solution)/shard_map/ppermute | solution.py:189
  102.4 1.2 %collective-permute-start.28 = (bf16[64,128]{1,0:T(8,128)(2,1)S(1)}, bf16[64,128]{1,0:T(8,128)(2,1)S(1)}, u32[]{:S(2)}, u32[]{:S(2)}) collective-permute-start(bf16[64,128]{1,0:T(8,128)(2,1)S(1)} %select_convert_fusion.1), channel_id=1, source_target_pairs={{0,1},{1,0},{2,3},{3,2},{4,5},{5,4},{6,7},{7,6},{8,9},{9,8},{10,11... | collective-permute-start | bytes 49160 | tf_op jit(solution)/shard_map/ppermute | solution.py:189

commit v6 on v5

v6 whole, which is shorter than its diff:
```python
import functools

import jax
import jax.numpy as jnp
from jax import lax
from jax.experimental import pallas as pl
from jax.experimental.pallas import tpu as pltpu
from jax.sharding import PartitionSpec as P

MODES = 64
ITERS = 3
LANES = 128

bf16 = jnp.bfloat16
f32 = jnp.float32
DIRECTIONS = ((-1, -1), (-1, 0), (-1, 1), (0, -1), (0, 1), (1, -1), (1, 0), (1, 1))
PACKED = ((4, 1), (2, 0), (7, 0), (3, 1), (0, 0), (5, 0), (6, 1), (1, 1))

vmem = pl.BlockSpec(memory_space=pltpu.VMEM)
smem = pl.BlockSpec(memory_space=pltpu.SMEM)
hbm = pl.BlockSpec(memory_space=pl.ANY)
shape_of = jax.ShapeDtypeStruct
params = pltpu.CompilerParams(vmem_limit_bytes=16 * 1024 * 1024)
large = pltpu.CompilerParams(vmem_limit_bytes=16 * 1024 * 1024)


def dot(a, b):
    return jnp.dot(a, b, preferred_element_type=f32)


def pick(face, sel_ref, flux_ref, packed_ref):
    at = 0
    for d, whole in PACKED:
        size = face if whole else face // 8
        rows = dot(sel_ref[d, :size, :], flux_ref[d * face : (d + 1) * face, :])
        packed_ref[at : at + size, :] = rows.astype(bf16)
        at += size


def load_kernel(face, chunk, ahead, u_hbm, k_hbm, s_hbm, nodes_hbm, mode_hbm, weight_ref, flux_ref, packed_ref, sel_ref, selt_ref, basis_ref, tall_ref, k_ref, s_ref, mixed, u_ref, nodes_ref, mode_ref, sems, small_sems):
    count = u_ref.shape[0] // chunk
    small = ((u_hbm, u_ref), (nodes_hbm, nodes_ref), (mode_hbm, mode_ref))
    small = [pltpu.make_async_copy(*pair, small_sems.at[i]) for i, pair in enumerate(small)]
    for copy in small:
        copy.start()
    copies = []
    for which, (source, target) in enumerate(((k_hbm, k_ref), (s_hbm, s_ref))):
        for i in range(count):
            rows = pl.ds(i * chunk, chunk)
            copies.append(pltpu.make_async_copy(source.at[rows], target.at[rows], sems.at[which, i]))
    for copy in copies[:ahead]:
        copy.start()
    modes = basis_ref.shape[0]
    slot = lax.broadcasted_iota(jnp.int32, (face, face), 0)
    mode = lax.broadcasted_iota(jnp.int32, (modes, LANES), 0)
    blocks = u_ref.shape[0] // LANES

    def prepare(step, steps):
        for d in range(8 * step // steps, 8 * (step + 1) // steps):
            chosen = (slot == nodes_ref[d : d + 1, :] - d * face).astype(f32)
            selt_ref[d] = chosen.astype(bf16)
            sel_ref[d] = chosen.T.astype(bf16)
        for i in range(blocks * step // steps, blocks * (step + 1) // steps):
            rows = pl.ds(i * LANES, LANES)
            part = jnp.where(mode == mode_ref[:, rows], weight_ref[:, rows].astype(f32), 0.0)
            basis_ref[:, rows] = part.astype(bf16)
            tall_ref[rows, :] = jnp.concatenate([part] * (LANES // modes)).T.astype(bf16)

    for copy in small:
        copy.wait()
    u = u_ref[...]
    for i in range(2 * count):
        prepare(i, 2 * count)
        copies[i].wait()
        if i + ahead < 2 * count:
            copies[i + ahead].start()
        rows = pl.ds(i % count * chunk, chunk)
        if i < count:
            mixed[rows, :] = (0.5 * u_ref[rows, :].astype(f32) + dot(k_ref[rows, :], u)).astype(bf16)
        else:
            flux_ref[rows, :] = dot(s_ref[rows, :], mixed[...]).astype(bf16)
    pick(face, sel_ref, flux_ref, packed_ref)


def load_products(trace, kernel, inverse, nodes, mode, weight):
    count, width = trace.shape
    face = nodes.shape[1]
    chunk = 256 if count % 256 == 0 else count
    return pl.pallas_call(
        functools.partial(load_kernel, face, chunk, 3),
        out_shape=[
            shape_of((count, width), bf16),
            shape_of((4 * (face + face // 8), width), bf16),
            shape_of((8, face, face), bf16),
            shape_of((8, face, face), bf16),
            shape_of((MODES, count), bf16),
            shape_of((count, LANES), bf16),
            pltpu.VMEM((count, count), bf16),
            pltpu.VMEM((count, count), bf16),
        ],
        in_specs=[hbm] * 5 + [vmem],
        out_specs=[vmem] * 8,
        scratch_shapes=[
            pltpu.VMEM((count, width), bf16),
            pltpu.VMEM((count, width), bf16),
            pltpu.VMEM(nodes.shape, jnp.int32),
            pltpu.VMEM(mode.shape, jnp.int32),
            pltpu.SemaphoreType.DMA((2, count // chunk)),
            pltpu.SemaphoreType.DMA((3,)),
        ],
        compiler_params=large,
        cost_estimate=pl.CostEstimate(
            flops=4 * count * count * 2 * LANES, bytes_accessed=4 * count * count, transcendentals=0
        ),
        name="load_products",
    )(trace, kernel, inverse, nodes, mode, weight)


def products_kernel(face, chunk, state_ref, res_ref, k_ref, s_ref, sel_ref, tall_ref, c_ref, u_ref, flux_ref, packed_ref, entering, mixed):
    count, width = u_ref.shape
    for i in range(count // chunk):
        rows = pl.ds(i * chunk, chunk)
        following = state_ref[rows, :].astype(f32) + 0.25 * res_ref[rows, :].astype(f32)
        if c_ref is not None:
            following += dot(tall_ref[rows, : c_ref.shape[0]], c_ref[...])
        u_ref[rows, :] = following.astype(bf16)
        entering[rows, :width] = following.astype(bf16)
        if c_ref is None:
            entering[rows, width:] = tall_ref[rows, :]
    u = entering[...]
    for i in range(count // chunk):
        rows = pl.ds(i * chunk, chunk)
        mixed[rows, :] = (0.5 * entering[rows, :].astype(f32) + dot(k_ref[rows, :], u)).astype(bf16)
    m = mixed[...]
    for i in range(count // chunk):
        rows = pl.ds(i * chunk, chunk)
        flux_ref[rows, :] = dot(s_ref[rows, :], m).astype(bf16)
    pick(face, sel_ref, flux_ref, packed_ref)


def products(state, residual, kernel, inverse, selector, tall, own):
    count, width = state.shape
    face = selector.shape[1]
    chunk = 256 if count % 256 == 0 else count
    wide = width + LANES if own is None else width
    operands = [state, residual, kernel, inverse, selector, tall]
    body = functools.partial(products_kernel, face, chunk)
    if own is None:
        inner = body
        body = lambda *refs: inner(*refs[:6], None, *refs[6:])
    else:
        operands.append(own)
    return pl.pallas_call(
        body,
        out_shape=[
            shape_of((count, width), bf16),
            shape_of((count, wide), bf16),
            shape_of((4 * (face + face // 8), wide), bf16),
        ],
        in_specs=[vmem] * len(operands),
        out_specs=[vmem] * 3,
        scratch_shapes=[pltpu.VMEM((count, wide), bf16), pltpu.VMEM((count, wide), bf16)],
        compiler_params=params,
        cost_estimate=pl.CostEstimate(
            flops=4 * count * count * 2 * LANES, bytes_accessed=4 * count * count, transcendentals=0
        ),
        name="products",
    )(*operands)


def arrivals(face):
    corner = face // 8
    found = {4: (0, 0), 3: (1, 0), 6: (2, 0), 1: (3, 0)}
    found |= {7: (2, face), 5: (2, face + corner), 2: (3, face), 0: (3, face + corner)}
    return [found[d] + (face if d in (1, 3, 4, 6) else corner,) for d in range(8)]


def couple_kernel(modes, selt_ref, w_ref, wrows_ref, out_ref):
    face = selt_ref.shape[1]
    lane = lax.broadcasted_iota(jnp.int32, (face, LANES), 1)
    for d, (group, at, size) in enumerate(arrivals(face)):
        theirs = dot(selt_ref[d, :, :size], wrows_ref[group, at : at + size, :])
        mine = w_ref[d * face : (d + 1) * face, :].astype(f32)
        out_ref[d, :, :face] = selt_ref[d]
        out_ref[d, :, face:] = jnp.where(lane < modes, theirs, mine).astype(bf16)


def couple(selector_t, wide, wide_rows):
    face = selector_t.shape[1]
    return pl.pallas_call(
        functools.partial(couple_kernel, MODES),
        out_shape=shape_of((8, face, face + LANES), bf16),
        in_specs=[vmem] * 3,
        out_specs=vmem,
        compiler_params=params,
        name="couple",
    )(selector_t, wide, wide_rows)


def first_update_kernel(rows_ref, flux_ref, load_ref, selt_ref, basis_ref, res_ref, rhs_ref):
    face = selt_ref.shape[1]
    for d, (group, at, size) in enumerate(arrivals(face)):
        band = slice(d * face, (d + 1) * face)
        placed = dot(selt_ref[d, :, :size], rows_ref[group, at : at + size, :])
        assembled = flux_ref[band, :].astype(f32) + placed
        res_ref[band, :] = (load_ref[band, :].astype(f32) - assembled).astype(bf16)
    rest = slice(8 * face, None)
    res_ref[rest, :] = (load_ref[rest, :].astype(f32) - flux_ref[rest, :].astype(f32)).astype(bf16)
    rhs_ref[...] = dot(basis_ref[...], res_ref[...]).astype(bf16)


def update_kernel(place, rows_ref, flux_ref, load_ref, couple_ref, basis_ref, c_ref, w_ref, res_ref, rhs_ref, own_ref, right):
    face = couple_ref.shape[1]
    modes = basis_ref.shape[0]
    own = c_ref[place[0], pl.ds(pl.multiple_of(place[1], modes), modes), :]
    own_ref[...] = own
    for d, (group, at, size) in enumerate(arrivals(face)):
        band = slice(d * face, (d + 1) * face)
        start = pl.multiple_of(place[2 * d + 3], modes)
        right[d, :size, :] = rows_ref[group, at : at + size, :]
        if size < face:
            right[d, size:face, :] = jnp.zeros((face - size, right.shape[2]), bf16)
        right[d, face : face + modes, :] = c_ref[place[2 * d + 2], pl.ds(start, modes), :]
        right[d, face + modes :, :] = own
        assembled = flux_ref[band, :].astype(f32) + dot(couple_ref[d], right[d])
        res_ref[band, :] = (load_ref[band, :].astype(f32) - assembled).astype(bf16)
    rest = slice(8 * face, None)
    assembled = flux_ref[rest, :].astype(f32) + dot(w_ref[rest, :modes], own)
    res_ref[rest, :] = (load_ref[rest, :].astype(f32) - assembled).astype(bf16)
    rhs = dot(basis_ref[...], res_ref[...]).astype(bf16)
    for i in range(rhs_ref.shape[0] // modes):
        rhs_ref[i * modes : (i + 1) * modes, :] = rhs


def settle_kernel(state_ref, res_ref, tall_ref, own_ref, out_ref, before_ref):
    res = res_ref[...]
    out_ref[...] = res
    product = dot(tall_ref[:, : own_ref.shape[0]], own_ref[...])
    before_ref[...] = state_ref[...].astype(f32) + 0.25 * res.astype(f32) + product


def settle(state, residual, tall, own):
    return pl.pallas_call(
        settle_kernel,
        out_shape=[shape_of(state.shape, bf16), shape_of(state.shape, f32)],
        in_specs=[vmem] * 4,
        out_specs=[vmem] * 2,
        compiler_params=params,
        name="settle",
    )(state, residual, tall, own)


def finish_kernel(before_ref, tall_ref, own_ref, trace_ref):
    trace_ref[...] = (before_ref[...] + dot(tall_ref[:, : own_ref.shape[0]], own_ref[...])).astype(bf16)


def finish(before, tall, own):
    return pl.pallas_call(
        finish_kernel,
        out_shape=shape_of(before.shape, bf16),
        in_specs=[vmem] * 3,
        out_specs=vmem,
        compiler_params=params,
        name="finish",
    )(before, tall, own)


def update(place, rows, flux, load, selector_t, basis, coarse, wide, coupling, copies=1):
    count, width = load.shape
    modes = basis.shape[0]
    face = selector_t.shape[1]
    outs = [shape_of((count, width), bf16), shape_of((copies * modes, width), bf16)]
    if coarse is None:
        operands = [rows, flux, load, selector_t, basis]
        return pl.pallas_call(
            first_update_kernel,
            out_shape=outs,
            in_specs=[vmem] * 5,
            out_specs=[vmem] * 2,
            compiler_params=params,
            name="first_update",
        )(*operands)
    operands = [place, rows, flux, load, coupling, basis, coarse, wide]
    return pl.pallas_call(
        update_kernel,
        out_shape=outs + [shape_of((modes, width), bf16)],
        in_specs=[smem] + [vmem] * 7,
        out_specs=[vmem] * 3,
        scratch_shapes=[pltpu.VMEM((8, face + LANES, width), bf16)],
        compiler_params=params,
        name="update",
    )(*operands)


def coarse_kernel(modes, place, pieces_ref, *refs):
    matrices, out_ref, full = refs[:-2], refs[-2], refs[-1]
    for m in range(pieces_ref.shape[0]):
        start = pl.multiple_of((place[0] ^ m) * modes, modes)
        full[pl.ds(start, modes), :] = pieces_ref[m]
    for i, matrix in enumerate(matrices):
        out_ref[i] = dot(matrix[...], full[...])


def coarse_product(place, pieces, matrices):
    count, modes, width = pieces.shape
    rows, depth = matrices[0].shape
    return pl.pallas_call(
        functools.partial(coarse_kernel, modes),
        out_shape=shape_of((len(matrices), rows, width), f32),
        in_specs=[smem] + [vmem] * (1 + len(matrices)),
        out_specs=vmem,
        scratch_shapes=[pltpu.VMEM((depth, width), bf16)],
        compiler_params=params,
        cost_estimate=pl.CostEstimate(
            flops=2 * len(matrices) * rows * depth * width,
            bytes_accessed=2 * len(matrices) * rows * depth,
            transcendentals=0,
        ),
        name="coarse_product",
    )(place, pieces, *matrices)


def swap(value, axis, bit):
    return lax.ppermute(value, axis, [(i, i ^ bit) for i in range(lax.axis_size(axis))])


def cross(value, axis):
    n = lax.axis_size(axis)
    return lax.ppermute(value, axis, [(i, (i + 1 if i % 2 else i - 1) % n) for i in range(n)])


def onward(value, axis):
    n = lax.axis_size(axis)
    ring = list(range(0, n, 2)) + list(range(n - 1, 0, -2))
    return lax.ppermute(value, axis, [(ring[i - 1], ring[i]) for i in range(n)])


def trade(forward, backward, axis):
    even = lax.axis_index(axis) % 2 == 0
    near = swap(jnp.where(even, forward, backward), axis, 1)
    far = cross(jnp.where(even, backward, forward), axis)
    return jnp.where(even, near, far), jnp.where(even, far, near)


def exchange(packed, face):
    corner = face // 8
    group = face + 2 * corner
    right, left = trade(packed[:group], packed[group : 2 * group], "col")
    six, one = packed[2 * group : 2 * group + face], packed[2 * group + face :]
    up = jnp.concatenate([six, right[face + corner :], left[face + corner :]])
    down = jnp.concatenate([one, right[face : face + corner], left[face : face + corner]])
    above, below = trade(up, down, "sub")
    return jnp.stack([right, left, above, below])


def sum_over_columns(value):
    bit = lax.axis_size("col") // 2
    while bit:
        value = value + swap(value.astype(bf16), "col", bit).astype(f32)
        bit //= 2
    return value.astype(bf16)


def share_of_sum(value):
    bit = lax.axis_size("col") // 2
    while bit:
        half = value.shape[0] // 2
        upper = (lax.axis_index("col") // bit) % 2 == 1
        low, high = value[:half], value[half:]
        got = swap(jnp.where(upper, low, high).astype(bf16), "col", bit)
        value = jnp.where(upper, high, low) + got.astype(f32)
        bit //= 2
    return value.astype(bf16)


def local(
    trace_start,
    neumann_load,
    double_layer,
    single_inverse,
    interface_nodes,
    node_mode,
    mode_weight,
    coarse_inverse,
):
    subs, cols = lax.axis_size("sub"), lax.axis_size("col")
    row, col = lax.axis_index("sub"), lax.axis_index("col")
    even_sub = row % 2 == 0
    trace = trace_start[0, 0]
    load = neumann_load[0, 0]
    width = trace.shape[1]
    interface = interface_nodes[0, 0]
    face = interface.shape[1]

    place = [jnp.zeros((), jnp.int32), col * MODES]
    for row_step, col_step in DIRECTIONS:
        source = {0: 0, 1: jnp.where(even_sub, 1, 2), -1: jnp.where(even_sub, 2, 1)}
        place += [source[row_step], jnp.clip(col + col_step, 0, cols - 1) * MODES]
    place = jnp.stack([jnp.asarray(p, jnp.int32) for p in place])
    row_place = jnp.reshape(row, (1,)).astype(jnp.int32)
    trace, place, row_place = lax.optimization_barrier((trace, place, row_place))

    flux, packed, selector, selector_t, basis, tall, kernel, inverse = load_products(
        *(
            pltpu.with_memory_space_constraint(whole, pltpu.HBM)
            for whole in (trace, double_layer[0, 0], single_inverse[0, 0], interface, node_mode[0])
        ),
        mode_weight[0],
    )
    near = swap(coarse_inverse, "sub", 1)
    packed, near = lax.optimization_barrier((packed, near))
    matrices = [coarse_inverse, near, onward(near, "sub")]
    rows = exchange(packed, face)
    state, own, coarse, wide, coupling = trace, None, None, None, None
    for iteration in range(ITERS):
        last = iteration == ITERS - 1
        residual, rhs, *own = update(
            place, rows, flux, load, selector_t, basis, coarse, wide, coupling, subs if last else 1
        )
        own = own[0] if own else None
        if last:
            residual, before = settle(state, residual, tall, own)
            gathered = lax.all_to_all(rhs, "sub", 0, 0, tiled=True)
            gathered, before = lax.optimization_barrier((gathered, before))
            gathered = gathered.reshape(subs, MODES, width)
            product = coarse_product(jnp.zeros_like(row_place), gathered, matrices[:1])
            final = share_of_sum(product[0])
            break
        got = swap(rhs, "sub", 1)
        pieces = jnp.stack([rhs, got])
        state, flux, packed = products(state, residual, kernel, inverse, selector, tall, own)
        pieces, packed, matrices = lax.optimization_barrier((pieces, packed, matrices))
        rows = exchange(packed, face)
        if iteration == 0:
            wide, wide_rows = flux[:, width:], rows[:, :, width:]
            flux, rows = flux[:, :width], rows[:, :, :width]
            coupling = couple(selector_t, wide, wide_rows)
        while pieces.shape[0] < subs:
            got = swap(pieces, "sub", pieces.shape[0])
            pieces = jnp.concatenate([pieces, got])
        coarse = sum_over_columns(coarse_product(row_place, pieces, matrices))
    trace = finish(before, tall, final)
    return trace[None, None], residual[None, None]


def solution(mesh):
    placed = (
        P("sub", "col", None, None),
        P("sub", "col", None, None),
        P("sub", "col", None, None),
        P("sub", "col", None, None),
        P("sub", "col", None, None),
        P("sub", "col", None),
        P("sub", "col", None),
        P("sub", "col"),
    )
    return jax.shard_map(
        local,
        mesh=mesh,
        in_specs=placed,
        out_specs=(P("sub", "col", None, None), P("sub", "col", None, None)),
        check_vma=False,
    )
```

time: 105 us -> 90.6 us (0.86)
  starting transfers between devices: 34.5 us -> 29 us
  local copies, waits for them, and re-layouts: 5.95 us -> 0.94 us
  other arithmetic: 3.13 us -> 0.66 us
    ppermute x7 -> x6, starting transfers between devices: 20.4 us -> 13 us  [cross(): lax.ppermute(value, axis, [(i, (i + 1 if i % 2 else i - 1) % n) for i in...]
    ppermute x22 -> x19, waiting for transfers between devices: 32.7 us -> 25.4 us  [swap(): lax.ppermute(value, axis, [(i, i ^ bit) for i in range(lax.axis_size(axis...]
    all_to_all x0 -> x1, waiting for transfers between devices: none -> 6.3 us  [local(): gathered = lax.all_to_all(rhs, 'sub', 0, 0, tiled=True)]
    unnamed x20 -> x8, local copies, waits for them, and re-layouts: 5.7 us -> 0.7 us
    all_to_all x0 -> x1, starting transfers between devices: none -> 3.37 us  [local(): gathered = lax.all_to_all(rhs, 'sub', 0, 0, tiled=True)]
    ppermute x22 -> x19, starting transfers between devices: 14.1 us -> 12.6 us  [swap(): lax.ppermute(value, axis, [(i, i ^ bit) for i in range(lax.axis_size(axis...]
    select_n x2 -> x0, other arithmetic: 1.32 us -> none  [the longest x1 1.28 us: local(): tall = jnp.where(mode[:, None] == lanes[None, :], weight[:, None], nothing)]
    ppermute x7 -> x6, waiting for transfers between devices: 7.43 us -> 8.18 us  [cross(): lax.ppermute(value, axis, [(i, (i + 1 if i % 2 else i - 1) % n) for i in...]
  transfers between devices with their start and end apart: 29 -> 27, of which waited for: 17 -> 17; matrix products, arithmetic and copies ran while one was open for 2% -> 1% of each run, Pallas kernels for 6% -> 16%
where the time goes in v6:
time: 90.6 us; the launch traced here: 90.3 us
  waiting for transfers between devices  39.9 us (44%)
  starting transfers between devices  29 us (32%)
  Pallas kernels  18.7 us (21%)
  between operations  1.14 us (1%)
  local copies, waits for them, and re-layouts  0.94 us (1%)
    ppermute x19, waiting for transfers between devices, swap(): lax.ppermute(value, axis, [(i, i ^ bit) for i in range(lax.axis_size(axis...  25.4 us
    ppermute x6, starting transfers between devices, cross(): lax.ppermute(value, axis, [(i, (i + 1 if i % 2 else i - 1) % n) for i in...  13 us
    ppermute x19, starting transfers between devices, swap(): lax.ppermute(value, axis, [(i, i ^ bit) for i in range(lax.axis_size(axis...  12.6 us
    ppermute x6, waiting for transfers between devices, cross(): lax.ppermute(value, axis, [(i, (i + 1 if i % 2 else i - 1) % n) for i in...  8.18 us
    pallas_call x1, Pallas kernels, load_products(): pl.pallas_call(functools.partial(load_kernel, face, chunk, 3), out_shape=...  6.54 us
    all_to_all x1, waiting for transfers between devices, local(): gathered = lax.all_to_all(rhs, 'sub', 0, 0, tiled=True)  6.3 us
    pallas_call x2, Pallas kernels, products(): pl.pallas_call(body, out_shape=[shape_of((count, width), bf16), shape_of(...  5.61 us
    all_to_all x1, starting transfers between devices, local(): gathered = lax.all_to_all(rhs, 'sub', 0, 0, tiled=True)  3.37 us
  transfers between devices with their start and end apart: 27, of which 17 were waited for; matrix products, arithmetic and copies ran while one was open for 1% of the time, Pallas kernels for 16%

profile of v6, /device:TPU:0, one launch (start us, length us, event | category | flops | bytes accessed | tf_op | source)
XLA Modules:
  0.0 90.3 jit_solution(13964592200270389473)
XLA Ops:
  0.6 3.0 %collective-permute-start = (bf16[256,512]{1,0:T(8,128)(2,1)}, bf16[256,512]{1,0:T(8,128)(2,1)S(1)}, u32[]{:S(2)}, u32[]{:S(2)}) collective-permute-start(bf16[256,512]{1,0:T(8,128)(2,1)} %refs_0_.2), channel_id=1, source_target_pairs={{0,4},{4,0},{8,12},{12,8},{16,20},{20,16},{24,28},{28,24},{1,5},{5... | collective-permute-start | bytes 786440 | tf_op jit(solution)/shard_map/ppermute | solution.py:324
  3.6 0.1 stack.99.place
  3.8 0.7 copy-done.3
  4.4 6.5 %load_products.1 = (bf16[1536,128]{1,0:T(8,128)(2,1)S(1)}, bf16[576,128]{1,0:T(8,128)(2,1)S(1)}, bf16[8,128,128]{2,1,0:T(8,128)(2,1)S(1)}, bf16[8,128,128]{2,1,0...) custom-call(bf16[1536,128]{1,0:T(8,128)(2,1)} %bitcast.48, ...), custom_call_target="tpu_custom_call" | custom-call | flops 2415919104 | bytes 9437184 | tf_op jit(solution)/shard_map/load_products/pallas_call | solution.py:89
  11.0 0.1 collective-permute-start.1
  11.1 1.6 %collective-permute-start.2 = (bf16[160,128]{1,0:T(8,128)(2,1)S(1)}, bf16[160,128]{1,0:T(8,128)(2,1)S(1)}, u32[]{:S(2)}, u32[]{:S(2)}) collective-permute-start(bf16[160,128]{1,0:T(8,128)(2,1)S(1)} %get-tuple-element.105), channel_id=1, source_target_pairs={{0,3},{1,2},{2,1},{3,0},{4,7},{5,6},{6,5},{7,4},{8,11},{9,10},{10,... | collective-permute-start | bytes 122888 | tf_op jit(solution)/shard_map/ppermute | solution.py:329
  12.7 1.8 %collective-permute-done.2 = bf16[160,128]{1,0:T(8,128)(2,1)S(1)} collective-permute-done((bf16[160,128]{1,0:T(8,128)(2,1)S(1)}, bf16[160,128]{1,0:T(8,128)(2,1)S(1)}, u32[]{:S(2)}, u32[]{:S(2)}) %collective-permute-start.2) | collective-permute-done | bytes 40992 | tf_op jit(solution)/shard_map/ppermute | solution.py:329
  14.6 1.0 %collective-permute-start.3 = (bf16[160,128]{1,0:T(8,128)(2,1)S(1)}, bf16[160,128]{1,0:T(8,128)(2,1)S(1)}, u32[]{:S(2)}, u32[]{:S(2)}) collective-permute-start(bf16[160,128]{1,0:T(8,128)(2,1)S(1)} %get-tuple-element.118), channel_id=1, source_target_pairs={{0,4},{4,0},{8,12},{12,8},{16,20},{20,16},{24,28},{28,24},{1,5},{5... | collective-permute-start | bytes 122888 | tf_op jit(solution)/shard_map/ppermute | solution.py:324
  15.6 4.2 %collective-permute-start.4 = (bf16[160,128]{1,0:T(8,128)(2,1)S(1)}, bf16[160,128]{1,0:T(8,128)(2,1)S(1)}, u32[]{:S(2)}, u32[]{:S(2)}) collective-permute-start(bf16[160,128]{1,0:T(8,128)(2,1)S(1)} %get-tuple-element.119), channel_id=1, source_target_pairs={{0,28},{4,8},{8,4},{12,16},{16,12},{20,24},{24,20},{28,0},{1,29},{... | collective-permute-start | bytes 122888 | tf_op jit(solution)/shard_map/ppermute | solution.py:329
  19.8 2.8 %collective-permute-done.4 = bf16[160,128]{1,0:T(8,128)(2,1)S(1)} collective-permute-done((bf16[160,128]{1,0:T(8,128)(2,1)S(1)}, bf16[160,128]{1,0:T(8,128)(2,1)S(1)}, u32[]{:S(2)}, u32[]{:S(2)}) %collective-permute-start.4) | collective-permute-done | bytes 40992 | tf_op jit(solution)/shard_map/ppermute | solution.py:329
  22.6 0.4 first_update.1
  23.1 2.7 %products.2 = (bf16[1536,128]{1,0:T(8,128)(2,1)S(1)}, bf16[1536,256]{1,0:T(8,128)(2,1)S(1)}, bf16[576,256]{1,0:T(8,128)(2,1)S(1)}) custom-call(bf16[1536,128]{1,0:T(8,128)(2,1)S(1)} %bitcast.49, bf16[1536,128]{1,0:T(8,128)(2,1)S(1)} %get-tuple-element.51.refs_1_, bf16[1536,1536]{1,0:T(8,128)(2,1)S(1)} %get-tuple-element.52.refs_2_.k_ref, ...), custom_call_target="tpu_custom_call" | custom-call | flops 2415919104 | bytes 9437184 | tf_op jit(solution)/shard_map/products/pallas_call | solution.py:153
  25.9 2.5 %collective-permute-done.5 = bf16[64,128]{1,0:T(8,128)(2,1)S(1)} collective-permute-done((bf16[64,128]{1,0:T(8,128)(2,1)S(1)}, bf16[64,128]{1,0:T(8,128)(2,1)S(1)}, u32[]{:S(2)}, u32[]{:S(2)}) %collective-permute-start.5) | collective-permute-done | bytes 16416 | tf_op jit(solution)/shard_map/ppermute | solution.py:324
  28.4 0.6 collective-permute-start.11
  29.1 1.6 %collective-permute-start.8 = (bf16[160,256]{1,0:T(8,128)(2,1)S(1)}, bf16[160,256]{1,0:T(8,128)(2,1)S(1)}, u32[]{:S(2)}, u32[]{:S(2)}) collective-permute-start(bf16[160,256]{1,0:T(8,128)(2,1)S(1)} %get-tuple-element.91), channel_id=1, source_target_pairs={{0,3},{1,2},{2,1},{3,0},{4,7},{5,6},{6,5},{7,4},{8,11},{9,10},{10,... | collective-permute-start | bytes 245768 | tf_op jit(solution)/shard_map/ppermute | solution.py:329
  30.8 1.6 %collective-permute-done.11 = bf16[2,64,128]{2,1,0:T(8,128)(2,1)S(1)} collective-permute-done((bf16[2,64,128]{2,1,0:T(8,128)(2,1)S(1)}, bf16[2,64,128]{2,1,0:T(8,128)(2,1)S(1)}, u32[]{:S(2)}, u32[]{:S(2)}) %collective-permute-start.11) | collective-permute-done | bytes 32800 | tf_op jit(solution)/shard_map/ppermute | solution.py:324
  32.4 1.0 %collective-permute-start.12 = (bf16[4,64,128]{2,1,0:T(8,128)(2,1)S(1)}, bf16[4,64,128]{2,1,0:T(8,128)(2,1)S(1)}, u32[]{:S(2)}, u32[]{:S(2)}) collective-permute-start(bf16[4,64,128]{2,1,0:T(8,128)(2,1)S(1)} %pad_maximum_fusion.7), channel_id=1, source_target_pairs={{0,16},{4,20},{8,24},{12,28},{16,0},{20,4},{24,8},{28,12},{1,17},{... | collective-permute-start | bytes 196616 | tf_op jit(solution)/shard_map/ppermute | solution.py:324
  33.5 2.3 %collective-permute-start.10 = (bf16[160,256]{1,0:T(8,128)(2,1)S(1)}, bf16[160,256]{1,0:T(8,128)(2,1)S(1)}, u32[]{:S(2)}, u32[]{:S(2)}) collective-permute-start(bf16[160,256]{1,0:T(8,128)(2,1)S(1)} %get-tuple-element.95), channel_id=1, source_target_pairs={{0,28},{4,8},{8,4},{12,16},{16,12},{20,24},{24,20},{28,0},{1,29},{... | collective-permute-start | bytes 245768 | tf_op jit(solution)/shard_map/ppermute | solution.py:329
  35.8 1.3 %collective-permute-start.9 = (bf16[160,256]{1,0:T(8,128)(2,1)S(1)}, bf16[160,256]{1,0:T(8,128)(2,1)S(1)}, u32[]{:S(2)}, u32[]{:S(2)}) collective-permute-start(bf16[160,256]{1,0:T(8,128)(2,1)S(1)} %get-tuple-element.94), channel_id=1, source_target_pairs={{0,4},{4,0},{8,12},{12,8},{16,20},{20,16},{24,28},{28,24},{1,5},{5... | collective-permute-start | bytes 245768 | tf_op jit(solution)/shard_map/ppermute | solution.py:324
  37.1 1.9 %collective-permute-done.12 = bf16[4,64,128]{2,1,0:T(8,128)(2,1)S(1)} collective-permute-done((bf16[4,64,128]{2,1,0:T(8,128)(2,1)S(1)}, bf16[4,64,128]{2,1,0:T(8,128)(2,1)S(1)}, u32[]{:S(2)}, u32[]{:S(2)}) %collective-permute-start.12) | collective-permute-done | bytes 65568 | tf_op jit(solution)/shard_map/ppermute | solution.py:324
  39.0 0.4 coarse_product.3
  39.4 1.6 %collective-permute-start.13 = (bf16[3,256,128]{2,1,0:T(8,128)(2,1)S(1)}, bf16[3,256,128]{2,1,0:T(8,128)(2,1)S(1)}, u32[]{:S(2)}, u32[]{:S(2)}) collective-permute-start(bf16[3,256,128]{2,1,0:T(8,128)(2,1)S(1)} %convert_element_type.48), channel_id=1, source_target_pairs={{0,2},{1,3},{2,0},{3,1},{4,6},{5,7},{6,4},{7,5},{8,10},{9,11},{10,... | collective-permute-start | bytes 589832 | tf_op jit(solution)/shard_map/ppermute | solution.py:324
  41.1 0.9 %collective-permute-done.9 = bf16[160,256]{1,0:T(8,128)(2,1)S(1)} collective-permute-done((bf16[160,256]{1,0:T(8,128)(2,1)S(1)}, bf16[160,256]{1,0:T(8,128)(2,1)S(1)}, u32[]{:S(2)}, u32[]{:S(2)}) %collective-permute-start.9) | collective-permute-done | bytes 81952 | tf_op jit(solution)/shard_map/ppermute | solution.py:324
  42.1 3.1 %collective-permute-done.13 = bf16[3,256,128]{2,1,0:T(8,128)(2,1)S(1)} collective-permute-done((bf16[3,256,128]{2,1,0:T(8,128)(2,1)S(1)}, bf16[3,256,128]{2,1,0:T(8,128)(2,1)S(1)}, u32[]{:S(2)}, u32[]{:S(2)}) %collective-permute-start.13) | collective-permute-done | bytes 196640 | tf_op jit(solution)/shard_map/ppermute | solution.py:324
  45.4 0.2 couple.1.couple_ref
  45.6 1.2 %collective-permute-done.14 = bf16[3,256,128]{2,1,0:T(8,128)(2,1)S(1)} collective-permute-done((bf16[3,256,128]{2,1,0:T(8,128)(2,1)S(1)}, bf16[3,256,128]{2,1,0:T(8,128)(2,1)S(1)}, u32[]{:S(2)}, u32[]{:S(2)}) %collective-permute-start.14) | collective-permute-done | bytes 196640 | tf_op jit(solution)/shard_map/ppermute | solution.py:324
  46.8 1.2 %update.2 = (bf16[1536,128]{1,0:T(8,128)(2,1)S(1)}, bf16[64,128]{1,0:T(8,128)(2,1)S(1)}, bf16[64,128]{1,0:T(8,128)(2,1)S(1)}) custom-call(s32[18]{0:T(128)S(1)} %stack.99.place, bf16[4,160,128]{2,1,0:T(8,128)(2,1)S(1)} %get-tuple-element.87.rows_ref, bf16[1536,128]{1,0:T(8,128)(2,1)S(1)} %get-tuple-element.85.flux_ref, bf16[1536,128]{1,0:T(8,128)(2,1)S(1)} %bitcast.46, ...), custom_call_target="tpu_custom_call" | custom-call | tf_op jit(solution)/shard_map/update/pallas_call | solution.py:284
  48.0 2.9 %products.3 = (bf16[1536,128]{1,0:T(8,128)(2,1)S(1)}, bf16[1536,128]{1,0:T(8,128)(2,1)S(1)}, bf16[576,128]{1,0:T(8,128)(2,1)S(1)}) custom-call(bf16[1536,128]{1,0:T(8,128)(2,1)S(1)} %get-tuple-element.66.state_ref, bf16[1536,128]{1,0:T(8,128)(2,1)S(1)} %get-tuple-element.67.res_ref, bf16[1536,1536]{1,0:T(8,128)(2,1)S(1)} %get-tuple-element.52.refs_2_.k_ref, ...), custom_call_target="tpu_custom_call" | custom-call | flops 2415919104 | bytes 9437184 | tf_op jit(solution)/shard_map/products/pallas_call | solution.py:153
  50.9 0.8 collective-permute-done.15
  51.9 1.6 %collective-permute-start.17 = (bf16[160,128]{1,0:T(8,128)(2,1)S(1)}, bf16[160,128]{1,0:T(8,128)(2,1)S(1)}, u32[]{:S(2)}, u32[]{:S(2)}) collective-permute-start(bf16[160,128]{1,0:T(8,128)(2,1)S(1)} %get-tuple-element.101), channel_id=1, source_target_pairs={{0,3},{1,2},{2,1},{3,0},{4,7},{5,6},{6,5},{7,4},{8,11},{9,10},{10,... | collective-permute-start | bytes 122888 | tf_op jit(solution)/shard_map/ppermute | solution.py:329
  53.5 2.2 %collective-permute-done.20 = bf16[2,64,128]{2,1,0:T(8,128)(2,1)S(1)} collective-permute-done((bf16[2,64,128]{2,1,0:T(8,128)(2,1)S(1)}, bf16[2,64,128]{2,1,0:T(8,128)(2,1)S(1)}, u32[]{:S(2)}, u32[]{:S(2)}) %collective-permute-start.20) | collective-permute-done | bytes 32800 | tf_op jit(solution)/shard_map/ppermute | solution.py:324
  55.8 5.2 %collective-permute-done.21 = bf16[4,64,128]{2,1,0:T(8,128)(2,1)S(1)} collective-permute-done((bf16[4,64,128]{2,1,0:T(8,128)(2,1)S(1)}, bf16[4,64,128]{2,1,0:T(8,128)(2,1)S(1)}, u32[]{:S(2)}, u32[]{:S(2)}) %collective-permute-start.21) | collective-permute-done | bytes 65568 | tf_op jit(solution)/shard_map/ppermute | solution.py:324
  61.1 0.4 coarse_product.4
  61.5 1.6 %collective-permute-start.22 = (bf16[3,256,128]{2,1,0:T(8,128)(2,1)S(1)}, bf16[3,256,128]{2,1,0:T(8,128)(2,1)S(1)}, u32[]{:S(2)}, u32[]{:S(2)}) collective-permute-start(bf16[3,256,128]{2,1,0:T(8,128)(2,1)S(1)} %convert_element_type.53), channel_id=1, source_target_pairs={{0,2},{1,3},{2,0},{3,1},{4,6},{5,7},{6,4},{7,5},{8,10},{9,11},{10,... | collective-permute-start | bytes 589832 | tf_op jit(solution)/shard_map/ppermute | solution.py:324
  63.1 1.3 %collective-permute-start.18 = (bf16[160,128]{1,0:T(8,128)(2,1)S(1)}, bf16[160,128]{1,0:T(8,128)(2,1)S(1)}, u32[]{:S(2)}, u32[]{:S(2)}) collective-permute-start(bf16[160,128]{1,0:T(8,128)(2,1)S(1)} %get-tuple-element.108), channel_id=1, source_target_pairs={{0,4},{4,0},{8,12},{12,8},{16,20},{20,16},{24,28},{28,24},{1,5},{5... | collective-permute-start | bytes 122888 | tf_op jit(solution)/shard_map/ppermute | solution.py:324
  64.4 1.7 %collective-permute-start.19 = (bf16[160,128]{1,0:T(8,128)(2,1)S(1)}, bf16[160,128]{1,0:T(8,128)(2,1)S(1)}, u32[]{:S(2)}, u32[]{:S(2)}) collective-permute-start(bf16[160,128]{1,0:T(8,128)(2,1)S(1)} %get-tuple-element.109), channel_id=1, source_target_pairs={{0,28},{4,8},{8,4},{12,16},{16,12},{20,24},{24,20},{28,0},{1,29},{... | collective-permute-start | bytes 122888 | tf_op jit(solution)/shard_map/ppermute | solution.py:329
  66.1 1.1 %collective-permute-done.22 = bf16[3,256,128]{2,1,0:T(8,128)(2,1)S(1)} collective-permute-done((bf16[3,256,128]{2,1,0:T(8,128)(2,1)S(1)}, bf16[3,256,128]{2,1,0:T(8,128)(2,1)S(1)}, u32[]{:S(2)}, u32[]{:S(2)}) %collective-permute-start.22) | collective-permute-done | bytes 196640 | tf_op jit(solution)/shard_map/ppermute | solution.py:324
  67.4 0.3 collective-permute-done.18
  67.6 3.5 %collective-permute-done.19 = bf16[160,128]{1,0:T(8,128)(2,1)S(1)} collective-permute-done((bf16[160,128]{1,0:T(8,128)(2,1)S(1)}, bf16[160,128]{1,0:T(8,128)(2,1)S(1)}, u32[]{:S(2)}, u32[]{:S(2)}) %collective-permute-start.19) | collective-permute-done | bytes 40992 | tf_op jit(solution)/shard_map/ppermute | solution.py:329
  71.3 1.8 %update.3 = (bf16[1536,128]{1,0:T(8,128)(2,1)S(1)}, bf16[512,128]{1,0:T(8,128)(2,1)}, bf16[64,128]{1,0:T(8,128)(2,1)S(1)}) custom-call(s32[18]{0:T(128)S(1)} %stack.99.place, bf16[4,160,128]{2,1,0:T(8,128)(2,1)S(1)} %pad_maximum_fusion.2.rows_ref, bf16[1536,128]{1,0:T(8,128)(2,1)S(1)} %get-tuple-element.71.flux_ref, bf16[1536,128]{1,0:T(8,128)(2,1)S(1)} %bitcast.47, ...), custom_call_target="tpu_custom_call" | custom-call | tf_op jit(solution)/shard_map/update/pallas_call | solution.py:284
  73.1 3.4 %all-to-all-start = ((bf16[8,64,128]{2,1,0:T(8,128)(2,1)}), bf16[8,64,128]{2,1,0:T(8,128)(2,1)S(1)}, u32[]{:S(2)}, u32[]{:S(2)}) async-start(bf16[8,64,128]{2,1,0:T(8,128)(2,1)} %bitcast.30), calls=%async_computation | async-start | bytes 262144 | tf_op jit(solution)/shard_map/all_to_all | solution.py:423
  76.5 0.9 %settle.1 = (bf16[1536,128]{1,0:T(8,128)(2,1)}, f32[1536,128]{1,0:T(8,128)S(1)}) custom-call(bf16[1536,128]{1,0:T(8,128)(2,1)S(1)} %get-tuple-element.77.state_ref, bf16[1536,128]{1,0:T(8,128)(2,1)S(1)} %get-tuple-element.78.res_ref, bf16[1536,128]{1,0:T(8,128)(2,1)S(1)} %get-tuple-element.55.refs_5_.tall_ref, bf16[64,128]{1,0:T(8,128)(2,1)S(1)} %get-tuple-element.79.own_ref), custom_call_target="tpu_custom_call" | custom-call | tf_op jit(solution)/shard_map/settle/pallas_call | solution.py:243
  77.5 6.3 %all-to-all-done = bf16[8,64,128]{2,1,0:T(8,128)(2,1)S(1)} async-done(((bf16[8,64,128]{2,1,0:T(8,128)(2,1)}), bf16[8,64,128]{2,1,0:T(8,128)(2,1)S(1)}, u32[]{:S(2)}, u32[]{:S(2)}) %all-to-all-start) | async-done | bytes 131104 | tf_op jit(solution)/shard_map/all_to_all | solution.py:423
  83.8 0.2 coarse_product.5
  84.0 0.6 collective-permute-start.24
  84.6 3.4 %collective-permute-done.24 = bf16[128,128]{1,0:T(8,128)(2,1)S(1)} collective-permute-done((bf16[128,128]{1,0:T(8,128)(2,1)S(1)}, bf16[128,128]{1,0:T(8,128)(2,1)S(1)}, u32[]{:S(2)}, u32[]{:S(2)}) %collective-permute-start.24) | collective-permute-done | bytes 32800 | tf_op jit(solution)/shard_map/ppermute | solution.py:324
  88.1 1.2 %collective-permute-done.25 = bf16[64,128]{1,0:T(8,128)(2,1)S(1)} collective-permute-done((bf16[64,128]{1,0:T(8,128)(2,1)S(1)}, bf16[64,128]{1,0:T(8,128)(2,1)S(1)}, u32[]{:S(2)}, u32[]{:S(2)}) %collective-permute-start.25) | collective-permute-done | bytes 16416 | tf_op jit(solution)/shard_map/ppermute | solution.py:324
  89.3 1.0 %finish.1 = bf16[1536,128]{1,0:T(8,128)(2,1)} custom-call(f32[1536,128]{1,0:T(8,128)S(1)} %get-tuple-element.81.before_ref, bf16[1536,128]{1,0:T(8,128)(2,1)S(1)} %get-tuple-element.55.refs_5_.tall_ref, bf16[64,128]{1,0:T(8,128)(2,1)S(1)} %add_convert_fusion.2.own_ref), custom_call_target="tpu_custom_call" | custom-call | tf_op jit(solution)/shard_map/finish/pallas_call | solution.py:258
  (68 shorter events, 1.5 us)
Async XLA Ops:
  0.6 10.4 %collective-permute-start = (bf16[256,512]{1,0:T(8,128)(2,1)}, bf16[256,512]{1,0:T(8,128)(2,1)S(1)}, u32[]{:S(2)}, u32[]{:S(2)}) collective-permute-start(bf16[256,512]{1,0:T(8,128)(2,1)} %refs_0_.2), channel_id=1, source_target_pairs={{0,4},{4,0},{8,12},{12,8},{16,20},{20,16},{24,28},{28,24},{1,5},{5... | collective-permute-start | bytes 786440 | tf_op jit(solution)/shard_map/ppermute | solution.py:324
  3.7 0.7 copy-start.3
  4.4 18.2 %copy-start = (bf16[1,1,1536,128]{3,2,1,0:T(8,128)(2,1)S(1)}, bf16[1,1,1536,128]{3,2,1,0:T(8,128)(2,1)}, u32[]{:S(2)}) copy-start(bf16[1,1,1536,128]{3,2,1,0:T(8,128)(2,1)} %param.9) | copy-start | bytes 1179652
  4.4 18.7 %copy-start.2 = (bf16[1,1,1536,128]{3,2,1,0:T(8,128)(2,1)S(1)}, bf16[1,1,1536,128]{3,2,1,0:T(8,128)(2,1)}, u32[]{:S(2)}) copy-start(bf16[1,1,1536,128]{3,2,1,0:T(8,128)(2,1)} %param.8) | copy-start | bytes 1179652
  11.0 1.7 %collective-permute-start.1 = (bf16[160,128]{1,0:T(8,128)(2,1)S(1)}, bf16[160,128]{1,0:T(8,128)(2,1)S(1)}, u32[]{:S(2)}, u32[]{:S(2)}) collective-permute-start(bf16[160,128]{1,0:T(8,128)(2,1)S(1)} %get-tuple-element.104), channel_id=1, source_target_pairs={{0,1},{1,0},{2,3},{3,2},{4,5},{5,4},{6,7},{7,6},{8,9},{9,8},{10,11... | collective-permute-start | bytes 122888 | tf_op jit(solution)/shard_map/ppermute | solution.py:324
  11.1 3.5 %collective-permute-start.2 = (bf16[160,128]{1,0:T(8,128)(2,1)S(1)}, bf16[160,128]{1,0:T(8,128)(2,1)S(1)}, u32[]{:S(2)}, u32[]{:S(2)}) collective-permute-start(bf16[160,128]{1,0:T(8,128)(2,1)S(1)} %get-tuple-element.105), channel_id=1, source_target_pairs={{0,3},{1,2},{2,1},{3,0},{4,7},{5,6},{6,5},{7,4},{8,11},{9,10},{10,... | collective-permute-start | bytes 122888 | tf_op jit(solution)/shard_map/ppermute | solution.py:329
  14.6 5.1 %collective-permute-start.3 = (bf16[160,128]{1,0:T(8,128)(2,1)S(1)}, bf16[160,128]{1,0:T(8,128)(2,1)S(1)}, u32[]{:S(2)}, u32[]{:S(2)}) collective-permute-start(bf16[160,128]{1,0:T(8,128)(2,1)S(1)} %get-tuple-element.118), channel_id=1, source_target_pairs={{0,4},{4,0},{8,12},{12,8},{16,20},{20,16},{24,28},{28,24},{1,5},{5... | collective-permute-start | bytes 122888 | tf_op jit(solution)/shard_map/ppermute | solution.py:324
  15.6 6.9 %collective-permute-start.4 = (bf16[160,128]{1,0:T(8,128)(2,1)S(1)}, bf16[160,128]{1,0:T(8,128)(2,1)S(1)}, u32[]{:S(2)}, u32[]{:S(2)}) collective-permute-start(bf16[160,128]{1,0:T(8,128)(2,1)S(1)} %get-tuple-element.119), channel_id=1, source_target_pairs={{0,28},{4,8},{8,4},{12,16},{16,12},{20,24},{24,20},{28,0},{1,29},{... | collective-permute-start | bytes 122888 | tf_op jit(solution)/shard_map/ppermute | solution.py:329
  19.8 8.6 %collective-permute-start.6 = (bf16[256,512]{1,0:T(8,128)(2,1)S(1)}, bf16[256,512]{1,0:T(8,128)(2,1)S(1)}, u32[]{:S(2)}, u32[]{:S(2)}) collective-permute-start(bf16[256,512]{1,0:T(8,128)(2,1)S(1)} %collective-permute-done.refs_1_), channel_id=1, source_target_pairs={{4,0},{0,8},{8,16},{16,24},{24,28},{28,20},{20,12},{12,4},{5,1},{1... | collective-permute-start | bytes 786440 | tf_op jit(solution)/shard_map/ppermute | solution.py:335
  23.0 5.4 %collective-permute-start.5 = (bf16[64,128]{1,0:T(8,128)(2,1)S(1)}, bf16[64,128]{1,0:T(8,128)(2,1)S(1)}, u32[]{:S(2)}, u32[]{:S(2)}) collective-permute-start(bf16[64,128]{1,0:T(8,128)(2,1)S(1)} %get-tuple-element.50), channel_id=1, source_target_pairs={{0,4},{4,0},{8,12},{12,8},{16,20},{20,16},{24,28},{28,24},{1,5},{5... | collective-permute-start | bytes 49160 | tf_op jit(solution)/shard_map/ppermute | solution.py:324
  23.1 15.9 %copy-start.1 = (bf16[256,512]{1,0:T(8,128)(2,1)S(1)}, bf16[256,512]{1,0:T(8,128)(2,1)}, u32[]{:S(2)}) copy-start(bf16[256,512]{1,0:T(8,128)(2,1)} %refs_0_.2) | copy-start | bytes 786436
  28.4 4.0 %collective-permute-start.11 = (bf16[2,64,128]{2,1,0:T(8,128)(2,1)S(1)}, bf16[2,64,128]{2,1,0:T(8,128)(2,1)S(1)}, u32[]{:S(2)}, u32[]{:S(2)}) collective-permute-start(bf16[2,64,128]{2,1,0:T(8,128)(2,1)S(1)} %pad_maximum_fusion.13), channel_id=1, source_target_pairs={{0,8},{4,12},{8,0},{12,4},{16,24},{20,28},{24,16},{28,20},{1,9},{5... | collective-permute-start | bytes 98312 | tf_op jit(solution)/shard_map/ppermute | solution.py:324
  29.1 4.4 %collective-permute-start.7 = (bf16[160,256]{1,0:T(8,128)(2,1)S(1)}, bf16[160,256]{1,0:T(8,128)(2,1)S(1)}, u32[]{:S(2)}, u32[]{:S(2)}) collective-permute-start(bf16[160,256]{1,0:T(8,128)(2,1)S(1)} %get-tuple-element.90), channel_id=1, source_target_pairs={{0,1},{1,0},{2,3},{3,2},{4,5},{5,4},{6,7},{7,6},{8,9},{9,8},{10,11... | collective-permute-start | bytes 245768 | tf_op jit(solution)/shard_map/ppermute | solution.py:324
  29.1 4.3 %collective-permute-start.8 = (bf16[160,256]{1,0:T(8,128)(2,1)S(1)}, bf16[160,256]{1,0:T(8,128)(2,1)S(1)}, u32[]{:S(2)}, u32[]{:S(2)}) collective-permute-start(bf16[160,256]{1,0:T(8,128)(2,1)S(1)} %get-tuple-element.91), channel_id=1, source_target_pairs={{0,3},{1,2},{2,1},{3,0},{4,7},{5,6},{6,5},{7,4},{8,11},{9,10},{10,... | collective-permute-start | bytes 245768 | tf_op jit(solution)/shard_map/ppermute | solution.py:329
  32.4 6.6 %collective-permute-start.12 = (bf16[4,64,128]{2,1,0:T(8,128)(2,1)S(1)}, bf16[4,64,128]{2,1,0:T(8,128)(2,1)S(1)}, u32[]{:S(2)}, u32[]{:S(2)}) collective-permute-start(bf16[4,64,128]{2,1,0:T(8,128)(2,1)S(1)} %pad_maximum_fusion.7), channel_id=1, source_target_pairs={{0,16},{4,20},{8,24},{12,28},{16,0},{20,4},{24,8},{28,12},{1,17},{... | collective-permute-start | bytes 196616 | tf_op jit(solution)/shard_map/ppermute | solution.py:324
  33.5 7.6 %collective-permute-start.10 = (bf16[160,256]{1,0:T(8,128)(2,1)S(1)}, bf16[160,256]{1,0:T(8,128)(2,1)S(1)}, u32[]{:S(2)}, u32[]{:S(2)}) collective-permute-start(bf16[160,256]{1,0:T(8,128)(2,1)S(1)} %get-tuple-element.95), channel_id=1, source_target_pairs={{0,28},{4,8},{8,4},{12,16},{16,12},{20,24},{24,20},{28,0},{1,29},{... | collective-permute-start | bytes 245768 | tf_op jit(solution)/shard_map/ppermute | solution.py:329
  35.8 6.2 %collective-permute-start.9 = (bf16[160,256]{1,0:T(8,128)(2,1)S(1)}, bf16[160,256]{1,0:T(8,128)(2,1)S(1)}, u32[]{:S(2)}, u32[]{:S(2)}) collective-permute-start(bf16[160,256]{1,0:T(8,128)(2,1)S(1)} %get-tuple-element.94), channel_id=1, source_target_pairs={{0,4},{4,0},{8,12},{12,8},{16,20},{20,16},{24,28},{28,24},{1,5},{5... | collective-permute-start | bytes 245768 | tf_op jit(solution)/shard_map/ppermute | solution.py:324
  39.4 5.7 %collective-permute-start.13 = (bf16[3,256,128]{2,1,0:T(8,128)(2,1)S(1)}, bf16[3,256,128]{2,1,0:T(8,128)(2,1)S(1)}, u32[]{:S(2)}, u32[]{:S(2)}) collective-permute-start(bf16[3,256,128]{2,1,0:T(8,128)(2,1)S(1)} %convert_element_type.48), channel_id=1, source_target_pairs={{0,2},{1,3},{2,0},{3,1},{4,6},{5,7},{6,4},{7,5},{8,10},{9,11},{10,... | collective-permute-start | bytes 589832 | tf_op jit(solution)/shard_map/ppermute | solution.py:324
  45.2 1.5 %collective-permute-start.14 = (bf16[3,256,128]{2,1,0:T(8,128)(2,1)S(1)}, bf16[3,256,128]{2,1,0:T(8,128)(2,1)S(1)}, u32[]{:S(2)}, u32[]{:S(2)}) collective-permute-start(bf16[3,256,128]{2,1,0:T(8,128)(2,1)S(1)} %fusion), channel_id=1, source_target_pairs={{0,1},{1,0},{2,3},{3,2},{4,5},{5,4},{6,7},{7,6},{8,9},{9,8},{10,11... | collective-permute-start | bytes 589832 | tf_op jit(solution)/shard_map/ppermute | solution.py:324
  48.0 3.8 %collective-permute-start.15 = (bf16[64,128]{1,0:T(8,128)(2,1)S(1)}, bf16[64,128]{1,0:T(8,128)(2,1)S(1)}, u32[]{:S(2)}, u32[]{:S(2)}) collective-permute-start(bf16[64,128]{1,0:T(8,128)(2,1)S(1)} %get-tuple-element.65), channel_id=1, source_target_pairs={{0,4},{4,0},{8,12},{12,8},{16,20},{20,16},{24,28},{28,24},{1,5},{5... | collective-permute-start | bytes 49160 | tf_op jit(solution)/shard_map/ppermute | solution.py:324
  51.8 3.9 %collective-permute-start.20 = (bf16[2,64,128]{2,1,0:T(8,128)(2,1)S(1)}, bf16[2,64,128]{2,1,0:T(8,128)(2,1)S(1)}, u32[]{:S(2)}, u32[]{:S(2)}) collective-permute-start(bf16[2,64,128]{2,1,0:T(8,128)(2,1)S(1)} %pad_maximum_fusion.14), channel_id=1, source_target_pairs={{0,8},{4,12},{8,0},{12,4},{16,24},{20,28},{24,16},{28,20},{1,9},{5... | collective-permute-start | bytes 98312 | tf_op jit(solution)/shard_map/ppermute | solution.py:324
  51.8 4.0 %collective-permute-start.16 = (bf16[160,128]{1,0:T(8,128)(2,1)S(1)}, bf16[160,128]{1,0:T(8,128)(2,1)S(1)}, u32[]{:S(2)}, u32[]{:S(2)}) collective-permute-start(bf16[160,128]{1,0:T(8,128)(2,1)S(1)} %get-tuple-element.100), channel_id=1, source_target_pairs={{0,1},{1,0},{2,3},{3,2},{4,5},{5,4},{6,7},{7,6},{8,9},{9,8},{10,11... | collective-permute-start | bytes 122888 | tf_op jit(solution)/shard_map/ppermute | solution.py:324
  51.9 3.9 %collective-permute-start.17 = (bf16[160,128]{1,0:T(8,128)(2,1)S(1)}, bf16[160,128]{1,0:T(8,128)(2,1)S(1)}, u32[]{:S(2)}, u32[]{:S(2)}) collective-permute-start(bf16[160,128]{1,0:T(8,128)(2,1)S(1)} %get-tuple-element.101), channel_id=1, source_target_pairs={{0,3},{1,2},{2,1},{3,0},{4,7},{5,6},{6,5},{7,4},{8,11},{9,10},{10,... | collective-permute-start | bytes 122888 | tf_op jit(solution)/shard_map/ppermute | solution.py:329
  55.7 5.4 %collective-permute-start.21 = (bf16[4,64,128]{2,1,0:T(8,128)(2,1)S(1)}, bf16[4,64,128]{2,1,0:T(8,128)(2,1)S(1)}, u32[]{:S(2)}, u32[]{:S(2)}) collective-permute-start(bf16[4,64,128]{2,1,0:T(8,128)(2,1)S(1)} %pad_maximum_fusion.8), channel_id=1, source_target_pairs={{0,16},{4,20},{8,24},{12,28},{16,0},{20,4},{24,8},{28,12},{1,17},{... | collective-permute-start | bytes 196616 | tf_op jit(solution)/shard_map/ppermute | solution.py:324
  61.5 5.7 %collective-permute-start.22 = (bf16[3,256,128]{2,1,0:T(8,128)(2,1)S(1)}, bf16[3,256,128]{2,1,0:T(8,128)(2,1)S(1)}, u32[]{:S(2)}, u32[]{:S(2)}) collective-permute-start(bf16[3,256,128]{2,1,0:T(8,128)(2,1)S(1)} %convert_element_type.53), channel_id=1, source_target_pairs={{0,2},{1,3},{2,0},{3,1},{4,6},{5,7},{6,4},{7,5},{8,10},{9,11},{10,... | collective-permute-start | bytes 589832 | tf_op jit(solution)/shard_map/ppermute | solution.py:324
  63.1 4.5 %collective-permute-start.18 = (bf16[160,128]{1,0:T(8,128)(2,1)S(1)}, bf16[160,128]{1,0:T(8,128)(2,1)S(1)}, u32[]{:S(2)}, u32[]{:S(2)}) collective-permute-start(bf16[160,128]{1,0:T(8,128)(2,1)S(1)} %get-tuple-element.108), channel_id=1, source_target_pairs={{0,4},{4,0},{8,12},{12,8},{16,20},{20,16},{24,28},{28,24},{1,5},{5... | collective-permute-start | bytes 122888 | tf_op jit(solution)/shard_map/ppermute | solution.py:324
  64.4 6.7 %collective-permute-start.19 = (bf16[160,128]{1,0:T(8,128)(2,1)S(1)}, bf16[160,128]{1,0:T(8,128)(2,1)S(1)}, u32[]{:S(2)}, u32[]{:S(2)}) collective-permute-start(bf16[160,128]{1,0:T(8,128)(2,1)S(1)} %get-tuple-element.109), channel_id=1, source_target_pairs={{0,28},{4,8},{8,4},{12,16},{16,12},{20,24},{24,20},{28,0},{1,29},{... | collective-permute-start | bytes 122888 | tf_op jit(solution)/shard_map/ppermute | solution.py:329
  67.3 3.9 %collective-permute-start.23 = (bf16[3,256,128]{2,1,0:T(8,128)(2,1)S(1)}, bf16[3,256,128]{2,1,0:T(8,128)(2,1)S(1)}, u32[]{:S(2)}, u32[]{:S(2)}) collective-permute-start(bf16[3,256,128]{2,1,0:T(8,128)(2,1)S(1)} %fusion.1), channel_id=1, source_target_pairs={{0,1},{1,0},{2,3},{3,2},{4,5},{5,4},{6,7},{7,6},{8,9},{9,8},{10,11... | collective-permute-start | bytes 589832 | tf_op jit(solution)/shard_map/ppermute | solution.py:324
  73.1 10.7 %all-to-all-start = ((bf16[8,64,128]{2,1,0:T(8,128)(2,1)}), bf16[8,64,128]{2,1,0:T(8,128)(2,1)S(1)}, u32[]{:S(2)}, u32[]{:S(2)}) async-start(bf16[8,64,128]{2,1,0:T(8,128)(2,1)} %bitcast.30), calls=%async_computation | async-start | bytes 262144 | tf_op jit(solution)/shard_map/all_to_all | solution.py:423
  84.0 4.0 %collective-permute-start.24 = (bf16[128,128]{1,0:T(8,128)(2,1)S(1)}, bf16[128,128]{1,0:T(8,128)(2,1)S(1)}, u32[]{:S(2)}, u32[]{:S(2)}) collective-permute-start(bf16[128,128]{1,0:T(8,128)(2,1)S(1)} %fusion.2), channel_id=1, source_target_pairs={{0,2},{1,3},{2,0},{3,1},{4,6},{5,7},{6,4},{7,5},{8,10},{9,11},{10,... | collective-permute-start | bytes 98312 | tf_op jit(solution)/shard_map/ppermute | solution.py:324
  88.0 1.2 %collective-permute-start.25 = (bf16[64,128]{1,0:T(8,128)(2,1)S(1)}, bf16[64,128]{1,0:T(8,128)(2,1)S(1)}, u32[]{:S(2)}, u32[]{:S(2)}) collective-permute-start(bf16[64,128]{1,0:T(8,128)(2,1)S(1)} %select_convert_fusion.1), channel_id=1, source_target_pairs={{0,1},{1,0},{2,3},{3,2},{4,5},{5,4},{6,7},{7,6},{8,9},{9,8},{10,11... | collective-permute-start | bytes 49160 | tf_op jit(solution)/shard_map/ppermute | solution.py:324

commit v7 on v6

--- a/solution.py
+++ b/solution.py
@@ -209,18 +209,25 @@
     rhs_ref[...] = dot(basis_ref[...], res_ref[...]).astype(bf16)
 
 
-def update_kernel(place, rows_ref, flux_ref, load_ref, couple_ref, basis_ref, c_ref, w_ref, res_ref, rhs_ref, own_ref, right):
+def update_kernel(half, row_ref, col_ref, rows_ref, flux_ref, load_ref, couple_ref, basis_ref, c_ref, w_ref, res_ref, rhs_ref, own_ref, right):
     face = couple_ref.shape[1]
     modes = basis_ref.shape[0]
-    own = c_ref[place[0], pl.ds(pl.multiple_of(place[1], modes), modes), :]
+    odd, col = row_ref[0] % 2, col_ref[0]
+    base = col // half * (half - 1)
+
+    def results(row_step, col_step):
+        source = (0, 1 + odd, 2 - odd)[row_step]
+        beside = jnp.clip(col + col_step, base, base + half) - base
+        return c_ref[source, pl.ds(pl.multiple_of(beside * modes, modes), modes), :]
+
+    own = results(0, 0)
     own_ref[...] = own
     for d, (group, at, size) in enumerate(arrivals(face)):
         band = slice(d * face, (d + 1) * face)
-        start = pl.multiple_of(place[2 * d + 3], modes)
         right[d, :size, :] = rows_ref[group, at : at + size, :]
         if size < face:
             right[d, size:face, :] = jnp.zeros((face - size, right.shape[2]), bf16)
-        right[d, face : face + modes, :] = c_ref[place[2 * d + 2], pl.ds(start, modes), :]
+        right[d, face : face + modes, :] = results(*DIRECTIONS[d])
         right[d, face + modes :, :] = own
         assembled = flux_ref[band, :].astype(f32) + dot(couple_ref[d], right[d])
         res_ref[band, :] = (load_ref[band, :].astype(f32) - assembled).astype(bf16)
@@ -232,40 +239,60 @@
         rhs_ref[i * modes : (i + 1) * modes, :] = rhs
 
 
-def settle_kernel(state_ref, res_ref, tall_ref, own_ref, out_ref, before_ref):
-    res = res_ref[...]
-    out_ref[...] = res
-    product = dot(tall_ref[:, : own_ref.shape[0]], own_ref[...])
-    before_ref[...] = state_ref[...].astype(f32) + 0.25 * res.astype(f32) + product
+def settle_kernel(chunk, state_ref, res_ref, tall_ref, own_ref, out_hbm, before_ref, sem):
+    copy = pltpu.make_async_copy(res_ref, out_hbm, sem)
+    copy.start()
+    for i in range(state_ref.shape[0] // chunk):
+        rows = pl.ds(i * chunk, chunk)
+        product = dot(tall_ref[rows, : own_ref.shape[0]], own_ref[...])
+        gained = state_ref[rows, :].astype(f32) + 0.25 * res_ref[rows, :].astype(f32)
+        before_ref[rows, :] = gained + product
+    copy.wait()
 
 
 def settle(state, residual, tall, own):
-    return pl.pallas_call(
-        settle_kernel,
+    count = state.shape[0]
+    return pl.pallas_call(
+        functools.partial(settle_kernel, 256 if count % 256 == 0 else count),
         out_shape=[shape_of(state.shape, bf16), shape_of(state.shape, f32)],
         in_specs=[vmem] * 4,
-        out_specs=[vmem] * 2,
+        out_specs=[hbm, vmem],
+        scratch_shapes=[pltpu.SemaphoreType.DMA],
         compiler_params=params,
         name="settle",
     )(state, residual, tall, own)
 
 
-def finish_kernel(before_ref, tall_ref, own_ref, trace_ref):
-    trace_ref[...] = (before_ref[...] + dot(tall_ref[:, : own_ref.shape[0]], own_ref[...])).astype(bf16)
+def finish_kernel(chunk, before_ref, tall_ref, own_ref, trace_hbm, trace, sems):
+    copies = []
+    for i in range(before_ref.shape[0] // chunk):
+        rows = pl.ds(i * chunk, chunk)
+        product = dot(tall_ref[rows, : own_ref.shape[0]], own_ref[...])
+        trace[rows, :] = (before_ref[rows, :] + product).astype(bf16)
+        copies.append(pltpu.make_async_copy(trace.at[rows], trace_hbm.at[rows], sems.at[i]))
+        copies[-1].start()
+    for copy in copies:
+        copy.wait()
 
 
 def finish(before, tall, own):
-    return pl.pallas_call(
-        finish_kernel,
+    count = before.shape[0]
+    chunk = 256 if count % 256 == 0 else count
+    return pl.pallas_call(
+        functools.partial(finish_kernel, chunk),
         out_shape=shape_of(before.shape, bf16),
         in_specs=[vmem] * 3,
-        out_specs=vmem,
+        out_specs=hbm,
+        scratch_shapes=[
+            pltpu.VMEM(before.shape, bf16),
+            pltpu.SemaphoreType.DMA((count // chunk,)),
+        ],
         compiler_params=params,
         name="finish",
     )(before, tall, own)
 
 
-def update(place, rows, flux, load, selector_t, basis, coarse, wide, coupling, copies=1):
+def update(place, half, rows, flux, load, selector_t, basis, coarse, wide, coupling, copies=1):
     count, width = load.shape
     modes = basis.shape[0]
     face = selector_t.shape[1]
@@ -280,11 +307,11 @@
             compiler_params=params,
             name="first_update",
         )(*operands)
-    operands = [place, rows, flux, load, coupling, basis, coarse, wide]
-    return pl.pallas_call(
-        update_kernel,
+    operands = [*place, rows, flux, load, coupling, basis, coarse, wide]
+    return pl.pallas_call(
+        functools.partial(update_kernel, half),
         out_shape=outs + [shape_of((modes, width), bf16)],
-        in_specs=[smem] + [vmem] * 7,
+        in_specs=[smem] * 2 + [vmem] * 7,
         out_specs=[vmem] * 3,
         scratch_shapes=[pltpu.VMEM((8, face + LANES, width), bf16)],
         compiler_params=params,
@@ -292,24 +319,36 @@
     )(*operands)
 
 
-def coarse_kernel(modes, place, pieces_ref, *refs):
-    matrices, out_ref, full = refs[:-2], refs[-2], refs[-1]
+def coarse_kernel(modes, half, ordered, row_ref, col_ref, pieces_ref, *refs):
+    matrices, (mine_ref, sent_ref, full, whole) = refs[:-4], refs[-4:]
     for m in range(pieces_ref.shape[0]):
-        start = pl.multiple_of((place[0] ^ m) * modes, modes)
-        full[pl.ds(start, modes), :] = pieces_ref[m]
+        block = m if ordered else row_ref[0] ^ m
+        full[pl.ds(pl.multiple_of(block * modes, modes), modes), :] = pieces_ref[m]
+    count = mine_ref.shape[1]
+    upper = col_ref[0] // half
+    mine = pl.multiple_of(upper * (2 * half * modes - count), modes)
+    sent = pl.multiple_of((1 - upper) * (2 * half * modes - count), modes)
     for i, matrix in enumerate(matrices):
-        out_ref[i] = dot(matrix[...], full[...])
-
-
-def coarse_product(place, pieces, matrices):
-    count, modes, width = pieces.shape
+        whole[i] = dot(matrix[...], full[...])
+        mine_ref[i] = whole[i, pl.ds(mine, count), :]
+        sent_ref[i] = whole[i, pl.ds(sent, count), :].astype(bf16)
+
+
+def coarse_product(place, half, pieces, matrices, count, ordered=False):
+    many, modes, width = pieces.shape
     rows, depth = matrices[0].shape
     return pl.pallas_call(
-        functools.partial(coarse_kernel, modes),
-        out_shape=shape_of((len(matrices), rows, width), f32),
-        in_specs=[smem] + [vmem] * (1 + len(matrices)),
-        out_specs=vmem,
-        scratch_shapes=[pltpu.VMEM((depth, width), bf16)],
+        functools.partial(coarse_kernel, modes, half, ordered),
+        out_shape=[
+            shape_of((len(matrices), count, width), f32),
+            shape_of((len(matrices), count, width), bf16),
+        ],
+        in_specs=[smem] * 2 + [vmem] * (1 + len(matrices)),
+        out_specs=[vmem] * 2,
+        scratch_shapes=[
+            pltpu.VMEM((depth, width), bf16),
+            pltpu.VMEM((len(matrices), rows, width), f32),
+        ],
         compiler_params=params,
         cost_estimate=pl.CostEstimate(
             flops=2 * len(matrices) * rows * depth * width,
@@ -317,16 +356,28 @@
             transcendentals=0,
         ),
         name="coarse_product",
-    )(place, pieces, *matrices)
-
-
-def swap(value, axis, bit):
-    return lax.ppermute(value, axis, [(i, i ^ bit) for i in range(lax.axis_size(axis))])
+    )(*place, pieces, *matrices)
+
+
+def swap(value, axis, mask):
+    return lax.ppermute(value, axis, [(i, i ^ mask) for i in range(lax.axis_size(axis))])
 
 
 def cross(value, axis):
-    n = lax.axis_size(axis)
-    return lax.ppermute(value, axis, [(i, (i + 1 if i % 2 else i - 1) % n) for i in range(n)])
+    subs, cols = lax.axis_size("sub"), lax.axis_size("col")
+    pairs = []
+    for sub in range(subs):
+        for col in range(cols):
+            to = [sub, col]
+            k = 0 if axis == "sub" else 1
+            n = (subs, cols)[k]
+            near = to[k] + 1 if to[k] % 2 else to[k] - 1
+            if 0 <= near < n or n <= 4:
+                to[k] = near % n
+            else:
+                to[1 - k] ^= 1
+            pairs.append((sub * cols + col, to[0] * cols + to[1]))
+    return lax.ppermute(value, ("sub", "col"), pairs)
 
 
 def onward(value, axis):
@@ -353,24 +404,27 @@
     return jnp.stack([right, left, above, below])
 
 
-def sum_over_columns(value):
+def sum_over_columns(value, sent):
     bit = lax.axis_size("col") // 2
     while bit:
-        value = value + swap(value.astype(bf16), "col", bit).astype(f32)
+        value = value + swap(sent, "col", bit).astype(f32)
+        sent = value.astype(bf16)
         bit //= 2
-    return value.astype(bf16)
-
-
-def share_of_sum(value):
+    return sent
+
+
+def share_of_sum(value, sent):
     bit = lax.axis_size("col") // 2
-    while bit:
+    while True:
+        value = value + swap(sent, "col", bit | 1).astype(f32)
+        bit //= 2
+        if not bit:
+            return value.astype(bf16)
         half = value.shape[0] // 2
         upper = (lax.axis_index("col") // bit) % 2 == 1
         low, high = value[:half], value[half:]
-        got = swap(jnp.where(upper, low, high).astype(bf16), "col", bit)
-        value = jnp.where(upper, high, low) + got.astype(f32)
-        bit //= 2
-    return value.astype(bf16)
+        sent = jnp.where(upper, low, high).astype(bf16)
+        value = jnp.where(upper, high, low)
 
 
 def local(
@@ -385,20 +439,15 @@
 ):
     subs, cols = lax.axis_size("sub"), lax.axis_size("col")
     row, col = lax.axis_index("sub"), lax.axis_index("col")
-    even_sub = row % 2 == 0
     trace = trace_start[0, 0]
     load = neumann_load[0, 0]
     width = trace.shape[1]
     interface = interface_nodes[0, 0]
     face = interface.shape[1]
 
-    place = [jnp.zeros((), jnp.int32), col * MODES]
-    for row_step, col_step in DIRECTIONS:
-        source = {0: 0, 1: jnp.where(even_sub, 1, 2), -1: jnp.where(even_sub, 2, 1)}
-        place += [source[row_step], jnp.clip(col + col_step, 0, cols - 1) * MODES]
-    place = jnp.stack([jnp.asarray(p, jnp.int32) for p in place])
-    row_place = jnp.reshape(row, (1,)).astype(jnp.int32)
-    trace, place, row_place = lax.optimization_barrier((trace, place, row_place))
+    half = cols // 2
+    place = [jnp.reshape(index, (1,)).astype(jnp.int32) for index in (row, col)]
+    trace, place = lax.optimization_barrier((trace, place))
 
     flux, packed, selector, selector_t, basis, tall, kernel, inverse = load_products(
         *(
@@ -415,7 +464,7 @@
     for iteration in range(ITERS):
         last = iteration == ITERS - 1
         residual, rhs, *own = update(
-            place, rows, flux, load, selector_t, basis, coarse, wide, coupling, subs if last else 1
+            place, half, rows, flux, load, selector_t, basis, coarse, wide, coupling, subs if last else 1
         )
         own = own[0] if own else None
         if last:
@@ -423,8 +472,10 @@
             gathered = lax.all_to_all(rhs, "sub", 0, 0, tiled=True)
             gathered, before = lax.optimization_barrier((gathered, before))
             gathered = gathered.reshape(subs, MODES, width)
-            product = coarse_product(jnp.zeros_like(row_place), gathered, matrices[:1])
-            final = share_of_sum(product[0])
+            value, sent = coarse_product(
+                place, half, gathered, matrices[:1], half * MODES, ordered=True
+            )
+            final = share_of_sum(value[0], sent[0])
             break
         got = swap(rhs, "sub", 1)
         pieces = jnp.stack([rhs, got])
@@ -438,7 +489,7 @@
         while pieces.shape[0] < subs:
             got = swap(pieces, "sub", pieces.shape[0])
             pieces = jnp.concatenate([pieces, got])
-        coarse = sum_over_columns(coarse_product(row_place, pieces, matrices))
+        coarse = sum_over_columns(*coarse_product(place, half, pieces, matrices, (half + 1) * MODES))
     trace = finish(before, tall, final)
     return trace[None, None], residual[None, None]
 

time: 90.6 us -> 84.4 us (0.932)
  waiting for transfers between devices: 39.9 us -> 27.8 us
  starting transfers between devices: 29 us -> 36.4 us
  Pallas kernels: 18.7 us -> 17.3 us
    ppermute x25, waiting for transfers between devices: 33.6 us -> 21.2 us  [the longest x19 19.3 us: swap(): lax.ppermute(value, axis, [(i, i ^ mask) for i in range(lax.axis_size(axi...]
    all_to_all x1, starting transfers between devices: 3.37 us -> 6.16 us  [local(): gathered = lax.all_to_all(rhs, 'sub', 0, 0, tiled=True)]
    ppermute x25, starting transfers between devices: 25.6 us -> 27.9 us  [the longest x19 22.9 us: swap(): lax.ppermute(value, axis, [(i, i ^ mask) for i in range(lax.axis_size(axi...]
    ppermute x1, starting transfers between devices: 0.01 us -> 2.32 us  [onward(): return lax.ppermute(value, axis, [(ring[i - 1], ring[i]) for i in range(n)])]
    pallas_call x7, Pallas kernels: 5.88 us -> 4.57 us  [the longest x2 1.87 us: update(): pl.pallas_call(functools.partial(update_kernel, half), out_shape=outs + [...]
  transfers between devices with their start and end apart: 27 -> 27, of which waited for: 17 -> 16; matrix products, arithmetic and copies ran while one was open for 1% -> 1% of each run, Pallas kernels for 16% -> 17%
where the time goes in v7:
time: 84.4 us; the launch traced here: 84.1 us
  starting transfers between devices  36.4 us (43%)
  waiting for transfers between devices  27.8 us (33%)
  Pallas kernels  17.3 us (20%)
  between operations  1.16 us (1%)
  local copies, waits for them, and re-layouts  0.85 us (1%)
    ppermute x19, starting transfers between devices, swap(): lax.ppermute(value, axis, [(i, i ^ mask) for i in range(lax.axis_size(axi...  22.9 us
    ppermute x19, waiting for transfers between devices, swap(): lax.ppermute(value, axis, [(i, i ^ mask) for i in range(lax.axis_size(axi...  19.3 us
    all_to_all x1, waiting for transfers between devices, local(): gathered = lax.all_to_all(rhs, 'sub', 0, 0, tiled=True)  6.58 us
    pallas_call x1, Pallas kernels, load_products(): pl.pallas_call(functools.partial(load_kernel, face, chunk, 3), out_shape=...  6.53 us
    all_to_all x1, starting transfers between devices, local(): gathered = lax.all_to_all(rhs, 'sub', 0, 0, tiled=True)  6.16 us
    pallas_call x2, Pallas kernels, products(): pl.pallas_call(body, out_shape=[shape_of((count, width), bf16), shape_of(...  5.61 us
    ppermute x6, starting transfers between devices, cross(): return lax.ppermute(value, ('sub', 'col'), pairs)  5.07 us
    ppermute x1, starting transfers between devices, onward(): return lax.ppermute(value, axis, [(ring[i - 1], ring[i]) for i in range(n)])  2.32 us
  transfers between devices with their start and end apart: 27, of which 16 were waited for; matrix products, arithmetic and copies ran while one was open for 1% of the time, Pallas kernels for 17%

profile of v7, /device:TPU:0, one launch (start us, length us, event | category | flops | bytes accessed | tf_op | source)
XLA Modules:
  0.0 84.1 jit_solution(18095712748321228950)
XLA Ops:
  0.6 3.0 %collective-permute-start = (bf16[256,512]{1,0:T(8,128)(2,1)}, bf16[256,512]{1,0:T(8,128)(2,1)S(1)}, u32[]{:S(2)}, u32[]{:S(2)}) collective-permute-start(bf16[256,512]{1,0:T(8,128)(2,1)} %refs_0_.2), channel_id=1, source_target_pairs={{0,4},{4,0},{8,12},{12,8},{16,20},{20,16},{24,28},{28,24},{1,5},{5... | collective-permute-start | bytes 786440 | tf_op jit(solution)/shard_map/ppermute | solution.py:363
  3.6 0.7 copy-done.3
  4.3 6.5 %load_products.1 = (bf16[1536,128]{1,0:T(8,128)(2,1)S(1)}, bf16[576,128]{1,0:T(8,128)(2,1)S(1)}, bf16[8,128,128]{2,1,0:T(8,128)(2,1)S(1)}, bf16[8,128,128]{2,1,0...) custom-call(bf16[1536,128]{1,0:T(8,128)(2,1)} %bitcast.42, ...), custom_call_target="tpu_custom_call" | custom-call | flops 2415919104 | bytes 9437184 | tf_op jit(solution)/shard_map/load_products/pallas_call | solution.py:89
  11.0 1.6 %collective-permute-start.2 = (bf16[160,128]{1,0:T(8,128)(2,1)S(1)}, bf16[160,128]{1,0:T(8,128)(2,1)S(1)}, u32[]{:S(2)}, u32[]{:S(2)}) collective-permute-start(bf16[160,128]{1,0:T(8,128)(2,1)S(1)} %get-tuple-element.117), channel_id=1, source_target_pairs={{0,3},{1,2},{2,1},{3,0},{4,7},{5,6},{6,5},{7,4},{8,11},{9,10},{10,... | collective-permute-start | bytes 122888 | tf_op jit(solution)/shard_map/ppermute | solution.py:380
  12.6 1.8 %collective-permute-done.2 = bf16[160,128]{1,0:T(8,128)(2,1)S(1)} collective-permute-done((bf16[160,128]{1,0:T(8,128)(2,1)S(1)}, bf16[160,128]{1,0:T(8,128)(2,1)S(1)}, u32[]{:S(2)}, u32[]{:S(2)}) %collective-permute-start.2) | collective-permute-done | bytes 40992 | tf_op jit(solution)/shard_map/ppermute | solution.py:380
  14.5 1.1 %collective-permute-start.3 = (bf16[160,128]{1,0:T(8,128)(2,1)S(1)}, bf16[160,128]{1,0:T(8,128)(2,1)S(1)}, u32[]{:S(2)}, u32[]{:S(2)}) collective-permute-start(bf16[160,128]{1,0:T(8,128)(2,1)S(1)} %get-tuple-element.130), channel_id=1, source_target_pairs={{0,4},{4,0},{8,12},{12,8},{16,20},{20,16},{24,28},{28,24},{1,5},{5... | collective-permute-start | bytes 122888 | tf_op jit(solution)/shard_map/ppermute | solution.py:363
  15.6 0.2 collective-permute-start.4
  15.8 2.3 %collective-permute-start.6 = (bf16[256,512]{1,0:T(8,128)(2,1)S(1)}, bf16[256,512]{1,0:T(8,128)(2,1)S(1)}, u32[]{:S(2)}, u32[]{:S(2)}) collective-permute-start(bf16[256,512]{1,0:T(8,128)(2,1)S(1)} %collective-permute-done.refs_1_), channel_id=1, source_target_pairs={{4,0},{0,8},{8,16},{16,24},{24,28},{28,20},{20,12},{12,4},{5,1},{1... | collective-permute-start | bytes 786440 | tf_op jit(solution)/shard_map/ppermute | solution.py:386
  18.1 0.5 collective-permute-done.3
  18.7 0.4 first_update.1
  19.1 3.0 %collective-permute-start.5 = (bf16[64,128]{1,0:T(8,128)(2,1)S(1)}, bf16[64,128]{1,0:T(8,128)(2,1)S(1)}, u32[]{:S(2)}, u32[]{:S(2)}) collective-permute-start(bf16[64,128]{1,0:T(8,128)(2,1)S(1)} %get-tuple-element.57), channel_id=1, source_target_pairs={{0,4},{4,0},{8,12},{12,8},{16,20},{20,16},{24,28},{28,24},{1,5},{5... | collective-permute-start | bytes 49160 | tf_op jit(solution)/shard_map/ppermute | solution.py:363
  22.1 2.7 %products.2 = (bf16[1536,128]{1,0:T(8,128)(2,1)S(1)}, bf16[1536,256]{1,0:T(8,128)(2,1)S(1)}, bf16[576,256]{1,0:T(8,128)(2,1)S(1)}) custom-call(bf16[1536,128]{1,0:T(8,128)(2,1)S(1)} %bitcast.43, bf16[1536,128]{1,0:T(8,128)(2,1)S(1)} %get-tuple-element.58.refs_1_, bf16[1536,1536]{1,0:T(8,128)(2,1)S(1)} %get-tuple-element.59.refs_2_.k_ref, ...), custom_call_target="tpu_custom_call" | custom-call | flops 2415919104 | bytes 9437184 | tf_op jit(solution)/shard_map/products/pallas_call | solution.py:153
  24.9 0.5 collective-permute-done.5
  25.4 1.2 %collective-permute-start.11 = (bf16[2,64,128]{2,1,0:T(8,128)(2,1)S(1)}, bf16[2,64,128]{2,1,0:T(8,128)(2,1)S(1)}, u32[]{:S(2)}, u32[]{:S(2)}) collective-permute-start(bf16[2,64,128]{2,1,0:T(8,128)(2,1)S(1)} %pad_maximum_fusion.13), channel_id=1, source_target_pairs={{0,8},{4,12},{8,0},{12,4},{16,24},{20,28},{24,16},{28,20},{1,9},{5... | collective-permute-start | bytes 98312 | tf_op jit(solution)/shard_map/ppermute | solution.py:363
  26.6 0.1 collective-permute-start.7
  26.7 1.6 %collective-permute-start.8 = (bf16[160,256]{1,0:T(8,128)(2,1)S(1)}, bf16[160,256]{1,0:T(8,128)(2,1)S(1)}, u32[]{:S(2)}, u32[]{:S(2)}) collective-permute-start(bf16[160,256]{1,0:T(8,128)(2,1)S(1)} %get-tuple-element.103), channel_id=1, source_target_pairs={{0,3},{1,2},{2,1},{3,0},{4,7},{5,6},{6,5},{7,4},{8,11},{9,10},{10,... | collective-permute-start | bytes 245768 | tf_op jit(solution)/shard_map/ppermute | solution.py:380
  28.3 1.1 %collective-permute-done.11 = bf16[2,64,128]{2,1,0:T(8,128)(2,1)S(1)} collective-permute-done((bf16[2,64,128]{2,1,0:T(8,128)(2,1)S(1)}, bf16[2,64,128]{2,1,0:T(8,128)(2,1)S(1)}, u32[]{:S(2)}, u32[]{:S(2)}) %collective-permute-start.11) | collective-permute-done | bytes 32800 | tf_op jit(solution)/shard_map/ppermute | solution.py:363
  29.4 2.2 %collective-permute-start.12 = (bf16[4,64,128]{2,1,0:T(8,128)(2,1)S(1)}, bf16[4,64,128]{2,1,0:T(8,128)(2,1)S(1)}, u32[]{:S(2)}, u32[]{:S(2)}) collective-permute-start(bf16[4,64,128]{2,1,0:T(8,128)(2,1)S(1)} %pad_maximum_fusion.7), channel_id=1, source_target_pairs={{0,16},{4,20},{8,24},{12,28},{16,0},{20,4},{24,8},{28,12},{1,17},{... | collective-permute-start | bytes 196616 | tf_op jit(solution)/shard_map/ppermute | solution.py:363
  31.7 1.9 %collective-permute-start.9 = (bf16[160,256]{1,0:T(8,128)(2,1)S(1)}, bf16[160,256]{1,0:T(8,128)(2,1)S(1)}, u32[]{:S(2)}, u32[]{:S(2)}) collective-permute-start(bf16[160,256]{1,0:T(8,128)(2,1)S(1)} %get-tuple-element.106), channel_id=1, source_target_pairs={{0,4},{4,0},{8,12},{12,8},{16,20},{20,16},{24,28},{28,24},{1,5},{5... | collective-permute-start | bytes 245768 | tf_op jit(solution)/shard_map/ppermute | solution.py:363
  33.6 1.7 %collective-permute-done.12 = bf16[4,64,128]{2,1,0:T(8,128)(2,1)S(1)} collective-permute-done((bf16[4,64,128]{2,1,0:T(8,128)(2,1)S(1)}, bf16[4,64,128]{2,1,0:T(8,128)(2,1)S(1)}, u32[]{:S(2)}, u32[]{:S(2)}) %collective-permute-start.12) | collective-permute-done | bytes 65568 | tf_op jit(solution)/shard_map/ppermute | solution.py:363
  35.3 0.4 coarse_product.3
  35.7 1.6 %collective-permute-start.13 = (bf16[3,192,128]{2,1,0:T(8,128)(2,1)S(1)}, bf16[3,192,128]{2,1,0:T(8,128)(2,1)S(1)}, u32[]{:S(2)}, u32[]{:S(2)}) collective-permute-start(bf16[3,192,128]{2,1,0:T(8,128)(2,1)S(1)} %get-tuple-element.72), channel_id=1, source_target_pairs={{0,2},{1,3},{2,0},{3,1},{4,6},{5,7},{6,4},{7,5},{8,10},{9,11},{10,... | collective-permute-start | bytes 442376 | tf_op jit(solution)/shard_map/ppermute | solution.py:363
  37.4 3.5 %collective-permute-done.13 = bf16[3,192,128]{2,1,0:T(8,128)(2,1)S(1)} collective-permute-done((bf16[3,192,128]{2,1,0:T(8,128)(2,1)S(1)}, bf16[3,192,128]{2,1,0:T(8,128)(2,1)S(1)}, u32[]{:S(2)}, u32[]{:S(2)}) %collective-permute-start.13) | collective-permute-done | bytes 147488 | tf_op jit(solution)/shard_map/ppermute | solution.py:363
  41.1 0.2 couple.1.couple_ref
  41.3 1.1 %collective-permute-done.14 = bf16[3,192,128]{2,1,0:T(8,128)(2,1)S(1)} collective-permute-done((bf16[3,192,128]{2,1,0:T(8,128)(2,1)S(1)}, bf16[3,192,128]{2,1,0:T(8,128)(2,1)S(1)}, u32[]{:S(2)}, u32[]{:S(2)}) %collective-permute-start.14) | collective-permute-done | bytes 147488 | tf_op jit(solution)/shard_map/ppermute | solution.py:363
  42.5 0.6 update.2
  43.1 0.7 collective-permute-start.15
  43.8 2.9 %products.3 = (bf16[1536,128]{1,0:T(8,128)(2,1)S(1)}, bf16[1536,128]{1,0:T(8,128)(2,1)S(1)}, bf16[576,128]{1,0:T(8,128)(2,1)S(1)}) custom-call(bf16[1536,128]{1,0:T(8,128)(2,1)S(1)} %get-tuple-element.74.state_ref, bf16[1536,128]{1,0:T(8,128)(2,1)S(1)} %get-tuple-element.75.res_ref, bf16[1536,1536]{1,0:T(8,128)(2,1)S(1)} %get-tuple-element.59.refs_2_.k_ref, ...), custom_call_target="tpu_custom_call" | custom-call | flops 2415919104 | bytes 9437184 | tf_op jit(solution)/shard_map/products/pallas_call | solution.py:153
  46.7 0.2 collective-permute-done.15
  46.9 1.5 %collective-permute-start.20 = (bf16[2,64,128]{2,1,0:T(8,128)(2,1)S(1)}, bf16[2,64,128]{2,1,0:T(8,128)(2,1)S(1)}, u32[]{:S(2)}, u32[]{:S(2)}) collective-permute-start(bf16[2,64,128]{2,1,0:T(8,128)(2,1)S(1)} %pad_maximum_fusion.14), channel_id=1, source_target_pairs={{0,8},{4,12},{8,0},{12,4},{16,24},{20,28},{24,16},{28,20},{1,9},{5... | collective-permute-start | bytes 98312 | tf_op jit(solution)/shard_map/ppermute | solution.py:363
  48.4 1.6 %collective-permute-start.17 = (bf16[160,128]{1,0:T(8,128)(2,1)S(1)}, bf16[160,128]{1,0:T(8,128)(2,1)S(1)}, u32[]{:S(2)}, u32[]{:S(2)}) collective-permute-start(bf16[160,128]{1,0:T(8,128)(2,1)S(1)} %get-tuple-element.113), channel_id=1, source_target_pairs={{0,3},{1,2},{2,1},{3,0},{4,7},{5,6},{6,5},{7,4},{8,11},{9,10},{10,... | collective-permute-start | bytes 122888 | tf_op jit(solution)/shard_map/ppermute | solution.py:380
  50.0 0.9 %collective-permute-done.20 = bf16[2,64,128]{2,1,0:T(8,128)(2,1)S(1)} collective-permute-done((bf16[2,64,128]{2,1,0:T(8,128)(2,1)S(1)}, bf16[2,64,128]{2,1,0:T(8,128)(2,1)S(1)}, u32[]{:S(2)}, u32[]{:S(2)}) %collective-permute-start.20) | collective-permute-done | bytes 32800 | tf_op jit(solution)/shard_map/ppermute | solution.py:363
  50.9 2.7 %collective-permute-start.21 = (bf16[4,64,128]{2,1,0:T(8,128)(2,1)S(1)}, bf16[4,64,128]{2,1,0:T(8,128)(2,1)S(1)}, u32[]{:S(2)}, u32[]{:S(2)}) collective-permute-start(bf16[4,64,128]{2,1,0:T(8,128)(2,1)S(1)} %pad_maximum_fusion.8), channel_id=1, source_target_pairs={{0,16},{4,20},{8,24},{12,28},{16,0},{20,4},{24,8},{28,12},{1,17},{... | collective-permute-start | bytes 196616 | tf_op jit(solution)/shard_map/ppermute | solution.py:363
  53.7 2.5 %collective-permute-done.21 = bf16[4,64,128]{2,1,0:T(8,128)(2,1)S(1)} collective-permute-done((bf16[4,64,128]{2,1,0:T(8,128)(2,1)S(1)}, bf16[4,64,128]{2,1,0:T(8,128)(2,1)S(1)}, u32[]{:S(2)}, u32[]{:S(2)}) %collective-permute-start.21) | collective-permute-done | bytes 65568 | tf_op jit(solution)/shard_map/ppermute | solution.py:363
  56.1 0.4 coarse_product.4
  56.5 1.6 %collective-permute-start.22 = (bf16[3,192,128]{2,1,0:T(8,128)(2,1)S(1)}, bf16[3,192,128]{2,1,0:T(8,128)(2,1)S(1)}, u32[]{:S(2)}, u32[]{:S(2)}) collective-permute-start(bf16[3,192,128]{2,1,0:T(8,128)(2,1)S(1)} %get-tuple-element.85), channel_id=1, source_target_pairs={{0,2},{1,3},{2,0},{3,1},{4,6},{5,7},{6,4},{7,5},{8,10},{9,11},{10,... | collective-permute-start | bytes 442376 | tf_op jit(solution)/shard_map/ppermute | solution.py:363
  58.1 2.0 %collective-permute-start.18 = (bf16[160,128]{1,0:T(8,128)(2,1)S(1)}, bf16[160,128]{1,0:T(8,128)(2,1)S(1)}, u32[]{:S(2)}, u32[]{:S(2)}) collective-permute-start(bf16[160,128]{1,0:T(8,128)(2,1)S(1)} %get-tuple-element.120), channel_id=1, source_target_pairs={{0,4},{4,0},{8,12},{12,8},{16,20},{20,16},{24,28},{28,24},{1,5},{5... | collective-permute-start | bytes 122888 | tf_op jit(solution)/shard_map/ppermute | solution.py:363
  60.1 1.6 %collective-permute-done.22 = bf16[3,192,128]{2,1,0:T(8,128)(2,1)S(1)} collective-permute-done((bf16[3,192,128]{2,1,0:T(8,128)(2,1)S(1)}, bf16[3,192,128]{2,1,0:T(8,128)(2,1)S(1)}, u32[]{:S(2)}, u32[]{:S(2)}) %collective-permute-start.22) | collective-permute-done | bytes 147488 | tf_op jit(solution)/shard_map/ppermute | solution.py:363
  61.9 0.4 collective-permute-done.18
  62.3 1.0 %collective-permute-done.23 = bf16[3,192,128]{2,1,0:T(8,128)(2,1)S(1)} collective-permute-done((bf16[3,192,128]{2,1,0:T(8,128)(2,1)S(1)}, bf16[3,192,128]{2,1,0:T(8,128)(2,1)S(1)}, u32[]{:S(2)}, u32[]{:S(2)}) %collective-permute-start.23) | collective-permute-done | bytes 147488 | tf_op jit(solution)/shard_map/ppermute | solution.py:363
  63.3 1.3 %update.3 = (bf16[1536,128]{1,0:T(8,128)(2,1)S(1)}, bf16[512,128]{1,0:T(8,128)(2,1)}, bf16[64,128]{1,0:T(8,128)(2,1)S(1)}) custom-call(s32[1]{0:T(128)} %bitcast.1.row_ref, s32[1]{0:T(128)} %bitcast.2.col_ref, bf16[4,160,128]{2,1,0:T(8,128)(2,1)S(1)} %pad_maximum_fusion.2.rows_ref, bf16[1536,128]{1,0:T(8,128)(2,1)S(1)} %get-tuple-element.79.flux_ref, ...), custom_call_target="tpu_custom_call" | custom-call | tf_op jit(solution)/shard_map/update/pallas_call | solution.py:311
  64.5 6.2 %all-to-all-start = ((bf16[8,64,128]{2,1,0:T(8,128)(2,1)}), bf16[8,64,128]{2,1,0:T(8,128)(2,1)S(1)}, u32[]{:S(2)}, u32[]{:S(2)}) async-start(bf16[8,64,128]{2,1,0:T(8,128)(2,1)} %bitcast.25), calls=%async_computation | async-start | bytes 262144 | tf_op jit(solution)/shard_map/all_to_all | solution.py:472
  70.7 0.8 settle.1
  71.5 6.6 %all-to-all-done = bf16[8,64,128]{2,1,0:T(8,128)(2,1)S(1)} async-done(((bf16[8,64,128]{2,1,0:T(8,128)(2,1)}), bf16[8,64,128]{2,1,0:T(8,128)(2,1)S(1)}, u32[]{:S(2)}, u32[]{:S(2)}) %all-to-all-start) | async-done | bytes 131104 | tf_op jit(solution)/shard_map/all_to_all | solution.py:472
  78.0 0.2 coarse_product.5
  78.4 3.3 %collective-permute-done.24 = bf16[128,128]{1,0:T(8,128)(2,1)S(1)} collective-permute-done((bf16[128,128]{1,0:T(8,128)(2,1)S(1)}, bf16[128,128]{1,0:T(8,128)(2,1)S(1)}, u32[]{:S(2)}, u32[]{:S(2)}) %collective-permute-start.24) | collective-permute-done | bytes 32800 | tf_op jit(solution)/shard_map/ppermute | solution.py:363
  81.8 1.2 %collective-permute-done.25 = bf16[64,128]{1,0:T(8,128)(2,1)S(1)} collective-permute-done((bf16[64,128]{1,0:T(8,128)(2,1)S(1)}, bf16[64,128]{1,0:T(8,128)(2,1)S(1)}, u32[]{:S(2)}, u32[]{:S(2)}) %collective-permute-start.25) | collective-permute-done | bytes 16416 | tf_op jit(solution)/shard_map/ppermute | solution.py:363
  83.0 1.0 %finish.1 = bf16[1536,128]{1,0:T(8,128)(2,1)} custom-call(f32[1536,128]{1,0:T(8,128)S(1)} %get-tuple-element.91.before_ref, bf16[1536,128]{1,0:T(8,128)(2,1)S(1)} %get-tuple-element.62.refs_5_.tall_ref, bf16[64,128]{1,0:T(8,128)(2,1)S(1)} %add_convert_fusion.2.own_ref), custom_call_target="tpu_custom_call" | custom-call | tf_op jit(solution)/shard_map/finish/pallas_call | solution.py:281
  (64 shorter events, 1.1 us)
Async XLA Ops:
  0.6 10.2 %collective-permute-start = (bf16[256,512]{1,0:T(8,128)(2,1)}, bf16[256,512]{1,0:T(8,128)(2,1)S(1)}, u32[]{:S(2)}, u32[]{:S(2)}) collective-permute-start(bf16[256,512]{1,0:T(8,128)(2,1)} %refs_0_.2), channel_id=1, source_target_pairs={{0,4},{4,0},{8,12},{12,8},{16,20},{20,16},{24,28},{28,24},{1,5},{5... | collective-permute-start | bytes 786440 | tf_op jit(solution)/shard_map/ppermute | solution.py:363
  3.6 0.7 copy-start.3
  4.3 14.3 %copy-start = (bf16[1,1,1536,128]{3,2,1,0:T(8,128)(2,1)S(1)}, bf16[1,1,1536,128]{3,2,1,0:T(8,128)(2,1)}, u32[]{:S(2)}) copy-start(bf16[1,1,1536,128]{3,2,1,0:T(8,128)(2,1)} %param.9) | copy-start | bytes 1179652
  4.3 17.7 %copy-start.2 = (bf16[1,1,1536,128]{3,2,1,0:T(8,128)(2,1)S(1)}, bf16[1,1,1536,128]{3,2,1,0:T(8,128)(2,1)}, u32[]{:S(2)}) copy-start(bf16[1,1,1536,128]{3,2,1,0:T(8,128)(2,1)} %param.8) | copy-start | bytes 1179652
  10.9 1.7 %collective-permute-start.1 = (bf16[160,128]{1,0:T(8,128)(2,1)S(1)}, bf16[160,128]{1,0:T(8,128)(2,1)S(1)}, u32[]{:S(2)}, u32[]{:S(2)}) collective-permute-start(bf16[160,128]{1,0:T(8,128)(2,1)S(1)} %get-tuple-element.116), channel_id=1, source_target_pairs={{0,1},{1,0},{2,3},{3,2},{4,5},{5,4},{6,7},{7,6},{8,9},{9,8},{10,11... | collective-permute-start | bytes 122888 | tf_op jit(solution)/shard_map/ppermute | solution.py:363
  11.0 3.5 %collective-permute-start.2 = (bf16[160,128]{1,0:T(8,128)(2,1)S(1)}, bf16[160,128]{1,0:T(8,128)(2,1)S(1)}, u32[]{:S(2)}, u32[]{:S(2)}) collective-permute-start(bf16[160,128]{1,0:T(8,128)(2,1)S(1)} %get-tuple-element.117), channel_id=1, source_target_pairs={{0,3},{1,2},{2,1},{3,0},{4,7},{5,6},{6,5},{7,4},{8,11},{9,10},{10,... | collective-permute-start | bytes 122888 | tf_op jit(solution)/shard_map/ppermute | solution.py:380
  14.5 4.1 %collective-permute-start.3 = (bf16[160,128]{1,0:T(8,128)(2,1)S(1)}, bf16[160,128]{1,0:T(8,128)(2,1)S(1)}, u32[]{:S(2)}, u32[]{:S(2)}) collective-permute-start(bf16[160,128]{1,0:T(8,128)(2,1)S(1)} %get-tuple-element.130), channel_id=1, source_target_pairs={{0,4},{4,0},{8,12},{12,8},{16,20},{20,16},{24,28},{28,24},{1,5},{5... | collective-permute-start | bytes 122888 | tf_op jit(solution)/shard_map/ppermute | solution.py:363
  15.6 3.0 %collective-permute-start.4 = (bf16[160,128]{1,0:T(8,128)(2,1)S(1)}, bf16[160,128]{1,0:T(8,128)(2,1)S(1)}, u32[]{:S(2)}, u32[]{:S(2)}) collective-permute-start(bf16[160,128]{1,0:T(8,128)(2,1)S(1)} %get-tuple-element.131), channel_id=1, source_target_pairs={{0,1},{1,0},{2,3},{3,2},{4,8},{5,9},{6,10},{7,11},{8,4},{9,5},{10,... | collective-permute-start | bytes 122888 | tf_op jit(solution)/shard_map/ppermute | solution.py:380
  15.8 9.6 %collective-permute-start.6 = (bf16[256,512]{1,0:T(8,128)(2,1)S(1)}, bf16[256,512]{1,0:T(8,128)(2,1)S(1)}, u32[]{:S(2)}, u32[]{:S(2)}) collective-permute-start(bf16[256,512]{1,0:T(8,128)(2,1)S(1)} %collective-permute-done.refs_1_), channel_id=1, source_target_pairs={{4,0},{0,8},{8,16},{16,24},{24,28},{28,20},{20,12},{12,4},{5,1},{1... | collective-permute-start | bytes 786440 | tf_op jit(solution)/shard_map/ppermute | solution.py:386
  19.1 6.3 %collective-permute-start.5 = (bf16[64,128]{1,0:T(8,128)(2,1)S(1)}, bf16[64,128]{1,0:T(8,128)(2,1)S(1)}, u32[]{:S(2)}, u32[]{:S(2)}) collective-permute-start(bf16[64,128]{1,0:T(8,128)(2,1)S(1)} %get-tuple-element.57), channel_id=1, source_target_pairs={{0,4},{4,0},{8,12},{12,8},{16,20},{20,16},{24,28},{28,24},{1,5},{5... | collective-permute-start | bytes 49160 | tf_op jit(solution)/shard_map/ppermute | solution.py:363
  22.1 13.3 %copy-start.1 = (bf16[256,512]{1,0:T(8,128)(2,1)S(1)}, bf16[256,512]{1,0:T(8,128)(2,1)}, u32[]{:S(2)}) copy-start(bf16[256,512]{1,0:T(8,128)(2,1)} %refs_0_.2) | copy-start | bytes 786436
  25.4 4.0 %collective-permute-start.11 = (bf16[2,64,128]{2,1,0:T(8,128)(2,1)S(1)}, bf16[2,64,128]{2,1,0:T(8,128)(2,1)S(1)}, u32[]{:S(2)}, u32[]{:S(2)}) collective-permute-start(bf16[2,64,128]{2,1,0:T(8,128)(2,1)S(1)} %pad_maximum_fusion.13), channel_id=1, source_target_pairs={{0,8},{4,12},{8,0},{12,4},{16,24},{20,28},{24,16},{28,20},{1,9},{5... | collective-permute-start | bytes 98312 | tf_op jit(solution)/shard_map/ppermute | solution.py:363
  26.6 5.0 %collective-permute-start.7 = (bf16[160,256]{1,0:T(8,128)(2,1)S(1)}, bf16[160,256]{1,0:T(8,128)(2,1)S(1)}, u32[]{:S(2)}, u32[]{:S(2)}) collective-permute-start(bf16[160,256]{1,0:T(8,128)(2,1)S(1)} %get-tuple-element.102), channel_id=1, source_target_pairs={{0,1},{1,0},{2,3},{3,2},{4,5},{5,4},{6,7},{7,6},{8,9},{9,8},{10,11... | collective-permute-start | bytes 245768 | tf_op jit(solution)/shard_map/ppermute | solution.py:363
  26.7 4.9 %collective-permute-start.8 = (bf16[160,256]{1,0:T(8,128)(2,1)S(1)}, bf16[160,256]{1,0:T(8,128)(2,1)S(1)}, u32[]{:S(2)}, u32[]{:S(2)}) collective-permute-start(bf16[160,256]{1,0:T(8,128)(2,1)S(1)} %get-tuple-element.103), channel_id=1, source_target_pairs={{0,3},{1,2},{2,1},{3,0},{4,7},{5,6},{6,5},{7,4},{8,11},{9,10},{10,... | collective-permute-start | bytes 245768 | tf_op jit(solution)/shard_map/ppermute | solution.py:380
  29.4 5.9 %collective-permute-start.12 = (bf16[4,64,128]{2,1,0:T(8,128)(2,1)S(1)}, bf16[4,64,128]{2,1,0:T(8,128)(2,1)S(1)}, u32[]{:S(2)}, u32[]{:S(2)}) collective-permute-start(bf16[4,64,128]{2,1,0:T(8,128)(2,1)S(1)} %pad_maximum_fusion.7), channel_id=1, source_target_pairs={{0,16},{4,20},{8,24},{12,28},{16,0},{20,4},{24,8},{28,12},{1,17},{... | collective-permute-start | bytes 196616 | tf_op jit(solution)/shard_map/ppermute | solution.py:363
  31.7 5.6 %collective-permute-start.9 = (bf16[160,256]{1,0:T(8,128)(2,1)S(1)}, bf16[160,256]{1,0:T(8,128)(2,1)S(1)}, u32[]{:S(2)}, u32[]{:S(2)}) collective-permute-start(bf16[160,256]{1,0:T(8,128)(2,1)S(1)} %get-tuple-element.106), channel_id=1, source_target_pairs={{0,4},{4,0},{8,12},{12,8},{16,20},{20,16},{24,28},{28,24},{1,5},{5... | collective-permute-start | bytes 245768 | tf_op jit(solution)/shard_map/ppermute | solution.py:363
  33.6 3.8 %collective-permute-start.10 = (bf16[160,256]{1,0:T(8,128)(2,1)S(1)}, bf16[160,256]{1,0:T(8,128)(2,1)S(1)}, u32[]{:S(2)}, u32[]{:S(2)}) collective-permute-start(bf16[160,256]{1,0:T(8,128)(2,1)S(1)} %get-tuple-element.107), channel_id=1, source_target_pairs={{0,1},{1,0},{2,3},{3,2},{4,8},{5,9},{6,10},{7,11},{8,4},{9,5},{10,... | collective-permute-start | bytes 245768 | tf_op jit(solution)/shard_map/ppermute | solution.py:380
  35.7 5.2 %collective-permute-start.13 = (bf16[3,192,128]{2,1,0:T(8,128)(2,1)S(1)}, bf16[3,192,128]{2,1,0:T(8,128)(2,1)S(1)}, u32[]{:S(2)}, u32[]{:S(2)}) collective-permute-start(bf16[3,192,128]{2,1,0:T(8,128)(2,1)S(1)} %get-tuple-element.72), channel_id=1, source_target_pairs={{0,2},{1,3},{2,0},{3,1},{4,6},{5,7},{6,4},{7,5},{8,10},{9,11},{10,... | collective-permute-start | bytes 442376 | tf_op jit(solution)/shard_map/ppermute | solution.py:363
  41.0 1.4 %collective-permute-start.14 = (bf16[3,192,128]{2,1,0:T(8,128)(2,1)S(1)}, bf16[3,192,128]{2,1,0:T(8,128)(2,1)S(1)}, u32[]{:S(2)}, u32[]{:S(2)}) collective-permute-start(bf16[3,192,128]{2,1,0:T(8,128)(2,1)S(1)} %fusion), channel_id=1, source_target_pairs={{0,1},{1,0},{2,3},{3,2},{4,5},{5,4},{6,7},{7,6},{8,9},{9,8},{10,11... | collective-permute-start | bytes 442376 | tf_op jit(solution)/shard_map/ppermute | solution.py:363
  43.1 3.8 %collective-permute-start.15 = (bf16[64,128]{1,0:T(8,128)(2,1)S(1)}, bf16[64,128]{1,0:T(8,128)(2,1)S(1)}, u32[]{:S(2)}, u32[]{:S(2)}) collective-permute-start(bf16[64,128]{1,0:T(8,128)(2,1)S(1)} %get-tuple-element.73), channel_id=1, source_target_pairs={{0,4},{4,0},{8,12},{12,8},{16,20},{20,16},{24,28},{28,24},{1,5},{5... | collective-permute-start | bytes 49160 | tf_op jit(solution)/shard_map/ppermute | solution.py:363
  46.9 4.0 %collective-permute-start.20 = (bf16[2,64,128]{2,1,0:T(8,128)(2,1)S(1)}, bf16[2,64,128]{2,1,0:T(8,128)(2,1)S(1)}, u32[]{:S(2)}, u32[]{:S(2)}) collective-permute-start(bf16[2,64,128]{2,1,0:T(8,128)(2,1)S(1)} %pad_maximum_fusion.14), channel_id=1, source_target_pairs={{0,8},{4,12},{8,0},{12,4},{16,24},{20,28},{24,16},{28,20},{1,9},{5... | collective-permute-start | bytes 98312 | tf_op jit(solution)/shard_map/ppermute | solution.py:363
  48.4 5.2 %collective-permute-start.16 = (bf16[160,128]{1,0:T(8,128)(2,1)S(1)}, bf16[160,128]{1,0:T(8,128)(2,1)S(1)}, u32[]{:S(2)}, u32[]{:S(2)}) collective-permute-start(bf16[160,128]{1,0:T(8,128)(2,1)S(1)} %get-tuple-element.112), channel_id=1, source_target_pairs={{0,1},{1,0},{2,3},{3,2},{4,5},{5,4},{6,7},{7,6},{8,9},{9,8},{10,11... | collective-permute-start | bytes 122888 | tf_op jit(solution)/shard_map/ppermute | solution.py:363
  48.4 5.2 %collective-permute-start.17 = (bf16[160,128]{1,0:T(8,128)(2,1)S(1)}, bf16[160,128]{1,0:T(8,128)(2,1)S(1)}, u32[]{:S(2)}, u32[]{:S(2)}) collective-permute-start(bf16[160,128]{1,0:T(8,128)(2,1)S(1)} %get-tuple-element.113), channel_id=1, source_target_pairs={{0,3},{1,2},{2,1},{3,0},{4,7},{5,6},{6,5},{7,4},{8,11},{9,10},{10,... | collective-permute-start | bytes 122888 | tf_op jit(solution)/shard_map/ppermute | solution.py:380
  50.9 5.2 %collective-permute-start.21 = (bf16[4,64,128]{2,1,0:T(8,128)(2,1)S(1)}, bf16[4,64,128]{2,1,0:T(8,128)(2,1)S(1)}, u32[]{:S(2)}, u32[]{:S(2)}) collective-permute-start(bf16[4,64,128]{2,1,0:T(8,128)(2,1)S(1)} %pad_maximum_fusion.8), channel_id=1, source_target_pairs={{0,16},{4,20},{8,24},{12,28},{16,0},{20,4},{24,8},{28,12},{1,17},{... | collective-permute-start | bytes 196616 | tf_op jit(solution)/shard_map/ppermute | solution.py:363
  56.5 5.2 %collective-permute-start.22 = (bf16[3,192,128]{2,1,0:T(8,128)(2,1)S(1)}, bf16[3,192,128]{2,1,0:T(8,128)(2,1)S(1)}, u32[]{:S(2)}, u32[]{:S(2)}) collective-permute-start(bf16[3,192,128]{2,1,0:T(8,128)(2,1)S(1)} %get-tuple-element.85), channel_id=1, source_target_pairs={{0,2},{1,3},{2,0},{3,1},{4,6},{5,7},{6,4},{7,5},{8,10},{9,11},{10,... | collective-permute-start | bytes 442376 | tf_op jit(solution)/shard_map/ppermute | solution.py:363
  58.1 4.1 %collective-permute-start.18 = (bf16[160,128]{1,0:T(8,128)(2,1)S(1)}, bf16[160,128]{1,0:T(8,128)(2,1)S(1)}, u32[]{:S(2)}, u32[]{:S(2)}) collective-permute-start(bf16[160,128]{1,0:T(8,128)(2,1)S(1)} %get-tuple-element.120), channel_id=1, source_target_pairs={{0,4},{4,0},{8,12},{12,8},{16,20},{20,16},{24,28},{28,24},{1,5},{5... | collective-permute-start | bytes 122888 | tf_op jit(solution)/shard_map/ppermute | solution.py:363
  60.1 2.1 %collective-permute-start.19 = (bf16[160,128]{1,0:T(8,128)(2,1)S(1)}, bf16[160,128]{1,0:T(8,128)(2,1)S(1)}, u32[]{:S(2)}, u32[]{:S(2)}) collective-permute-start(bf16[160,128]{1,0:T(8,128)(2,1)S(1)} %get-tuple-element.121), channel_id=1, source_target_pairs={{0,1},{1,0},{2,3},{3,2},{4,8},{5,9},{6,10},{7,11},{8,4},{9,5},{10,... | collective-permute-start | bytes 122888 | tf_op jit(solution)/shard_map/ppermute | solution.py:380
  61.8 1.4 %collective-permute-start.23 = (bf16[3,192,128]{2,1,0:T(8,128)(2,1)S(1)}, bf16[3,192,128]{2,1,0:T(8,128)(2,1)S(1)}, u32[]{:S(2)}, u32[]{:S(2)}) collective-permute-start(bf16[3,192,128]{2,1,0:T(8,128)(2,1)S(1)} %fusion.1), channel_id=1, source_target_pairs={{0,1},{1,0},{2,3},{3,2},{4,5},{5,4},{6,7},{7,6},{8,9},{9,8},{10,11... | collective-permute-start | bytes 442376 | tf_op jit(solution)/shard_map/ppermute | solution.py:363
  64.5 13.5 %all-to-all-start = ((bf16[8,64,128]{2,1,0:T(8,128)(2,1)}), bf16[8,64,128]{2,1,0:T(8,128)(2,1)S(1)}, u32[]{:S(2)}, u32[]{:S(2)}) async-start(bf16[8,64,128]{2,1,0:T(8,128)(2,1)} %bitcast.25), calls=%async_computation | async-start | bytes 262144 | tf_op jit(solution)/shard_map/all_to_all | solution.py:472
  78.3 3.4 %collective-permute-start.24 = (bf16[128,128]{1,0:T(8,128)(2,1)S(1)}, bf16[128,128]{1,0:T(8,128)(2,1)S(1)}, u32[]{:S(2)}, u32[]{:S(2)}) collective-permute-start(bf16[128,128]{1,0:T(8,128)(2,1)S(1)} %bitcast.47), channel_id=1, source_target_pairs={{0,3},{1,2},{2,1},{3,0},{4,7},{5,6},{6,5},{7,4},{8,11},{9,10},{10,... | collective-permute-start | bytes 98312 | tf_op jit(solution)/shard_map/ppermute | solution.py:363
  81.7 1.2 %collective-permute-start.25 = (bf16[64,128]{1,0:T(8,128)(2,1)S(1)}, bf16[64,128]{1,0:T(8,128)(2,1)S(1)}, u32[]{:S(2)}, u32[]{:S(2)}) collective-permute-start(bf16[64,128]{1,0:T(8,128)(2,1)S(1)} %select_convert_fusion), channel_id=1, source_target_pairs={{0,1},{1,0},{2,3},{3,2},{4,5},{5,4},{6,7},{7,6},{8,9},{9,8},{10,11... | collective-permute-start | bytes 49160 | tf_op jit(solution)/shard_map/ppermute | solution.py:363

commit v8 on v7

--- a/solution.py
+++ b/solution.py
@@ -319,10 +319,10 @@
     )(*operands)
 
 
-def coarse_kernel(modes, half, ordered, row_ref, col_ref, pieces_ref, *refs):
+def coarse_kernel(modes, half, order, row_ref, col_ref, pieces_ref, *refs):
     matrices, (mine_ref, sent_ref, full, whole) = refs[:-4], refs[-4:]
     for m in range(pieces_ref.shape[0]):
-        block = m if ordered else row_ref[0] ^ m
+        block = row_ref[0] ^ order[m] if order else m
         full[pl.ds(pl.multiple_of(block * modes, modes), modes), :] = pieces_ref[m]
     count = mine_ref.shape[1]
     upper = col_ref[0] // half
@@ -334,11 +334,11 @@
         sent_ref[i] = whole[i, pl.ds(sent, count), :].astype(bf16)
 
 
-def coarse_product(place, half, pieces, matrices, count, ordered=False):
+def coarse_product(place, half, pieces, matrices, count, order=None):
     many, modes, width = pieces.shape
     rows, depth = matrices[0].shape
     return pl.pallas_call(
-        functools.partial(coarse_kernel, modes, half, ordered),
+        functools.partial(coarse_kernel, modes, half, order),
         out_shape=[
             shape_of((len(matrices), count, width), f32),
             shape_of((len(matrices), count, width), bf16),
@@ -473,12 +473,13 @@
             gathered, before = lax.optimization_barrier((gathered, before))
             gathered = gathered.reshape(subs, MODES, width)
             value, sent = coarse_product(
-                place, half, gathered, matrices[:1], half * MODES, ordered=True
+                place, half, gathered, matrices[:1], half * MODES
             )
             final = share_of_sum(value[0], sent[0])
             break
-        got = swap(rhs, "sub", 1)
-        pieces = jnp.stack([rhs, got])
+        bits = [subs >> i for i in range(1, subs.bit_length())]
+        order = [0, bits[0]]
+        pieces = jnp.stack([rhs, swap(rhs, "sub", bits[0])])
         state, flux, packed = products(state, residual, kernel, inverse, selector, tall, own)
         pieces, packed, matrices = lax.optimization_barrier((pieces, packed, matrices))
         rows = exchange(packed, face)
@@ -486,10 +487,10 @@
             wide, wide_rows = flux[:, width:], rows[:, :, width:]
             flux, rows = flux[:, :width], rows[:, :, :width]
             coupling = couple(selector_t, wide, wide_rows)
-        while pieces.shape[0] < subs:
-            got = swap(pieces, "sub", pieces.shape[0])
-            pieces = jnp.concatenate([pieces, got])
-        coarse = sum_over_columns(*coarse_product(place, half, pieces, matrices, (half + 1) * MODES))
+        for bit in bits[1:]:
+            order += [m ^ bit for m in order]
+            pieces = jnp.concatenate([pieces, swap(pieces, "sub", bit)])
+        coarse = sum_over_columns(*coarse_product(place, half, pieces, matrices, (half + 1) * MODES, order))
     trace = finish(before, tall, final)
     return trace[None, None], residual[None, None]
 

time: 84.4 us -> 83.1 us (0.985)
  starting transfers between devices: 36.4 us -> 35.2 us
    all_to_all x1, starting transfers between devices: 6.16 us -> 4.61 us  [local(): gathered = lax.all_to_all(rhs, 'sub', 0, 0, tiled=True)]
  transfers between devices with their start and end apart: 27 -> 27, of which waited for: 16 -> 17; matrix products, arithmetic and copies ran while one was open for 1% -> 1% of each run, Pallas kernels for 17% -> 17%
where the time goes in v8:
time: 83.1 us; the launch traced here: 82.8 us
  starting transfers between devices  35.2 us (42%)
  waiting for transfers between devices  27.6 us (33%)
  Pallas kernels  17.3 us (21%)
  between operations  1.18 us (1%)
  local copies, waits for them, and re-layouts  0.85 us (1%)
    ppermute x19, starting transfers between devices, swap(): lax.ppermute(value, axis, [(i, i ^ mask) for i in range(lax.axis_size(axi...  23.1 us
    ppermute x19, waiting for transfers between devices, swap(): lax.ppermute(value, axis, [(i, i ^ mask) for i in range(lax.axis_size(axi...  19.1 us
    all_to_all x1, waiting for transfers between devices, local(): gathered = lax.all_to_all(rhs, 'sub', 0, 0, tiled=True)  6.58 us
    pallas_call x1, Pallas kernels, load_products(): pl.pallas_call(functools.partial(load_kernel, face, chunk, 3), out_shape=...  6.53 us
    pallas_call x2, Pallas kernels, products(): pl.pallas_call(body, out_shape=[shape_of((count, width), bf16), shape_of(...  5.62 us
    ppermute x6, starting transfers between devices, cross(): return lax.ppermute(value, ('sub', 'col'), pairs)  5.15 us
    all_to_all x1, starting transfers between devices, local(): gathered = lax.all_to_all(rhs, 'sub', 0, 0, tiled=True)  4.61 us
    ppermute x1, starting transfers between devices, onward(): return lax.ppermute(value, axis, [(ring[i - 1], ring[i]) for i in range(n)])  2.32 us
  transfers between devices with their start and end apart: 27, of which 17 were waited for; matrix products, arithmetic and copies ran while one was open for 1% of the time, Pallas kernels for 17%

profile of v8, /device:TPU:0, one launch (start us, length us, event | category | flops | bytes accessed | tf_op | source)
XLA Modules:
  0.0 82.8 jit_solution(15997434078494450656)
XLA Ops:
  0.6 3.0 %collective-permute-start = (bf16[256,512]{1,0:T(8,128)(2,1)}, bf16[256,512]{1,0:T(8,128)(2,1)S(1)}, u32[]{:S(2)}, u32[]{:S(2)}) collective-permute-start(bf16[256,512]{1,0:T(8,128)(2,1)} %refs_0_.2), channel_id=1, source_target_pairs={{0,4},{4,0},{8,12},{12,8},{16,20},{20,16},{24,28},{28,24},{1,5},{5... | collective-permute-start | bytes 786440 | tf_op jit(solution)/shard_map/ppermute | solution.py:363
  3.6 0.7 copy-done.3
  4.3 6.5 %load_products.1 = (bf16[1536,128]{1,0:T(8,128)(2,1)S(1)}, bf16[576,128]{1,0:T(8,128)(2,1)S(1)}, bf16[8,128,128]{2,1,0:T(8,128)(2,1)S(1)}, bf16[8,128,128]{2,1,0...) custom-call(bf16[1536,128]{1,0:T(8,128)(2,1)} %bitcast.42, ...), custom_call_target="tpu_custom_call" | custom-call | flops 2415919104 | bytes 9437184 | tf_op jit(solution)/shard_map/load_products/pallas_call | solution.py:89
  11.0 1.6 %collective-permute-start.2 = (bf16[160,128]{1,0:T(8,128)(2,1)S(1)}, bf16[160,128]{1,0:T(8,128)(2,1)S(1)}, u32[]{:S(2)}, u32[]{:S(2)}) collective-permute-start(bf16[160,128]{1,0:T(8,128)(2,1)S(1)} %get-tuple-element.117), channel_id=1, source_target_pairs={{0,3},{1,2},{2,1},{3,0},{4,7},{5,6},{6,5},{7,4},{8,11},{9,10},{10,... | collective-permute-start | bytes 122888 | tf_op jit(solution)/shard_map/ppermute | solution.py:380
  12.6 1.8 %collective-permute-done.2 = bf16[160,128]{1,0:T(8,128)(2,1)S(1)} collective-permute-done((bf16[160,128]{1,0:T(8,128)(2,1)S(1)}, bf16[160,128]{1,0:T(8,128)(2,1)S(1)}, u32[]{:S(2)}, u32[]{:S(2)}) %collective-permute-start.2) | collective-permute-done | bytes 40992 | tf_op jit(solution)/shard_map/ppermute | solution.py:380
  14.5 1.1 %collective-permute-start.3 = (bf16[160,128]{1,0:T(8,128)(2,1)S(1)}, bf16[160,128]{1,0:T(8,128)(2,1)S(1)}, u32[]{:S(2)}, u32[]{:S(2)}) collective-permute-start(bf16[160,128]{1,0:T(8,128)(2,1)S(1)} %get-tuple-element.130), channel_id=1, source_target_pairs={{0,4},{4,0},{8,12},{12,8},{16,20},{20,16},{24,28},{28,24},{1,5},{5... | collective-permute-start | bytes 122888 | tf_op jit(solution)/shard_map/ppermute | solution.py:363
  15.6 0.2 collective-permute-start.4
  15.8 2.3 %collective-permute-start.6 = (bf16[256,512]{1,0:T(8,128)(2,1)S(1)}, bf16[256,512]{1,0:T(8,128)(2,1)S(1)}, u32[]{:S(2)}, u32[]{:S(2)}) collective-permute-start(bf16[256,512]{1,0:T(8,128)(2,1)S(1)} %collective-permute-done.refs_1_), channel_id=1, source_target_pairs={{4,0},{0,8},{8,16},{16,24},{24,28},{28,20},{20,12},{12,4},{5,1},{1... | collective-permute-start | bytes 786440 | tf_op jit(solution)/shard_map/ppermute | solution.py:386
  18.1 0.5 collective-permute-done.3
  18.7 0.4 first_update.1
  19.1 4.6 %collective-permute-start.5 = (bf16[64,128]{1,0:T(8,128)(2,1)S(1)}, bf16[64,128]{1,0:T(8,128)(2,1)S(1)}, u32[]{:S(2)}, u32[]{:S(2)}) collective-permute-start(bf16[64,128]{1,0:T(8,128)(2,1)S(1)} %get-tuple-element.57), channel_id=1, source_target_pairs={{0,16},{4,20},{8,24},{12,28},{16,0},{20,4},{24,8},{28,12},{1,17},{... | collective-permute-start | bytes 49160 | tf_op jit(solution)/shard_map/ppermute | solution.py:363
  23.6 2.7 %products.2 = (bf16[1536,128]{1,0:T(8,128)(2,1)S(1)}, bf16[1536,256]{1,0:T(8,128)(2,1)S(1)}, bf16[576,256]{1,0:T(8,128)(2,1)S(1)}) custom-call(bf16[1536,128]{1,0:T(8,128)(2,1)S(1)} %bitcast.43, bf16[1536,128]{1,0:T(8,128)(2,1)S(1)} %get-tuple-element.58.refs_1_, bf16[1536,1536]{1,0:T(8,128)(2,1)S(1)} %get-tuple-element.59.refs_2_.k_ref, ...), custom_call_target="tpu_custom_call" | custom-call | flops 2415919104 | bytes 9437184 | tf_op jit(solution)/shard_map/products/pallas_call | solution.py:153
  26.5 1.6 %collective-permute-start.11 = (bf16[2,64,128]{2,1,0:T(8,128)(2,1)S(1)}, bf16[2,64,128]{2,1,0:T(8,128)(2,1)S(1)}, u32[]{:S(2)}, u32[]{:S(2)}) collective-permute-start(bf16[2,64,128]{2,1,0:T(8,128)(2,1)S(1)} %pad_maximum_fusion.13), channel_id=1, source_target_pairs={{0,8},{4,12},{8,0},{12,4},{16,24},{20,28},{24,16},{28,20},{1,9},{5... | collective-permute-start | bytes 98312 | tf_op jit(solution)/shard_map/ppermute | solution.py:363
  28.2 1.6 %collective-permute-start.8 = (bf16[160,256]{1,0:T(8,128)(2,1)S(1)}, bf16[160,256]{1,0:T(8,128)(2,1)S(1)}, u32[]{:S(2)}, u32[]{:S(2)}) collective-permute-start(bf16[160,256]{1,0:T(8,128)(2,1)S(1)} %get-tuple-element.103), channel_id=1, source_target_pairs={{0,3},{1,2},{2,1},{3,0},{4,7},{5,6},{6,5},{7,4},{8,11},{9,10},{10,... | collective-permute-start | bytes 245768 | tf_op jit(solution)/shard_map/ppermute | solution.py:380
  29.9 0.6 collective-permute-done.11
  30.5 1.9 %collective-permute-start.12 = (bf16[4,64,128]{2,1,0:T(8,128)(2,1)S(1)}, bf16[4,64,128]{2,1,0:T(8,128)(2,1)S(1)}, u32[]{:S(2)}, u32[]{:S(2)}) collective-permute-start(bf16[4,64,128]{2,1,0:T(8,128)(2,1)S(1)} %pad_maximum_fusion.7), channel_id=1, source_target_pairs={{0,4},{4,0},{8,12},{12,8},{16,20},{20,16},{24,28},{28,24},{1,5},{5... | collective-permute-start | bytes 196616 | tf_op jit(solution)/shard_map/ppermute | solution.py:363
  32.4 0.1 collective-permute-done.8
  32.6 1.7 %collective-permute-start.9 = (bf16[160,256]{1,0:T(8,128)(2,1)S(1)}, bf16[160,256]{1,0:T(8,128)(2,1)S(1)}, u32[]{:S(2)}, u32[]{:S(2)}) collective-permute-start(bf16[160,256]{1,0:T(8,128)(2,1)S(1)} %get-tuple-element.106), channel_id=1, source_target_pairs={{0,4},{4,0},{8,12},{12,8},{16,20},{20,16},{24,28},{28,24},{1,5},{5... | collective-permute-start | bytes 245768 | tf_op jit(solution)/shard_map/ppermute | solution.py:363
  34.4 0.4 collective-permute-done.12
  34.9 0.4 coarse_product.3
  35.2 1.6 %collective-permute-start.13 = (bf16[3,192,128]{2,1,0:T(8,128)(2,1)S(1)}, bf16[3,192,128]{2,1,0:T(8,128)(2,1)S(1)}, u32[]{:S(2)}, u32[]{:S(2)}) collective-permute-start(bf16[3,192,128]{2,1,0:T(8,128)(2,1)S(1)} %get-tuple-element.72), channel_id=1, source_target_pairs={{0,2},{1,3},{2,0},{3,1},{4,6},{5,7},{6,4},{7,5},{8,10},{9,11},{10,... | collective-permute-start | bytes 442376 | tf_op jit(solution)/shard_map/ppermute | solution.py:363
  36.8 1.4 %collective-permute-done.9 = bf16[160,256]{1,0:T(8,128)(2,1)S(1)} collective-permute-done((bf16[160,256]{1,0:T(8,128)(2,1)S(1)}, bf16[160,256]{1,0:T(8,128)(2,1)S(1)}, u32[]{:S(2)}, u32[]{:S(2)}) %collective-permute-start.9) | collective-permute-done | bytes 81952 | tf_op jit(solution)/shard_map/ppermute | solution.py:363
  38.4 2.7 %collective-permute-done.13 = bf16[3,192,128]{2,1,0:T(8,128)(2,1)S(1)} collective-permute-done((bf16[3,192,128]{2,1,0:T(8,128)(2,1)S(1)}, bf16[3,192,128]{2,1,0:T(8,128)(2,1)S(1)}, u32[]{:S(2)}, u32[]{:S(2)}) %collective-permute-start.13) | collective-permute-done | bytes 147488 | tf_op jit(solution)/shard_map/ppermute | solution.py:363
  41.2 0.2 couple.1.couple_ref
  41.4 1.1 %collective-permute-done.14 = bf16[3,192,128]{2,1,0:T(8,128)(2,1)S(1)} collective-permute-done((bf16[3,192,128]{2,1,0:T(8,128)(2,1)S(1)}, bf16[3,192,128]{2,1,0:T(8,128)(2,1)S(1)}, u32[]{:S(2)}, u32[]{:S(2)}) %collective-permute-start.14) | collective-permute-done | bytes 147488 | tf_op jit(solution)/shard_map/ppermute | solution.py:363
  42.6 0.6 update.2
  43.2 1.5 %collective-permute-start.15 = (bf16[64,128]{1,0:T(8,128)(2,1)S(1)}, bf16[64,128]{1,0:T(8,128)(2,1)S(1)}, u32[]{:S(2)}, u32[]{:S(2)}) collective-permute-start(bf16[64,128]{1,0:T(8,128)(2,1)S(1)} %get-tuple-element.73), channel_id=1, source_target_pairs={{0,16},{4,20},{8,24},{12,28},{16,0},{20,4},{24,8},{28,12},{1,17},{... | collective-permute-start | bytes 49160 | tf_op jit(solution)/shard_map/ppermute | solution.py:363
  44.7 2.9 %products.3 = (bf16[1536,128]{1,0:T(8,128)(2,1)S(1)}, bf16[1536,128]{1,0:T(8,128)(2,1)S(1)}, bf16[576,128]{1,0:T(8,128)(2,1)S(1)}) custom-call(bf16[1536,128]{1,0:T(8,128)(2,1)S(1)} %get-tuple-element.74.state_ref, bf16[1536,128]{1,0:T(8,128)(2,1)S(1)} %get-tuple-element.75.res_ref, bf16[1536,1536]{1,0:T(8,128)(2,1)S(1)} %get-tuple-element.59.refs_2_.k_ref, ...), custom_call_target="tpu_custom_call" | custom-call | flops 2415919104 | bytes 9437184 | tf_op jit(solution)/shard_map/products/pallas_call | solution.py:153
  47.6 0.4 collective-permute-done.15
  48.0 1.5 %collective-permute-start.20 = (bf16[2,64,128]{2,1,0:T(8,128)(2,1)S(1)}, bf16[2,64,128]{2,1,0:T(8,128)(2,1)S(1)}, u32[]{:S(2)}, u32[]{:S(2)}) collective-permute-start(bf16[2,64,128]{2,1,0:T(8,128)(2,1)S(1)} %pad_maximum_fusion.14), channel_id=1, source_target_pairs={{0,8},{4,12},{8,0},{12,4},{16,24},{20,28},{24,16},{28,20},{1,9},{5... | collective-permute-start | bytes 98312 | tf_op jit(solution)/shard_map/ppermute | solution.py:363
  49.5 1.6 %collective-permute-start.17 = (bf16[160,128]{1,0:T(8,128)(2,1)S(1)}, bf16[160,128]{1,0:T(8,128)(2,1)S(1)}, u32[]{:S(2)}, u32[]{:S(2)}) collective-permute-start(bf16[160,128]{1,0:T(8,128)(2,1)S(1)} %get-tuple-element.113), channel_id=1, source_target_pairs={{0,3},{1,2},{2,1},{3,0},{4,7},{5,6},{6,5},{7,4},{8,11},{9,10},{10,... | collective-permute-start | bytes 122888 | tf_op jit(solution)/shard_map/ppermute | solution.py:380
  51.1 0.9 %collective-permute-done.20 = bf16[2,64,128]{2,1,0:T(8,128)(2,1)S(1)} collective-permute-done((bf16[2,64,128]{2,1,0:T(8,128)(2,1)S(1)}, bf16[2,64,128]{2,1,0:T(8,128)(2,1)S(1)}, u32[]{:S(2)}, u32[]{:S(2)}) %collective-permute-start.20) | collective-permute-done | bytes 32800 | tf_op jit(solution)/shard_map/ppermute | solution.py:363
  52.0 1.3 %collective-permute-start.21 = (bf16[4,64,128]{2,1,0:T(8,128)(2,1)S(1)}, bf16[4,64,128]{2,1,0:T(8,128)(2,1)S(1)}, u32[]{:S(2)}, u32[]{:S(2)}) collective-permute-start(bf16[4,64,128]{2,1,0:T(8,128)(2,1)S(1)} %pad_maximum_fusion.8), channel_id=1, source_target_pairs={{0,4},{4,0},{8,12},{12,8},{16,20},{20,16},{24,28},{28,24},{1,5},{5... | collective-permute-start | bytes 196616 | tf_op jit(solution)/shard_map/ppermute | solution.py:363
  53.4 3.0 %collective-permute-done.21 = bf16[4,64,128]{2,1,0:T(8,128)(2,1)S(1)} collective-permute-done((bf16[4,64,128]{2,1,0:T(8,128)(2,1)S(1)}, bf16[4,64,128]{2,1,0:T(8,128)(2,1)S(1)}, u32[]{:S(2)}, u32[]{:S(2)}) %collective-permute-start.21) | collective-permute-done | bytes 65568 | tf_op jit(solution)/shard_map/ppermute | solution.py:363
  56.4 0.4 coarse_product.4
  56.8 1.6 %collective-permute-start.22 = (bf16[3,192,128]{2,1,0:T(8,128)(2,1)S(1)}, bf16[3,192,128]{2,1,0:T(8,128)(2,1)S(1)}, u32[]{:S(2)}, u32[]{:S(2)}) collective-permute-start(bf16[3,192,128]{2,1,0:T(8,128)(2,1)S(1)} %get-tuple-element.85), channel_id=1, source_target_pairs={{0,2},{1,3},{2,0},{3,1},{4,6},{5,7},{6,4},{7,5},{8,10},{9,11},{10,... | collective-permute-start | bytes 442376 | tf_op jit(solution)/shard_map/ppermute | solution.py:363
  58.4 1.3 %collective-permute-start.18 = (bf16[160,128]{1,0:T(8,128)(2,1)S(1)}, bf16[160,128]{1,0:T(8,128)(2,1)S(1)}, u32[]{:S(2)}, u32[]{:S(2)}) collective-permute-start(bf16[160,128]{1,0:T(8,128)(2,1)S(1)} %get-tuple-element.120), channel_id=1, source_target_pairs={{0,4},{4,0},{8,12},{12,8},{16,20},{20,16},{24,28},{28,24},{1,5},{5... | collective-permute-start | bytes 122888 | tf_op jit(solution)/shard_map/ppermute | solution.py:363
  59.7 2.3 %collective-permute-done.22 = bf16[3,192,128]{2,1,0:T(8,128)(2,1)S(1)} collective-permute-done((bf16[3,192,128]{2,1,0:T(8,128)(2,1)S(1)}, bf16[3,192,128]{2,1,0:T(8,128)(2,1)S(1)}, u32[]{:S(2)}, u32[]{:S(2)}) %collective-permute-start.22) | collective-permute-done | bytes 147488 | tf_op jit(solution)/shard_map/ppermute | solution.py:363
  62.1 0.4 collective-permute-done.18
  62.5 1.0 %collective-permute-done.23 = bf16[3,192,128]{2,1,0:T(8,128)(2,1)S(1)} collective-permute-done((bf16[3,192,128]{2,1,0:T(8,128)(2,1)S(1)}, bf16[3,192,128]{2,1,0:T(8,128)(2,1)S(1)}, u32[]{:S(2)}, u32[]{:S(2)}) %collective-permute-start.23) | collective-permute-done | bytes 147488 | tf_op jit(solution)/shard_map/ppermute | solution.py:363
  63.5 1.3 %update.3 = (bf16[1536,128]{1,0:T(8,128)(2,1)S(1)}, bf16[512,128]{1,0:T(8,128)(2,1)}, bf16[64,128]{1,0:T(8,128)(2,1)S(1)}) custom-call(s32[1]{0:T(128)} %bitcast.1.row_ref, s32[1]{0:T(128)} %bitcast.2.col_ref, bf16[4,160,128]{2,1,0:T(8,128)(2,1)S(1)} %pad_maximum_fusion.2.rows_ref, bf16[1536,128]{1,0:T(8,128)(2,1)S(1)} %get-tuple-element.79.flux_ref, ...), custom_call_target="tpu_custom_call" | custom-call | tf_op jit(solution)/shard_map/update/pallas_call | solution.py:311
  64.8 4.6 %all-to-all-start = ((bf16[8,64,128]{2,1,0:T(8,128)(2,1)}), bf16[8,64,128]{2,1,0:T(8,128)(2,1)S(1)}, u32[]{:S(2)}, u32[]{:S(2)}) async-start(bf16[8,64,128]{2,1,0:T(8,128)(2,1)} %bitcast.25), calls=%async_computation | async-start | bytes 262144 | tf_op jit(solution)/shard_map/all_to_all | solution.py:472
  69.4 0.8 settle.1
  70.1 6.6 %all-to-all-done = bf16[8,64,128]{2,1,0:T(8,128)(2,1)S(1)} async-done(((bf16[8,64,128]{2,1,0:T(8,128)(2,1)}), bf16[8,64,128]{2,1,0:T(8,128)(2,1)S(1)}, u32[]{:S(2)}, u32[]{:S(2)}) %all-to-all-start) | async-done | bytes 131104 | tf_op jit(solution)/shard_map/all_to_all | solution.py:472
  76.7 0.2 coarse_product.5
  77.0 3.3 %collective-permute-done.24 = bf16[128,128]{1,0:T(8,128)(2,1)S(1)} collective-permute-done((bf16[128,128]{1,0:T(8,128)(2,1)S(1)}, bf16[128,128]{1,0:T(8,128)(2,1)S(1)}, u32[]{:S(2)}, u32[]{:S(2)}) %collective-permute-start.24) | collective-permute-done | bytes 32800 | tf_op jit(solution)/shard_map/ppermute | solution.py:363
  80.5 1.2 %collective-permute-done.25 = bf16[64,128]{1,0:T(8,128)(2,1)S(1)} collective-permute-done((bf16[64,128]{1,0:T(8,128)(2,1)S(1)}, bf16[64,128]{1,0:T(8,128)(2,1)S(1)}, u32[]{:S(2)}, u32[]{:S(2)}) %collective-permute-start.25) | collective-permute-done | bytes 16416 | tf_op jit(solution)/shard_map/ppermute | solution.py:363
  81.6 1.0 %finish.1 = bf16[1536,128]{1,0:T(8,128)(2,1)} custom-call(f32[1536,128]{1,0:T(8,128)S(1)} %get-tuple-element.91.before_ref, bf16[1536,128]{1,0:T(8,128)(2,1)S(1)} %get-tuple-element.62.refs_5_.tall_ref, bf16[64,128]{1,0:T(8,128)(2,1)S(1)} %add_convert_fusion.2.own_ref), custom_call_target="tpu_custom_call" | custom-call | tf_op jit(solution)/shard_map/finish/pallas_call | solution.py:281
  (64 shorter events, 1.2 us)
Async XLA Ops:
  0.6 10.2 %collective-permute-start = (bf16[256,512]{1,0:T(8,128)(2,1)}, bf16[256,512]{1,0:T(8,128)(2,1)S(1)}, u32[]{:S(2)}, u32[]{:S(2)}) collective-permute-start(bf16[256,512]{1,0:T(8,128)(2,1)} %refs_0_.2), channel_id=1, source_target_pairs={{0,4},{4,0},{8,12},{12,8},{16,20},{20,16},{24,28},{28,24},{1,5},{5... | collective-permute-start | bytes 786440 | tf_op jit(solution)/shard_map/ppermute | solution.py:363
  3.6 0.7 copy-start.3
  4.3 14.3 %copy-start = (bf16[1,1,1536,128]{3,2,1,0:T(8,128)(2,1)S(1)}, bf16[1,1,1536,128]{3,2,1,0:T(8,128)(2,1)}, u32[]{:S(2)}) copy-start(bf16[1,1,1536,128]{3,2,1,0:T(8,128)(2,1)} %param.9) | copy-start | bytes 1179652
  4.3 19.3 %copy-start.2 = (bf16[1,1,1536,128]{3,2,1,0:T(8,128)(2,1)S(1)}, bf16[1,1,1536,128]{3,2,1,0:T(8,128)(2,1)}, u32[]{:S(2)}) copy-start(bf16[1,1,1536,128]{3,2,1,0:T(8,128)(2,1)} %param.8) | copy-start | bytes 1179652
  10.9 1.7 %collective-permute-start.1 = (bf16[160,128]{1,0:T(8,128)(2,1)S(1)}, bf16[160,128]{1,0:T(8,128)(2,1)S(1)}, u32[]{:S(2)}, u32[]{:S(2)}) collective-permute-start(bf16[160,128]{1,0:T(8,128)(2,1)S(1)} %get-tuple-element.116), channel_id=1, source_target_pairs={{0,1},{1,0},{2,3},{3,2},{4,5},{5,4},{6,7},{7,6},{8,9},{9,8},{10,11... | collective-permute-start | bytes 122888 | tf_op jit(solution)/shard_map/ppermute | solution.py:363
  11.0 3.5 %collective-permute-start.2 = (bf16[160,128]{1,0:T(8,128)(2,1)S(1)}, bf16[160,128]{1,0:T(8,128)(2,1)S(1)}, u32[]{:S(2)}, u32[]{:S(2)}) collective-permute-start(bf16[160,128]{1,0:T(8,128)(2,1)S(1)} %get-tuple-element.117), channel_id=1, source_target_pairs={{0,3},{1,2},{2,1},{3,0},{4,7},{5,6},{6,5},{7,4},{8,11},{9,10},{10,... | collective-permute-start | bytes 122888 | tf_op jit(solution)/shard_map/ppermute | solution.py:380
  14.5 4.1 %collective-permute-start.3 = (bf16[160,128]{1,0:T(8,128)(2,1)S(1)}, bf16[160,128]{1,0:T(8,128)(2,1)S(1)}, u32[]{:S(2)}, u32[]{:S(2)}) collective-permute-start(bf16[160,128]{1,0:T(8,128)(2,1)S(1)} %get-tuple-element.130), channel_id=1, source_target_pairs={{0,4},{4,0},{8,12},{12,8},{16,20},{20,16},{24,28},{28,24},{1,5},{5... | collective-permute-start | bytes 122888 | tf_op jit(solution)/shard_map/ppermute | solution.py:363
  15.6 3.0 %collective-permute-start.4 = (bf16[160,128]{1,0:T(8,128)(2,1)S(1)}, bf16[160,128]{1,0:T(8,128)(2,1)S(1)}, u32[]{:S(2)}, u32[]{:S(2)}) collective-permute-start(bf16[160,128]{1,0:T(8,128)(2,1)S(1)} %get-tuple-element.131), channel_id=1, source_target_pairs={{0,1},{1,0},{2,3},{3,2},{4,8},{5,9},{6,10},{7,11},{8,4},{9,5},{10,... | collective-permute-start | bytes 122888 | tf_op jit(solution)/shard_map/ppermute | solution.py:380
  15.8 10.7 %collective-permute-start.6 = (bf16[256,512]{1,0:T(8,128)(2,1)S(1)}, bf16[256,512]{1,0:T(8,128)(2,1)S(1)}, u32[]{:S(2)}, u32[]{:S(2)}) collective-permute-start(bf16[256,512]{1,0:T(8,128)(2,1)S(1)} %collective-permute-done.refs_1_), channel_id=1, source_target_pairs={{4,0},{0,8},{8,16},{16,24},{24,28},{28,20},{20,12},{12,4},{5,1},{1... | collective-permute-start | bytes 786440 | tf_op jit(solution)/shard_map/ppermute | solution.py:386
  19.1 7.4 %collective-permute-start.5 = (bf16[64,128]{1,0:T(8,128)(2,1)S(1)}, bf16[64,128]{1,0:T(8,128)(2,1)S(1)}, u32[]{:S(2)}, u32[]{:S(2)}) collective-permute-start(bf16[64,128]{1,0:T(8,128)(2,1)S(1)} %get-tuple-element.57), channel_id=1, source_target_pairs={{0,16},{4,20},{8,24},{12,28},{16,0},{20,4},{24,8},{28,12},{1,17},{... | collective-permute-start | bytes 49160 | tf_op jit(solution)/shard_map/ppermute | solution.py:363
  23.6 11.2 %copy-start.1 = (bf16[256,512]{1,0:T(8,128)(2,1)S(1)}, bf16[256,512]{1,0:T(8,128)(2,1)}, u32[]{:S(2)}) copy-start(bf16[256,512]{1,0:T(8,128)(2,1)} %refs_0_.2) | copy-start | bytes 786436
  26.5 4.0 %collective-permute-start.11 = (bf16[2,64,128]{2,1,0:T(8,128)(2,1)S(1)}, bf16[2,64,128]{2,1,0:T(8,128)(2,1)S(1)}, u32[]{:S(2)}, u32[]{:S(2)}) collective-permute-start(bf16[2,64,128]{2,1,0:T(8,128)(2,1)S(1)} %pad_maximum_fusion.13), channel_id=1, source_target_pairs={{0,8},{4,12},{8,0},{12,4},{16,24},{20,28},{24,16},{28,20},{1,9},{5... | collective-permute-start | bytes 98312 | tf_op jit(solution)/shard_map/ppermute | solution.py:363
  28.2 4.2 %collective-permute-start.7 = (bf16[160,256]{1,0:T(8,128)(2,1)S(1)}, bf16[160,256]{1,0:T(8,128)(2,1)S(1)}, u32[]{:S(2)}, u32[]{:S(2)}) collective-permute-start(bf16[160,256]{1,0:T(8,128)(2,1)S(1)} %get-tuple-element.102), channel_id=1, source_target_pairs={{0,1},{1,0},{2,3},{3,2},{4,5},{5,4},{6,7},{7,6},{8,9},{9,8},{10,11... | collective-permute-start | bytes 245768 | tf_op jit(solution)/shard_map/ppermute | solution.py:363
  28.2 4.2 %collective-permute-start.8 = (bf16[160,256]{1,0:T(8,128)(2,1)S(1)}, bf16[160,256]{1,0:T(8,128)(2,1)S(1)}, u32[]{:S(2)}, u32[]{:S(2)}) collective-permute-start(bf16[160,256]{1,0:T(8,128)(2,1)S(1)} %get-tuple-element.103), channel_id=1, source_target_pairs={{0,3},{1,2},{2,1},{3,0},{4,7},{5,6},{6,5},{7,4},{8,11},{9,10},{10,... | collective-permute-start | bytes 245768 | tf_op jit(solution)/shard_map/ppermute | solution.py:380
  30.5 4.3 %collective-permute-start.12 = (bf16[4,64,128]{2,1,0:T(8,128)(2,1)S(1)}, bf16[4,64,128]{2,1,0:T(8,128)(2,1)S(1)}, u32[]{:S(2)}, u32[]{:S(2)}) collective-permute-start(bf16[4,64,128]{2,1,0:T(8,128)(2,1)S(1)} %pad_maximum_fusion.7), channel_id=1, source_target_pairs={{0,4},{4,0},{8,12},{12,8},{16,20},{20,16},{24,28},{28,24},{1,5},{5... | collective-permute-start | bytes 196616 | tf_op jit(solution)/shard_map/ppermute | solution.py:363
  32.6 5.7 %collective-permute-start.9 = (bf16[160,256]{1,0:T(8,128)(2,1)S(1)}, bf16[160,256]{1,0:T(8,128)(2,1)S(1)}, u32[]{:S(2)}, u32[]{:S(2)}) collective-permute-start(bf16[160,256]{1,0:T(8,128)(2,1)S(1)} %get-tuple-element.106), channel_id=1, source_target_pairs={{0,4},{4,0},{8,12},{12,8},{16,20},{20,16},{24,28},{28,24},{1,5},{5... | collective-permute-start | bytes 245768 | tf_op jit(solution)/shard_map/ppermute | solution.py:363
  34.3 4.0 %collective-permute-start.10 = (bf16[160,256]{1,0:T(8,128)(2,1)S(1)}, bf16[160,256]{1,0:T(8,128)(2,1)S(1)}, u32[]{:S(2)}, u32[]{:S(2)}) collective-permute-start(bf16[160,256]{1,0:T(8,128)(2,1)S(1)} %get-tuple-element.107), channel_id=1, source_target_pairs={{0,1},{1,0},{2,3},{3,2},{4,8},{5,9},{6,10},{7,11},{8,4},{9,5},{10,... | collective-permute-start | bytes 245768 | tf_op jit(solution)/shard_map/ppermute | solution.py:380
  35.2 5.8 %collective-permute-start.13 = (bf16[3,192,128]{2,1,0:T(8,128)(2,1)S(1)}, bf16[3,192,128]{2,1,0:T(8,128)(2,1)S(1)}, u32[]{:S(2)}, u32[]{:S(2)}) collective-permute-start(bf16[3,192,128]{2,1,0:T(8,128)(2,1)S(1)} %get-tuple-element.72), channel_id=1, source_target_pairs={{0,2},{1,3},{2,0},{3,1},{4,6},{5,7},{6,4},{7,5},{8,10},{9,11},{10,... | collective-permute-start | bytes 442376 | tf_op jit(solution)/shard_map/ppermute | solution.py:363
  41.1 1.4 %collective-permute-start.14 = (bf16[3,192,128]{2,1,0:T(8,128)(2,1)S(1)}, bf16[3,192,128]{2,1,0:T(8,128)(2,1)S(1)}, u32[]{:S(2)}, u32[]{:S(2)}) collective-permute-start(bf16[3,192,128]{2,1,0:T(8,128)(2,1)S(1)} %fusion), channel_id=1, source_target_pairs={{0,1},{1,0},{2,3},{3,2},{4,5},{5,4},{6,7},{7,6},{8,9},{9,8},{10,11... | collective-permute-start | bytes 442376 | tf_op jit(solution)/shard_map/ppermute | solution.py:363
  43.2 4.8 %collective-permute-start.15 = (bf16[64,128]{1,0:T(8,128)(2,1)S(1)}, bf16[64,128]{1,0:T(8,128)(2,1)S(1)}, u32[]{:S(2)}, u32[]{:S(2)}) collective-permute-start(bf16[64,128]{1,0:T(8,128)(2,1)S(1)} %get-tuple-element.73), channel_id=1, source_target_pairs={{0,16},{4,20},{8,24},{12,28},{16,0},{20,4},{24,8},{28,12},{1,17},{... | collective-permute-start | bytes 49160 | tf_op jit(solution)/shard_map/ppermute | solution.py:363
  48.0 4.0 %collective-permute-start.20 = (bf16[2,64,128]{2,1,0:T(8,128)(2,1)S(1)}, bf16[2,64,128]{2,1,0:T(8,128)(2,1)S(1)}, u32[]{:S(2)}, u32[]{:S(2)}) collective-permute-start(bf16[2,64,128]{2,1,0:T(8,128)(2,1)S(1)} %pad_maximum_fusion.14), channel_id=1, source_target_pairs={{0,8},{4,12},{8,0},{12,4},{16,24},{20,28},{24,16},{28,20},{1,9},{5... | collective-permute-start | bytes 98312 | tf_op jit(solution)/shard_map/ppermute | solution.py:363
  49.5 3.9 %collective-permute-start.16 = (bf16[160,128]{1,0:T(8,128)(2,1)S(1)}, bf16[160,128]{1,0:T(8,128)(2,1)S(1)}, u32[]{:S(2)}, u32[]{:S(2)}) collective-permute-start(bf16[160,128]{1,0:T(8,128)(2,1)S(1)} %get-tuple-element.112), channel_id=1, source_target_pairs={{0,1},{1,0},{2,3},{3,2},{4,5},{5,4},{6,7},{7,6},{8,9},{9,8},{10,11... | collective-permute-start | bytes 122888 | tf_op jit(solution)/shard_map/ppermute | solution.py:363
  49.5 3.9 %collective-permute-start.17 = (bf16[160,128]{1,0:T(8,128)(2,1)S(1)}, bf16[160,128]{1,0:T(8,128)(2,1)S(1)}, u32[]{:S(2)}, u32[]{:S(2)}) collective-permute-start(bf16[160,128]{1,0:T(8,128)(2,1)S(1)} %get-tuple-element.113), channel_id=1, source_target_pairs={{0,3},{1,2},{2,1},{3,0},{4,7},{5,6},{6,5},{7,4},{8,11},{9,10},{10,... | collective-permute-start | bytes 122888 | tf_op jit(solution)/shard_map/ppermute | solution.py:380
  52.0 4.3 %collective-permute-start.21 = (bf16[4,64,128]{2,1,0:T(8,128)(2,1)S(1)}, bf16[4,64,128]{2,1,0:T(8,128)(2,1)S(1)}, u32[]{:S(2)}, u32[]{:S(2)}) collective-permute-start(bf16[4,64,128]{2,1,0:T(8,128)(2,1)S(1)} %pad_maximum_fusion.8), channel_id=1, source_target_pairs={{0,4},{4,0},{8,12},{12,8},{16,20},{20,16},{24,28},{28,24},{1,5},{5... | collective-permute-start | bytes 196616 | tf_op jit(solution)/shard_map/ppermute | solution.py:363
  56.8 5.2 %collective-permute-start.22 = (bf16[3,192,128]{2,1,0:T(8,128)(2,1)S(1)}, bf16[3,192,128]{2,1,0:T(8,128)(2,1)S(1)}, u32[]{:S(2)}, u32[]{:S(2)}) collective-permute-start(bf16[3,192,128]{2,1,0:T(8,128)(2,1)S(1)} %get-tuple-element.85), channel_id=1, source_target_pairs={{0,2},{1,3},{2,0},{3,1},{4,6},{5,7},{6,4},{7,5},{8,10},{9,11},{10,... | collective-permute-start | bytes 442376 | tf_op jit(solution)/shard_map/ppermute | solution.py:363
  58.4 4.1 %collective-permute-start.18 = (bf16[160,128]{1,0:T(8,128)(2,1)S(1)}, bf16[160,128]{1,0:T(8,128)(2,1)S(1)}, u32[]{:S(2)}, u32[]{:S(2)}) collective-permute-start(bf16[160,128]{1,0:T(8,128)(2,1)S(1)} %get-tuple-element.120), channel_id=1, source_target_pairs={{0,4},{4,0},{8,12},{12,8},{16,20},{20,16},{24,28},{28,24},{1,5},{5... | collective-permute-start | bytes 122888 | tf_op jit(solution)/shard_map/ppermute | solution.py:363
  59.7 2.7 %collective-permute-start.19 = (bf16[160,128]{1,0:T(8,128)(2,1)S(1)}, bf16[160,128]{1,0:T(8,128)(2,1)S(1)}, u32[]{:S(2)}, u32[]{:S(2)}) collective-permute-start(bf16[160,128]{1,0:T(8,128)(2,1)S(1)} %get-tuple-element.121), channel_id=1, source_target_pairs={{0,1},{1,0},{2,3},{3,2},{4,8},{5,9},{6,10},{7,11},{8,4},{9,5},{10,... | collective-permute-start | bytes 122888 | tf_op jit(solution)/shard_map/ppermute | solution.py:380
  62.0 1.4 %collective-permute-start.23 = (bf16[3,192,128]{2,1,0:T(8,128)(2,1)S(1)}, bf16[3,192,128]{2,1,0:T(8,128)(2,1)S(1)}, u32[]{:S(2)}, u32[]{:S(2)}) collective-permute-start(bf16[3,192,128]{2,1,0:T(8,128)(2,1)S(1)} %fusion.1), channel_id=1, source_target_pairs={{0,1},{1,0},{2,3},{3,2},{4,5},{5,4},{6,7},{7,6},{8,9},{9,8},{10,11... | collective-permute-start | bytes 442376 | tf_op jit(solution)/shard_map/ppermute | solution.py:363
  64.8 12.0 %all-to-all-start = ((bf16[8,64,128]{2,1,0:T(8,128)(2,1)}), bf16[8,64,128]{2,1,0:T(8,128)(2,1)S(1)}, u32[]{:S(2)}, u32[]{:S(2)}) async-start(bf16[8,64,128]{2,1,0:T(8,128)(2,1)} %bitcast.25), calls=%async_computation | async-start | bytes 262144 | tf_op jit(solution)/shard_map/all_to_all | solution.py:472
  76.9 3.4 %collective-permute-start.24 = (bf16[128,128]{1,0:T(8,128)(2,1)S(1)}, bf16[128,128]{1,0:T(8,128)(2,1)S(1)}, u32[]{:S(2)}, u32[]{:S(2)}) collective-permute-start(bf16[128,128]{1,0:T(8,128)(2,1)S(1)} %bitcast.47), channel_id=1, source_target_pairs={{0,3},{1,2},{2,1},{3,0},{4,7},{5,6},{6,5},{7,4},{8,11},{9,10},{10,... | collective-permute-start | bytes 98312 | tf_op jit(solution)/shard_map/ppermute | solution.py:363
  80.4 1.2 %collective-permute-start.25 = (bf16[64,128]{1,0:T(8,128)(2,1)S(1)}, bf16[64,128]{1,0:T(8,128)(2,1)S(1)}, u32[]{:S(2)}, u32[]{:S(2)}) collective-permute-start(bf16[64,128]{1,0:T(8,128)(2,1)S(1)} %select_convert_fusion), channel_id=1, source_target_pairs={{0,1},{1,0},{2,3},{3,2},{4,5},{5,4},{6,7},{7,6},{8,9},{9,8},{10,11... | collective-permute-start | bytes 49160 | tf_op jit(solution)/shard_map/ppermute | solution.py:363

commit v9 on v8

--- a/solution.py
+++ b/solution.py
@@ -21,7 +21,6 @@
 hbm = pl.BlockSpec(memory_space=pl.ANY)
 shape_of = jax.ShapeDtypeStruct
 params = pltpu.CompilerParams(vmem_limit_bytes=16 * 1024 * 1024)
-large = pltpu.CompilerParams(vmem_limit_bytes=16 * 1024 * 1024)
 
 
 def dot(a, b):
@@ -37,86 +36,118 @@
         at += size
 
 
-def load_kernel(face, chunk, ahead, u_hbm, k_hbm, s_hbm, nodes_hbm, mode_hbm, weight_ref, flux_ref, packed_ref, sel_ref, selt_ref, basis_ref, tall_ref, k_ref, s_ref, mixed, u_ref, nodes_ref, mode_ref, sems, small_sems):
-    count = u_ref.shape[0] // chunk
-    small = ((u_hbm, u_ref), (nodes_hbm, nodes_ref), (mode_hbm, mode_ref))
-    small = [pltpu.make_async_copy(*pair, small_sems.at[i]) for i, pair in enumerate(small)]
+def load_kernel(face, chunk, ahead, u_hbm, k_hbm, s_hbm, nodes_hbm, flux_ref, packed_ref, mixed, sel_ref, selt_ref, k_ref, s_ref, u_ref, nodes_ref, sems, small_sems):
+    small = [
+        pltpu.make_async_copy(nodes_hbm, nodes_ref, small_sems.at[0]),
+        pltpu.make_async_copy(u_hbm, u_ref, small_sems.at[1]),
+    ]
     for copy in small:
         copy.start()
-    copies = []
+    parts, copies = [], []
     for which, (source, target) in enumerate(((k_hbm, k_ref), (s_hbm, s_ref))):
-        for i in range(count):
+        for i in range(target.shape[0] // chunk):
             rows = pl.ds(i * chunk, chunk)
+            parts.append((which, rows))
             copies.append(pltpu.make_async_copy(source.at[rows], target.at[rows], sems.at[which, i]))
     for copy in copies[:ahead]:
         copy.start()
-    modes = basis_ref.shape[0]
+    for copy in small:
+        copy.wait()
     slot = lax.broadcasted_iota(jnp.int32, (face, face), 0)
-    mode = lax.broadcasted_iota(jnp.int32, (modes, LANES), 0)
-    blocks = u_ref.shape[0] // LANES
-
-    def prepare(step, steps):
-        for d in range(8 * step // steps, 8 * (step + 1) // steps):
+    u = u_ref[...]
+    for i, (which, rows) in enumerate(parts):
+        for d in range(8 * i // len(parts), 8 * (i + 1) // len(parts)):
             chosen = (slot == nodes_ref[d : d + 1, :] - d * face).astype(f32)
             selt_ref[d] = chosen.astype(bf16)
             sel_ref[d] = chosen.T.astype(bf16)
-        for i in range(blocks * step // steps, blocks * (step + 1) // steps):
-            rows = pl.ds(i * LANES, LANES)
-            part = jnp.where(mode == mode_ref[:, rows], weight_ref[:, rows].astype(f32), 0.0)
-            basis_ref[:, rows] = part.astype(bf16)
-            tall_ref[rows, :] = jnp.concatenate([part] * (LANES // modes)).T.astype(bf16)
-
-    for copy in small:
-        copy.wait()
-    u = u_ref[...]
-    for i in range(2 * count):
-        prepare(i, 2 * count)
         copies[i].wait()
-        if i + ahead < 2 * count:
+        if i + ahead < len(parts):
             copies[i + ahead].start()
-        rows = pl.ds(i % count * chunk, chunk)
-        if i < count:
+        if which == 0:
             mixed[rows, :] = (0.5 * u_ref[rows, :].astype(f32) + dot(k_ref[rows, :], u)).astype(bf16)
         else:
             flux_ref[rows, :] = dot(s_ref[rows, :], mixed[...]).astype(bf16)
     pick(face, sel_ref, flux_ref, packed_ref)
 
 
-def load_products(trace, kernel, inverse, nodes, mode, weight):
+def load_products(trace, kernel, inverse, nodes):
     count, width = trace.shape
     face = nodes.shape[1]
-    chunk = 256 if count % 256 == 0 else count
-    return pl.pallas_call(
-        functools.partial(load_kernel, face, chunk, 3),
+    chunk = 256 if count % 256 == 0 and 8 * face % 256 == 0 else face
+    return pl.pallas_call(
+        functools.partial(load_kernel, face, chunk, 4),
         out_shape=[
+            shape_of((8 * face, width), bf16),
+            shape_of((4 * (face + face // 8), width), bf16),
             shape_of((count, width), bf16),
-            shape_of((4 * (face + face // 8), width), bf16),
             shape_of((8, face, face), bf16),
             shape_of((8, face, face), bf16),
-            shape_of((MODES, count), bf16),
-            shape_of((count, LANES), bf16),
             pltpu.VMEM((count, count), bf16),
-            pltpu.VMEM((count, count), bf16),
+            pltpu.VMEM((8 * face, count), bf16),
         ],
-        in_specs=[hbm] * 5 + [vmem],
-        out_specs=[vmem] * 8,
+        in_specs=[hbm] * 4,
+        out_specs=[vmem] * 7,
         scratch_shapes=[
             pltpu.VMEM((count, width), bf16),
-            pltpu.VMEM((count, width), bf16),
             pltpu.VMEM(nodes.shape, jnp.int32),
-            pltpu.VMEM(mode.shape, jnp.int32),
             pltpu.SemaphoreType.DMA((2, count // chunk)),
-            pltpu.SemaphoreType.DMA((3,)),
+            pltpu.SemaphoreType.DMA((2,)),
         ],
-        compiler_params=large,
+        compiler_params=params,
         cost_estimate=pl.CostEstimate(
             flops=4 * count * count * 2 * LANES, bytes_accessed=4 * count * count, transcendentals=0
         ),
         name="load_products",
-    )(trace, kernel, inverse, nodes, mode, weight)
-
-
-def products_kernel(face, chunk, state_ref, res_ref, k_ref, s_ref, sel_ref, tall_ref, c_ref, u_ref, flux_ref, packed_ref, entering, mixed):
+    )(trace, kernel, inverse, nodes)
+
+
+def load_rest_kernel(mixed_ref, s_hbm, flux_ref, s_ref, sem):
+    rest = s_ref.shape[0]
+    copy = pltpu.make_async_copy(s_hbm.at[pl.ds(s_hbm.shape[0] - rest, rest)], s_ref, sem)
+    copy.start()
+    copy.wait()
+    flux_ref[...] = dot(s_ref[...], mixed_ref[...]).astype(bf16)
+
+
+def load_rest(mixed, inverse, rest):
+    count, width = mixed.shape
+    return pl.pallas_call(
+        load_rest_kernel,
+        out_shape=[shape_of((rest, width), bf16), pltpu.VMEM((rest, count), bf16)],
+        in_specs=[vmem, hbm],
+        out_specs=[vmem] * 2,
+        scratch_shapes=[pltpu.SemaphoreType.DMA],
+        compiler_params=params,
+        cost_estimate=pl.CostEstimate(
+            flops=2 * rest * count * LANES, bytes_accessed=2 * rest * count, transcendentals=0
+        ),
+        name="load_rest",
+    )(mixed, inverse)
+
+
+def prepare_kernel(mode_ref, weight_ref, basis_ref, tall_ref):
+    modes = basis_ref.shape[0]
+    mode = lax.broadcasted_iota(jnp.int32, (modes, LANES), 0)
+    for i in range(tall_ref.shape[0] // LANES):
+        rows = pl.ds(i * LANES, LANES)
+        part = jnp.where(mode == mode_ref[:, rows], weight_ref[:, rows].astype(f32), 0.0)
+        basis_ref[:, rows] = part.astype(bf16)
+        tall_ref[rows, :] = jnp.concatenate([part] * (LANES // modes)).T.astype(bf16)
+
+
+def prepare(mode, weight):
+    count = mode.shape[1]
+    return pl.pallas_call(
+        prepare_kernel,
+        out_shape=[shape_of((MODES, count), bf16), shape_of((count, LANES), bf16)],
+        in_specs=[vmem] * 2,
+        out_specs=[vmem] * 2,
+        compiler_params=params,
+        name="prepare",
+    )(mode, weight)
+
+
+def products_kernel(face, chunk, state_ref, res_ref, k_ref, top_ref, rest_ref, sel_ref, tall_ref, c_ref, u_ref, flux_ref, packed_ref, entering, mixed):
     count, width = u_ref.shape
     for i in range(count // chunk):
         rows = pl.ds(i * chunk, chunk)
@@ -132,22 +163,24 @@
         rows = pl.ds(i * chunk, chunk)
         mixed[rows, :] = (0.5 * entering[rows, :].astype(f32) + dot(k_ref[rows, :], u)).astype(bf16)
     m = mixed[...]
-    for i in range(count // chunk):
-        rows = pl.ds(i * chunk, chunk)
-        flux_ref[rows, :] = dot(s_ref[rows, :], m).astype(bf16)
+    top = top_ref.shape[0]
+    for i in range(0, top, chunk):
+        flux_ref[i : i + chunk, :] = dot(top_ref[i : i + chunk, :], m).astype(bf16)
+    for i in range(0, count - top, chunk):
+        flux_ref[top + i : top + i + chunk, :] = dot(rest_ref[i : i + chunk, :], m).astype(bf16)
     pick(face, sel_ref, flux_ref, packed_ref)
 
 
 def products(state, residual, kernel, inverse, selector, tall, own):
     count, width = state.shape
     face = selector.shape[1]
-    chunk = 256 if count % 256 == 0 else count
+    chunk = 256 if count % 256 == 0 and 8 * face % 256 == 0 else face
     wide = width + LANES if own is None else width
-    operands = [state, residual, kernel, inverse, selector, tall]
+    operands = [state, residual, kernel, *inverse, selector, tall]
     body = functools.partial(products_kernel, face, chunk)
     if own is None:
         inner = body
-        body = lambda *refs: inner(*refs[:6], None, *refs[6:])
+        body = lambda *refs: inner(*refs[:7], None, *refs[7:])
     else:
         operands.append(own)
     return pl.pallas_call(
@@ -197,7 +230,7 @@
     )(selector_t, wide, wide_rows)
 
 
-def first_update_kernel(rows_ref, flux_ref, load_ref, selt_ref, basis_ref, res_ref, rhs_ref):
+def first_update_kernel(rows_ref, flux_ref, rest_ref, load_ref, selt_ref, basis_ref, res_ref, rhs_ref):
     face = selt_ref.shape[1]
     for d, (group, at, size) in enumerate(arrivals(face)):
         band = slice(d * face, (d + 1) * face)
@@ -205,7 +238,7 @@
         assembled = flux_ref[band, :].astype(f32) + placed
         res_ref[band, :] = (load_ref[band, :].astype(f32) - assembled).astype(bf16)
     rest = slice(8 * face, None)
-    res_ref[rest, :] = (load_ref[rest, :].astype(f32) - flux_ref[rest, :].astype(f32)).astype(bf16)
+    res_ref[rest, :] = (load_ref[rest, :].astype(f32) - rest_ref[...].astype(f32)).astype(bf16)
     rhs_ref[...] = dot(basis_ref[...], res_ref[...]).astype(bf16)
 
 
@@ -298,11 +331,11 @@
     face = selector_t.shape[1]
     outs = [shape_of((count, width), bf16), shape_of((copies * modes, width), bf16)]
     if coarse is None:
-        operands = [rows, flux, load, selector_t, basis]
+        operands = [rows, *flux, load, selector_t, basis]
         return pl.pallas_call(
             first_update_kernel,
             out_shape=outs,
-            in_specs=[vmem] * 5,
+            in_specs=[vmem] * 6,
             out_specs=[vmem] * 2,
             compiler_params=params,
             name="first_update",
@@ -386,22 +419,29 @@
     return lax.ppermute(value, axis, [(ring[i - 1], ring[i]) for i in range(n)])
 
 
-def trade(forward, backward, axis):
-    even = lax.axis_index(axis) % 2 == 0
+def trade(forward, backward, axis, even, meanwhile=None, first=()):
     near = swap(jnp.where(even, forward, backward), axis, 1)
-    far = cross(jnp.where(even, backward, forward), axis)
-    return jnp.where(even, near, far), jnp.where(even, far, near)
-
-
-def exchange(packed, face):
+    far = jnp.where(even, backward, forward)
+    far, first = lax.optimization_barrier((far, first))
+    far = cross(far, axis)
+    done = None
+    if meanwhile is not None:
+        near, done = meanwhile(near)
+        far, done = lax.optimization_barrier((far, done))
+    return jnp.where(even, near, far), jnp.where(even, far, near), done, first
+
+
+def exchange(packed, face, even, meanwhile=None, first=()):
     corner = face // 8
     group = face + 2 * corner
-    right, left = trade(packed[:group], packed[group : 2 * group], "col")
+    right, left, done, first = trade(
+        packed[:group], packed[group : 2 * group], "col", even[1], meanwhile, first
+    )
     six, one = packed[2 * group : 2 * group + face], packed[2 * group + face :]
     up = jnp.concatenate([six, right[face + corner :], left[face + corner :]])
     down = jnp.concatenate([one, right[face : face + corner], left[face : face + corner]])
-    above, below = trade(up, down, "sub")
-    return jnp.stack([right, left, above, below])
+    above, below, _, _ = trade(up, down, "sub", even[0])
+    return jnp.stack([right, left, above, below]), done, first
 
 
 def sum_over_columns(value, sent):
@@ -447,19 +487,24 @@
 
     half = cols // 2
     place = [jnp.reshape(index, (1,)).astype(jnp.int32) for index in (row, col)]
-    trace, place = lax.optimization_barrier((trace, place))
-
-    flux, packed, selector, selector_t, basis, tall, kernel, inverse = load_products(
-        *(
-            pltpu.with_memory_space_constraint(whole, pltpu.HBM)
-            for whole in (trace, double_layer[0, 0], single_inverse[0, 0], interface, node_mode[0])
-        ),
-        mode_weight[0],
+    even = [row % 2 == 0, col % 2 == 0]
+    trace, place, even = lax.optimization_barrier((trace, place, even))
+
+    in_hbm = lambda value: pltpu.with_memory_space_constraint(value, pltpu.HBM)
+    inverse = in_hbm(single_inverse[0, 0])
+    edge, packed, mixed, selector, selector_t, kernel, top = load_products(
+        in_hbm(trace), in_hbm(double_layer[0, 0]), inverse, in_hbm(interface)
     )
     near = swap(coarse_inverse, "sub", 1)
-    packed, near = lax.optimization_barrier((packed, near))
+
+    def beside(near):
+        near, ready = lax.optimization_barrier((near, mixed))
+        return near, load_rest(ready, inverse, trace.shape[0] - edge.shape[0])
+
+    basis, tall = prepare(node_mode[0], mode_weight[0])
+    rows, (beyond, bottom), near = exchange(packed, face, even, beside, near)
     matrices = [coarse_inverse, near, onward(near, "sub")]
-    rows = exchange(packed, face)
+    inverse, flux = (top, bottom), (edge, beyond)
     state, own, coarse, wide, coupling = trace, None, None, None, None
     for iteration in range(ITERS):
         last = iteration == ITERS - 1
@@ -482,7 +527,7 @@
         pieces = jnp.stack([rhs, swap(rhs, "sub", bits[0])])
         state, flux, packed = products(state, residual, kernel, inverse, selector, tall, own)
         pieces, packed, matrices = lax.optimization_barrier((pieces, packed, matrices))
-        rows = exchange(packed, face)
+        rows, _, _ = exchange(packed, face, even)
         if iteration == 0:
             wide, wide_rows = flux[:, width:], rows[:, :, width:]
             flux, rows = flux[:, :width], rows[:, :, :width]

time: 83.1 us -> 82.8 us (level)
  starting transfers between devices: 35.2 us -> 33.8 us
  Pallas kernels: 17.3 us -> 18.6 us
    ppermute x19, waiting for transfers between devices: 19.1 us -> 20.9 us  [swap(): lax.ppermute(value, axis, [(i, i ^ mask) for i in range(lax.axis_size(axi...]
    ppermute x6, starting transfers between devices: 5.15 us -> 3.74 us  [cross(): return lax.ppermute(value, ('sub', 'col'), pairs)]
    ppermute x6, waiting for transfers between devices: 1.95 us -> 0.66 us  [cross(): return lax.ppermute(value, ('sub', 'col'), pairs)]
    pallas_call x2 -> x4, Pallas kernels: 6.95 us -> 8.2 us  [the longest x1 5.62 us: load_products(): pl.pallas_call(functools.partial(load_kernel, face, chunk, 4), out_shape=...]
    ppermute x19, starting transfers between devices: 23.1 us -> 24.1 us  [swap(): lax.ppermute(value, axis, [(i, i ^ mask) for i in range(lax.axis_size(axi...]
  transfers between devices with their start and end apart: 27 -> 27, of which waited for: 17 -> 15; matrix products, arithmetic and copies ran while one was open for 1% -> 1% of each run, Pallas kernels for 17% -> 18%
where the time goes in v9:
time: 82.8 us; the launch traced here: 82.5 us
  starting transfers between devices  33.8 us (41%)
  waiting for transfers between devices  28.2 us (34%)
  Pallas kernels  18.6 us (22%)
  between operations  1.24 us (1%)
    ppermute x19, starting transfers between devices, swap(): lax.ppermute(value, axis, [(i, i ^ mask) for i in range(lax.axis_size(axi...  24.1 us
    ppermute x19, waiting for transfers between devices, swap(): lax.ppermute(value, axis, [(i, i ^ mask) for i in range(lax.axis_size(axi...  20.9 us
    all_to_all x1, waiting for transfers between devices, local(): gathered = lax.all_to_all(rhs, 'sub', 0, 0, tiled=True)  6.58 us
    pallas_call x1, Pallas kernels, load_products(): pl.pallas_call(functools.partial(load_kernel, face, chunk, 4), out_shape=...  5.62 us
    pallas_call x2, Pallas kernels, products(): pl.pallas_call(body, out_shape=[shape_of((count, width), bf16), shape_of(...  5.6 us
    all_to_all x1, starting transfers between devices, local(): gathered = lax.all_to_all(rhs, 'sub', 0, 0, tiled=True)  4.19 us
    ppermute x6, starting transfers between devices, cross(): return lax.ppermute(value, ('sub', 'col'), pairs)  3.74 us
    pallas_call x1, Pallas kernels, load_rest(): pl.pallas_call(load_rest_kernel, out_shape=[shape_of((rest, width), bf16)...  1.99 us
  transfers between devices with their start and end apart: 27, of which 15 were waited for; matrix products, arithmetic and copies ran while one was open for 1% of the time, Pallas kernels for 18%

profile of v9, /device:TPU:0, one launch (start us, length us, event | category | flops | bytes accessed | tf_op | source)
XLA Modules:
  0.0 82.5 jit_solution(2848053380997261983)
XLA Ops:
  0.6 3.0 %collective-permute-start.1 = (bf16[256,512]{1,0:T(8,128)(2,1)}, bf16[256,512]{1,0:T(8,128)(2,1)S(1)}, u32[]{:S(2)}, u32[]{:S(2)}) collective-permute-start(bf16[256,512]{1,0:T(8,128)(2,1)} %refs_0_.2), channel_id=1, source_target_pairs={{0,4},{4,0},{8,12},{12,8},{16,20},{20,16},{24,28},{28,24},{1,5},{5... | collective-permute-start | bytes 786440 | tf_op jit(solution)/shard_map/ppermute | solution.py:396
  3.6 5.6 %load_products.1 = (bf16[1024,128]{1,0:T(8,128)(2,1)S(1)}, bf16[576,128]{1,0:T(8,128)(2,1)S(1)}, bf16[1536,128]{1,0:T(8,128)(2,1)S(1)}, bf16[8,128,128]{2,1,0:T(...) custom-call(bf16[1536,128]{1,0:T(8,128)(2,1)} %bitcast.42, ...), custom_call_target="tpu_custom_call" | custom-call | flops 2415919104 | bytes 9437184 | tf_op jit(solution)/shard_map/load_products/pallas_call | solution.py:77
  9.3 0.1 collective-permute-start
  9.4 0.7 collective-permute-done.1.refs_1_
  10.2 0.9 %collective-permute-start.2 = (bf16[160,128]{1,0:T(8,128)(2,1)S(1)}, bf16[160,128]{1,0:T(8,128)(2,1)S(1)}, u32[]{:S(2)}, u32[]{:S(2)}) collective-permute-start(bf16[160,128]{1,0:T(8,128)(2,1)S(1)} %get-tuple-element.66), channel_id=1, source_target_pairs={{0,3},{1,2},{2,1},{3,0},{4,7},{5,6},{6,5},{7,4},{8,11},{9,10},{10,... | collective-permute-start | bytes 122888 | tf_op jit(solution)/shard_map/ppermute | solution.py:413
  11.0 2.0 %load_rest.1 = (bf16[512,128]{1,0:T(8,128)(2,1)S(1)}, bf16[512,1536]{1,0:T(8,128)(2,1)S(1)}) custom-call(bf16[1536,128]{1,0:T(8,128)(2,1)S(1)} %get-tuple-element.67.mixed_ref, bf16[1536,1536]{1,0:T(8,128)(2,1)} %bitcast.50), custom_call_target="tpu_custom_call" | custom-call | flops 201326592 | bytes 1572864 | tf_op jit(solution)/shard_map/load_rest/pallas_call | solution.py:114
  13.0 0.7 collective-permute-done.2
  13.8 2.0 %collective-permute-start.3 = (bf16[160,128]{1,0:T(8,128)(2,1)S(1)}, bf16[160,128]{1,0:T(8,128)(2,1)S(1)}, u32[]{:S(2)}, u32[]{:S(2)}) collective-permute-start(bf16[160,128]{1,0:T(8,128)(2,1)S(1)} %get-tuple-element.150), channel_id=1, source_target_pairs={{0,4},{4,0},{8,12},{12,8},{16,20},{20,16},{24,28},{28,24},{1,5},{5... | collective-permute-start | bytes 122888 | tf_op jit(solution)/shard_map/ppermute | solution.py:396
  15.8 0.2 prepare.1
  16.0 1.8 %collective-permute-start.6 = (bf16[256,512]{1,0:T(8,128)(2,1)S(1)}, bf16[256,512]{1,0:T(8,128)(2,1)S(1)}, u32[]{:S(2)}, u32[]{:S(2)}) collective-permute-start(bf16[256,512]{1,0:T(8,128)(2,1)S(1)} %collective-permute-done.1.refs_1_), channel_id=1, source_target_pairs={{4,0},{0,8},{8,16},{16,24},{24,28},{28,20},{20,12},{12,4},{5,1},{1... | collective-permute-start | bytes 786440 | tf_op jit(solution)/shard_map/ppermute | solution.py:419
  17.9 0.4 first_update.1
  18.3 5.5 %collective-permute-start.5 = (bf16[64,128]{1,0:T(8,128)(2,1)S(1)}, bf16[64,128]{1,0:T(8,128)(2,1)S(1)}, u32[]{:S(2)}, u32[]{:S(2)}) collective-permute-start(bf16[64,128]{1,0:T(8,128)(2,1)S(1)} %get-tuple-element.76), channel_id=1, source_target_pairs={{0,16},{4,20},{8,24},{12,28},{16,0},{20,4},{24,8},{28,12},{1,17},{... | collective-permute-start | bytes 49160 | tf_op jit(solution)/shard_map/ppermute | solution.py:396
  23.8 2.7 %products.2 = (bf16[1536,128]{1,0:T(8,128)(2,1)S(1)}, bf16[1536,256]{1,0:T(8,128)(2,1)S(1)}, bf16[576,256]{1,0:T(8,128)(2,1)S(1)}) custom-call(bf16[1536,128]{1,0:T(8,128)(2,1)S(1)} %bitcast.43, bf16[1536,128]{1,0:T(8,128)(2,1)S(1)} %get-tuple-element.77.refs_1_, bf16[1536,1536]{1,0:T(8,128)(2,1)S(1)} %get-tuple-element.78.refs_2_.k_ref, ...), custom_call_target="tpu_custom_call" | custom-call | flops 2415919104 | bytes 9437184 | tf_op jit(solution)/shard_map/products/pallas_call | solution.py:186
  26.7 1.6 %collective-permute-start.11 = (bf16[2,64,128]{2,1,0:T(8,128)(2,1)S(1)}, bf16[2,64,128]{2,1,0:T(8,128)(2,1)S(1)}, u32[]{:S(2)}, u32[]{:S(2)}) collective-permute-start(bf16[2,64,128]{2,1,0:T(8,128)(2,1)S(1)} %pad_maximum_fusion.13), channel_id=1, source_target_pairs={{0,8},{4,12},{8,0},{12,4},{16,24},{20,28},{24,16},{28,20},{1,9},{5... | collective-permute-start | bytes 98312 | tf_op jit(solution)/shard_map/ppermute | solution.py:396
  28.4 1.3 %collective-permute-start.8 = (bf16[160,256]{1,0:T(8,128)(2,1)S(1)}, bf16[160,256]{1,0:T(8,128)(2,1)S(1)}, u32[]{:S(2)}, u32[]{:S(2)}) collective-permute-start(bf16[160,256]{1,0:T(8,128)(2,1)S(1)} %get-tuple-element.123), channel_id=1, source_target_pairs={{0,3},{1,2},{2,1},{3,0},{4,7},{5,6},{6,5},{7,4},{8,11},{9,10},{10,... | collective-permute-start | bytes 245768 | tf_op jit(solution)/shard_map/ppermute | solution.py:413
  29.7 1.0 %collective-permute-done.11 = bf16[2,64,128]{2,1,0:T(8,128)(2,1)S(1)} collective-permute-done((bf16[2,64,128]{2,1,0:T(8,128)(2,1)S(1)}, bf16[2,64,128]{2,1,0:T(8,128)(2,1)S(1)}, u32[]{:S(2)}, u32[]{:S(2)}) %collective-permute-start.11) | collective-permute-done | bytes 32800 | tf_op jit(solution)/shard_map/ppermute | solution.py:396
  30.7 2.0 %collective-permute-start.12 = (bf16[4,64,128]{2,1,0:T(8,128)(2,1)S(1)}, bf16[4,64,128]{2,1,0:T(8,128)(2,1)S(1)}, u32[]{:S(2)}, u32[]{:S(2)}) collective-permute-start(bf16[4,64,128]{2,1,0:T(8,128)(2,1)S(1)} %pad_maximum_fusion.7), channel_id=1, source_target_pairs={{0,4},{4,0},{8,12},{12,8},{16,20},{20,16},{24,28},{28,24},{1,5},{5... | collective-permute-start | bytes 196616 | tf_op jit(solution)/shard_map/ppermute | solution.py:396
  32.8 1.8 %collective-permute-start.9 = (bf16[160,256]{1,0:T(8,128)(2,1)S(1)}, bf16[160,256]{1,0:T(8,128)(2,1)S(1)}, u32[]{:S(2)}, u32[]{:S(2)}) collective-permute-start(bf16[160,256]{1,0:T(8,128)(2,1)S(1)} %get-tuple-element.126), channel_id=1, source_target_pairs={{0,4},{4,0},{8,12},{12,8},{16,20},{20,16},{24,28},{28,24},{1,5},{5... | collective-permute-start | bytes 245768 | tf_op jit(solution)/shard_map/ppermute | solution.py:396
  34.6 0.1 collective-permute-start.10
  34.7 0.4 collective-permute-done.12
  35.1 0.4 coarse_product.3
  35.4 1.2 %collective-permute-start.13 = (bf16[3,192,128]{2,1,0:T(8,128)(2,1)S(1)}, bf16[3,192,128]{2,1,0:T(8,128)(2,1)S(1)}, u32[]{:S(2)}, u32[]{:S(2)}) collective-permute-start(bf16[3,192,128]{2,1,0:T(8,128)(2,1)S(1)} %get-tuple-element.92), channel_id=1, source_target_pairs={{0,2},{1,3},{2,0},{3,1},{4,6},{5,7},{6,4},{7,5},{8,10},{9,11},{10,... | collective-permute-start | bytes 442376 | tf_op jit(solution)/shard_map/ppermute | solution.py:396
  36.7 1.9 %collective-permute-done.9 = bf16[160,256]{1,0:T(8,128)(2,1)S(1)} collective-permute-done((bf16[160,256]{1,0:T(8,128)(2,1)S(1)}, bf16[160,256]{1,0:T(8,128)(2,1)S(1)}, u32[]{:S(2)}, u32[]{:S(2)}) %collective-permute-start.9) | collective-permute-done | bytes 81952 | tf_op jit(solution)/shard_map/ppermute | solution.py:396
  38.6 2.7 %collective-permute-done.13 = bf16[3,192,128]{2,1,0:T(8,128)(2,1)S(1)} collective-permute-done((bf16[3,192,128]{2,1,0:T(8,128)(2,1)S(1)}, bf16[3,192,128]{2,1,0:T(8,128)(2,1)S(1)}, u32[]{:S(2)}, u32[]{:S(2)}) %collective-permute-start.13) | collective-permute-done | bytes 147488 | tf_op jit(solution)/shard_map/ppermute | solution.py:396
  41.5 0.2 couple.1.couple_ref
  41.7 1.1 %collective-permute-done.14 = bf16[3,192,128]{2,1,0:T(8,128)(2,1)S(1)} collective-permute-done((bf16[3,192,128]{2,1,0:T(8,128)(2,1)S(1)}, bf16[3,192,128]{2,1,0:T(8,128)(2,1)S(1)}, u32[]{:S(2)}, u32[]{:S(2)}) %collective-permute-start.14) | collective-permute-done | bytes 147488 | tf_op jit(solution)/shard_map/ppermute | solution.py:396
  42.9 0.6 update.2
  43.5 1.5 %collective-permute-start.15 = (bf16[64,128]{1,0:T(8,128)(2,1)S(1)}, bf16[64,128]{1,0:T(8,128)(2,1)S(1)}, u32[]{:S(2)}, u32[]{:S(2)}) collective-permute-start(bf16[64,128]{1,0:T(8,128)(2,1)S(1)} %get-tuple-element.93), channel_id=1, source_target_pairs={{0,16},{4,20},{8,24},{12,28},{16,0},{20,4},{24,8},{28,12},{1,17},{... | collective-permute-start | bytes 49160 | tf_op jit(solution)/shard_map/ppermute | solution.py:396
  45.0 2.9 %products.3 = (bf16[1536,128]{1,0:T(8,128)(2,1)S(1)}, bf16[1536,128]{1,0:T(8,128)(2,1)S(1)}, bf16[576,128]{1,0:T(8,128)(2,1)S(1)}) custom-call(bf16[1536,128]{1,0:T(8,128)(2,1)S(1)} %get-tuple-element.94.state_ref, bf16[1536,128]{1,0:T(8,128)(2,1)S(1)} %get-tuple-element.95.res_ref, bf16[1536,1536]{1,0:T(8,128)(2,1)S(1)} %get-tuple-element.78.refs_2_.k_ref, ...), custom_call_target="tpu_custom_call" | custom-call | flops 2415919104 | bytes 9437184 | tf_op jit(solution)/shard_map/products/pallas_call | solution.py:186
  47.9 0.3 collective-permute-done.15
  48.2 1.5 %collective-permute-start.20 = (bf16[2,64,128]{2,1,0:T(8,128)(2,1)S(1)}, bf16[2,64,128]{2,1,0:T(8,128)(2,1)S(1)}, u32[]{:S(2)}, u32[]{:S(2)}) collective-permute-start(bf16[2,64,128]{2,1,0:T(8,128)(2,1)S(1)} %pad_maximum_fusion.14), channel_id=1, source_target_pairs={{0,8},{4,12},{8,0},{12,4},{16,24},{20,28},{24,16},{28,20},{1,9},{5... | collective-permute-start | bytes 98312 | tf_op jit(solution)/shard_map/ppermute | solution.py:396
  49.7 1.5 %collective-permute-start.17 = (bf16[160,128]{1,0:T(8,128)(2,1)S(1)}, bf16[160,128]{1,0:T(8,128)(2,1)S(1)}, u32[]{:S(2)}, u32[]{:S(2)}) collective-permute-start(bf16[160,128]{1,0:T(8,128)(2,1)S(1)} %get-tuple-element.133), channel_id=1, source_target_pairs={{0,3},{1,2},{2,1},{3,0},{4,7},{5,6},{6,5},{7,4},{8,11},{9,10},{10,... | collective-permute-start | bytes 122888 | tf_op jit(solution)/shard_map/ppermute | solution.py:413
  51.2 1.0 %collective-permute-done.20 = bf16[2,64,128]{2,1,0:T(8,128)(2,1)S(1)} collective-permute-done((bf16[2,64,128]{2,1,0:T(8,128)(2,1)S(1)}, bf16[2,64,128]{2,1,0:T(8,128)(2,1)S(1)}, u32[]{:S(2)}, u32[]{:S(2)}) %collective-permute-start.20) | collective-permute-done | bytes 32800 | tf_op jit(solution)/shard_map/ppermute | solution.py:396
  52.2 1.5 %collective-permute-start.21 = (bf16[4,64,128]{2,1,0:T(8,128)(2,1)S(1)}, bf16[4,64,128]{2,1,0:T(8,128)(2,1)S(1)}, u32[]{:S(2)}, u32[]{:S(2)}) collective-permute-start(bf16[4,64,128]{2,1,0:T(8,128)(2,1)S(1)} %pad_maximum_fusion.8), channel_id=1, source_target_pairs={{0,4},{4,0},{8,12},{12,8},{16,20},{20,16},{24,28},{28,24},{1,5},{5... | collective-permute-start | bytes 196616 | tf_op jit(solution)/shard_map/ppermute | solution.py:396
  53.7 2.8 %collective-permute-done.21 = bf16[4,64,128]{2,1,0:T(8,128)(2,1)S(1)} collective-permute-done((bf16[4,64,128]{2,1,0:T(8,128)(2,1)S(1)}, bf16[4,64,128]{2,1,0:T(8,128)(2,1)S(1)}, u32[]{:S(2)}, u32[]{:S(2)}) %collective-permute-start.21) | collective-permute-done | bytes 65568 | tf_op jit(solution)/shard_map/ppermute | solution.py:396
  56.5 0.4 coarse_product.4
  56.9 0.8 %collective-permute-start.22 = (bf16[3,192,128]{2,1,0:T(8,128)(2,1)S(1)}, bf16[3,192,128]{2,1,0:T(8,128)(2,1)S(1)}, u32[]{:S(2)}, u32[]{:S(2)}) collective-permute-start(bf16[3,192,128]{2,1,0:T(8,128)(2,1)S(1)} %get-tuple-element.105), channel_id=1, source_target_pairs={{0,2},{1,3},{2,0},{3,1},{4,6},{5,7},{6,4},{7,5},{8,10},{9,11},{10,... | collective-permute-start | bytes 442376 | tf_op jit(solution)/shard_map/ppermute | solution.py:396
  57.8 1.2 %collective-permute-start.18 = (bf16[160,128]{1,0:T(8,128)(2,1)S(1)}, bf16[160,128]{1,0:T(8,128)(2,1)S(1)}, u32[]{:S(2)}, u32[]{:S(2)}) collective-permute-start(bf16[160,128]{1,0:T(8,128)(2,1)S(1)} %get-tuple-element.140), channel_id=1, source_target_pairs={{0,4},{4,0},{8,12},{12,8},{16,20},{20,16},{24,28},{28,24},{1,5},{5... | collective-permute-start | bytes 122888 | tf_op jit(solution)/shard_map/ppermute | solution.py:396
  59.0 3.2 %collective-permute-done.22 = bf16[3,192,128]{2,1,0:T(8,128)(2,1)S(1)} collective-permute-done((bf16[3,192,128]{2,1,0:T(8,128)(2,1)S(1)}, bf16[3,192,128]{2,1,0:T(8,128)(2,1)S(1)}, u32[]{:S(2)}, u32[]{:S(2)}) %collective-permute-start.22) | collective-permute-done | bytes 147488 | tf_op jit(solution)/shard_map/ppermute | solution.py:396
  62.3 1.3 %collective-permute-done.23 = bf16[3,192,128]{2,1,0:T(8,128)(2,1)S(1)} collective-permute-done((bf16[3,192,128]{2,1,0:T(8,128)(2,1)S(1)}, bf16[3,192,128]{2,1,0:T(8,128)(2,1)S(1)}, u32[]{:S(2)}, u32[]{:S(2)}) %collective-permute-start.23) | collective-permute-done | bytes 147488 | tf_op jit(solution)/shard_map/ppermute | solution.py:396
  63.7 1.3 %update.3 = (bf16[1536,128]{1,0:T(8,128)(2,1)S(1)}, bf16[512,128]{1,0:T(8,128)(2,1)}, bf16[64,128]{1,0:T(8,128)(2,1)S(1)}) custom-call(s32[1]{0:T(128)} %bitcast.1.row_ref, s32[1]{0:T(128)} %bitcast.2.col_ref, bf16[4,160,128]{2,1,0:T(8,128)(2,1)S(1)} %pad_maximum_fusion.2.rows_ref, bf16[1536,128]{1,0:T(8,128)(2,1)S(1)} %get-tuple-element.99.flux_ref, ...), custom_call_target="tpu_custom_call" | custom-call | tf_op jit(solution)/shard_map/update/pallas_call | solution.py:344
  64.9 4.2 %all-to-all-start = ((bf16[8,64,128]{2,1,0:T(8,128)(2,1)}), bf16[8,64,128]{2,1,0:T(8,128)(2,1)S(1)}, u32[]{:S(2)}, u32[]{:S(2)}) async-start(bf16[8,64,128]{2,1,0:T(8,128)(2,1)} %bitcast.25), calls=%async_computation | async-start | bytes 262144 | tf_op jit(solution)/shard_map/all_to_all | solution.py:517
  69.1 0.8 settle.1
  69.9 6.6 %all-to-all-done = bf16[8,64,128]{2,1,0:T(8,128)(2,1)S(1)} async-done(((bf16[8,64,128]{2,1,0:T(8,128)(2,1)}), bf16[8,64,128]{2,1,0:T(8,128)(2,1)S(1)}, u32[]{:S(2)}, u32[]{:S(2)}) %all-to-all-start) | async-done | bytes 131104 | tf_op jit(solution)/shard_map/all_to_all | solution.py:517
  76.5 0.2 coarse_product.5
  76.8 3.3 %collective-permute-done.24 = bf16[128,128]{1,0:T(8,128)(2,1)S(1)} collective-permute-done((bf16[128,128]{1,0:T(8,128)(2,1)S(1)}, bf16[128,128]{1,0:T(8,128)(2,1)S(1)}, u32[]{:S(2)}, u32[]{:S(2)}) %collective-permute-start.24) | collective-permute-done | bytes 32800 | tf_op jit(solution)/shard_map/ppermute | solution.py:396
  80.2 1.2 %collective-permute-done.25 = bf16[64,128]{1,0:T(8,128)(2,1)S(1)} collective-permute-done((bf16[64,128]{1,0:T(8,128)(2,1)S(1)}, bf16[64,128]{1,0:T(8,128)(2,1)S(1)}, u32[]{:S(2)}, u32[]{:S(2)}) %collective-permute-start.25) | collective-permute-done | bytes 16416 | tf_op jit(solution)/shard_map/ppermute | solution.py:396
  81.4 1.0 %finish.1 = bf16[1536,128]{1,0:T(8,128)(2,1)} custom-call(f32[1536,128]{1,0:T(8,128)S(1)} %get-tuple-element.111.before_ref, bf16[1536,128]{1,0:T(8,128)(2,1)S(1)} %get-tuple-element.82.refs_6_.tall_ref, bf16[64,128]{1,0:T(8,128)(2,1)S(1)} %add_convert_fusion.2.own_ref), custom_call_target="tpu_custom_call" | custom-call | tf_op jit(solution)/shard_map/finish/pallas_call | solution.py:314
  (68 shorter events, 1.1 us)
Async XLA Ops:
  0.6 9.5 %collective-permute-start.1 = (bf16[256,512]{1,0:T(8,128)(2,1)}, bf16[256,512]{1,0:T(8,128)(2,1)S(1)}, u32[]{:S(2)}, u32[]{:S(2)}) collective-permute-start(bf16[256,512]{1,0:T(8,128)(2,1)} %refs_0_.2), channel_id=1, source_target_pairs={{0,4},{4,0},{8,12},{12,8},{16,20},{20,16},{24,28},{28,24},{1,5},{5... | collective-permute-start | bytes 786440 | tf_op jit(solution)/shard_map/ppermute | solution.py:396
  9.3 6.5 %copy-start.3 = (s32[1,1,1536]{2,1,0:T(1,128)S(1)}, s32[1,1,1536]{2,1,0:T(1,128)}, u32[]{:S(2)}) copy-start(s32[1,1,1536]{2,1,0:T(1,128)} %param.13) | copy-start | bytes 18436
  9.3 6.5 %copy-start.4 = (bf16[1,1,1536]{2,1,0:T(2,128)(2,1)S(1)}, bf16[1,1,1536]{2,1,0:T(2,128)(2,1)}, u32[]{:S(2)}) copy-start(bf16[1,1,1536]{2,1,0:T(2,128)(2,1)} %param.14) | copy-start | bytes 9220
  9.3 8.6 %copy-start = (bf16[1,1,1536,128]{3,2,1,0:T(8,128)(2,1)S(1)}, bf16[1,1,1536,128]{3,2,1,0:T(8,128)(2,1)}, u32[]{:S(2)}) copy-start(bf16[1,1,1536,128]{3,2,1,0:T(8,128)(2,1)} %param.9) | copy-start | bytes 1179652
  9.3 14.5 %copy-start.2 = (bf16[1,1,1536,128]{3,2,1,0:T(8,128)(2,1)S(1)}, bf16[1,1,1536,128]{3,2,1,0:T(8,128)(2,1)}, u32[]{:S(2)}) copy-start(bf16[1,1,1536,128]{3,2,1,0:T(8,128)(2,1)} %param.8) | copy-start | bytes 1179652
  9.3 1.7 %collective-permute-start = (bf16[160,128]{1,0:T(8,128)(2,1)S(1)}, bf16[160,128]{1,0:T(8,128)(2,1)S(1)}, u32[]{:S(2)}, u32[]{:S(2)}) collective-permute-start(bf16[160,128]{1,0:T(8,128)(2,1)S(1)} %get-tuple-element.136), channel_id=1, source_target_pairs={{0,1},{1,0},{2,3},{3,2},{4,5},{5,4},{6,7},{7,6},{8,9},{9,8},{10,11... | collective-permute-start | bytes 122888 | tf_op jit(solution)/shard_map/ppermute | solution.py:396
  10.2 3.5 %collective-permute-start.2 = (bf16[160,128]{1,0:T(8,128)(2,1)S(1)}, bf16[160,128]{1,0:T(8,128)(2,1)S(1)}, u32[]{:S(2)}, u32[]{:S(2)}) collective-permute-start(bf16[160,128]{1,0:T(8,128)(2,1)S(1)} %get-tuple-element.66), channel_id=1, source_target_pairs={{0,3},{1,2},{2,1},{3,0},{4,7},{5,6},{6,5},{7,4},{8,11},{9,10},{10,... | collective-permute-start | bytes 122888 | tf_op jit(solution)/shard_map/ppermute | solution.py:413
  13.8 4.1 %collective-permute-start.3 = (bf16[160,128]{1,0:T(8,128)(2,1)S(1)}, bf16[160,128]{1,0:T(8,128)(2,1)S(1)}, u32[]{:S(2)}, u32[]{:S(2)}) collective-permute-start(bf16[160,128]{1,0:T(8,128)(2,1)S(1)} %get-tuple-element.150), channel_id=1, source_target_pairs={{0,4},{4,0},{8,12},{12,8},{16,20},{20,16},{24,28},{28,24},{1,5},{5... | collective-permute-start | bytes 122888 | tf_op jit(solution)/shard_map/ppermute | solution.py:396
  15.8 2.0 %collective-permute-start.4 = (bf16[160,128]{1,0:T(8,128)(2,1)S(1)}, bf16[160,128]{1,0:T(8,128)(2,1)S(1)}, u32[]{:S(2)}, u32[]{:S(2)}) collective-permute-start(bf16[160,128]{1,0:T(8,128)(2,1)S(1)} %get-tuple-element.151), channel_id=1, source_target_pairs={{0,1},{1,0},{2,3},{3,2},{4,8},{5,9},{6,10},{7,11},{8,4},{9,5},{10,... | collective-permute-start | bytes 122888 | tf_op jit(solution)/shard_map/ppermute | solution.py:413
  16.0 10.7 %collective-permute-start.6 = (bf16[256,512]{1,0:T(8,128)(2,1)S(1)}, bf16[256,512]{1,0:T(8,128)(2,1)S(1)}, u32[]{:S(2)}, u32[]{:S(2)}) collective-permute-start(bf16[256,512]{1,0:T(8,128)(2,1)S(1)} %collective-permute-done.1.refs_1_), channel_id=1, source_target_pairs={{4,0},{0,8},{8,16},{16,24},{24,28},{28,20},{20,12},{12,4},{5,1},{1... | collective-permute-start | bytes 786440 | tf_op jit(solution)/shard_map/ppermute | solution.py:419
  18.3 8.3 %collective-permute-start.5 = (bf16[64,128]{1,0:T(8,128)(2,1)S(1)}, bf16[64,128]{1,0:T(8,128)(2,1)S(1)}, u32[]{:S(2)}, u32[]{:S(2)}) collective-permute-start(bf16[64,128]{1,0:T(8,128)(2,1)S(1)} %get-tuple-element.76), channel_id=1, source_target_pairs={{0,16},{4,20},{8,24},{12,28},{16,0},{20,4},{24,8},{28,12},{1,17},{... | collective-permute-start | bytes 49160 | tf_op jit(solution)/shard_map/ppermute | solution.py:396
  23.8 11.2 %copy-start.1 = (bf16[256,512]{1,0:T(8,128)(2,1)S(1)}, bf16[256,512]{1,0:T(8,128)(2,1)}, u32[]{:S(2)}) copy-start(bf16[256,512]{1,0:T(8,128)(2,1)} %refs_0_.2) | copy-start | bytes 786436
  26.7 4.0 %collective-permute-start.11 = (bf16[2,64,128]{2,1,0:T(8,128)(2,1)S(1)}, bf16[2,64,128]{2,1,0:T(8,128)(2,1)S(1)}, u32[]{:S(2)}, u32[]{:S(2)}) collective-permute-start(bf16[2,64,128]{2,1,0:T(8,128)(2,1)S(1)} %pad_maximum_fusion.13), channel_id=1, source_target_pairs={{0,8},{4,12},{8,0},{12,4},{16,24},{20,28},{24,16},{28,20},{1,9},{5... | collective-permute-start | bytes 98312 | tf_op jit(solution)/shard_map/ppermute | solution.py:396
  28.3 4.3 %collective-permute-start.7 = (bf16[160,256]{1,0:T(8,128)(2,1)S(1)}, bf16[160,256]{1,0:T(8,128)(2,1)S(1)}, u32[]{:S(2)}, u32[]{:S(2)}) collective-permute-start(bf16[160,256]{1,0:T(8,128)(2,1)S(1)} %get-tuple-element.122), channel_id=1, source_target_pairs={{0,1},{1,0},{2,3},{3,2},{4,5},{5,4},{6,7},{7,6},{8,9},{9,8},{10,11... | collective-permute-start | bytes 245768 | tf_op jit(solution)/shard_map/ppermute | solution.py:396
  28.4 4.2 %collective-permute-start.8 = (bf16[160,256]{1,0:T(8,128)(2,1)S(1)}, bf16[160,256]{1,0:T(8,128)(2,1)S(1)}, u32[]{:S(2)}, u32[]{:S(2)}) collective-permute-start(bf16[160,256]{1,0:T(8,128)(2,1)S(1)} %get-tuple-element.123), channel_id=1, source_target_pairs={{0,3},{1,2},{2,1},{3,0},{4,7},{5,6},{6,5},{7,4},{8,11},{9,10},{10,... | collective-permute-start | bytes 245768 | tf_op jit(solution)/shard_map/ppermute | solution.py:413
  30.7 4.3 %collective-permute-start.12 = (bf16[4,64,128]{2,1,0:T(8,128)(2,1)S(1)}, bf16[4,64,128]{2,1,0:T(8,128)(2,1)S(1)}, u32[]{:S(2)}, u32[]{:S(2)}) collective-permute-start(bf16[4,64,128]{2,1,0:T(8,128)(2,1)S(1)} %pad_maximum_fusion.7), channel_id=1, source_target_pairs={{0,4},{4,0},{8,12},{12,8},{16,20},{20,16},{24,28},{28,24},{1,5},{5... | collective-permute-start | bytes 196616 | tf_op jit(solution)/shard_map/ppermute | solution.py:396
  32.8 5.8 %collective-permute-start.9 = (bf16[160,256]{1,0:T(8,128)(2,1)S(1)}, bf16[160,256]{1,0:T(8,128)(2,1)S(1)}, u32[]{:S(2)}, u32[]{:S(2)}) collective-permute-start(bf16[160,256]{1,0:T(8,128)(2,1)S(1)} %get-tuple-element.126), channel_id=1, source_target_pairs={{0,4},{4,0},{8,12},{12,8},{16,20},{20,16},{24,28},{28,24},{1,5},{5... | collective-permute-start | bytes 245768 | tf_op jit(solution)/shard_map/ppermute | solution.py:396
  34.6 4.0 %collective-permute-start.10 = (bf16[160,256]{1,0:T(8,128)(2,1)S(1)}, bf16[160,256]{1,0:T(8,128)(2,1)S(1)}, u32[]{:S(2)}, u32[]{:S(2)}) collective-permute-start(bf16[160,256]{1,0:T(8,128)(2,1)S(1)} %get-tuple-element.127), channel_id=1, source_target_pairs={{0,1},{1,0},{2,3},{3,2},{4,8},{5,9},{6,10},{7,11},{8,4},{9,5},{10,... | collective-permute-start | bytes 245768 | tf_op jit(solution)/shard_map/ppermute | solution.py:413
  35.4 5.9 %collective-permute-start.13 = (bf16[3,192,128]{2,1,0:T(8,128)(2,1)S(1)}, bf16[3,192,128]{2,1,0:T(8,128)(2,1)S(1)}, u32[]{:S(2)}, u32[]{:S(2)}) collective-permute-start(bf16[3,192,128]{2,1,0:T(8,128)(2,1)S(1)} %get-tuple-element.92), channel_id=1, source_target_pairs={{0,2},{1,3},{2,0},{3,1},{4,6},{5,7},{6,4},{7,5},{8,10},{9,11},{10,... | collective-permute-start | bytes 442376 | tf_op jit(solution)/shard_map/ppermute | solution.py:396
  41.4 1.4 %collective-permute-start.14 = (bf16[3,192,128]{2,1,0:T(8,128)(2,1)S(1)}, bf16[3,192,128]{2,1,0:T(8,128)(2,1)S(1)}, u32[]{:S(2)}, u32[]{:S(2)}) collective-permute-start(bf16[3,192,128]{2,1,0:T(8,128)(2,1)S(1)} %fusion), channel_id=1, source_target_pairs={{0,1},{1,0},{2,3},{3,2},{4,5},{5,4},{6,7},{7,6},{8,9},{9,8},{10,11... | collective-permute-start | bytes 442376 | tf_op jit(solution)/shard_map/ppermute | solution.py:396
  43.5 4.7 %collective-permute-start.15 = (bf16[64,128]{1,0:T(8,128)(2,1)S(1)}, bf16[64,128]{1,0:T(8,128)(2,1)S(1)}, u32[]{:S(2)}, u32[]{:S(2)}) collective-permute-start(bf16[64,128]{1,0:T(8,128)(2,1)S(1)} %get-tuple-element.93), channel_id=1, source_target_pairs={{0,16},{4,20},{8,24},{12,28},{16,0},{20,4},{24,8},{28,12},{1,17},{... | collective-permute-start | bytes 49160 | tf_op jit(solution)/shard_map/ppermute | solution.py:396
  48.2 4.0 %collective-permute-start.20 = (bf16[2,64,128]{2,1,0:T(8,128)(2,1)S(1)}, bf16[2,64,128]{2,1,0:T(8,128)(2,1)S(1)}, u32[]{:S(2)}, u32[]{:S(2)}) collective-permute-start(bf16[2,64,128]{2,1,0:T(8,128)(2,1)S(1)} %pad_maximum_fusion.14), channel_id=1, source_target_pairs={{0,8},{4,12},{8,0},{12,4},{16,24},{20,28},{24,16},{28,20},{1,9},{5... | collective-permute-start | bytes 98312 | tf_op jit(solution)/shard_map/ppermute | solution.py:396
  49.7 4.0 %collective-permute-start.16 = (bf16[160,128]{1,0:T(8,128)(2,1)S(1)}, bf16[160,128]{1,0:T(8,128)(2,1)S(1)}, u32[]{:S(2)}, u32[]{:S(2)}) collective-permute-start(bf16[160,128]{1,0:T(8,128)(2,1)S(1)} %get-tuple-element.132), channel_id=1, source_target_pairs={{0,1},{1,0},{2,3},{3,2},{4,5},{5,4},{6,7},{7,6},{8,9},{9,8},{10,11... | collective-permute-start | bytes 122888 | tf_op jit(solution)/shard_map/ppermute | solution.py:396
  49.7 4.0 %collective-permute-start.17 = (bf16[160,128]{1,0:T(8,128)(2,1)S(1)}, bf16[160,128]{1,0:T(8,128)(2,1)S(1)}, u32[]{:S(2)}, u32[]{:S(2)}) collective-permute-start(bf16[160,128]{1,0:T(8,128)(2,1)S(1)} %get-tuple-element.133), channel_id=1, source_target_pairs={{0,3},{1,2},{2,1},{3,0},{4,7},{5,6},{6,5},{7,4},{8,11},{9,10},{10,... | collective-permute-start | bytes 122888 | tf_op jit(solution)/shard_map/ppermute | solution.py:413
  52.2 4.3 %collective-permute-start.21 = (bf16[4,64,128]{2,1,0:T(8,128)(2,1)S(1)}, bf16[4,64,128]{2,1,0:T(8,128)(2,1)S(1)}, u32[]{:S(2)}, u32[]{:S(2)}) collective-permute-start(bf16[4,64,128]{2,1,0:T(8,128)(2,1)S(1)} %pad_maximum_fusion.8), channel_id=1, source_target_pairs={{0,4},{4,0},{8,12},{12,8},{16,20},{20,16},{24,28},{28,24},{1,5},{5... | collective-permute-start | bytes 196616 | tf_op jit(solution)/shard_map/ppermute | solution.py:396
  56.9 5.2 %collective-permute-start.22 = (bf16[3,192,128]{2,1,0:T(8,128)(2,1)S(1)}, bf16[3,192,128]{2,1,0:T(8,128)(2,1)S(1)}, u32[]{:S(2)}, u32[]{:S(2)}) collective-permute-start(bf16[3,192,128]{2,1,0:T(8,128)(2,1)S(1)} %get-tuple-element.105), channel_id=1, source_target_pairs={{0,2},{1,3},{2,0},{3,1},{4,6},{5,7},{6,4},{7,5},{8,10},{9,11},{10,... | collective-permute-start | bytes 442376 | tf_op jit(solution)/shard_map/ppermute | solution.py:396
  57.8 4.5 %collective-permute-start.18 = (bf16[160,128]{1,0:T(8,128)(2,1)S(1)}, bf16[160,128]{1,0:T(8,128)(2,1)S(1)}, u32[]{:S(2)}, u32[]{:S(2)}) collective-permute-start(bf16[160,128]{1,0:T(8,128)(2,1)S(1)} %get-tuple-element.140), channel_id=1, source_target_pairs={{0,4},{4,0},{8,12},{12,8},{16,20},{20,16},{24,28},{28,24},{1,5},{5... | collective-permute-start | bytes 122888 | tf_op jit(solution)/shard_map/ppermute | solution.py:396
  59.0 3.3 %collective-permute-start.19 = (bf16[160,128]{1,0:T(8,128)(2,1)S(1)}, bf16[160,128]{1,0:T(8,128)(2,1)S(1)}, u32[]{:S(2)}, u32[]{:S(2)}) collective-permute-start(bf16[160,128]{1,0:T(8,128)(2,1)S(1)} %get-tuple-element.141), channel_id=1, source_target_pairs={{0,1},{1,0},{2,3},{3,2},{4,8},{5,9},{6,10},{7,11},{8,4},{9,5},{10,... | collective-permute-start | bytes 122888 | tf_op jit(solution)/shard_map/ppermute | solution.py:413
  62.2 1.4 %collective-permute-start.23 = (bf16[3,192,128]{2,1,0:T(8,128)(2,1)S(1)}, bf16[3,192,128]{2,1,0:T(8,128)(2,1)S(1)}, u32[]{:S(2)}, u32[]{:S(2)}) collective-permute-start(bf16[3,192,128]{2,1,0:T(8,128)(2,1)S(1)} %fusion.1), channel_id=1, source_target_pairs={{0,1},{1,0},{2,3},{3,2},{4,5},{5,4},{6,7},{7,6},{8,9},{9,8},{10,11... | collective-permute-start | bytes 442376 | tf_op jit(solution)/shard_map/ppermute | solution.py:396
  64.9 11.5 %all-to-all-start = ((bf16[8,64,128]{2,1,0:T(8,128)(2,1)}), bf16[8,64,128]{2,1,0:T(8,128)(2,1)S(1)}, u32[]{:S(2)}, u32[]{:S(2)}) async-start(bf16[8,64,128]{2,1,0:T(8,128)(2,1)} %bitcast.25), calls=%async_computation | async-start | bytes 262144 | tf_op jit(solution)/shard_map/all_to_all | solution.py:517
  76.7 3.4 %collective-permute-start.24 = (bf16[128,128]{1,0:T(8,128)(2,1)S(1)}, bf16[128,128]{1,0:T(8,128)(2,1)S(1)}, u32[]{:S(2)}, u32[]{:S(2)}) collective-permute-start(bf16[128,128]{1,0:T(8,128)(2,1)S(1)} %bitcast.48), channel_id=1, source_target_pairs={{0,3},{1,2},{2,1},{3,0},{4,7},{5,6},{6,5},{7,4},{8,11},{9,10},{10,... | collective-permute-start | bytes 98312 | tf_op jit(solution)/shard_map/ppermute | solution.py:396
  80.2 1.2 %collective-permute-start.25 = (bf16[64,128]{1,0:T(8,128)(2,1)S(1)}, bf16[64,128]{1,0:T(8,128)(2,1)S(1)}, u32[]{:S(2)}, u32[]{:S(2)}) collective-permute-start(bf16[64,128]{1,0:T(8,128)(2,1)S(1)} %select_convert_fusion), channel_id=1, source_target_pairs={{0,1},{1,0},{2,3},{3,2},{4,5},{5,4},{6,7},{7,6},{8,9},{9,8},{10,11... | collective-permute-start | bytes 49160 | tf_op jit(solution)/shard_map/ppermute | solution.py:396
